TPU v7x, 128 devices: a whole 4x4x4 slice. The times are simulated.
128 devices in a mesh: dp: 8 (over z_lo, x), seq: 16 (over y, z_hi, core).
Axes of the slice: x: 4, y: 4, z: 4 (z_hi: 2, z_lo: 2; z = z_hi * 2 + z_lo), core: 2. Of those that a mesh axis runs over, the one named last changes fastest.
Arguments:
- tokens: bfloat16 [8, 2048, 512], P('dp', 'seq'), may hold values from -6 to 6
- lengths: int32 [8], P('dp'), may hold values from 1408 to 2048, as said below
- norm1_gain: bfloat16 [512], P(('dp', 'seq')), may hold values from 0.099609375 to 1.8984375
- norm1_bias: bfloat16 [512], P(('dp', 'seq')), may hold values from -2 to 2
- w_query: bfloat16 [512, 512], P(('dp', 'seq')), may hold values from -0.375 to 0.375
- w_key: bfloat16 [512, 512], P(('dp', 'seq')), may hold values from -0.375 to 0.375
- w_value: bfloat16 [512, 512], P(('dp', 'seq')), may hold values from -0.25 to 0.25
- w_output: bfloat16 [512, 512], P(('dp', 'seq')), may hold values from -1.5 to 1.5
- norm2_gain: bfloat16 [512], P(('dp', 'seq')), may hold values from 0.099609375 to 1.8984375
- norm2_bias: bfloat16 [512], P(('dp', 'seq')), may hold values from -2 to 2
- w_gate: bfloat16 [512, 2048], P(('dp', 'seq')), may hold values from -0.25 to 0.25
- w_up: bfloat16 [512, 2048], P(('dp', 'seq')), may hold values from -0.25 to 0.25
- w_down: bfloat16 [2048, 512], P(('dp', 'seq')), may hold values from -0.25 to 0.25
- cotangent: bfloat16 [8, 2048, 512], P('dp', 'seq'), may hold values from -6 to 6
Outputs:
- layer_output: bfloat16 [8, 2048, 512], P('dp', 'seq')
- grad_tokens: float32 [8, 2048, 512], P('dp', 'seq')
- grad_norm1_gain: float32 [512], P(('dp', 'seq'))
- grad_norm1_bias: float32 [512], P(('dp', 'seq'))
- grad_w_query: float32 [512, 512], P(('dp', 'seq'))
- grad_w_key: float32 [512, 512], P(('dp', 'seq'))
- grad_w_value: float32 [512, 512], P(('dp', 'seq'))
- grad_w_output: float32 [512, 512], P(('dp', 'seq'))
- grad_norm2_gain: float32 [512], P(('dp', 'seq'))
- grad_norm2_bias: float32 [512], P(('dp', 'seq'))
- grad_w_gate: float32 [512, 2048], P(('dp', 'seq'))
- grad_w_up: float32 [512, 2048], P(('dp', 'seq'))
- grad_w_down: float32 [2048, 512], P(('dp', 'seq'))
Inputs may be any that keep to these rules, and one draw needn't show every extreme that they name: `lengths`: in each group of 1 consecutive windows one window is longer than 1920, and some window has length 2048.
All inputs are finite; a program needn't handle non-finite values.
Results may differ from a plain program's by a relative error of at most 0.025.
Values may be sent and summed in bfloat16 or wider, within the bound.
No kernel may reach another device: no remote copies, remote signals or barrier semaphores. Data moves between devices by JAX's collectives and lax.ppermute only.
A program may use at most 128 MiB of HBM per device.

v0:
```python
import jax
import jax.numpy as jnp
from jax import lax
from jax.sharding import PartitionSpec as P

HEAD = 32


eps_norm = 1e-05
masked_score = -1000000000.0


def rotate(values, positions, sign_value):
    half_size = HEAD // 2
    frequency = 10000.0 ** (-2.0 * jnp.arange(half_size, dtype=jnp.float32) / HEAD)
    angles = positions.astype(jnp.float32)[:, None] * frequency[None, :]
    cosine = jnp.cos(angles)[:, None, :]
    sine_part = sign_value * jnp.sin(angles)[:, None, :]
    shaped = values.reshape(values.shape[0], -1, HEAD)
    first_half = shaped[..., :half_size]
    second_half = shaped[..., half_size:]
    turned = jnp.concatenate(
        [
            first_half * cosine - second_half * sine_part,
            second_half * cosine + first_half * sine_part,
        ],
        -1,
    )
    return turned.reshape(values.shape)


def norm_forward(values, norm_gain, norm_bias):
    row_mean = jnp.mean(values, -1, keepdims=True)
    centered = values - row_mean
    variance = jnp.mean(centered * centered, -1, keepdims=True)
    inv_std = lax.rsqrt(variance + eps_norm)
    scaled = centered * inv_std
    return (scaled * norm_gain + norm_bias, scaled, inv_std)


def norm_backward(grad_normed, scaled, inv_std, norm_gain):
    grad_scaled = grad_normed * norm_gain
    return inv_std * (
        grad_scaled
        - jnp.mean(grad_scaled, -1, keepdims=True)
        - scaled * jnp.mean(grad_scaled * scaled, -1, keepdims=True)
    )


def score_block(queries, keys_all, length):
    query_heads = queries.reshape(queries.shape[0], -1, HEAD)
    key_heads = keys_all.reshape(keys_all.shape[0], -1, HEAD)
    scores = jnp.einsum(
        "qhd,khd->hqk", query_heads, key_heads, preferred_element_type=jnp.float32
    ) * HEAD ** (-0.5)
    key_index = jnp.arange(keys_all.shape[0])
    return jnp.where(key_index[None, None, :] < length, scores, masked_score)


def attend_forward(inputs):
    queries, keys_all, values_all, length = inputs
    scores = score_block(queries, keys_all, length)
    row_max = jnp.max(scores, -1, keepdims=True)
    weights = jnp.exp(scores - row_max)
    row_sum = jnp.sum(weights, -1, keepdims=True)
    soft_low = (weights / row_sum).astype(jnp.bfloat16)
    value_heads = values_all.reshape(values_all.shape[0], -1, HEAD)
    mixed_rows = jnp.einsum(
        "hqk,khd->qhd", soft_low, value_heads, preferred_element_type=jnp.float32
    )
    return (mixed_rows.reshape(queries.shape[0], -1), row_max, row_sum)


def attend_backward(inputs):
    queries, keys_all, values_all, length, row_max, row_sum, grad_mixed = inputs
    scores = score_block(queries, keys_all, length)
    soft_weights = jnp.exp(scores - row_max) / row_sum
    query_heads = queries.reshape(queries.shape[0], -1, HEAD)
    key_heads = keys_all.reshape(keys_all.shape[0], -1, HEAD)
    value_heads = values_all.reshape(values_all.shape[0], -1, HEAD)
    grad_heads = grad_mixed.reshape(grad_mixed.shape[0], -1, HEAD)
    grad_soft = jnp.einsum(
        "qhd,khd->hqk", grad_heads, value_heads, preferred_element_type=jnp.float32
    )
    inner_sum = jnp.sum(soft_weights * grad_soft, -1, keepdims=True)
    grad_scores = (soft_weights * (grad_soft - inner_sum)).astype(jnp.bfloat16)
    score_scale = HEAD ** (-0.5)
    grad_query = (
        jnp.einsum("hqk,khd->qhd", grad_scores, key_heads, preferred_element_type=jnp.float32)
        * score_scale
    )
    grad_key = (
        jnp.einsum("hqk,qhd->khd", grad_scores, query_heads, preferred_element_type=jnp.float32)
        * score_scale
    )
    grad_value = jnp.einsum(
        "hqk,qhd->khd",
        soft_weights.astype(jnp.bfloat16),
        grad_heads,
        preferred_element_type=jnp.float32,
    )
    return (
        grad_query.reshape(queries.shape[0], -1),
        grad_key.reshape(keys_all.shape[0], -1),
        grad_value.reshape(keys_all.shape[0], -1),
    )


def shards(
    tokens,
    lengths,
    norm1_gain,
    norm1_bias,
    w_query,
    w_key,
    w_value,
    w_output,
    norm2_gain,
    norm2_bias,
    w_gate,
    w_up,
    w_down,
    cotangent,
):
    gathered = (
        lax.all_gather(norm1_gain, ("dp", "seq"), axis=0, tiled=True),
        lax.all_gather(norm1_bias, ("dp", "seq"), axis=0, tiled=True),
        lax.all_gather(w_query, ("dp", "seq"), axis=0, tiled=True),
        lax.all_gather(w_key, ("dp", "seq"), axis=0, tiled=True),
        lax.all_gather(w_value, ("dp", "seq"), axis=0, tiled=True),
        lax.all_gather(w_output, ("dp", "seq"), axis=0, tiled=True),
        lax.all_gather(norm2_gain, ("dp", "seq"), axis=0, tiled=True),
        lax.all_gather(norm2_bias, ("dp", "seq"), axis=0, tiled=True),
        lax.all_gather(w_gate, ("dp", "seq"), axis=0, tiled=True),
        lax.all_gather(w_up, ("dp", "seq"), axis=0, tiled=True),
        lax.all_gather(w_down, ("dp", "seq"), axis=0, tiled=True),
    )
    (
        gain_one,
        bias_one,
        query_full,
        key_full,
        value_full,
        output_full,
        gain_two,
        bias_two,
        gate_full,
        up_full,
        down_full,
    ) = gathered
    window_count, row_count, model_width = tokens.shape
    key_start = lax.axis_index("seq") * row_count
    own_place = key_start + jnp.arange(row_count)
    positions = jnp.tile(own_place, window_count)
    row_live = (own_place[None, :] < lengths[:, None]).astype(jnp.float32).reshape(-1, 1)
    inputs_flat = tokens.astype(jnp.float32).reshape(-1, model_width)
    normed_first, scaled_first, inv_first = norm_forward(
        inputs_flat, gain_one.astype(jnp.float32), bias_one.astype(jnp.float32)
    )
    normed_first = normed_first.astype(jnp.bfloat16)
    queries = rotate(
        jnp.dot(normed_first, query_full, preferred_element_type=jnp.float32), positions, 1.0
    ).astype(jnp.bfloat16)
    keys_own = rotate(
        jnp.dot(normed_first, key_full, preferred_element_type=jnp.float32), positions, 1.0
    ).astype(jnp.bfloat16)
    values_own = jnp.dot(normed_first, value_full, preferred_element_type=jnp.float32).astype(
        jnp.bfloat16
    )
    queries_win = queries.reshape(window_count, row_count, model_width)
    keys_win = keys_own.reshape(window_count, row_count, model_width)
    values_win = values_own.reshape(window_count, row_count, model_width)
    keys_all, values_all = (
        lax.all_gather(keys_win, "seq", axis=1, tiled=True),
        lax.all_gather(values_win, "seq", axis=1, tiled=True),
    )
    mixed_rows, row_max, row_sum = lax.map(
        attend_forward, (queries_win, keys_all, values_all, lengths)
    )
    mixed_low = mixed_rows.reshape(-1, model_width).astype(jnp.bfloat16)
    middle = inputs_flat + jnp.dot(mixed_low, output_full, preferred_element_type=jnp.float32)
    normed_second, scaled_second, inv_second = norm_forward(
        middle, gain_two.astype(jnp.float32), bias_two.astype(jnp.float32)
    )
    normed_second = normed_second.astype(jnp.bfloat16)
    gate_lin = jnp.dot(normed_second, gate_full, preferred_element_type=jnp.float32)
    up_lin = jnp.dot(normed_second, up_full, preferred_element_type=jnp.float32)
    gate_sigmoid = jax.nn.sigmoid(gate_lin)
    hidden = (gate_lin * gate_sigmoid * up_lin).astype(jnp.bfloat16)
    result = (middle + jnp.dot(hidden, down_full, preferred_element_type=jnp.float32)) * row_live
    layer_output = result.astype(jnp.bfloat16).reshape(window_count, row_count, model_width)
    back_rows = (
        lax.all_gather(norm1_gain, ("dp", "seq"), axis=0, tiled=True),
        lax.all_gather(norm1_bias, ("dp", "seq"), axis=0, tiled=True),
        lax.all_gather(w_query, ("dp", "seq"), axis=0, tiled=True),
        lax.all_gather(w_key, ("dp", "seq"), axis=0, tiled=True),
        lax.all_gather(w_value, ("dp", "seq"), axis=0, tiled=True),
        lax.all_gather(w_output, ("dp", "seq"), axis=0, tiled=True),
        lax.all_gather(norm2_gain, ("dp", "seq"), axis=0, tiled=True),
        lax.all_gather(norm2_bias, ("dp", "seq"), axis=0, tiled=True),
        lax.all_gather(w_gate, ("dp", "seq"), axis=0, tiled=True),
        lax.all_gather(w_up, ("dp", "seq"), axis=0, tiled=True),
        lax.all_gather(w_down, ("dp", "seq"), axis=0, tiled=True),
    )
    (
        gain_one_b,
        bias_one_b,
        query_back,
        key_back,
        value_back,
        output_back,
        gain_two_b,
        bias_two_b,
        gate_back,
        up_back,
        down_back,
    ) = back_rows
    grad_out = cotangent.astype(jnp.float32).reshape(-1, model_width) * row_live
    grad_out_low = grad_out.astype(jnp.bfloat16)
    grad_down = jnp.einsum("tf,td->fd", hidden, grad_out_low, preferred_element_type=jnp.float32)
    grad_hidden = jnp.einsum(
        "td,fd->tf", grad_out_low, down_back, preferred_element_type=jnp.float32
    )
    grad_up_lin = (grad_hidden * gate_lin * gate_sigmoid).astype(jnp.bfloat16)
    grad_gate_lin = (
        grad_hidden * up_lin * gate_sigmoid * (1.0 + gate_lin * (1.0 - gate_sigmoid))
    ).astype(jnp.bfloat16)
    grad_gate = jnp.einsum(
        "td,tf->df", normed_second, grad_gate_lin, preferred_element_type=jnp.float32
    )
    grad_up = jnp.einsum(
        "td,tf->df", normed_second, grad_up_lin, preferred_element_type=jnp.float32
    )
    grad_second = jnp.einsum(
        "tf,df->td", grad_gate_lin, gate_back, preferred_element_type=jnp.float32
    ) + jnp.einsum("tf,df->td", grad_up_lin, up_back, preferred_element_type=jnp.float32)
    grad_gain_two = jnp.sum(grad_second * scaled_second, 0)
    grad_bias_two = jnp.sum(grad_second, 0)
    grad_middle = grad_out + norm_backward(
        grad_second, scaled_second, inv_second, gain_two_b.astype(jnp.float32)
    )
    grad_middle_low = grad_middle.astype(jnp.bfloat16)
    grad_output_w = jnp.einsum(
        "td,te->de", mixed_low, grad_middle_low, preferred_element_type=jnp.float32
    )
    grad_mixed = jnp.einsum(
        "te,de->td", grad_middle_low, output_back, preferred_element_type=jnp.float32
    ).astype(jnp.bfloat16)
    grad_mixed_win = grad_mixed.reshape(window_count, row_count, model_width)
    keys_back, values_back = (
        lax.all_gather(keys_win, "seq", axis=1, tiled=True),
        lax.all_gather(values_win, "seq", axis=1, tiled=True),
    )
    grad_query_rot, grad_key_part, grad_value_part = lax.map(
        attend_backward,
        (queries_win, keys_back, values_back, lengths, row_max, row_sum, grad_mixed_win),
    )
    grad_key_sum, grad_value_sum = (
        lax.psum_scatter(
            grad_key_part.astype(jnp.bfloat16), "seq", scatter_dimension=1, tiled=True
        ).astype(jnp.float32),
        lax.psum_scatter(
            grad_value_part.astype(jnp.bfloat16), "seq", scatter_dimension=1, tiled=True
        ).astype(jnp.float32),
    )
    grad_query_lin = rotate(grad_query_rot.reshape(-1, model_width), positions, -1.0).astype(
        jnp.bfloat16
    )
    grad_key_lin = rotate(grad_key_sum.reshape(-1, model_width), positions, -1.0).astype(
        jnp.bfloat16
    )
    grad_value_lin = grad_value_sum.reshape(-1, model_width).astype(jnp.bfloat16)
    grad_query_w = jnp.einsum(
        "td,te->de", normed_first, grad_query_lin, preferred_element_type=jnp.float32
    )
    grad_key_w = jnp.einsum(
        "td,te->de", normed_first, grad_key_lin, preferred_element_type=jnp.float32
    )
    grad_value_w = jnp.einsum(
        "td,te->de", normed_first, grad_value_lin, preferred_element_type=jnp.float32
    )
    grad_first = jnp.einsum(
        "te,de->td", grad_query_lin, query_back, preferred_element_type=jnp.float32
    )
    grad_first = grad_first + jnp.einsum(
        "te,de->td", grad_key_lin, key_back, preferred_element_type=jnp.float32
    )
    grad_first = grad_first + jnp.einsum(
        "te,de->td", grad_value_lin, value_back, preferred_element_type=jnp.float32
    )
    grad_gain_one = jnp.sum(grad_first * scaled_first, 0)
    grad_bias_one = jnp.sum(grad_first, 0)
    grad_input = grad_middle + norm_backward(
        grad_first, scaled_first, inv_first, gain_one_b.astype(jnp.float32)
    )
    owned = (
        lax.psum_scatter(grad_gain_one, ("dp", "seq"), scatter_dimension=0, tiled=True),
        lax.psum_scatter(grad_bias_one, ("dp", "seq"), scatter_dimension=0, tiled=True),
        lax.psum_scatter(grad_query_w, ("dp", "seq"), scatter_dimension=0, tiled=True),
        lax.psum_scatter(grad_key_w, ("dp", "seq"), scatter_dimension=0, tiled=True),
        lax.psum_scatter(grad_value_w, ("dp", "seq"), scatter_dimension=0, tiled=True),
        lax.psum_scatter(grad_output_w, ("dp", "seq"), scatter_dimension=0, tiled=True),
        lax.psum_scatter(grad_gain_two, ("dp", "seq"), scatter_dimension=0, tiled=True),
        lax.psum_scatter(grad_bias_two, ("dp", "seq"), scatter_dimension=0, tiled=True),
        lax.psum_scatter(grad_gate, ("dp", "seq"), scatter_dimension=0, tiled=True),
        lax.psum_scatter(grad_up, ("dp", "seq"), scatter_dimension=0, tiled=True),
        lax.psum_scatter(grad_down, ("dp", "seq"), scatter_dimension=0, tiled=True),
    )
    return (layer_output, grad_input.reshape(window_count, row_count, model_width)) + tuple(owned)


def solution(mesh):
    return jax.shard_map(
        shards,
        mesh=mesh,
        in_specs=(
            P("dp", "seq", None),
            P("dp"),
            P(("dp", "seq")),
            P(("dp", "seq")),
            P(("dp", "seq"), None),
            P(("dp", "seq"), None),
            P(("dp", "seq"), None),
            P(("dp", "seq"), None),
            P(("dp", "seq")),
            P(("dp", "seq")),
            P(("dp", "seq"), None),
            P(("dp", "seq"), None),
            P(("dp", "seq"), None),
            P("dp", "seq", None),
        ),
        out_specs=(
            P("dp", "seq", None),
            P("dp", "seq", None),
            P(("dp", "seq")),
            P(("dp", "seq")),
            P(("dp", "seq"), None),
            P(("dp", "seq"), None),
            P(("dp", "seq"), None),
            P(("dp", "seq"), None),
            P(("dp", "seq")),
            P(("dp", "seq")),
            P(("dp", "seq"), None),
            P(("dp", "seq"), None),
            P(("dp", "seq"), None),
        ),
        check_vma=False,
    )
```

profile of v0, /device:TPU:1, one launch (start us, length us, event | category | flops | bytes accessed | tf_op | source)
XLA Modules:
  0.0 2251.2 jit_solution(9715163327178578314)
XLA Ops:
  7.3 181.8 %all-gather.1 = bf16[128,4,512]{2,1,0:T(4,128)(2,1)S(1)} all-gather(bf16[1,4,512]{2,1,0:T(4,128)(2,1)} %bitcast.181), channel_id=1, replica_groups=mesh['dp'=8,'seq'=16] {'dp','seq'}, dimensions={0}, use_global_device_ids=true | all-gather | bytes 528384 | tf_op jit(solution)/shard_map/all_gather | solution.py:130
  192.7 61.8 %all-reduce.16 = (bf16[512]{0:T(512)(128)(2,1)S(1)}, bf16[512]{0:T(512)(128)(2,1)S(1)}, bf16[512]{0:T(512)(128)(2,1)S(1)}, bf16[512]{0:T(512)(128)(2,1)S(1)}) all-reduce(bf16[512]{0:T(512)(128)(2,1)S(1)} %dynamic-update-slice.1, bf16[512]{0:T(512)(128)(2,1)S(1)} %dynamic-update-slice, ...), channel_id=1, replica_groups=mesh['dp'=8,'seq'=16] {'dp','seq'}, use_global_device_ids=true, to_apply=%add.1 | all-reduce | flops 2048 | bytes 8192
  258.6 175.6 %all-gather.2 = bf16[128,4,512]{2,1,0:T(4,128)(2,1)S(1)} all-gather(bf16[1,4,512]{2,1,0:T(4,128)(2,1)} %bitcast.182), channel_id=1, replica_groups=mesh['dp'=8,'seq'=16] {'dp','seq'}, dimensions={0}, use_global_device_ids=true | all-gather | bytes 528384 | tf_op jit(solution)/shard_map/all_gather | solution.py:128
  434.5 172.0 %all-gather.3 = bf16[128,4,512]{2,1,0:T(4,128)(2,1)S(1)} all-gather(bf16[1,4,512]{2,1,0:T(4,128)(2,1)S(1)} %bitcast.183), channel_id=1, replica_groups=mesh['dp'=8,'seq'=16] {'dp','seq'}, dimensions={0}, use_global_device_ids=true | all-gather | bytes 528384 | tf_op jit(solution)/shard_map/all_gather | solution.py:129
  611.8 174.8 %all-gather.4 = bf16[128,4,512]{2,1,0:T(4,128)(2,1)S(1)} all-gather(bf16[1,4,512]{2,1,0:T(4,128)(2,1)S(1)} %bitcast.184), channel_id=1, replica_groups=mesh['dp'=8,'seq'=16] {'dp','seq'}, dimensions={0}, use_global_device_ids=true | all-gather | bytes 528384 | tf_op jit(solution)/shard_map/all_gather | solution.py:131
  786.8 4.2 copy.37
  791.0 9.9 fusion.81
  800.9 9.5 fusion.17
  811.3 38.2 %all-gather.19.cloned.1.call-done = bf16[128,4,2048]{2,1,0:T(4,128)(2,1)} async-done(((bf16[1,4,2048]{2,1,0:T(4,128)(2,1)}), bf16[128,4,2048]{2,1,0:T(4,128)(2,1)}) %all-gather.19.cloned.1.call-update) | async-done | bytes 2097168 | tf_op jit(solution)/shard_map/all_gather | solution.py:134
  849.5 2.5 reshape.463
  852.1 191.9 %all-gather.21.cloned.1.call-done = bf16[128,4,2048]{2,1,0:T(4,128)(2,1)} async-done(((bf16[1,4,2048]{2,1,0:T(4,128)(2,1)}), bf16[128,4,2048]{2,1,0:T(4,128)(2,1)}) %all-gather.21.cloned.1.call-update) | async-done | bytes 2097168 | tf_op jit(solution)/shard_map/all_gather | solution.py:135
  1044.0 4.0 reshape.465
  1051.3 187.1 %all-gather.15.cloned.1.call-done = bf16[2048,512]{1,0:T(8,128)(2,1)} async-done(((bf16[16,512]{1,0:T(8,128)(2,1)}), bf16[2048,512]{1,0:T(8,128)(2,1)}) %all-gather.15.cloned.1.call-update) | async-done | bytes 2097168 | tf_op jit(solution)/shard_map/all_gather | solution.py:136
  1238.4 4.1 multiply_convert_fusion.2
  1246.8 16.7 multiply_reduce_fusion
  1263.5 7.5 multiply_convert_fusion
  1272.2 2.0 copy-done
  1274.3 7.6 copy.41
  1281.9 4.1 copy.50
  1286.1 7.1 fusion.9
  1293.2 7.6 copy.43
  1300.7 4.3 copy.49
  1306.5 2.7 fusion.87
  1309.2 2.8 fusion.88
  1311.9 6.3 fusion.14
  1318.3 35.8 %reduce-scatter.10.cloned.1.call-done = bf16[128,512]{1,0:T(8,128)(2,1)} async-done(((bf16[2048,512]{1,0:T(8,128)(2,1)}), bf16[128,512]{1,0:T(8,128)(2,1)}) %reduce-scatter.10.cloned.1.call-update) | async-done | bytes 131088
  1355.3 72.5 %reduce-scatter.12.cloned.1.call-done = bf16[128,512]{1,0:T(8,128)(2,1)} async-done(((bf16[2048,512]{1,0:T(8,128)(2,1)}), bf16[128,512]{1,0:T(8,128)(2,1)}) %reduce-scatter.12.cloned.1.call-update) | async-done | bytes 131088
  1434.5 2.7 fusion.63
  1437.3 2.8 fusion.20
  1441.2 66.5 %all-reduce.14 = (f32[512]{0:T(512)S(1)}, f32[512]{0:T(512)S(1)}, f32[512]{0:T(512)S(1)}, f32[512]{0:T(512)S(1)}) all-reduce(f32[512]{0:T(512)S(1)} %get-tuple-element.61, f32[512]{0:T(512)S(1)} %get-tuple-element.77, f32[512]{0:T(512)S(1)} %copy-done.34, f32[512]{0:T(512)S(1)} %copy-done.35), channel_id=5, replica_groups=mesh['dp'=8,'seq'=16] {'dp','seq'}, use_global_device_ids=true, to_apply=%region_14.15.clone | all-reduce | flops 2048 | bytes 16384
  1510.9 95.2 %all-reduce.19.cloned.1.call-done = (f32[512,512]{1,0:T(8,128)}, f32[512,512]{1,0:T(8,128)}, f32[512,512]{1,0:T(8,128)}, f32[512,512]{1,0:T(8,128)}, f32[512,2048]{1,0:T(8,128)}, /*index=5*/f32[512,2048]{1,0:T(8,128)}) async-done(((f32[512,512]{1,0:T(8,128)}, f32[512,512]{1,0:T(8,128)}, f32[512,512]{1,0:T(8,128)}, f32[512,512]{1,0:T(8,128)}, f32[512,2048]{1,0:T(8,128)}, /*index=5*/f32[512,2048]{1,0:T(8,128)}), ...) | async-done | bytes 12582928
  1614.3 630.4 %reduce-scatter.8.cloned.1.call-done = f32[16,512]{1,0:T(8,128)} async-done(((f32[2048,512]{1,0:T(8,128)}), f32[16,512]{1,0:T(8,128)}) %reduce-scatter.8.cloned.1.call-update) | async-done | bytes 32784 | tf_op jit(solution)/shard_map/reduce_scatter | solution.py:307
  (192 shorter events, 44.2 us)
Async XLA Ops:
  7.2 600.4 %copy-start.3 = (bf16[1,128,512]{2,1,0:T(8,128)(2,1)S(1)}, bf16[1,128,512]{2,1,0:T(8,128)(2,1)}, u32[]{:S(2)}) copy-start(bf16[1,128,512]{2,1,0:T(8,128)(2,1)} %param.14) | copy-start | bytes 393220
  7.2 427.3 %copy-start.43 = (bf16[4,512]{1,0:T(4,128)(2,1)S(1)}, bf16[4,512]{1,0:T(4,128)(2,1)}, u32[]{:S(2)}) copy-start(bf16[4,512]{1,0:T(4,128)(2,1)} %param.19) | copy-start | bytes 12292
  7.2 779.6 %all-gather.17.cloned.1.call-start = ((), (), s32[]{:S(2)}) async-start(), calls=%async_computation.6 | async-start | bytes 2228224 | tf_op jit(solution)/shard_map/all_gather | solution.py:175
  189.2 245.3 %copy-start.11 = (bf16[512,512]{1,0:T(8,128)(2,1)}, bf16[512,512]{1,0:T(8,128)(2,1)S(1)}, u32[]{:S(2)}) copy-start(bf16[512,512]{1,0:T(8,128)(2,1)S(1)} %reshape.455) | copy-start | bytes 1572868
  256.6 351.8 %copy-start.30 = (f32[128]{0:T(128)}, f32[128]{0:T(128)S(1)}, u32[]{:S(2)}) copy-start(f32[128]{0:T(128)S(1)} %add_rsqrt_fusion.1) | copy-start | bytes 1540
  258.5 532.5 %all-gather.13.cloned.1.call-start = ((), (), s32[]{:S(2)}) async-start(), calls=%async_computation.3 | async-start | bytes 2228224 | tf_op jit(solution)/shard_map/all_gather | solution.py:174
  258.6 353.2 %copy-start.44 = (bf16[4,512]{1,0:T(4,128)(2,1)S(1)}, bf16[4,512]{1,0:T(4,128)(2,1)}, u32[]{:S(2)}) copy-start(bf16[4,512]{1,0:T(4,128)(2,1)} %param.21) | copy-start | bytes 12292
  606.6 184.3 %copy-start.4 = (bf16[512,512]{1,0:T(8,128)(2,1)}, bf16[512,512]{1,0:T(8,128)(2,1)S(1)}, u32[]{:S(2)}) copy-start(bf16[512,512]{1,0:T(8,128)(2,1)S(1)} %reshape.459) | copy-start | bytes 1572868
  607.6 183.4 %copy-start.27 = (f32[128,16]{0,1:T(8,128)}, f32[128,16]{0,1:T(8,128)S(1)}, u32[]{:S(2)}) copy-start(f32[128,16]{0,1:T(8,128)S(1)} %get-tuple-element.109) | copy-start | bytes 24580
  608.5 192.4 %copy-start.22 = (bf16[128,16,16]{0,2,1:T(8,128)(2,1)}, bf16[128,16,16]{0,2,1:T(8,128)(2,1)S(1)}, u32[]{:S(2)}) copy-start(bf16[128,16,16]{0,2,1:T(8,128)(2,1)S(1)} %get-tuple-element.99) | copy-start | bytes 196612
  608.5 192.4 %copy-start.24 = (bf16[128,16,16]{0,2,1:T(8,128)(2,1)}, bf16[128,16,16]{0,2,1:T(8,128)(2,1)S(1)}, u32[]{:S(2)}) copy-start(bf16[128,16,16]{0,2,1:T(8,128)(2,1)S(1)} %get-tuple-element.100) | copy-start | bytes 196612
  609.2 240.3 %all-gather.19.cloned.1.call-start = ((), (), s32[]{:S(2)}) async-start(), calls=%async_computation.7 | async-start | bytes 2113536 | tf_op jit(solution)/shard_map/all_gather | solution.py:134
  609.9 434.0 %all-gather.21.cloned.1.call-start = ((), (), s32[]{:S(2)}) async-start(), calls=%async_computation.8 | async-start | bytes 2113536 | tf_op jit(solution)/shard_map/all_gather | solution.py:135
  610.5 627.9 %all-gather.15.cloned.1.call-start = ((), (), s32[]{:S(2)}) async-start(), calls=%async_computation.4 | async-start | bytes 2113536 | tf_op jit(solution)/shard_map/all_gather | solution.py:136
  611.1 742.9 %reduce-scatter.10.cloned.1.call-start = ((), (), s32[]{:S(2)}) async-start(), calls=%async_computation.9 | async-start | bytes 2228224
  786.7 23.7 %copy-start.6 = (bf16[512,512]{1,0:T(8,128)(2,1)}, bf16[512,512]{1,0:T(8,128)(2,1)S(1)}, u32[]{:S(2)}) copy-start(bf16[512,512]{1,0:T(8,128)(2,1)S(1)} %reshape.461) | copy-start | bytes 1572868
  786.8 451.6 %copy-start.38 = (f32[128]{0:T(128)}, f32[128]{0:T(128)S(1)}, u32[]{:S(2)}) copy-start(f32[128]{0:T(128)S(1)} %compare_convert_fusion) | copy-start | bytes 1540
  800.9 9.5 copy-start.32
  811.0 237.0 %copy-start.41 = (f32[128]{0:T(128)}, f32[128]{0:T(128)S(1)}, u32[]{:S(2)}) copy-start(f32[128]{0:T(128)S(1)} %add_rsqrt_fusion) | copy-start | bytes 1540
  1048.0 190.4 %copy-start.18 = (bf16[1,128,512]{2,1,0:T(8,128)(2,1)S(1)}, bf16[1,128,512]{2,1,0:T(8,128)(2,1)}, u32[]{:S(2)}) copy-start(bf16[1,128,512]{2,1,0:T(8,128)(2,1)} %param.27) | copy-start | bytes 393220
  1246.8 16.7 slice-start
  1246.8 16.7 slice-start.1
  1246.8 16.7 slice-start.2
  1246.8 16.7 slice-start.3
  1263.5 7.5 copy-start.23
  1263.5 7.5 copy-start.25
  1286.0 141.8 %reduce-scatter.12.cloned.1.call-start = ((), (), s32[]{:S(2)}) async-start(), calls=%async_computation.10 | async-start | bytes 2228224
  1305.1 301.1 %all-reduce.19.cloned.1.call-start = ((), (), s32[]{:S(2)}) async-start(), calls=%async_computation.11 | async-start | bytes 25165824
  1311.9 117.1 %copy-start.28 = (f32[128,16]{0,1:T(8,128)S(1)}, f32[128,16]{0,1:T(8,128)}, u32[]{:S(2)}) copy-start(f32[128,16]{0,1:T(8,128)} %copy-done.27) | copy-start | bytes 24580
  1311.9 117.1 %copy-start.29 = (f32[128,16]{0,1:T(8,128)S(1)}, f32[128,16]{0,1:T(8,128)}, u32[]{:S(2)}) copy-start(f32[128,16]{0,1:T(8,128)} %get-tuple-element.107) | copy-start | bytes 24580
  1311.9 117.3 %copy-start.31 = (f32[128]{0:T(128)S(1)}, f32[128]{0:T(128)}, u32[]{:S(2)}) copy-start(f32[128]{0:T(128)} %copy-done.30) | copy-start | bytes 1540
  1433.5 811.2 %reduce-scatter.8.cloned.1.call-start = ((), (), s32[]{:S(2)}) async-start(), calls=%async_computation.5 | async-start | bytes 4227072 | tf_op jit(solution)/shard_map/reduce_scatter | solution.py:307
  (26 other events, 82.4 us)
Sparse Core Ops, SparseCore 0:
  258.6 46.1 all-gather.16
  609.3 46.1 all-gather.12
  657.3 192.2 all-gather.18
  851.1 192.8 all-gather.20
  1045.6 192.7 all-gather.14
  1286.1 67.8 reduce-scatter.9
  1358.0 69.8 reduce-scatter.11
  1433.7 172.3 all-reduce.18
  1609.2 635.4 reduce-scatter.7
where the time goes:
time: 2260 us; the launch traced here: 2250 us
  waiting for transfers between devices  1250 us (55%)
  blocking collectives  832 us (37%)
  matrix products  80.7 us (4%)
  local copies, waits for them, and re-layouts  56.9 us (3%)
    reduce_scatter x1, waiting for transfers between devices, shards(): lax.psum_scatter(grad_down, ('dp', 'seq'), scatter_dimension=0, tiled=True)  630 us
    unnamed x12, waiting for transfers between devices  205 us
    all_gather x1, waiting for transfers between devices, shards(): lax.all_gather(w_up, ('dp', 'seq'), axis=0, tiled=True)  192 us
    all_gather x1, waiting for transfers between devices, shards(): lax.all_gather(w_down, ('dp', 'seq'), axis=0, tiled=True)  187 us
    all_gather x1, blocking collectives, shards(): lax.all_gather(w_value, ('dp', 'seq'), axis=0, tiled=True)  182 us
    all_gather x1, blocking collectives, shards(): lax.all_gather(w_query, ('dp', 'seq'), axis=0, tiled=True)  176 us
    all_gather x1, blocking collectives, shards(): lax.all_gather(w_output, ('dp', 'seq'), axis=0, tiled=True)  175 us
    all_gather x1, blocking collectives, shards(): lax.all_gather(w_key, ('dp', 'seq'), axis=0, tiled=True)  172 us
  transfers between devices with their start and end apart: 9, of which 7 were waited for; matrix products, arithmetic and copies ran while one was open for 4% of the time, Pallas kernels for 0%

commit v1 on v0

v1 whole, which is shorter than its diff:
```python
import math

import jax
import jax.numpy as jnp
import numpy as np
from jax import lax
from jax.experimental import pallas as pl
from jax.experimental.pallas import tpu as pltpu
from jax.sharding import PartitionSpec as P

HEADS = 16
HEAD = 32
HALF = HEAD // 2
D = 512
FF = 2048
LEN = 2048
ROWS = 128
TEAM = 4
TEAM_ROWS = TEAM * ROWS
FF_PART = FF // TEAM
DEVICES = 128
SEQ = 16
DP = 8
AUG = 48

EPS = 1e-05
MASKED = -1.0e9
SCALE = HEAD**-0.5
LOG2E = math.log2(math.e)
LN2 = math.log(2.0)

f32 = jnp.float32
bf16 = jnp.bfloat16
BOTH = ("dp", "seq")


def nn(a, b):
    return lax.dot_general(a, b, (((1,), (0,)), ((), ())), preferred_element_type=f32)


def nt(a, b):
    return lax.dot_general(a, b, (((1,), (1,)), ((), ())), preferred_element_type=f32)


def tn(a, b):
    return lax.dot_general(a, b, (((0,), (0,)), ((), ())), preferred_element_type=f32)


def norm_parts(x):
    centered = x - jnp.mean(x, -1, keepdims=True)
    inv = lax.rsqrt(jnp.mean(centered * centered, -1, keepdims=True) + EPS)
    return centered * inv, inv


def norm_back(grad, scaled, inv, gain):
    e = grad * gain
    return inv * (
        e - jnp.mean(e, -1, keepdims=True) - scaled * jnp.mean(e * scaled, -1, keepdims=True)
    )


def split3(row):
    hi = row.astype(bf16)
    rest = row - hi.astype(f32)
    mid = rest.astype(bf16)
    low = (rest - mid.astype(f32)).astype(bf16)
    return [hi.astype(f32), mid.astype(f32), low.astype(f32)]


def key_columns(keys_t, length):
    place = lax.broadcasted_iota(jnp.int32, (1, LEN), 1)
    mask = jnp.where(place < length, 0.0, MASKED).astype(f32)
    ones = jnp.ones((3, LEN), f32)
    pad = jnp.zeros((128 - HEAD - 4, LEN), f32)
    return jnp.concatenate([keys_t, mask, ones, pad], 0).T.astype(bf16)[:, :AUG]


def with_rows(data_t, rows):
    pad = jnp.zeros((AUG - HEAD - len(rows), data_t.shape[1]), f32)
    return jnp.concatenate([data_t.astype(f32)] + rows + [pad], 0).astype(bf16)


def attend_kernel(
    place, length, near, far, head_cols, cos, sin,
    sent, q_out, k_out, v_out, o_out, lse_out, team_tokens,
    q_t, k_t, v_t,
):
    core = place[0]
    team = place[1]
    cols = head_cols[...].astype(f32).T
    gain = cols[96:97, :]
    bias = cols[97:98, :]
    weights_t = cols[0:96, :].astype(bf16)
    for which, source in ((0, near), (1, far)):
        parity = core if which == 0 else 1 - core
        for pair in range(4):
            x = source[2 * pair : 2 * pair + 2].reshape(2 * ROWS, D).astype(f32)
            scaled, _ = norm_parts(x)
            normed = (scaled * gain + bias).astype(bf16)
            lin = nt(weights_t, normed)
            for one in range(2):
                at = pl.multiple_of((2 * (2 * pair + one) + parity) * ROWS, ROWS)
                here = pl.ds(at, ROWS)
                part = lin[:, one * ROWS : (one + 1) * ROWS]
                c = cos[:, here]
                s = sin[:, here]
                q1, q2 = part[0:16], part[16:32]
                k1, k2 = part[32:48], part[48:64]
                fold = SCALE * LOG2E
                q_t[:, here] = (
                    jnp.concatenate([q1 * c - q2 * s, q2 * c + q1 * s], 0) * fold
                ).astype(bf16)
                k_t[:, here] = jnp.concatenate([k1 * c - k2 * s, k2 * c + k1 * s], 0).astype(bf16)
                v_t[:, here] = part[64:96].astype(bf16)
        for one in range(2):
            team_tokens[2 * one + parity] = source[2 * team + one]
    q_out[...] = q_t[...]
    k_out[...] = k_t[...]
    v_out[...] = v_t[...]
    keys = key_columns(k_t[...].astype(f32), length[0])
    one_row = jnp.ones((1, LEN), f32)
    values_t = with_rows(v_t[...], [one_row])
    tile = TEAM_ROWS
    for i in range(LEN // tile):
        here = slice(i * tile, (i + 1) * tile)
        queries_t = with_rows(q_t[:, here], [jnp.ones((1, tile), f32)])
        scores = nn(keys, queries_t)
        top = jnp.max(scores, axis=0, keepdims=True)
        weights = jnp.exp2(scores - top).astype(bf16)
        mixed = nn(values_t, weights)
        total = mixed[HEAD : HEAD + 1]
        out = mixed[:HEAD] / total
        o_out[:, here] = out
        lse_out[:, here] = top + jnp.log2(total)
        low = out.astype(bf16)
        for t in range(TEAM):
            sent[TEAM * i + t] = low


def feed_kernel(place, length, mixed, tokens, cot, weights, head_cols, sent, swapped, grads, norm_rows):
    team = place[1]
    member = place[2]
    cols = head_cols[...].astype(f32).T
    gain = cols[98:99, :]
    bias = cols[99:100, :]
    w_gate = weights[:, 0:512]
    w_up = weights[:, 512:1024]
    w_down = weights[:, 1024:1536]
    w_out = weights[:, 1536:2048]
    mixed_t = mixed[...].reshape(D, TEAM_ROWS)
    row = lax.broadcasted_iota(jnp.int32, (TEAM_ROWS, 1), 0)
    live = (team * TEAM_ROWS + row) < length[0]
    own = (row // ROWS) == member
    middle = tokens[...].reshape(TEAM_ROWS, D).astype(f32) + tn(mixed_t, w_out)
    scaled, inv = norm_parts(middle)
    normed = (scaled * gain + bias).astype(bf16)
    gate = nn(normed, w_gate)
    up = nn(normed, w_up)
    sig = jax.nn.sigmoid(gate)
    act = gate * sig
    hidden = (act * up).astype(bf16)
    out_part = nn(hidden, w_down) + jnp.where(own, middle, 0.0)
    d_out = jnp.where(live, cot[...].reshape(TEAM_ROWS, D).astype(f32), 0.0)
    d_out_low = d_out.astype(bf16)
    d_hidden = nt(d_out_low, w_down)
    d_up = (d_hidden * act).astype(bf16)
    d_gate = (d_hidden * up * sig * (1.0 + gate * (1.0 - sig))).astype(bf16)
    d_normed = nt(d_gate, w_gate) + nt(d_up, w_up)
    d_middle = jnp.where(own, d_out, 0.0) + norm_back(d_normed, scaled, inv, gain)
    d_middle_low = d_middle.astype(bf16)
    sent[...] = nt(w_out, d_middle_low).astype(bf16).reshape(HEADS, HEAD, TEAM_ROWS)
    swapped[:, :, 0:D] = d_middle_low.reshape(TEAM, ROWS, D)
    swapped[:, :, D : 2 * D] = out_part.astype(bf16).reshape(TEAM, ROWS, D)
    grads[:, 0:512] = tn(normed, d_gate).astype(bf16)
    grads[:, 512:1024] = tn(normed, d_up).astype(bf16)
    grads[:, 1024:1536] = tn(hidden, d_out_low).astype(bf16)
    grads[:, 1536:2048] = nn(mixed_t, d_middle_low).astype(bf16)
    norm_rows[0:1, :] = jnp.sum(d_normed * scaled, 0, keepdims=True)
    norm_rows[1:2, :] = jnp.sum(d_normed, 0, keepdims=True)
    norm_rows[2:8, :] = jnp.zeros((6, D), f32)


def attend_back_kernel(
    length, d_mixed, q_in, k_in, v_in, o_in, lse_in, cos, sin, sent, d_o, probs, d_scores, dq, dk, dv
):
    for y in range(LEN // TEAM_ROWS):
        total = d_mixed[TEAM * y].astype(f32)
        for t in range(1, TEAM):
            total = total + d_mixed[TEAM * y + t].astype(f32)
        d_o[:, y * TEAM_ROWS : (y + 1) * TEAM_ROWS] = total.astype(bf16)
    keys_t = k_in[...]
    keys = key_columns(keys_t.astype(f32), length[0])
    ones = jnp.ones((4, LEN), f32)
    pad = jnp.zeros((128 - HEAD - 4, LEN), f32)
    values = jnp.concatenate([v_in[...].astype(f32), ones, pad], 0).T.astype(bf16)[:, :AUG]
    d_o_t = d_o[...]
    inner = jnp.sum(d_o_t.astype(f32) * o_in[...], 0, keepdims=True)
    zero_row = jnp.zeros((1, LEN), f32)
    one_row = jnp.ones((1, LEN), f32)
    q_rows = with_rows(q_in[...], [one_row] + split3(-lse_in[...]))
    do_rows = with_rows(d_o_t, [zero_row] + split3(-inner))
    tile = 512
    for i in range(LEN // tile):
        here = slice(i * tile, (i + 1) * tile)
        p = jnp.exp2(nn(keys, q_rows[:, here]))
        ds = (p * nn(values, do_rows[:, here])).astype(bf16)
        probs[:, here] = p.astype(bf16)
        d_scores[:, here] = ds
        dq[:, here] = nn(keys_t, ds) * SCALE
    dk[...] = nt(q_in[...], d_scores[...]) * LN2
    dv[...] = nt(d_o_t, probs[...])
    c = cos[...]
    s = sin[...]
    q1, q2 = dq[0:HALF], dq[HALF:HEAD]
    k1, k2 = dk[0:HALF], dk[HALF:HEAD]
    dq_t = jnp.concatenate([q1 * c + q2 * s, q2 * c - q1 * s], 0).astype(bf16)
    dk_t = jnp.concatenate([k1 * c + k2 * s, k2 * c - k1 * s], 0).astype(bf16)
    dv_t = dv[...].astype(bf16)
    for b in range(SEQ):
        here = slice(b * ROWS, (b + 1) * ROWS)
        sent[b, 0:32] = dq_t[:, here]
        sent[b, 32:64] = dk_t[:, here]
        sent[b, 64:96] = dv_t[:, here]


def head_grad_kernel(place, near, far, head_cols, d_lin, norm_rows, sent):
    core = place[0]
    cols = head_cols[...].astype(f32).T
    gain = cols[96:97, :]
    bias = cols[97:98, :]
    weights_t = cols[0:96, :].astype(bf16)
    total = jnp.zeros((96, D), f32)
    d_gain = jnp.zeros((1, D), f32)
    d_bias = jnp.zeros((1, D), f32)
    for which, source in ((0, near), (1, far)):
        parity = core if which == 0 else 1 - core
        for pair in range(4):
            x = source[2 * pair : 2 * pair + 2].reshape(2 * ROWS, D).astype(f32)
            scaled, _ = norm_parts(x)
            normed = (scaled * gain + bias).astype(bf16)
            d_part = jnp.concatenate(
                [d_lin[2 * (2 * pair) + parity], d_lin[2 * (2 * pair + 1) + parity]], 1
            )
            total = total + nn(d_part, normed)
            d_normed = tn(d_part, weights_t)
            d_gain = d_gain + jnp.sum(d_normed * scaled, 0, keepdims=True)
            d_bias = d_bias + jnp.sum(d_normed, 0, keepdims=True)
    pad = jnp.zeros((28, D), f32)
    sent[...] = jnp.concatenate([total, d_gain, d_bias, norm_rows[0:2, :], pad], 0).T


def input_grad_kernel(place, length, tokens, d_lin, weights, swapped, head_cols, grad_tokens, layer_output):
    seq = place[3]
    cols = head_cols[...].astype(f32).T
    gain = cols[96:97, :]
    scaled, inv = norm_parts(tokens[0].astype(f32))
    d_t = jnp.zeros((D, ROWS), f32)
    for part in range(3):
        d_part = d_lin[:, part * HEAD : (part + 1) * HEAD, :].reshape(D, ROWS)
        d_t = d_t + nn(weights[:, part * D : (part + 1) * D], d_part)
    total = swapped[0].astype(f32)
    for t in range(1, TEAM):
        total = total + swapped[t].astype(f32)
    grad_tokens[0] = total[:, 0:D] + norm_back(d_t.T, scaled, inv, gain)
    row = lax.broadcasted_iota(jnp.int32, (ROWS, 1), 0)
    live = (seq * ROWS + row) < length[0]
    layer_output[0] = jnp.where(live, total[:, D : 2 * D], 0.0).astype(bf16)


VM = pl.BlockSpec(memory_space=pltpu.VMEM)
SM = pl.BlockSpec(memory_space=pltpu.SMEM)


def call(kernel, specs, outs, scratch=(), flops=0, size=0):
    return pl.pallas_call(
        kernel,
        out_shape=tuple(jax.ShapeDtypeStruct(shape, kind) for shape, kind in outs),
        in_specs=specs,
        out_specs=tuple(VM for _ in outs),
        scratch_shapes=[pltpu.VMEM(shape, kind) for shape, kind in scratch],
        compiler_params=pltpu.CompilerParams(vmem_limit_bytes=56 * 2**20),
        cost_estimate=pl.CostEstimate(flops=flops, bytes_accessed=size, transcendentals=0),
    )


def rope_tables():
    freq = 10000.0 ** (-2.0 * np.arange(HALF) / HEAD)
    angles = freq[:, None] * np.arange(LEN)[None, :]
    return np.cos(angles).astype(np.float32), np.sin(angles).astype(np.float32)


def column_order():
    order = np.arange(512).reshape(4, 8, TEAM, 4).transpose(2, 0, 1, 3).reshape(-1)
    table = np.zeros((512, 512), np.float32)
    table[order, np.arange(512)] = 1.0
    return table


def exchange(value, axes, groups=None):
    return lax.all_to_all(value, axes, 0, 0, tiled=True, axis_index_groups=groups)


def shards(
    tokens, lengths, norm1_gain, norm1_bias, w_query, w_key, w_value, w_output,
    norm2_gain, norm2_bias, w_gate, w_up, w_down, cotangent,
):
    seq = lax.axis_index("seq")
    place = jnp.stack([seq % 2, seq // TEAM, seq % TEAM, seq]).astype(jnp.int32)
    cos, sin = (jnp.asarray(t) for t in rope_tables())
    order = column_order()

    same_core = [[2 * chip + core for chip in range(8)] for core in range(2)]
    near = exchange(jnp.broadcast_to(tokens, (8, ROWS, D)), "seq", same_core)
    far = lax.ppermute(near, "seq", [(i, i ^ 1) for i in range(SEQ)])

    by_head = [w.reshape(4, HEADS, HEAD).transpose(1, 0, 2) for w in (w_query, w_key, w_value)]
    norms = jnp.stack([norm1_gain, norm1_bias, norm2_gain, norm2_bias], 1)
    norms = jnp.broadcast_to(norms[None], (HEADS, 4, 4))
    pad = jnp.zeros((HEADS, 4, 28), bf16)
    head_msg = jnp.concatenate(by_head + [norms, pad], 2)
    head_msg = jnp.broadcast_to(head_msg[None], (DP, HEADS, 4, 128)).reshape(DEVICES, 4, 128)
    head_cols = exchange(head_msg, BOTH).reshape(D, 128)

    wide = jnp.concatenate([w_gate, w_up], 0).reshape(2 * 4 * 4, 512)
    wide = jnp.dot(wide, jnp.asarray(order, bf16), preferred_element_type=f32).astype(bf16)
    wide = wide.reshape(2, 4, 4, TEAM, 128).transpose(3, 1, 0, 2, 4).reshape(TEAM, 4, 1024)
    down = w_down.reshape(TEAM, 4, D)
    out = jnp.broadcast_to(w_output[None], (TEAM, 4, D))
    feed_msg = jnp.concatenate([wide, down, out], 2)
    feed_msg = jnp.broadcast_to(feed_msg[None], (DEVICES // TEAM, TEAM, 4, 2048))
    feed_weights = exchange(feed_msg.reshape(DEVICES, 4, 2048), BOTH).reshape(D, 2048)

    teams = [[TEAM * j + t for t in range(TEAM)] for j in range(SEQ // TEAM)]
    team_cot = exchange(jnp.broadcast_to(cotangent, (TEAM, ROWS, D)), "seq", teams)

    sent, q_t, k_t, v_t, o_t, lse, team_tokens = call(
        attend_kernel,
        [SM, SM] + [VM] * 5,
        [
            ((SEQ, HEAD, TEAM_ROWS), bf16),
            ((HEAD, LEN), bf16),
            ((HEAD, LEN), bf16),
            ((HEAD, LEN), bf16),
            ((HEAD, LEN), f32),
            ((1, LEN), f32),
            ((TEAM, ROWS, D), bf16),
        ],
        [((HEAD, LEN), bf16)] * 3,
        flops=8 * 10**9,
        size=8 * 10**6,
    )(place, lengths, near, far, head_cols, cos, sin)
    mixed = exchange(sent, "seq")

    rows_msg = jnp.concatenate([w_query, w_key, w_value], 1)
    rows_msg = jnp.broadcast_to(rows_msg[None], (DEVICES, 4, 3 * D))
    row_weights = exchange(rows_msg, BOTH).reshape(D, 3 * D)

    d_sent, swapped, grads, norm_rows = call(
        feed_kernel,
        [SM, SM] + [VM] * 5,
        [
            ((HEADS, HEAD, TEAM_ROWS), bf16),
            ((TEAM, ROWS, 2 * D), bf16),
            ((D, 2048), bf16),
            ((8, D), f32),
        ],
        flops=4 * 10**9,
        size=10 * 10**6,
    )(place, lengths, mixed, team_tokens, team_cot, feed_weights, head_cols)
    d_mixed = exchange(d_sent, "seq")
    feed_grads = exchange(grads.reshape(DEVICES, 4, 2048), BOTH)
    swapped = exchange(swapped, "seq", teams)

    (lin_sent,) = call(
        attend_back_kernel,
        [SM] + [VM] * 8,
        [((SEQ, 96, ROWS), bf16)],
        [
            ((HEAD, LEN), bf16),
            ((LEN, LEN), bf16),
            ((LEN, LEN), bf16),
            ((HEAD, LEN), f32),
            ((HEAD, LEN), f32),
            ((HEAD, LEN), f32),
        ],
        flops=12 * 10**9,
        size=8 * 10**6,
    )(lengths, d_mixed, q_t, k_t, v_t, o_t, lse, cos, sin)
    d_lin = exchange(lin_sent, "seq")

    (head_grads,) = call(
        head_grad_kernel,
        [SM] + [VM] * 5,
        [((D, 128), f32)],
        flops=2 * 10**9,
        size=5 * 10**6,
    )(place, near, far, head_cols, lin_sent, norm_rows)
    head_grads = exchange(head_grads.reshape(DEVICES, 4, 128), BOTH)

    grad_tokens, layer_output = call(
        input_grad_kernel,
        [SM, SM] + [VM] * 5,
        [((1, ROWS, D), f32), ((1, ROWS, D), bf16)],
        flops=10**9,
        size=4 * 10**6,
    )(place, lengths, tokens, d_lin, row_weights, swapped, head_cols)

    summed = jnp.sum(feed_grads.reshape(DEVICES // TEAM, TEAM, 4, 2048).astype(f32), 0)
    grad_output = jnp.sum(summed[:, :, 1536:], 0)
    grad_down = summed[:, :, 1024:1536].reshape(16, D)
    wide = summed[:, :, :1024].reshape(TEAM, 4, 2, 4, 128).transpose(2, 1, 3, 0, 4)
    wide = jnp.dot(
        wide.reshape(2 * 4 * 4, 512),
        jnp.asarray(order.T),
        precision=lax.Precision.HIGHEST,
        preferred_element_type=f32,
    ).reshape(2, 4, FF)
    per_head = jnp.sum(head_grads.reshape(DP, HEADS, 4, 128), 0)
    grad_query, grad_key, grad_value = (
        per_head[:, :, i * HEAD : (i + 1) * HEAD].transpose(1, 0, 2).reshape(4, D) for i in range(3)
    )
    norm_grads = jnp.sum(per_head[:, :, 96:100], 0)
    return (
        layer_output,
        grad_tokens,
        norm_grads[:, 0],
        norm_grads[:, 1],
        grad_query,
        grad_key,
        grad_value,
        grad_output,
        norm_grads[:, 2],
        norm_grads[:, 3],
        wide[0],
        wide[1],
        grad_down,
    )


def solution(mesh):
    flat = P(BOTH)
    rows = P(BOTH, None)
    blocks = P("dp", "seq", None)
    return jax.shard_map(
        shards,
        mesh=mesh,
        in_specs=(
            blocks, P("dp"), flat, flat, rows, rows, rows, rows, flat, flat, rows, rows, rows, blocks,
        ),
        out_specs=(
            blocks, blocks, flat, flat, rows, rows, rows, rows, flat, flat, rows, rows, rows,
        ),
        check_vma=False,
    )
```

time: 2260 us -> 258 us (0.11)
  waiting for transfers between devices: 1250 us -> 84.7 us
  blocking collectives: 832 us -> 68.5 us
  matrix products: 80.7 us -> 0.89 us
  Pallas kernels: 0 us -> 40.3 us
  starting transfers between devices: 0.36 us -> 32.8 us
  local copies, waits for them, and re-layouts: 56.9 us -> 25.1 us
    all_gather x4 -> x0, blocking collectives: 704 us -> none  [the longest x1 182 us: shards(): lax.all_gather(w_value, ('dp', 'seq'), axis=0, tiled=True)]
    reduce_scatter x1 -> x0, waiting for transfers between devices: 630 us -> none  [shards(): lax.psum_scatter(grad_down, ('dp', 'seq'), scatter_dimension=0, tiled=True)]
    all_gather x5 -> x0, waiting for transfers between devices: 417 us -> none  [the longest x1 192 us: shards(): lax.all_gather(w_up, ('dp', 'seq'), axis=0, tiled=True)]
    unnamed x12 -> x0, waiting for transfers between devices: 205 us -> none
    unnamed x2 -> x0, blocking collectives: 128 us -> none
    all_to_all x0 -> x7, waiting for transfers between devices: none -> 83.5 us  [exchange(): lax.all_to_all(value, axes, 0, 0, tiled=True, axis_index_groups=groups)]
    dot_general x26 -> x2, matrix products: 70.8 us -> 0.89 us  [the longest x1 0.7 us: shards(): jnp.dot(wide.reshape(2 * 4 * 4, 512), jnp.asarray(order.T), precision=lax...]
    all_to_all x0 -> x4, blocking collectives: none -> 68.5 us  [exchange(): lax.all_to_all(value, axes, 0, 0, tiled=True, axis_index_groups=groups)]
  transfers between devices with their start and end apart: 9 -> 8, of which waited for: 7 -> 8; matrix products, arithmetic and copies ran while one was open for 4% -> 5% of each run, Pallas kernels for 0% -> 13%
where the time goes in v1:
time: 258 us; the launch traced here: 257 us
  waiting for transfers between devices  84.7 us (33%)
  blocking collectives  68.5 us (27%)
  Pallas kernels  40.3 us (16%)
  starting transfers between devices  32.8 us (13%)
  local copies, waits for them, and re-layouts  25.1 us (10%)
  other arithmetic  3.18 us (1%)
    all_to_all x7, waiting for transfers between devices, exchange(): lax.all_to_all(value, axes, 0, 0, tiled=True, axis_index_groups=groups)  83.5 us
    all_to_all x4, blocking collectives, exchange(): lax.all_to_all(value, axes, 0, 0, tiled=True, axis_index_groups=groups)  68.5 us
    all_to_all x7, starting transfers between devices, exchange(): lax.all_to_all(value, axes, 0, 0, tiled=True, axis_index_groups=groups)  31.7 us
    pallas_call x1, Pallas kernels, shards(): call(attend_back_kernel, [SM] + [VM] * 8, [((SEQ, 96, ROWS), bf16)], [((H...  12.9 us
    pallas_call x1, Pallas kernels, shards(): call(attend_kernel, [SM, SM] + [VM] * 5, [((SEQ, HEAD, TEAM_ROWS), bf16),...  11 us
    pallas_call x1, Pallas kernels, shards(): call(feed_kernel, [SM, SM] + [VM] * 5, [((HEADS, HEAD, TEAM_ROWS), bf16),...  8.11 us
  transfers between devices with their start and end apart: 8, of which 8 were waited for; matrix products, arithmetic and copies ran while one was open for 5% of the time, Pallas kernels for 13%

profile of v1, /device:TPU:1, one launch (start us, length us, event | category | flops | bytes accessed | tf_op | source)
XLA Modules:
  0.0 257.0 jit_solution(8602229455077378154)
XLA Ops:
  4.0 21.4 %all_to_all.55 = bf16[128,4,128]{2,1,0:T(4,128)(2,1)} all-to-all(bf16[128,4,128]{2,1,0:T(4,128)(2,1)S(1)} %bitcast.41), channel_id=1, replica_groups=mesh['dp'=8,'seq'=16] {'dp','seq'}, dimensions={0} | all-to-all | bytes 262144 | tf_op jit(solution)/shard_map/all_to_all | solution.py:300
  26.4 12.9 %all_to_all.56.cot = bf16[4,128,512]{2,1,0:T(8,128)(2,1)} all-to-all(bf16[4,128,512]{2,1,0:T(8,128)(2,1)S(1)} %broadcast_in_dim.26), channel_id=1, replica_groups={{0,1,2,3},{4,5,6,7},{8,9,10,11},{12,13,14,15},{16,17,18,19},{20,21,22,2..., dimensions={0} | all-to-all | bytes 1048576 | tf_op jit(solution)/shard_map/all_to_all | solution.py:300
  39.4 1.1 broadcast_in_dim.21
  40.4 3.6 %all-to-all-start = ((bf16[8,128,512]{2,1,0:T(8,128)(2,1)}), bf16[8,128,512]{2,1,0:T(8,128)(2,1)S(1)}, u32[]{:S(2)}, u32[]{:S(2)}) async-start(bf16[8,128,512]{2,1,0:T(8,128)(2,1)} %broadcast_in_dim.21), calls=%async_computation | async-start | bytes 2097152 | tf_op jit(solution)/shard_map/all_to_all | solution.py:300
  44.5 15.0 %all-to-all-done.near = bf16[8,128,512]{2,1,0:T(8,128)(2,1)S(1)} async-done(((bf16[8,128,512]{2,1,0:T(8,128)(2,1)}), bf16[8,128,512]{2,1,0:T(8,128)(2,1)S(1)}, u32[]{:S(2)}, u32[]{:S(2)}) %all-to-all-start) | async-done | bytes 1048608 | tf_op jit(solution)/shard_map/all_to_all | solution.py:300
  59.5 2.4 broadcast_in_dim.55
  61.9 5.8 %all-to-all-start.4 = ((bf16[128,4,2048]{2,1,0:T(4,128)(2,1)}), bf16[128,4,2048]{2,1,0:T(4,128)(2,1)S(1)}, u32[]{:S(2)}, u32[]{:S(2)}) async-start(bf16[128,4,2048]{2,1,0:T(4,128)(2,1)} %bitcast.38), calls=%async_computation.4 | async-start | bytes 4194304 | tf_op jit(solution)/shard_map/all_to_all | solution.py:300
  67.7 1.1 collective-permute-start
  70.1 1.2 collective-permute-done.far
  71.3 11.0 %shard_map.273 = (bf16[16,32,512]{2,1,0:T(8,128)(2,1)}, bf16[32,2048]{1,0:T(8,128)(2,1)}, bf16[32,2048]{1,0:T(8,128)(2,1)}, bf16[32,2048]{1,0:T(8,128)(2,1)}, f3...) custom-call(s32[4]{0:T(128)} %pad_add_fusion.place, s32[1]{0:T(128)S(6)} %copy.63.length, ...), custom_call_target="tpu_custom_call" | custom-call | flops 8000000000 | bytes 8000000 | tf_op jit(solution)/shard_map/pallas_call | solution.py:336
  82.3 15.4 %all-to-all-done.4 = bf16[128,4,2048]{2,1,0:T(4,128)(2,1)S(1)} async-done(((bf16[128,4,2048]{2,1,0:T(4,128)(2,1)}), bf16[128,4,2048]{2,1,0:T(4,128)(2,1)S(1)}, u32[]{:S(2)}, u32[]{:S(2)}) %all-to-all-start.4) | async-done | bytes 2097184 | tf_op jit(solution)/shard_map/all_to_all | solution.py:300
  97.7 4.2 %all-to-all-start.2 = ((bf16[16,32,512]{2,1,0:T(8,128)(2,1)}), bf16[16,32,512]{2,1,0:T(8,128)(2,1)S(1)}, u32[]{:S(2)}, u32[]{:S(2)}) async-start(bf16[16,32,512]{2,1,0:T(8,128)(2,1)} %get-tuple-element.26), calls=%async_computation.2 | async-start | bytes 1048576 | tf_op jit(solution)/shard_map/all_to_all | solution.py:300
  101.9 2.0 reshape.112.weights
  103.9 9.1 %all-to-all-done.2.mixed = bf16[16,32,512]{2,1,0:T(8,128)(2,1)S(1)} async-done(((bf16[16,32,512]{2,1,0:T(8,128)(2,1)}), bf16[16,32,512]{2,1,0:T(8,128)(2,1)S(1)}, u32[]{:S(2)}, u32[]{:S(2)}) %all-to-all-start.2) | async-done | bytes 524320 | tf_op jit(solution)/shard_map/all_to_all | solution.py:300
  113.9 8.1 %shard_map.274 = (bf16[16,32,512]{2,1,0:T(8,128)(2,1)}, bf16[4,128,1024]{2,1,0:T(8,128)(2,1)}, bf16[512,2048]{1,0:T(8,128)(2,1)}, f32[8,512]{1,0:T(8,128)}) custom-call(s32[4]{0:T(128)} %pad_add_fusion.place, s32[1]{0:T(128)S(6)} %copy.63.length, bf16[16,32,512]{2,1,0:T(8,128)(2,1)} %copy-done.6, bf16[4,128,512]{2,1,0:T(8,128)(2,1)} %get-tuple-element.27.tokens, ...), custom_call_target="tpu_custom_call" | custom-call | flops 4000000000 | bytes 10000000 | tf_op jit(solution)/shard_map/pallas_call | solution.py:358
  122.0 4.7 %all-to-all-start.5 = ((bf16[16,32,512]{2,1,0:T(8,128)(2,1)}), bf16[16,32,512]{2,1,0:T(8,128)(2,1)S(1)}, u32[]{:S(2)}, u32[]{:S(2)}) async-start(bf16[16,32,512]{2,1,0:T(8,128)(2,1)} %get-tuple-element.28), calls=%async_computation.5 | async-start | bytes 1048576 | tf_op jit(solution)/shard_map/all_to_all | solution.py:300
  126.7 11.1 %all-to-all-done.5.d_mixed = bf16[16,32,512]{2,1,0:T(8,128)(2,1)S(1)} async-done(((bf16[16,32,512]{2,1,0:T(8,128)(2,1)}), bf16[16,32,512]{2,1,0:T(8,128)(2,1)S(1)}, u32[]{:S(2)}, u32[]{:S(2)}) %all-to-all-start.5) | async-done | bytes 524320 | tf_op jit(solution)/shard_map/all_to_all | solution.py:300
  137.9 1.6 broadcast_in_dim.56
  139.4 4.8 %all-to-all-start.7 = ((bf16[128,4,1536]{2,1,0:T(4,128)(2,1)}), bf16[128,4,1536]{2,1,0:T(4,128)(2,1)S(1)}, u32[]{:S(2)}, u32[]{:S(2)}) async-start(bf16[128,4,1536]{2,1,0:T(4,128)(2,1)} %broadcast_in_dim.56), calls=%async_computation.7 | async-start | bytes 3145728 | tf_op jit(solution)/shard_map/all_to_all | solution.py:300
  144.2 12.9 %shard_map.275.d_lin = bf16[16,96,128]{2,1,0:T(8,128)(2,1)} custom-call(s32[1]{0:T(128)S(6)} %copy.63.length, bf16[16,32,512]{2,1,0:T(8,128)(2,1)} %copy-done.5, bf16[32,2048]{1,0:T(8,128)(2,1)} %get-tuple-element.29.q_in, bf16[32,2048]{1,0:T(8,128)(2,1)} %get-tuple-element.30.k_in, bf16[32,2048]{1,0:T(8,128)(2,1)} %get-tuple-element.31.v_in, ...), custom_call_target="tpu_custom_call" | custom-call | flops 12000000000 | bytes 8000000 | tf_op jit(solution)/shard_map/pallas_call | solution.py:374
  157.1 4.9 %shard_map.277 = f32[512,128]{1,0:T(8,128)} custom-call(s32[4]{0:T(128)} %pad_add_fusion.place, bf16[8,128,512]{2,1,0:T(8,128)(2,1)} %copy-done.2, bf16[8,128,512]{2,1,0:T(8,128)(2,1)} %collective-permute-done.far, bf16[512,128]{1,0:T(8,128)(2,1)} %bitcast.49, bf16[16,96,128]{2,1,0:T(8,128)(2,1)} %shard_map.275.d_lin, f32[8,512]{1,0:T(8,128)} %get-tuple-element.37.norm_rows), custom_call_target="tpu_custom_call" | custom-call | flops 2000000000 | bytes 5000000 | tf_op jit(solution)/shard_map/pallas_call | solution.py:391
  162.0 6.9 %all-to-all-done.7 = bf16[128,4,1536]{2,1,0:T(4,128)(2,1)S(1)} async-done(((bf16[128,4,1536]{2,1,0:T(4,128)(2,1)}), bf16[128,4,1536]{2,1,0:T(4,128)(2,1)S(1)}, u32[]{:S(2)}, u32[]{:S(2)}) %all-to-all-start.7) | async-done | bytes 1572896 | tf_op jit(solution)/shard_map/all_to_all | solution.py:300
  168.9 15.6 %all_to_all.57 = f32[128,4,128]{2,1,0:T(4,128)S(1)} all-to-all(f32[128,4,128]{2,1,0:T(4,128)} %bitcast.43), channel_id=1, replica_groups=mesh['dp'=8,'seq'=16] {'dp','seq'}, dimensions={0} | all-to-all | bytes 524288 | tf_op jit(solution)/shard_map/all_to_all | solution.py:300
  184.5 18.5 %all_to_all.58.swapped = bf16[4,128,1024]{2,1,0:T(8,128)(2,1)} all-to-all(bf16[4,128,1024]{2,1,0:T(8,128)(2,1)S(1)} %copy-done.3), channel_id=1, replica_groups={{0,1,2,3},{4,5,6,7},{8,9,10,11},{12,13,14,15},{16,17,18,19},{20,21,22,2..., dimensions={0} | all-to-all | bytes 2097152 | tf_op jit(solution)/shard_map/all_to_all | solution.py:300
  203.0 4.4 %all-to-all-start.6 = ((bf16[16,96,128]{2,1,0:T(8,128)(2,1)}), bf16[16,96,128]{2,1,0:T(8,128)(2,1)S(1)}, u32[]{:S(2)}, u32[]{:S(2)}) async-start(bf16[16,96,128]{2,1,0:T(8,128)(2,1)} %shard_map.275.d_lin), calls=%async_computation.6 | async-start | bytes 786432 | tf_op jit(solution)/shard_map/all_to_all | solution.py:300
  207.3 4.1 %reshape.119 = bf16[128,4,2048]{2,1,0:T(4,128)(2,1)} reshape(bf16[512,2048]{1,0:T(8,128)(2,1)} %get-tuple-element.38) | data formatting | bytes 4194304 | tf_op jit(solution)/shard_map/reshape | solution.py:371
  211.4 6.0 %all-to-all-done.6.d_lin = bf16[16,96,128]{2,1,0:T(8,128)(2,1)S(1)} async-done(((bf16[16,96,128]{2,1,0:T(8,128)(2,1)}), bf16[16,96,128]{2,1,0:T(8,128)(2,1)S(1)}, u32[]{:S(2)}, u32[]{:S(2)}) %all-to-all-start.6) | async-done | bytes 393248 | tf_op jit(solution)/shard_map/all_to_all | solution.py:300
  218.2 4.2 %all-to-all-start.10 = ((bf16[128,4,2048]{2,1,0:T(4,128)(2,1)}), bf16[128,4,2048]{2,1,0:T(4,128)(2,1)S(1)}, u32[]{:S(2)}, u32[]{:S(2)}) async-start(bf16[128,4,2048]{2,1,0:T(4,128)(2,1)} %reshape.119), calls=%async_computation.10 | async-start | bytes 4194304 | tf_op jit(solution)/shard_map/all_to_all | solution.py:300
  222.5 3.8 %reshape.113.weights = bf16[512,1536]{1,0:T(8,128)(2,1)} reshape(bf16[128,4,1536]{2,1,0:T(4,128)(2,1)} %copy-done) | data formatting | bytes 3145728 | tf_op jit(solution)/shard_map/reshape | solution.py:356
  229.3 3.4 %shard_map.276 = (f32[1,128,512]{2,1,0:T(8,128)}, bf16[1,128,512]{2,1,0:T(8,128)(2,1)}) custom-call(s32[4]{0:T(128)} %pad_add_fusion.place, s32[1]{0:T(128)S(6)} %copy.63.length, bf16[1,128,512]{2,1,0:T(8,128)(2,1)} %tokens.1, bf16[16,96,128]{2,1,0:T(8,128)(2,1)} %copy-done.7, bf16[512,1536]{1,0:T(8,128)(2,1)} %reshape.113.weights, ...), custom_call_target="tpu_custom_call" | custom-call | flops 1000000000 | bytes 4000000 | tf_op jit(solution)/shard_map/pallas_call | solution.py:400
  232.7 19.9 %all-to-all-done.10 = bf16[128,4,2048]{2,1,0:T(4,128)(2,1)S(1)} async-done(((bf16[128,4,2048]{2,1,0:T(4,128)(2,1)}), bf16[128,4,2048]{2,1,0:T(4,128)(2,1)S(1)}, u32[]{:S(2)}, u32[]{:S(2)}) %all-to-all-start.10) | async-done | bytes 2097184 | tf_op jit(solution)/shard_map/all_to_all | solution.py:300
  252.6 1.0 convert_reduce_fusion
  (73 shorter events, 13.2 us)
Async XLA Ops:
  0.6 38.7 %copy-start.8 = (bf16[1,128,512]{2,1,0:T(8,128)(2,1)S(1)}, bf16[1,128,512]{2,1,0:T(8,128)(2,1)}, u32[]{:S(2)}) copy-start(bf16[1,128,512]{2,1,0:T(8,128)(2,1)} %tokens.1) | copy-start | bytes 393220
  26.4 17.6 %copy-start.13 = (bf16[4,2048]{1,0:T(4,128)(2,1)S(1)}, bf16[4,2048]{1,0:T(4,128)(2,1)}, u32[]{:S(2)}) copy-start(bf16[4,2048]{1,0:T(4,128)(2,1)} %param.29) | copy-start | bytes 49156
  26.4 17.6 %copy-start.14 = (bf16[4,2048]{1,0:T(4,128)(2,1)S(1)}, bf16[4,2048]{1,0:T(4,128)(2,1)}, u32[]{:S(2)}) copy-start(bf16[4,2048]{1,0:T(4,128)(2,1)} %param.28) | copy-start | bytes 49156
  26.4 17.7 %copy-start.4 = (bf16[512,512]{1,0:T(8,128)(2,1)S(1)}, bf16[512,512]{1,0:T(8,128)(2,1)}, u32[]{:S(2)}) copy-start(bf16[512,512]{1,0:T(8,128)(2,1)} %constant.52.clone) | copy-start | bytes 1572868
  39.4 5.0 %copy-start.9 = (bf16[16,512]{1,0:T(8,128)(2,1)S(1)}, bf16[16,512]{1,0:T(8,128)(2,1)}, u32[]{:S(2)}) copy-start(bf16[16,512]{1,0:T(8,128)(2,1)} %param.30) | copy-start | bytes 49156
  39.4 5.0 %copy-start.15 = (bf16[4,512]{1,0:T(4,128)(2,1)S(1)}, bf16[4,512]{1,0:T(4,128)(2,1)}, u32[]{:S(2)}) copy-start(bf16[4,512]{1,0:T(4,128)(2,1)} %param.25) | copy-start | bytes 12292
  40.4 19.1 %all-to-all-start = ((bf16[8,128,512]{2,1,0:T(8,128)(2,1)}), bf16[8,128,512]{2,1,0:T(8,128)(2,1)S(1)}, u32[]{:S(2)}, u32[]{:S(2)}) async-start(bf16[8,128,512]{2,1,0:T(8,128)(2,1)} %broadcast_in_dim.21), calls=%async_computation | async-start | bytes 2097152 | tf_op jit(solution)/shard_map/all_to_all | solution.py:300
  59.5 8.2 %copy-start.2 = (bf16[8,128,512]{2,1,0:T(8,128)(2,1)}, bf16[8,128,512]{2,1,0:T(8,128)(2,1)S(1)}, u32[]{:S(2)}) copy-start(bf16[8,128,512]{2,1,0:T(8,128)(2,1)S(1)} %all-to-all-done.near) | copy-start | bytes 3145732
  61.9 35.8 %all-to-all-start.4 = ((bf16[128,4,2048]{2,1,0:T(4,128)(2,1)}), bf16[128,4,2048]{2,1,0:T(4,128)(2,1)S(1)}, u32[]{:S(2)}, u32[]{:S(2)}) async-start(bf16[128,4,2048]{2,1,0:T(4,128)(2,1)} %bitcast.38), calls=%async_computation.4 | async-start | bytes 4194304 | tf_op jit(solution)/shard_map/all_to_all | solution.py:300
  67.7 3.6 %collective-permute-start = (bf16[8,128,512]{2,1,0:T(8,128)(2,1)S(1)}, bf16[8,128,512]{2,1,0:T(8,128)(2,1)}, u32[]{:S(2)}, u32[]{:S(2)}) collective-permute-start(bf16[8,128,512]{2,1,0:T(8,128)(2,1)S(1)} %all-to-all-done.near), channel_id=1, source_target_pairs={{0,1},{1,0},{2,3},{3,2},{4,5},{5,4},{6,7},{7,6},{8,9},{9,8},{10,11... | collective-permute-start | bytes 3145736 | tf_op jit(solution)/shard_map/ppermute | solution.py:314
  97.7 15.3 %all-to-all-start.2 = ((bf16[16,32,512]{2,1,0:T(8,128)(2,1)}), bf16[16,32,512]{2,1,0:T(8,128)(2,1)S(1)}, u32[]{:S(2)}, u32[]{:S(2)}) async-start(bf16[16,32,512]{2,1,0:T(8,128)(2,1)} %get-tuple-element.26), calls=%async_computation.2 | async-start | bytes 1048576 | tf_op jit(solution)/shard_map/all_to_all | solution.py:300
  113.0 0.8 copy-start.6
  113.9 12.8 %copy-start.10 = (bf16[4,512]{1,0:T(4,128)(2,1)S(1)}, bf16[4,512]{1,0:T(4,128)(2,1)}, u32[]{:S(2)}) copy-start(bf16[4,512]{1,0:T(4,128)(2,1)} %param.22) | copy-start | bytes 12292
  113.9 12.8 %copy-start.11 = (bf16[4,512]{1,0:T(4,128)(2,1)S(1)}, bf16[4,512]{1,0:T(4,128)(2,1)}, u32[]{:S(2)}) copy-start(bf16[4,512]{1,0:T(4,128)(2,1)} %param.23) | copy-start | bytes 12292
  113.9 12.8 %copy-start.12 = (bf16[4,512]{1,0:T(4,128)(2,1)S(1)}, bf16[4,512]{1,0:T(4,128)(2,1)}, u32[]{:S(2)}) copy-start(bf16[4,512]{1,0:T(4,128)(2,1)} %param.24) | copy-start | bytes 12292
  122.0 15.9 %all-to-all-start.5 = ((bf16[16,32,512]{2,1,0:T(8,128)(2,1)}), bf16[16,32,512]{2,1,0:T(8,128)(2,1)S(1)}, u32[]{:S(2)}, u32[]{:S(2)}) async-start(bf16[16,32,512]{2,1,0:T(8,128)(2,1)} %get-tuple-element.28), calls=%async_computation.5 | async-start | bytes 1048576 | tf_op jit(solution)/shard_map/all_to_all | solution.py:300
  137.8 1.6 copy-start.5
  139.4 29.4 %all-to-all-start.7 = ((bf16[128,4,1536]{2,1,0:T(4,128)(2,1)}), bf16[128,4,1536]{2,1,0:T(4,128)(2,1)S(1)}, u32[]{:S(2)}, u32[]{:S(2)}) async-start(bf16[128,4,1536]{2,1,0:T(4,128)(2,1)} %broadcast_in_dim.56), calls=%async_computation.7 | async-start | bytes 3145728 | tf_op jit(solution)/shard_map/all_to_all | solution.py:300
  157.1 27.4 %copy-start.3 = (bf16[4,128,1024]{2,1,0:T(8,128)(2,1)S(1)}, bf16[4,128,1024]{2,1,0:T(8,128)(2,1)}, u32[]{:S(2)}) copy-start(bf16[4,128,1024]{2,1,0:T(8,128)(2,1)} %get-tuple-element.34) | copy-start | bytes 3145732
  168.9 42.6 %copy-start = (bf16[128,4,1536]{2,1,0:T(4,128)(2,1)}, bf16[128,4,1536]{2,1,0:T(4,128)(2,1)S(1)}, u32[]{:S(2)}) copy-start(bf16[128,4,1536]{2,1,0:T(4,128)(2,1)S(1)} %all-to-all-done.7) | copy-start | bytes 4718596
  203.0 14.5 %all-to-all-start.6 = ((bf16[16,96,128]{2,1,0:T(8,128)(2,1)}), bf16[16,96,128]{2,1,0:T(8,128)(2,1)S(1)}, u32[]{:S(2)}, u32[]{:S(2)}) async-start(bf16[16,96,128]{2,1,0:T(8,128)(2,1)} %shard_map.275.d_lin), calls=%async_computation.6 | async-start | bytes 786432 | tf_op jit(solution)/shard_map/all_to_all | solution.py:300
  217.5 0.7 copy-start.7
  218.2 34.3 %all-to-all-start.10 = ((bf16[128,4,2048]{2,1,0:T(4,128)(2,1)}), bf16[128,4,2048]{2,1,0:T(4,128)(2,1)S(1)}, u32[]{:S(2)}, u32[]{:S(2)}) async-start(bf16[128,4,2048]{2,1,0:T(4,128)(2,1)} %reshape.119), calls=%async_computation.10 | async-start | bytes 4194304 | tf_op jit(solution)/shard_map/all_to_all | solution.py:300
  232.7 21.6 %copy-start.1 = (f32[512,512]{1,0:T(8,128)S(1)}, f32[512,512]{1,0:T(8,128)}, u32[]{:S(2)}) copy-start(f32[512,512]{1,0:T(8,128)} %constant.53.clone) | copy-start | bytes 3145732

commit v2 on v1

v2 whole, which is shorter than its diff:
```python
import math

import jax
import jax.numpy as jnp
import numpy as np
from jax import lax
from jax.experimental import pallas as pl
from jax.experimental.pallas import tpu as pltpu
from jax.sharding import Mesh
from jax.sharding import PartitionSpec as P

HEADS = 16
HEAD = 32
HALF = HEAD // 2
D = 512
FF = 2048
LEN = 2048
ROWS = 128
TEAM = 4
TEAM_ROWS = TEAM * ROWS
FF_PART = FF // TEAM
DEVICES = 128
SEQ = 16
DP = 8
AUG = 48

EPS = 1e-05
MASKED = -1.0e9
SCALE = HEAD**-0.5
LOG2E = math.log2(math.e)
LN2 = math.log(2.0)

f32 = jnp.float32
bf16 = jnp.bfloat16
WINDOW = ("y", "z", "core")
CHIPS = ("y", "z")
SLICE = ("z_lo", "y", "z", "core")
ALL = ("z_lo", "x", "y", "z", "core")


def nn(a, b):
    return lax.dot_general(a, b, (((1,), (0,)), ((), ())), preferred_element_type=f32)


def nt(a, b):
    return lax.dot_general(a, b, (((1,), (1,)), ((), ())), preferred_element_type=f32)


def tn(a, b):
    return lax.dot_general(a, b, (((0,), (0,)), ((), ())), preferred_element_type=f32)


def norm_parts(x):
    centered = x - jnp.mean(x, -1, keepdims=True)
    inv = lax.rsqrt(jnp.mean(centered * centered, -1, keepdims=True) + EPS)
    return centered * inv, inv


def norm_back(grad, scaled, inv, gain):
    e = grad * gain
    return inv * (
        e - jnp.mean(e, -1, keepdims=True) - scaled * jnp.mean(e * scaled, -1, keepdims=True)
    )


def split3(row):
    hi = row.astype(bf16)
    rest = row - hi.astype(f32)
    mid = rest.astype(bf16)
    low = (rest - mid.astype(f32)).astype(bf16)
    return [hi.astype(f32), mid.astype(f32), low.astype(f32)]


def key_columns(keys_t, length):
    place = lax.broadcasted_iota(jnp.int32, (1, LEN), 1)
    mask = jnp.where(place < length, 0.0, MASKED).astype(f32)
    ones = jnp.ones((3, LEN), f32)
    pad = jnp.zeros((128 - HEAD - 4, LEN), f32)
    return jnp.concatenate([keys_t, mask, ones, pad], 0).T.astype(bf16)[:, :AUG]


def with_rows(data_t, rows):
    pad = jnp.zeros((AUG - HEAD - len(rows), data_t.shape[1]), f32)
    return jnp.concatenate([data_t.astype(f32)] + rows + [pad], 0).astype(bf16)


def after(value, *others):
    def kernel(*refs):
        pass

    return pl.pallas_call(
        kernel,
        out_shape=jax.ShapeDtypeStruct(value.shape, value.dtype),
        in_specs=[pl.BlockSpec(memory_space=pl.ANY)] * (1 + len(others)),
        out_specs=pl.BlockSpec(memory_space=pl.ANY),
        input_output_aliases={0: 0},
    )(value, *others)


def copy_after(value, other):
    def kernel(value_ref, other_ref, out_ref):
        out_ref[...] = value_ref[...]

    return call(kernel, [VM, HBM], [(value.shape, value.dtype)])(value, other)[0]


FEED_LANES = FF_PART * 3 + D
GRAD_LANES = FEED_LANES + 128
MSG_ROWS = ROWS + 48


def pack_kernel(
    tokens, w_query, w_key, w_value, w_output, w_gate, w_up, w_down, gain1, bias1, gain2, bias2,
    order, sent,
):
    narrow = [w[...].astype(f32) for w in (w_query, w_key, w_value)]
    gate = w_gate[...].astype(f32)
    up = w_up[...].astype(f32)
    down = w_down[...].astype(f32)
    pieces = []
    for u in range(4):
        here = slice(512 * u, 512 * (u + 1))
        pieces.append(jnp.concatenate([gate[:, here], up[:, here]], 0))
    wide = nn(jnp.concatenate(pieces, 0).astype(bf16), order[...])
    lane = lax.broadcasted_iota(jnp.int32, (4, 128), 1)
    row = lax.broadcasted_iota(jnp.int32, (4, 128), 0)
    norms = jnp.zeros((4, 128), f32)
    for n, ref in enumerate((gain1, bias1, gain2, bias2)):
        for i in range(4):
            value = ref[i : i + 1].astype(f32).reshape(1, 1)
            norms = norms + jnp.where((lane == 96 + n) & (row == i), value, 0.0)
    out = w_output[...].astype(f32)
    nothing = jnp.zeros((4, 512), f32)
    for z in range(2):
        mine = []
        for t in (2 * z, 2 * z + 1):
            cols = slice(128 * t, 128 * (t + 1))
            mine.append(jnp.concatenate([wide[8 * u : 8 * u + 4, cols] for u in range(4)], 1))
            mine.append(jnp.concatenate([wide[8 * u + 4 : 8 * u + 8, cols] for u in range(4)], 1))
            mine.append(down[4 * t : 4 * t + 4])
        mine = jnp.concatenate(mine + [out] + narrow, 0)
        for y in range(4):
            tile = slice(128 * y, 128 * (y + 1))
            heads = []
            for t in (2 * z, 2 * z + 1):
                q, k, v = (
                    pltpu.roll(w[:, tile], (HEAD * (i - t)) % 128, 1)
                    for i, w in enumerate(narrow)
                )
                heads.append(
                    jnp.where(
                        lane < 32, q, jnp.where(lane < 64, k, jnp.where(lane < 96, v, norms))
                    )
                )
            heads = jnp.concatenate(heads + [nothing[:, :256]], 1)
            low = jnp.concatenate([mine, heads, nothing], 0).astype(bf16)
            sent[2 * y + z, 0:ROWS, :] = tokens[0]
            sent[2 * y + z, ROWS:, :] = low


def unpack_kernel(place, near, far, cot, feed, head, whole, rows, arrived):
    loads = [
        pltpu.make_async_copy(source.at[:, ROWS:, :], rows.at[i], arrived.at[i])
        for i, source in enumerate((near, far))
    ]
    for load in loads:
        load.start()
    for load in loads:
        load.wait()
    second = place[0] == 1
    for group in range(4):
        blocks = []
        for chip in (2 * group, 2 * group + 1):
            own = rows[0, chip].astype(f32)
            other = rows[1, chip].astype(f32)
            blocks += [jnp.where(second, other, own), jnp.where(second, own, other)]
        here = slice(16 * group, 16 * (group + 1))
        for i in range(3):
            cols = jnp.concatenate(
                [
                    jnp.where(second, b[4 * (i + 3) : 4 * (i + 4)], b[4 * i : 4 * (i + 1)])
                    for b in blocks
                ],
                0,
            )
            feed[0, here, D * i : D * (i + 1)] = cols.astype(bf16)
        for i in range(4):
            cols = jnp.concatenate([b[4 * (i + 6) : 4 * (i + 7)] for b in blocks], 0).astype(bf16)
            if i == 0:
                feed[0, here, 3 * D : 4 * D] = cols
            else:
                whole[0, here, D * (i - 1) : D * i] = cols
        cols = jnp.concatenate(
            [jnp.where(second, b[40:44, 128:256], b[40:44, 0:128]) for b in blocks], 0
        )
        head[0, here, :] = cols.astype(bf16)


def block_of(place, chip, other):
    return 2 * chip + (place[0] ^ other)


def attend_kernel(
    place, length, near, far, h0, h1, h2, h3, h4, h5, h6, h7, cos, sin,
    sent, q_out, k_out, v_out, o_out, lse_out, cols_out,
    q_t, k_t, v_t, head_cols,
):
    for step, head in enumerate((h0, h1, h2, h3, h4, h5, h6, h7)):
        k, by = step // 4, step % 4
        head_cols[(place[5] ^ k) * 4 + lax.rem(place[4] + 4 - by, 4)] = head[0]
    cols = head_cols[...].reshape(D, 128).astype(f32).T
    cols_out[...] = cols
    gain = cols[96:97, :]
    bias = cols[97:98, :]
    weights_t = cols[0:96, :].astype(bf16)
    for index in range(8):
        source, first = (near, far)[index // 4], 2 * (index % 4)
        x = source[first : first + 2, 0:ROWS, :].reshape(2 * ROWS, D).astype(f32)
        scaled, _ = norm_parts(x)
        normed = (scaled * gain + bias).astype(bf16)
        lin = nt(weights_t, normed)
        for one in range(2):
            block = block_of(place, first + one, index // 4)
            here = pl.ds(pl.multiple_of(block * ROWS, ROWS), ROWS)
            part = lin[:, one * ROWS : (one + 1) * ROWS]
            c = cos[:, here]
            s = sin[:, here]
            q1, q2 = part[0:16], part[16:32]
            k1, k2 = part[32:48], part[48:64]
            fold = SCALE * LOG2E
            q_t[:, here] = (
                jnp.concatenate([q1 * c - q2 * s, q2 * c + q1 * s], 0) * fold
            ).astype(bf16)
            k_t[:, here] = jnp.concatenate([k1 * c - k2 * s, k2 * c + k1 * s], 0).astype(bf16)
            v_t[:, here] = part[64:96].astype(bf16)
    q_out[...] = q_t[...]
    k_out[...] = k_t[...]
    v_out[...] = v_t[...]
    keys = key_columns(k_t[...].astype(f32), length[0])
    one_row = jnp.ones((1, LEN), f32)
    values_t = with_rows(v_t[...], [one_row])
    tile = TEAM_ROWS
    for i in range(LEN // tile):
        here = slice(i * tile, (i + 1) * tile)
        queries_t = with_rows(q_t[:, here], [jnp.ones((1, tile), f32)])
        scores = nn(keys, queries_t)
        top = jnp.max(scores, axis=0, keepdims=True)
        weights = jnp.exp2(scores - top).astype(bf16)
        mixed = nn(values_t, weights)
        total = mixed[HEAD : HEAD + 1]
        out = mixed[:HEAD] / total
        o_out[:, here] = out
        lse_out[:, here] = top + jnp.log2(total)
        low = out.astype(bf16)
        for t in range(TEAM):
            sent[TEAM * i + t] = low


def load_part(place, weights, parts, arrived, i):
    return [
        pltpu.make_async_copy(
            weights.at[x, place[5] ^ k, :, 512 * i : 512 * (i + 1)],
            parts.at[i, k, x],
            arrived.at[8 * i + 4 * k + x],
        )
        for k in range(2)
        for x in range(4)
    ]


def finish(copies):
    for copy in copies:
        copy.wait()


def feed_kernel(
    place, length, mixed, near, far, cot_near, cot_far, weights, head_cols, other,
    sent, kept, swapped, grads, norm_rows,
    tokens, cot, back, ahead, parts, arrived, tokens_arrived,
):
    core, team, z = place[0], place[1], place[2]
    token_loads = []
    for one in range(2):
        for other, source in enumerate((near, far)):
            here = pl.ds(pl.multiple_of((2 * (z ^ one) + (core ^ other)) * ROWS, ROWS), ROWS)
            token_loads.append(
                pltpu.make_async_copy(
                    source.at[2 * team + (z ^ one), 0:ROWS, :],
                    tokens.at[here, :],
                    tokens_arrived.at[2 * one + other],
                )
            )
    for load in token_loads:
        load.start()
    member = 2 * z + core
    for one in range(2):
        here = pl.ds(pl.multiple_of((2 * (z ^ one) + core) * ROWS, ROWS), ROWS)
        there = pl.ds(pl.multiple_of((2 * (z ^ one) + 1 - core) * ROWS, ROWS), ROWS)
        cot[here, :] = cot_near[one]
        cot[there, :] = cot_far[one]
    gain = head_cols[98:99, :]
    bias = head_cols[99:100, :]
    loads = [load_part(place, weights, parts, arrived, i) for i in (3, 0, 1, 2)]
    for load in loads:
        for copy in load:
            copy.start()
    mixed_t = mixed[...].reshape(D, TEAM_ROWS)
    finish(token_loads)
    finish(loads[0])
    w_out = parts[3].reshape(D, D)
    row = lax.broadcasted_iota(jnp.int32, (TEAM_ROWS, 1), 0)
    live = (team * TEAM_ROWS + row) < length[0]
    own = (row // ROWS) == member
    middle = tokens[...].astype(f32) + tn(mixed_t, w_out)
    scaled, inv = norm_parts(middle)
    normed = (scaled * gain + bias).astype(bf16)
    finish(loads[1])
    w_gate = parts[0].reshape(D, FF_PART)
    gate = nn(normed, w_gate)
    finish(loads[2])
    w_up = parts[1].reshape(D, FF_PART)
    up = nn(normed, w_up)
    finish(loads[3])
    w_down = parts[2].reshape(FF_PART, D)
    sig = jax.nn.sigmoid(gate)
    act = gate * sig
    hidden = (act * up).astype(bf16)
    out_part = nn(hidden, w_down) + jnp.where(own, middle, 0.0)
    d_out = jnp.where(live, cot[...].astype(f32), 0.0)
    d_out_low = d_out.astype(bf16)
    d_hidden = nt(d_out_low, w_down)
    d_up = (d_hidden * act).astype(bf16)
    d_gate = (d_hidden * up * sig * (1.0 + gate * (1.0 - sig))).astype(bf16)
    d_normed = nt(d_gate, w_gate) + nt(d_up, w_up)
    d_middle = jnp.where(own, d_out, 0.0) + norm_back(d_normed, scaled, inv, gain)
    d_middle_low = d_middle.astype(bf16)
    sent[...] = nt(w_out, d_middle_low).astype(bf16).reshape(HEADS, HEAD, TEAM_ROWS)
    back[...] = d_middle_low
    ahead[...] = out_part.astype(bf16)
    for one in range(2):
        for target, other in ((kept, core), (swapped, 1 - core)):
            here = pl.ds(pl.multiple_of((2 * (z ^ one) + other) * ROWS, ROWS), ROWS)
            target[one, :, 0:D] = back[here, :]
            target[one, :, D : 2 * D] = ahead[here, :]
    for i, grad in enumerate(
        (
            tn(normed, d_gate),
            tn(normed, d_up),
            tn(hidden, d_out_low),
            nn(mixed_t, d_middle_low),
        )
    ):
        low = grad.astype(bf16)
        for k in range(2):
            for x in range(4):
                at = 64 * (4 * k + x)
                grads[x, k, :, D * i : D * (i + 1)] = low[at : at + 64]
    norm_rows[0:1, :] = jnp.sum(d_normed * scaled, 0, keepdims=True)
    norm_rows[1:2, :] = jnp.sum(d_normed, 0, keepdims=True)
    norm_rows[2:8, :] = jnp.zeros((6, D), f32)


def add_kernel(kept, arrived, own, other):
    own[...] = (kept[0].astype(f32) + arrived[0].astype(f32)).astype(bf16)
    other[...] = (kept[1].astype(f32) + arrived[1].astype(f32)).astype(bf16)


def attend_back_kernel(
    length, d_mixed, q_in, k_in, v_in, o_in, lse_in, cos, sin, sent, d_o, probs, d_scores, dq, dk, dv
):
    for y in range(LEN // TEAM_ROWS):
        total = d_mixed[TEAM * y].astype(f32)
        for t in range(1, TEAM):
            total = total + d_mixed[TEAM * y + t].astype(f32)
        d_o[:, y * TEAM_ROWS : (y + 1) * TEAM_ROWS] = total.astype(bf16)
    keys_t = k_in[...]
    keys = key_columns(keys_t.astype(f32), length[0])
    ones = jnp.ones((4, LEN), f32)
    pad = jnp.zeros((128 - HEAD - 4, LEN), f32)
    values = jnp.concatenate([v_in[...].astype(f32), ones, pad], 0).T.astype(bf16)[:, :AUG]
    d_o_t = d_o[...]
    inner = jnp.sum(d_o_t.astype(f32) * o_in[...], 0, keepdims=True)
    zero_row = jnp.zeros((1, LEN), f32)
    one_row = jnp.ones((1, LEN), f32)
    q_rows = with_rows(q_in[...], [one_row] + split3(-lse_in[...]))
    do_rows = with_rows(d_o_t, [zero_row] + split3(-inner))
    tile = 512
    for i in range(LEN // tile):
        here = slice(i * tile, (i + 1) * tile)
        p = jnp.exp2(nn(keys, q_rows[:, here]))
        ds = (p * nn(values, do_rows[:, here])).astype(bf16)
        probs[:, here] = p.astype(bf16)
        d_scores[:, here] = ds
        dq[:, here] = nn(keys_t, ds) * SCALE
    dk[...] = nt(q_in[...], d_scores[...]) * LN2
    dv[...] = nt(d_o_t, probs[...])
    c = cos[...]
    s = sin[...]
    q1, q2 = dq[0:HALF], dq[HALF:HEAD]
    k1, k2 = dk[0:HALF], dk[HALF:HEAD]
    dq_t = jnp.concatenate([q1 * c + q2 * s, q2 * c - q1 * s], 0).astype(bf16)
    dk_t = jnp.concatenate([k1 * c + k2 * s, k2 * c - k1 * s], 0).astype(bf16)
    dv_t = dv[...].astype(bf16)
    for b in range(SEQ):
        here = slice(b * ROWS, (b + 1) * ROWS)
        sent[b, 0:32] = dq_t[:, here]
        sent[b, 32:64] = dk_t[:, here]
        sent[b, 64:96] = dv_t[:, here]


def head_grad_kernel(
    near, far, head_cols, d_lin, norm_rows, place, sent0, sent1, sent2, sent3, table
):
    gain = head_cols[96:97, :]
    bias = head_cols[97:98, :]
    weights_t = head_cols[0:96, :].astype(bf16)
    total = jnp.zeros((96, D), f32)
    d_gain = jnp.zeros((1, D), f32)
    d_bias = jnp.zeros((1, D), f32)
    for index in range(8):
        source, first = (near, far)[index // 4], 2 * (index % 4)
        x = source[first : first + 2, 0:ROWS, :].reshape(2 * ROWS, D).astype(f32)
        scaled, _ = norm_parts(x)
        normed = (scaled * gain + bias).astype(bf16)
        d_part = jnp.concatenate(
            [d_lin[block_of(place, first + one, index // 4)] for one in range(2)], 1
        )
        total = total + nn(d_part, normed)
        d_normed = tn(d_part, weights_t)
        d_gain = d_gain + jnp.sum(d_normed * scaled, 0, keepdims=True)
        d_bias = d_bias + jnp.sum(d_normed, 0, keepdims=True)
    pad = jnp.zeros((28, D), f32)
    table[...] = jnp.concatenate([total, d_gain, d_bias, norm_rows[0:2, :], pad], 0).T
    for step, sent in enumerate((sent0, sent1, sent2, sent3)):
        x = lax.rem(place[4] + step, 4)
        for k in range(2):
            at = pl.multiple_of((4 * k + x) * 64, 64)
            sent[k] = table[pl.ds(at, 64), :].astype(bf16)


def regroup_kernel(part0, part1, part2, part3, feed, sent):
    heads = part0[...].astype(f32)
    for part in (part1, part2, part3):
        heads = heads + part[...].astype(f32)
    total = jnp.concatenate([feed[...].astype(f32), heads.reshape(128, 128)], 1)
    for d in range(SEQ * 2):
        sent[d] = total[4 * d : 4 * d + 4].astype(bf16)


def input_grad_kernel(
    place, length, tokens, d_lin, weights, w0, w1, head_cols,
    grad_tokens, layer_output,
    parts, arrived,
):
    loads = [load_part(place, weights, parts, arrived, i) for i in range(3)]
    for load in loads:
        for copy in load:
            copy.start()
    seq = place[3]
    gain = head_cols[96:97, :]
    scaled, inv = norm_parts(tokens[0].astype(f32))
    d_t = jnp.zeros((D, ROWS), f32)
    for part, load in enumerate(loads):
        d_part = d_lin[:, part * HEAD : (part + 1) * HEAD, :].reshape(D, ROWS)
        finish(load)
        d_t = d_t + nn(parts[part].reshape(D, D), d_part)
    total = w0[...].astype(f32) + w1[...].astype(f32)
    grad_tokens[0] = total[:, 0:D] + norm_back(d_t.T, scaled, inv, gain)
    row = lax.broadcasted_iota(jnp.int32, (ROWS, 1), 0)
    live = (seq * ROWS + row) < length[0]
    layer_output[0] = jnp.where(live, total[:, D : 2 * D], 0.0).astype(bf16)


def sum_kernel(
    parts, order, gain1, bias1, grad_query, grad_key, grad_value, grad_output, gain2, bias2,
    grad_gate, grad_up, grad_down,
):
    members = []
    for t in range(TEAM):
        total = parts[t, :, :FEED_LANES].astype(f32)
        for other in range(1, 2 * SEQ // TEAM):
            total = total + parts[TEAM * other + t, :, :FEED_LANES].astype(f32)
        members.append(total)
        grad_down[4 * t : 4 * t + 4, :] = total[:, 1024:1536]
    grad_output[...] = sum(m[:, 1536:2048] for m in members)
    pieces = []
    for u in range(4):
        for at in (128 * u, 512 + 128 * u):
            pieces.append(jnp.concatenate([m[:, at : at + 128] for m in members], 1))
    wide = jnp.concatenate(pieces, 0)
    high = wide.astype(bf16)
    low = (wide - high.astype(f32)).astype(bf16)
    wide = nt(high, order[...]) + nt(low, order[...])
    for u in range(4):
        here = slice(512 * u, 512 * (u + 1))
        grad_gate[:, here] = wide[8 * u : 8 * u + 4]
        grad_up[:, here] = wide[8 * u + 4 : 8 * u + 8]
    heads = [
        parts[h, :, FEED_LANES:].astype(f32) + parts[SEQ + h, :, FEED_LANES:].astype(f32)
        for h in range(HEADS)
    ]
    lane = lax.broadcasted_iota(jnp.int32, (4, 128), 1)
    row = lax.broadcasted_iota(jnp.int32, (4, 128), 0)
    for i, grad in enumerate((grad_query, grad_key, grad_value)):
        for u in range(4):
            tile = jnp.zeros((4, 128), f32)
            for r in range(4):
                moved = pltpu.roll(heads[4 * u + r], (HEAD * (r - i)) % 128, 1)
                tile = jnp.where(lane // HEAD == r, moved, tile)
            grad[:, 128 * u : 128 * (u + 1)] = tile
    norms = sum(heads)
    for n, grad in enumerate((gain1, bias1, gain2, bias2)):
        column = jnp.where(lane == row, norms[:, 96 + n : 97 + n], 0.0)
        grad[...] = jnp.sum(column, 0)[0:4]


VM = pl.BlockSpec(memory_space=pltpu.VMEM)
SM = pl.BlockSpec(memory_space=pltpu.SMEM)
HBM = pl.BlockSpec(memory_space=pl.ANY)


def call(kernel, specs, outs, scratch=()):
    return pl.pallas_call(
        kernel,
        out_shape=tuple(jax.ShapeDtypeStruct(shape, kind) for shape, kind in outs),
        in_specs=specs,
        out_specs=tuple(VM for _ in outs),
        scratch_shapes=[
            pltpu.SemaphoreType.DMA((s,)) if isinstance(s, int) else pltpu.VMEM(*s) for s in scratch
        ],
        compiler_params=pltpu.CompilerParams(vmem_limit_bytes=56 * 2**20),
        cost_estimate=pl.CostEstimate(flops=0, bytes_accessed=0, transcendentals=0),
    )


def rope_tables():
    freq = 10000.0 ** (-2.0 * np.arange(HALF) / HEAD)
    angles = freq[:, None] * np.arange(LEN)[None, :]
    return np.cos(angles).astype(np.float32), np.sin(angles).astype(np.float32)


def column_order():
    order = np.arange(512).reshape(4, 8, TEAM, 4).transpose(2, 0, 1, 3).reshape(-1)
    table = np.zeros((512, 512), np.float32)
    table[order, np.arange(512)] = 1.0
    return table


def exchange(value, axes):
    return lax.all_to_all(value, axes, 0, 0, tiled=True)


def swap(value, axis):
    return lax.ppermute(value, axis, [(0, 1), (1, 0)])


def step_dp(value, k, by):
    if k == by == 0:
        return value
    moves = [
        (4 * z + x, 4 * (z ^ k) + (x + by) % 4) for z in range(2) for x in range(4)
    ]
    return lax.ppermute(value, ("z_lo", "x"), moves)


def shift(value, by):
    return lax.ppermute(value, "x", [(i, (i + by) % 4) for i in range(4)])


def shards(
    tokens, lengths, norm1_gain, norm1_bias, w_query, w_key, w_value, w_output,
    norm2_gain, norm2_bias, w_gate, w_up, w_down, cotangent,
):
    y = lax.axis_index("y")
    z = lax.axis_index("z")
    core = lax.axis_index("core")
    place = jnp.stack([core, y, z, 4 * y + 2 * z + core, lax.axis_index("x"), lax.axis_index("z_lo")]).astype(jnp.int32)
    cos, sin = (jnp.asarray(table) for table in rope_tables())
    order = jnp.asarray(column_order(), bf16)

    (packed,) = call(
        pack_kernel,
        [VM] * 13,
        [((8, MSG_ROWS, D), bf16)],
    )(
        tokens, w_query, w_key, w_value, w_output, w_gate, w_up, w_down,
        norm1_gain, norm1_bias, norm2_gain, norm2_bias, order,
    )
    near = exchange(packed, CHIPS)
    cot_pair = jnp.concatenate([cotangent, swap(cotangent, "z")], 0)
    near = after(near, cot_pair)
    far = swap(near, "core")
    cot_far = swap(cot_pair, "core")

    feed_rows, head, whole = call(
        unpack_kernel,
        [SM, HBM, HBM, HBM],
        [((1, 64, FEED_LANES), bf16), ((1, 64, 128), bf16), ((1, 64, 3 * D), bf16)],
        [((2, 8, 48, D), bf16), 2],
    )(place, near, far, cot_far)
    heads = [step_dp(head, k, by) for k in range(2) for by in range(4)]
    feed_rows = jnp.concatenate([feed_rows, swap(feed_rows, "z_lo")], 0)
    feed_weights = lax.all_gather(after(feed_rows, *heads[1:]), "x")
    whole_other = swap(whole, "z_lo")

    sent, q_t, k_t, v_t, o_t, lse, head_cols = call(
        attend_kernel,
        [SM, SM] + [VM] * 12,
        [
            ((SEQ, HEAD, TEAM_ROWS), bf16),
            ((HEAD, LEN), bf16),
            ((HEAD, LEN), bf16),
            ((HEAD, LEN), bf16),
            ((HEAD, LEN), f32),
            ((1, LEN), f32),
            ((128, D), f32),
        ],
        [((HEAD, LEN), bf16)] * 3
        + [((DP, 64, 128), bf16)],
    )(place, lengths, near, far, *heads, cos, sin)
    mixed = exchange(after(sent, whole_other), WINDOW)
    whole = jnp.concatenate([whole, whole_other], 0)
    d_sent, kept, swapped, grads, norm_rows = call(
        feed_kernel,
        [SM, SM, VM, HBM, HBM, VM, VM, HBM, VM, HBM],
        [((HEADS, HEAD, TEAM_ROWS), bf16)]
        + [((2, ROWS, 2 * D), bf16)] * 2
        + [((4, 2, 64, FEED_LANES), bf16), ((8, D), f32)],
        [((TEAM_ROWS, D), bf16)] * 4 + [((4, 2, 4, 64, 512), bf16), 32, 4],
    )(
        place, lengths, mixed, near, far, cot_pair, cot_far,
        feed_weights, head_cols, whole,
    )
    row_weights = lax.all_gather(after(whole, grads), "x")
    d_mixed = exchange(d_sent, WINDOW)
    feed_grads = lax.psum_scatter(
        grads.reshape(D, FEED_LANES), "x", scatter_dimension=0, tiled=True
    )
    w0, w1 = call(add_kernel, [VM] * 2, [((ROWS, 2 * D), bf16)] * 2)(kept, swap(swapped, "core"))
    w1 = swap(w1, "z")
    (lin_sent,) = call(
        attend_back_kernel,
        [SM] + [VM] * 8,
        [((SEQ, 96, ROWS), bf16)],
        [
            ((HEAD, LEN), bf16),
            ((LEN, LEN), bf16),
            ((LEN, LEN), bf16),
            ((HEAD, LEN), f32),
            ((HEAD, LEN), f32),
            ((HEAD, LEN), f32),
        ],
    )(lengths, d_mixed, q_t, k_t, v_t, o_t, lse, cos, sin)
    lin_sent = after(lin_sent, w1)
    back = exchange(lin_sent, WINDOW)
    head_grads = call(
        head_grad_kernel,
        [VM] * 5 + [SM],
        [((2, 64, 128), bf16)] * 4,
        [((D, 128), f32)],
    )(near, far, head_cols, lin_sent, norm_rows, place)
    head_grads = [head_grads[0]] + [shift(head_grads[step], step) for step in range(1, 4)]
    (grad_sent,) = call(
        regroup_kernel,
        [VM] * 5,
        [((2 * SEQ, 4, GRAD_LANES), bf16)],
    )(*head_grads, feed_grads)
    grad_parts = exchange(after(grad_sent, back), SLICE)

    grad_tokens, layer_output = call(
        input_grad_kernel,
        [SM, SM] + [VM] * 2 + [HBM] + [VM] * 3,
        [((1, ROWS, D), f32), ((1, ROWS, D), bf16)],
        [((3, 2, 4, 64, 512), bf16), 24],
    )(place, lengths, tokens, back, row_weights, w0, w1, head_cols)
    weight_grads = call(
        sum_kernel,
        [VM] * 2,
        [((4,), f32)] * 2 + [((4, D), f32)] * 4 + [((4,), f32)] * 2
        + [((4, FF), f32)] * 2 + [((16, D), f32)],
    )(grad_parts, order)
    return (layer_output, grad_tokens) + tuple(weight_grads)


def solution(mesh):
    flat = P(ALL)
    rows = P(ALL, None)
    blocks = P(("z_lo", "x"), WINDOW, None)
    return jax.shard_map(
        shards,
        mesh=Mesh(mesh.devices.reshape(2, 4, 4, 2, 2), ALL),
        in_specs=(
            blocks, P(("z_lo", "x")), flat, flat, rows, rows, rows, rows, flat, flat, rows, rows, rows, blocks,
        ),
        out_specs=(
            blocks, blocks, flat, flat, rows, rows, rows, rows, flat, flat, rows, rows, rows,
        ),
        check_vma=False,
    )
```

time: 258 us -> 192 us (0.74)
  blocking collectives: 68.5 us -> 0 us
  waiting for transfers between devices: 84.7 us -> 51 us
  starting transfers between devices: 32.8 us -> 56.9 us
  Pallas kernels: 40.3 us -> 55.4 us
  local copies, waits for them, and re-layouts: 25.1 us -> 11.3 us
  between operations: 1.63 us -> 14.7 us
    all_to_all x4 -> x0, blocking collectives: 68.5 us -> none  [exchange(): lax.all_to_all(value, axes, 0, 0, tiled=True, axis_index_groups=groups)]
    all_to_all x7 -> x5, waiting for transfers between devices: 83.5 us -> 23.3 us  [exchange(): return lax.all_to_all(value, axes, 0, 0, tiled=True)]
    ppermute x1 -> x17, waiting for transfers between devices: 1.17 us -> 26.9 us  [the longest x7 21 us: swap(): return lax.ppermute(value, axis, [(0, 1), (1, 0)])]
    ppermute x1 -> x17, starting transfers between devices: 1.15 us -> 23.3 us  [the longest x7 10.9 us: swap(): return lax.ppermute(value, axis, [(0, 1), (1, 0)])]
    pallas_call x4 -> x15, Pallas kernels: 27.4 us -> 42.5 us  [the longest x1 11.2 us: shards(): call(attend_kernel, [SM, SM] + [VM] * 12, [((SEQ, HEAD, TEAM_ROWS), bf16)...]
    reshape x16 -> x0, local copies, waits for them, and re-layouts: 15 us -> none  [the longest x1 4.09 us: shards(): feed_grads = exchange(grads.reshape(DEVICES, 4, 2048), BOTH)]
    unnamed x32 -> x54, local copies, waits for them, and re-layouts: 1.63 us -> 10.7 us
    broadcast_in_dim x8 -> x0, local copies, waits for them, and re-layouts: 6.03 us -> none  [the longest x1 2.39 us: shards(): jnp.broadcast_to(feed_msg[None], (DEVICES // TEAM, TEAM, 4, 2048))]
  transfers between devices with their start and end apart: 8 -> 25, of which waited for: 8 -> 11; matrix products, arithmetic and copies ran while one was open for 5% -> 1% of each run, Pallas kernels for 13% -> 20%
where the time goes in v2:
time: 192 us; the launch traced here: 191 us
  starting transfers between devices  56.9 us (30%)
  Pallas kernels  55.4 us (29%)
  waiting for transfers between devices  51 us (27%)
  between operations  14.7 us (8%)
  local copies, waits for them, and re-layouts  11.3 us (6%)
    all_to_all x5, starting transfers between devices, exchange(): return lax.all_to_all(value, axes, 0, 0, tiled=True)  33.3 us
    all_to_all x5, waiting for transfers between devices, exchange(): return lax.all_to_all(value, axes, 0, 0, tiled=True)  23.3 us
    ppermute x7, waiting for transfers between devices, swap(): return lax.ppermute(value, axis, [(0, 1), (1, 0)])  21 us
    pallas_call x1, Pallas kernels, shards(): call(attend_back_kernel, [SM] + [VM] * 8, [((SEQ, 96, ROWS), bf16)], [((H...  12.9 us
    pallas_call x1, Pallas kernels, shards(): call(attend_kernel, [SM, SM] + [VM] * 12, [((SEQ, HEAD, TEAM_ROWS), bf16)...  11.2 us
    ppermute x7, starting transfers between devices, swap(): return lax.ppermute(value, axis, [(0, 1), (1, 0)])  10.9 us
    unnamed x54, local copies, waits for them, and re-layouts  10.7 us
    pallas_call x1, Pallas kernels, shards(): call(feed_kernel, [SM, SM, VM, HBM, HBM, VM, VM, HBM, VM, HBM], [((HEADS,...  9.81 us
  transfers between devices with their start and end apart: 25, of which 11 were waited for; matrix products, arithmetic and copies ran while one was open for 1% of the time, Pallas kernels for 20%

profile of v2, /device:TPU:1, one launch (start us, length us, event | category | flops | bytes accessed | tf_op | source)
XLA Modules:
  0.0 191.1 jit_solution(6086783309692169942)
XLA Ops:
  7.2 2.6 %shard_map.264 = bf16[8,176,512]{2,1,0:T(8,128)(2,1)} custom-call(bf16[1,128,512]{2,1,0:T(8,128)(2,1)} %tokens.3, bf16[4,512]{1,0:T(4,128)(2,1)} %w_query.1, bf16[4,512]{1,0:T(4,128)(2,1)} %w_key.1, bf16[4,512]{1,0:T(4,128)(2,1)} %w_value.1, bf16[4,512]{1,0:T(4,128)(2,1)} %w_output.1, bf16[4,2048]{1,0:T(4,128)(2,1)} %w_gate.1, bf16[4,2048]{1,0:T(4,128)(2,1)} %w_up.1, ...), custom_call_target="tpu_custom_call" | custom-call | tf_op jit(solution)/shard_map/pallas_call | solution.py:581
  9.8 8.5 %all-to-all-start = ((bf16[8,176,512]{2,1,0:T(8,128)(2,1)}), bf16[8,176,512]{2,1,0:T(8,128)(2,1)S(1)}, u32[]{:S(2)}, u32[]{:S(2)}) async-start(bf16[8,176,512]{2,1,0:T(8,128)(2,1)} %shard_map.264), calls=%async_computation | async-start | bytes 2883584 | tf_op jit(solution)/shard_map/all_to_all | solution.py:550
  18.3 3.0 %collective-permute-start = (bf16[1,128,512]{2,1,0:T(8,128)(2,1)S(1)}, bf16[1,128,512]{2,1,0:T(8,128)(2,1)S(1)}, u32[]{:S(2)}, u32[]{:S(2)}) collective-permute-start(bf16[1,128,512]{2,1,0:T(8,128)(2,1)S(1)} %copy-done.14), channel_id=1, source_target_pairs={{0,2},{2,0},{1,3},{3,1},{4,6},{6,4},{5,7},{7,5},{8,10},{10,8},{9,1... | collective-permute-start | bytes 393224 | tf_op jit(solution)/shard_map/ppermute | solution.py:554
  21.3 18.1 %collective-permute-done = bf16[1,128,512]{2,1,0:T(8,128)(2,1)S(1)} collective-permute-done((bf16[1,128,512]{2,1,0:T(8,128)(2,1)S(1)}, bf16[1,128,512]{2,1,0:T(8,128)(2,1)S(1)}, u32[]{:S(2)}, u32[]{:S(2)}) %collective-permute-start) | collective-permute-done | bytes 131104 | tf_op jit(solution)/shard_map/ppermute | solution.py:554
  41.3 1.9 collective-permute-start.1
  43.7 2.8 %collective-permute-done.2.cot.cot_far = bf16[2,128,512]{2,1,0:T(8,128)(2,1)S(1)} collective-permute-done((bf16[2,128,512]{2,1,0:T(8,128)(2,1)}, bf16[2,128,512]{2,1,0:T(8,128)(2,1)S(1)}, u32[]{:S(2)}, u32[]{:S(2)}) %collective-permute-start.2) | collective-permute-done | bytes 262176 | tf_op jit(solution)/shard_map/ppermute | solution.py:554
  47.3 1.2 copy-done.1
  48.4 2.8 %shard_map.266 = (bf16[1,64,2048]{2,1,0:T(8,128)(2,1)}, bf16[1,64,128]{2,1,0:T(8,128)(2,1)}, bf16[1,64,1536]{2,1,0:T(8,128)(2,1)}) custom-call(s32[6]{0:T(128)} %stack.27.place, bf16[8,176,512]{2,1,0:T(8,128)(2,1)} %shard_map.265.near, bf16[8,176,512]{2,1,0:T(8,128)(2,1)} %copy-done.1, bf16[2,128,512]{2,1,0:T(8,128)(2,1)} %copy-done.8), custom_call_target="tpu_custom_call" | custom-call | tf_op jit(solution)/shard_map/pallas_call | solution.py:595
  52.0 2.9 %collective-permute-start.9 = (bf16[1,64,128]{2,1,0:T(8,128)(2,1)}, bf16[1,64,128]{2,1,0:T(8,128)(2,1)S(1)}, u32[]{:S(2)}, u32[]{:S(2)}) collective-permute-start(bf16[1,64,128]{2,1,0:T(8,128)(2,1)} %get-tuple-element.47.h0), channel_id=1, source_target_pairs={{0,112},{16,64},{32,80},{48,96},{64,48},{80,0},{96,16},{112,32},{1... | collective-permute-start | bytes 49160 | tf_op jit(solution)/shard_map/ppermute | solution.py:563
  57.7 2.1 %collective-permute-start.5 = (bf16[1,64,128]{2,1,0:T(8,128)(2,1)}, bf16[1,64,128]{2,1,0:T(8,128)(2,1)S(1)}, u32[]{:S(2)}, u32[]{:S(2)}) collective-permute-start(bf16[1,64,128]{2,1,0:T(8,128)(2,1)} %get-tuple-element.47.h0), channel_id=1, source_target_pairs={{0,48},{16,0},{32,16},{48,32},{64,112},{80,64},{96,80},{112,96},{1... | collective-permute-start | bytes 49160 | tf_op jit(solution)/shard_map/ppermute | solution.py:563
  61.6 1.8 pad_maximum_fusion.refs_0_
  67.4 11.2 %shard_map.267 = (bf16[16,32,512]{2,1,0:T(8,128)(2,1)}, bf16[32,2048]{1,0:T(8,128)(2,1)}, bf16[32,2048]{1,0:T(8,128)(2,1)}, bf16[32,2048]{1,0:T(8,128)(2,1)}, f3...) custom-call(s32[6]{0:T(128)} %stack.27.place, s32[1]{0:T(128)S(6)} %copy.44.length, ...), custom_call_target="tpu_custom_call" | custom-call | tf_op jit(solution)/shard_map/pallas_call | solution.py:606
  79.3 8.4 %all-to-all-start.1 = ((bf16[16,32,512]{2,1,0:T(8,128)(2,1)}), bf16[16,32,512]{2,1,0:T(8,128)(2,1)S(1)}, u32[]{:S(2)}, u32[]{:S(2)}) async-start(bf16[16,32,512]{2,1,0:T(8,128)(2,1)} %shard_map.268), calls=%async_computation.1 | async-start | bytes 1048576 | tf_op jit(solution)/shard_map/all_to_all | solution.py:550
  88.1 10.8 %all-to-all-done.1.mixed = bf16[16,32,512]{2,1,0:T(8,128)(2,1)S(1)} async-done(((bf16[16,32,512]{2,1,0:T(8,128)(2,1)}), bf16[16,32,512]{2,1,0:T(8,128)(2,1)S(1)}, u32[]{:S(2)}, u32[]{:S(2)}) %all-to-all-start.1) | async-done | bytes 524320 | tf_op jit(solution)/shard_map/all_to_all | solution.py:550
  99.7 9.8 %shard_map.270 = (bf16[16,32,512]{2,1,0:T(8,128)(2,1)}, bf16[2,128,1024]{2,1,0:T(8,128)(2,1)}, bf16[2,128,1024]{2,1,0:T(8,128)(2,1)}, bf16[4,2,64,2048]{3,2,1,0:T(8,128)(2,1)}, f32[8,512]{1,0:T(8,128)}) custom-call(s32[6]{0:T(128)} %stack.27.place, s32[1]{0:T(128)S(6)} %copy.44.length, bf16[16,32,512]{2,1,0:T(8,128)(2,1)} %copy-done.6, ...), custom_call_target="tpu_custom_call" | custom-call | tf_op jit(solution)/shard_map/pallas_call | solution.py:623
  110.6 1.3 collective-permute-start.12
  111.9 3.5 %all-to-all-start.2 = ((bf16[16,32,512]{2,1,0:T(8,128)(2,1)}), bf16[16,32,512]{2,1,0:T(8,128)(2,1)S(1)}, u32[]{:S(2)}, u32[]{:S(2)}) async-start(bf16[16,32,512]{2,1,0:T(8,128)(2,1)} %get-tuple-element.52), calls=%async_computation.2 | async-start | bytes 1048576 | tf_op jit(solution)/shard_map/all_to_all | solution.py:550
  116.2 2.1 %shard_map.272 = (bf16[128,1024]{1,0:T(8,128)(2,1)}, bf16[128,1024]{1,0:T(8,128)(2,1)}) custom-call(bf16[2,128,1024]{2,1,0:T(8,128)(2,1)} %get-tuple-element.58.kept, bf16[2,128,1024]{2,1,0:T(8,128)(2,1)} %copy-done.12), custom_call_target="tpu_custom_call" | custom-call | tf_op jit(solution)/shard_map/pallas_call | solution.py:639
  118.3 2.8 %collective-permute-start.13 = (bf16[128,1024]{1,0:T(8,128)(2,1)}, bf16[128,1024]{1,0:T(8,128)(2,1)S(1)}, u32[]{:S(2)}, u32[]{:S(2)}) collective-permute-start(bf16[128,1024]{1,0:T(8,128)(2,1)} %get-tuple-element.60), channel_id=1, source_target_pairs={{0,2},{2,0},{1,3},{3,1},{4,6},{6,4},{5,7},{7,5},{8,10},{10,8},{9,1... | collective-permute-start | bytes 786440 | tf_op jit(solution)/shard_map/ppermute | solution.py:554
  121.1 5.4 %all-to-all-done.2.d_mixed = bf16[16,32,512]{2,1,0:T(8,128)(2,1)S(1)} async-done(((bf16[16,32,512]{2,1,0:T(8,128)(2,1)}), bf16[16,32,512]{2,1,0:T(8,128)(2,1)S(1)}, u32[]{:S(2)}, u32[]{:S(2)}) %all-to-all-start.2) | async-done | bytes 524320 | tf_op jit(solution)/shard_map/all_to_all | solution.py:550
  127.3 12.9 %shard_map.271.refs_0_ = bf16[16,96,128]{2,1,0:T(8,128)(2,1)} custom-call(s32[1]{0:T(128)S(6)} %copy.44.length, bf16[16,32,512]{2,1,0:T(8,128)(2,1)} %copy-done.5, bf16[32,2048]{1,0:T(8,128)(2,1)} %get-tuple-element.53.q_in, bf16[32,2048]{1,0:T(8,128)(2,1)} %get-tuple-element.54.k_in, bf16[32,2048]{1,0:T(8,128)(2,1)} %get-tuple-element.55.v_in, ...), custom_call_target="tpu_custom_call" | custom-call | tf_op jit(solution)/shard_map/pallas_call | solution.py:641
  141.0 4.7 %all-to-all-start.3 = ((bf16[16,96,128]{2,1,0:T(8,128)(2,1)}), bf16[16,96,128]{2,1,0:T(8,128)(2,1)S(1)}, u32[]{:S(2)}, u32[]{:S(2)}) async-start(bf16[16,96,128]{2,1,0:T(8,128)(2,1)} %shard_map.273.d_lin), calls=%async_computation.3 | async-start | bytes 786432 | tf_op jit(solution)/shard_map/all_to_all | solution.py:550
  145.6 5.1 %shard_map.276 = (bf16[2,64,128]{2,1,0:T(8,128)(2,1)}, bf16[2,64,128]{2,1,0:T(8,128)(2,1)}, bf16[2,64,128]{2,1,0:T(8,128)(2,1)}, bf16[2,64,128]{2,1,0:T(8,128)(2,1)}) custom-call(bf16[8,176,512]{2,1,0:T(8,128)(2,1)} %shard_map.265.near, bf16[8,176,512]{2,1,0:T(8,128)(2,1)} %copy-done.1, f32[128,512]{1,0:T(8,128)} %get-tuple-element.51.head_cols, ...), custom_call_target="tpu_custom_call" | custom-call | tf_op jit(solution)/shard_map/pallas_call | solution.py:656
  150.9 1.7 collective-permute-start.15
  152.5 1.6 collective-permute-start.16
  154.1 2.4 %collective-permute-done.14.part1 = bf16[2,64,128]{2,1,0:T(8,128)(2,1)S(1)} collective-permute-done((bf16[2,64,128]{2,1,0:T(8,128)(2,1)}, bf16[2,64,128]{2,1,0:T(8,128)(2,1)S(1)}, u32[]{:S(2)}, u32[]{:S(2)}) %collective-permute-start.14) | collective-permute-done | bytes 32800 | tf_op jit(solution)/shard_map/ppermute | solution.py:567
  156.6 1.4 collective-permute-done.16.part3
  158.6 2.0 %shard_map.277.refs_0_ = bf16[32,4,2176]{2,1,0:T(4,128)(2,1)} custom-call(bf16[2,64,128]{2,1,0:T(8,128)(2,1)} %get-tuple-element.66.part0, bf16[2,64,128]{2,1,0:T(8,128)(2,1)} %copy-done.22, bf16[2,64,128]{2,1,0:T(8,128)(2,1)} %copy-done.23, bf16[2,64,128]{2,1,0:T(8,128)(2,1)} %copy-done.24, bf16[128,2048]{1,0:T(8,128)(2,1)} %reduce-scatter.2.cloned.1.call-done.feed), custom_call_target="tpu_custom_call" | custom-call | tf_op jit(solution)/shard_map/pallas_call | solution.py:663
  161.4 8.3 %all-to-all-start.4 = ((bf16[32,4,2176]{2,1,0:T(4,128)(2,1)}), bf16[32,4,2176]{2,1,0:T(4,128)(2,1)S(1)}, u32[]{:S(2)}, u32[]{:S(2)}) async-start(bf16[32,4,2176]{2,1,0:T(4,128)(2,1)} %shard_map.278), calls=%async_computation.5 | async-start | bytes 1114112 | tf_op jit(solution)/shard_map/all_to_all | solution.py:550
  169.7 4.6 %shard_map.275 = (f32[1,128,512]{2,1,0:T(8,128)}, bf16[1,128,512]{2,1,0:T(8,128)(2,1)}) custom-call(s32[6]{0:T(128)} %stack.27.place, s32[1]{0:T(128)S(6)} %copy.44.length, bf16[1,128,512]{2,1,0:T(8,128)(2,1)} %tokens.3, bf16[16,96,128]{2,1,0:T(8,128)(2,1)} %copy-done.3, bf16[4,2,64,1536]{3,2,1,0:T(8,128)(2,1)} %bitcast.11, ...), custom_call_target="tpu_custom_call" | custom-call | tf_op jit(solution)/shard_map/pallas_call | solution.py:670
  174.3 7.2 %all-to-all-done.4.parts = bf16[32,4,2176]{2,1,0:T(4,128)(2,1)S(1)} async-done(((bf16[32,4,2176]{2,1,0:T(4,128)(2,1)}), bf16[32,4,2176]{2,1,0:T(4,128)(2,1)S(1)}, u32[]{:S(2)}, u32[]{:S(2)}) %all-to-all-start.4) | async-done | bytes 557088 | tf_op jit(solution)/shard_map/all_to_all | solution.py:550
  182.3 2.3 %shard_map.279 = (f32[4]{0:T(128)}, f32[4]{0:T(128)}, f32[4,512]{1,0:T(4,128)}, f32[4,512]{1,0:T(4,128)}, f32[4,512]{1,0:T(4,128)}, /*index=5*/f32[4,512]{1,0:T(...) custom-call(bf16[32,4,2176]{2,1,0:T(4,128)(2,1)} %copy-done.4, ...), custom_call_target="tpu_custom_call" | custom-call | tf_op jit(solution)/shard_map/pallas_call | solution.py:676
  (95 shorter events, 19.4 us)
Async XLA Ops:
  9.8 8.5 %copy-start.14 = (bf16[1,128,512]{2,1,0:T(8,128)(2,1)S(1)}, bf16[1,128,512]{2,1,0:T(8,128)(2,1)}, u32[]{:S(2)}) copy-start(bf16[1,128,512]{2,1,0:T(8,128)(2,1)} %param.30) | copy-start | bytes 393220
  9.8 29.7 %all-to-all-start = ((bf16[8,176,512]{2,1,0:T(8,128)(2,1)}), bf16[8,176,512]{2,1,0:T(8,128)(2,1)S(1)}, u32[]{:S(2)}, u32[]{:S(2)}) async-start(bf16[8,176,512]{2,1,0:T(8,128)(2,1)} %shard_map.264), calls=%async_computation | async-start | bytes 2883584 | tf_op jit(solution)/shard_map/all_to_all | solution.py:550
  18.2 80.7 %all-gather.5.cloned.1.call-start = ((), (), s32[]{:S(2)}) async-start(), calls=%async_computation.7 | async-start | bytes 2621440 | tf_op jit(solution)/shard_map/all_gather | solution.py:603
  18.3 21.1 %collective-permute-start = (bf16[1,128,512]{2,1,0:T(8,128)(2,1)S(1)}, bf16[1,128,512]{2,1,0:T(8,128)(2,1)S(1)}, u32[]{:S(2)}, u32[]{:S(2)}) collective-permute-start(bf16[1,128,512]{2,1,0:T(8,128)(2,1)S(1)} %copy-done.14), channel_id=1, source_target_pairs={{0,2},{2,0},{1,3},{3,1},{4,6},{6,4},{5,7},{7,5},{8,10},{10,8},{9,1... | collective-permute-start | bytes 393224 | tf_op jit(solution)/shard_map/ppermute | solution.py:554
  41.3 5.3 %collective-permute-start.1 = (bf16[8,176,512]{2,1,0:T(8,128)(2,1)}, bf16[8,176,512]{2,1,0:T(8,128)(2,1)S(1)}, u32[]{:S(2)}, u32[]{:S(2)}) collective-permute-start(bf16[8,176,512]{2,1,0:T(8,128)(2,1)} %shard_map.265.near), channel_id=1, source_target_pairs={{0,1},{1,0},{2,3},{3,2},{4,5},{5,4},{6,7},{7,6},{8,9},{9,8},{10,11... | collective-permute-start | bytes 4325384 | tf_op jit(solution)/shard_map/ppermute | solution.py:554
  43.1 3.4 %collective-permute-start.2 = (bf16[2,128,512]{2,1,0:T(8,128)(2,1)}, bf16[2,128,512]{2,1,0:T(8,128)(2,1)S(1)}, u32[]{:S(2)}, u32[]{:S(2)}) collective-permute-start(bf16[2,128,512]{2,1,0:T(8,128)(2,1)} %copy-done.7), channel_id=1, source_target_pairs={{0,1},{1,0},{2,3},{3,2},{4,5},{5,4},{6,7},{7,6},{8,9},{9,8},{10,11... | collective-permute-start | bytes 786440 | tf_op jit(solution)/shard_map/ppermute | solution.py:554
  51.2 14.6 %copy-start.13 = (bf16[1,64,1536]{2,1,0:T(8,128)(2,1)S(1)}, bf16[1,64,1536]{2,1,0:T(8,128)(2,1)}, u32[]{:S(2)}) copy-start(bf16[1,64,1536]{2,1,0:T(8,128)(2,1)} %get-tuple-element.49) | copy-start | bytes 589828
  51.2 9.8 %collective-permute-start.11 = (bf16[1,64,2048]{2,1,0:T(8,128)(2,1)}, bf16[1,64,2048]{2,1,0:T(8,128)(2,1)S(1)}, u32[]{:S(2)}, u32[]{:S(2)}) collective-permute-start(bf16[1,64,2048]{2,1,0:T(8,128)(2,1)} %get-tuple-element.50), channel_id=1, source_target_pairs={{0,64},{64,0},{1,65},{65,1},{2,66},{66,2},{3,67},{67,3},{4,68},{68... | collective-permute-start | bytes 786440 | tf_op jit(solution)/shard_map/ppermute | solution.py:554
  52.0 5.7 %collective-permute-start.9 = (bf16[1,64,128]{2,1,0:T(8,128)(2,1)}, bf16[1,64,128]{2,1,0:T(8,128)(2,1)S(1)}, u32[]{:S(2)}, u32[]{:S(2)}) collective-permute-start(bf16[1,64,128]{2,1,0:T(8,128)(2,1)} %get-tuple-element.47.h0), channel_id=1, source_target_pairs={{0,112},{16,64},{32,80},{48,96},{64,48},{80,0},{96,16},{112,32},{1... | collective-permute-start | bytes 49160 | tf_op jit(solution)/shard_map/ppermute | solution.py:563
  55.0 5.3 %collective-permute-start.8 = (bf16[1,64,128]{2,1,0:T(8,128)(2,1)}, bf16[1,64,128]{2,1,0:T(8,128)(2,1)S(1)}, u32[]{:S(2)}, u32[]{:S(2)}) collective-permute-start(bf16[1,64,128]{2,1,0:T(8,128)(2,1)} %get-tuple-element.47.h0), channel_id=1, source_target_pairs={{0,96},{16,112},{32,64},{48,80},{64,32},{80,48},{96,0},{112,16},{1... | collective-permute-start | bytes 49160 | tf_op jit(solution)/shard_map/ppermute | solution.py:563
  55.9 7.4 %collective-permute-start.7 = (bf16[1,64,128]{2,1,0:T(8,128)(2,1)}, bf16[1,64,128]{2,1,0:T(8,128)(2,1)S(1)}, u32[]{:S(2)}, u32[]{:S(2)}) collective-permute-start(bf16[1,64,128]{2,1,0:T(8,128)(2,1)} %get-tuple-element.47.h0), channel_id=1, source_target_pairs={{0,80},{16,96},{32,112},{48,64},{64,16},{80,32},{96,48},{112,0},{1... | collective-permute-start | bytes 49160 | tf_op jit(solution)/shard_map/ppermute | solution.py:563
  57.0 6.4 %collective-permute-start.6 = (bf16[1,64,128]{2,1,0:T(8,128)(2,1)}, bf16[1,64,128]{2,1,0:T(8,128)(2,1)S(1)}, u32[]{:S(2)}, u32[]{:S(2)}) collective-permute-start(bf16[1,64,128]{2,1,0:T(8,128)(2,1)} %get-tuple-element.47.h0), channel_id=1, source_target_pairs={{0,64},{16,80},{32,96},{48,112},{64,0},{80,16},{96,32},{112,48},{1... | collective-permute-start | bytes 49160 | tf_op jit(solution)/shard_map/ppermute | solution.py:563
  57.7 7.3 %copy-start.15 = (bf16[1,64,128]{2,1,0:T(8,128)(2,1)}, bf16[1,64,128]{2,1,0:T(8,128)(2,1)S(1)}, u32[]{:S(2)}) copy-start(bf16[1,64,128]{2,1,0:T(8,128)(2,1)S(1)} %collective-permute-done.9.h7.refs_7_) | copy-start | bytes 49156
  57.7 5.7 %collective-permute-start.5 = (bf16[1,64,128]{2,1,0:T(8,128)(2,1)}, bf16[1,64,128]{2,1,0:T(8,128)(2,1)S(1)}, u32[]{:S(2)}, u32[]{:S(2)}) collective-permute-start(bf16[1,64,128]{2,1,0:T(8,128)(2,1)} %get-tuple-element.47.h0), channel_id=1, source_target_pairs={{0,48},{16,0},{32,16},{48,32},{64,112},{80,64},{96,80},{112,96},{1... | collective-permute-start | bytes 49160 | tf_op jit(solution)/shard_map/ppermute | solution.py:563
  60.2 4.8 %copy-start.16 = (bf16[1,64,128]{2,1,0:T(8,128)(2,1)}, bf16[1,64,128]{2,1,0:T(8,128)(2,1)S(1)}, u32[]{:S(2)}) copy-start(bf16[1,64,128]{2,1,0:T(8,128)(2,1)S(1)} %collective-permute-done.8.h6.refs_6_) | copy-start | bytes 49156
  60.2 4.3 %collective-permute-start.4 = (bf16[1,64,128]{2,1,0:T(8,128)(2,1)}, bf16[1,64,128]{2,1,0:T(8,128)(2,1)S(1)}, u32[]{:S(2)}, u32[]{:S(2)}) collective-permute-start(bf16[1,64,128]{2,1,0:T(8,128)(2,1)} %get-tuple-element.47.h0), channel_id=1, source_target_pairs={{0,32},{16,48},{32,0},{48,16},{64,96},{80,112},{96,64},{112,80},{1... | collective-permute-start | bytes 49160 | tf_op jit(solution)/shard_map/ppermute | solution.py:563
  61.1 4.0 %collective-permute-start.3 = (bf16[1,64,128]{2,1,0:T(8,128)(2,1)}, bf16[1,64,128]{2,1,0:T(8,128)(2,1)S(1)}, u32[]{:S(2)}, u32[]{:S(2)}) collective-permute-start(bf16[1,64,128]{2,1,0:T(8,128)(2,1)} %get-tuple-element.47.h0), channel_id=1, source_target_pairs={{0,16},{16,32},{32,48},{48,0},{64,80},{80,96},{96,112},{112,64},{1... | collective-permute-start | bytes 49160 | tf_op jit(solution)/shard_map/ppermute | solution.py:563
  63.4 1.7 copy-start.17
  65.8 12.9 %collective-permute-start.10 = (bf16[1,64,1536]{2,1,0:T(8,128)(2,1)S(1)}, bf16[1,64,1536]{2,1,0:T(8,128)(2,1)S(1)}, u32[]{:S(2)}, u32[]{:S(2)}) collective-permute-start(bf16[1,64,1536]{2,1,0:T(8,128)(2,1)S(1)} %copy-done.13), channel_id=1, source_target_pairs={{0,64},{64,0},{1,65},{65,1},{2,66},{66,2},{3,67},{67,3},{4,68},{68... | collective-permute-start | bytes 589832 | tf_op jit(solution)/shard_map/ppermute | solution.py:554
  79.3 8.7 %copy-start.11 = (bf16[1,64,1536]{2,1,0:T(8,128)(2,1)S(1)}, bf16[1,64,1536]{2,1,0:T(8,128)(2,1)}, u32[]{:S(2)}) copy-start(bf16[1,64,1536]{2,1,0:T(8,128)(2,1)} %copy-done.10) | copy-start | bytes 589828
  79.3 19.6 %all-to-all-start.1 = ((bf16[16,32,512]{2,1,0:T(8,128)(2,1)}), bf16[16,32,512]{2,1,0:T(8,128)(2,1)S(1)}, u32[]{:S(2)}, u32[]{:S(2)}) async-start(bf16[16,32,512]{2,1,0:T(8,128)(2,1)} %shard_map.268), calls=%async_computation.1 | async-start | bytes 1048576 | tf_op jit(solution)/shard_map/all_to_all | solution.py:550
  87.7 70.2 %reduce-scatter.2.cloned.1.call-start = ((), (), s32[]{:S(2)}) async-start(), calls=%async_computation.6 | async-start | bytes 2621440 | tf_op jit(solution)/shard_map/reduce_scatter | solution.py:636
  88.1 10.8 %copy-start.2 = (bf16[2,64,1536]{2,1,0:T(8,128)(2,1)}, bf16[2,64,1536]{2,1,0:T(8,128)(2,1)S(1)}, u32[]{:S(2)}) copy-start(bf16[2,64,1536]{2,1,0:T(8,128)(2,1)S(1)} %constant_dynamic-update-slice_fusion.2.other.refs_0_) | copy-start | bytes 1179652
  109.6 60.1 %all-gather.7.cloned.1.call-start = ((), (), s32[]{:S(2)}) async-start(), calls=%async_computation.8 | async-start | bytes 1966080 | tf_op jit(solution)/shard_map/all_gather | solution.py:634
  110.6 4.8 %collective-permute-start.12 = (bf16[2,128,1024]{2,1,0:T(8,128)(2,1)S(1)}, bf16[2,128,1024]{2,1,0:T(8,128)(2,1)S(1)}, u32[]{:S(2)}, u32[]{:S(2)}) collective-permute-start(bf16[2,128,1024]{2,1,0:T(8,128)(2,1)S(1)} %copy-done.25), channel_id=1, source_target_pairs={{0,1},{1,0},{2,3},{3,2},{4,5},{5,4},{6,7},{7,6},{8,9},{9,8},{10,11... | collective-permute-start | bytes 1572872 | tf_op jit(solution)/shard_map/ppermute | solution.py:554
  111.9 14.6 %all-to-all-start.2 = ((bf16[16,32,512]{2,1,0:T(8,128)(2,1)}), bf16[16,32,512]{2,1,0:T(8,128)(2,1)S(1)}, u32[]{:S(2)}, u32[]{:S(2)}) async-start(bf16[16,32,512]{2,1,0:T(8,128)(2,1)} %get-tuple-element.52), calls=%async_computation.2 | async-start | bytes 1048576 | tf_op jit(solution)/shard_map/all_to_all | solution.py:550
  118.3 21.9 %collective-permute-start.13 = (bf16[128,1024]{1,0:T(8,128)(2,1)}, bf16[128,1024]{1,0:T(8,128)(2,1)S(1)}, u32[]{:S(2)}, u32[]{:S(2)}) collective-permute-start(bf16[128,1024]{1,0:T(8,128)(2,1)} %get-tuple-element.60), channel_id=1, source_target_pairs={{0,2},{2,0},{1,3},{3,1},{4,6},{6,4},{5,7},{7,5},{8,10},{10,8},{9,1... | collective-permute-start | bytes 786440 | tf_op jit(solution)/shard_map/ppermute | solution.py:554
  141.0 19.7 %all-to-all-start.3 = ((bf16[16,96,128]{2,1,0:T(8,128)(2,1)}), bf16[16,96,128]{2,1,0:T(8,128)(2,1)S(1)}, u32[]{:S(2)}, u32[]{:S(2)}) async-start(bf16[16,96,128]{2,1,0:T(8,128)(2,1)} %shard_map.273.d_lin), calls=%async_computation.3 | async-start | bytes 786432 | tf_op jit(solution)/shard_map/all_to_all | solution.py:550
  150.7 5.8 %collective-permute-start.14 = (bf16[2,64,128]{2,1,0:T(8,128)(2,1)}, bf16[2,64,128]{2,1,0:T(8,128)(2,1)S(1)}, u32[]{:S(2)}, u32[]{:S(2)}) collective-permute-start(bf16[2,64,128]{2,1,0:T(8,128)(2,1)} %get-tuple-element.67), channel_id=1, source_target_pairs={{0,16},{16,32},{32,48},{48,0},{1,17},{17,33},{33,49},{49,1},{2,18}... | collective-permute-start | bytes 98312 | tf_op jit(solution)/shard_map/ppermute | solution.py:567
  150.9 5.7 %collective-permute-start.15 = (bf16[2,64,128]{2,1,0:T(8,128)(2,1)}, bf16[2,64,128]{2,1,0:T(8,128)(2,1)S(1)}, u32[]{:S(2)}, u32[]{:S(2)}) collective-permute-start(bf16[2,64,128]{2,1,0:T(8,128)(2,1)} %get-tuple-element.68), channel_id=1, source_target_pairs={{0,32},{16,48},{32,0},{48,16},{1,33},{17,49},{33,1},{49,17},{2,34}... | collective-permute-start | bytes 98312 | tf_op jit(solution)/shard_map/ppermute | solution.py:567
  152.5 5.4 %collective-permute-start.16 = (bf16[2,64,128]{2,1,0:T(8,128)(2,1)}, bf16[2,64,128]{2,1,0:T(8,128)(2,1)S(1)}, u32[]{:S(2)}, u32[]{:S(2)}) collective-permute-start(bf16[2,64,128]{2,1,0:T(8,128)(2,1)} %get-tuple-element.69), channel_id=1, source_target_pairs={{0,48},{16,0},{32,16},{48,32},{1,49},{17,1},{33,17},{49,33},{2,50}... | collective-permute-start | bytes 98312 | tf_op jit(solution)/shard_map/ppermute | solution.py:567
  161.4 20.1 %all-to-all-start.4 = ((bf16[32,4,2176]{2,1,0:T(4,128)(2,1)}), bf16[32,4,2176]{2,1,0:T(4,128)(2,1)S(1)}, u32[]{:S(2)}, u32[]{:S(2)}) async-start(bf16[32,4,2176]{2,1,0:T(4,128)(2,1)} %shard_map.278), calls=%async_computation.5 | async-start | bytes 1114112 | tf_op jit(solution)/shard_map/all_to_all | solution.py:550
  (19 other events, 18.2 us)
Sparse Core Ops, SparseCore 0:
  65.9 31.0 all-gather.4
  109.7 26.7 reduce-scatter.1
  138.3 27.5 all-gather.6

commit v3 on v2

--- a/solution.py
+++ b/solution.py
@@ -35,6 +35,7 @@
 WINDOW = ("y", "z", "core")
 CHIPS = ("y", "z")
 SLICE = ("z_lo", "y", "z", "core")
+WINDOWS = ("z_lo", "x")
 ALL = ("z_lo", "x", "y", "z", "core")
 
 
@@ -84,24 +85,19 @@
     return jnp.concatenate([data_t.astype(f32)] + rows + [pad], 0).astype(bf16)
 
 
-def after(value, *others):
+def after(value, *others, place=pltpu.HBM):
     def kernel(*refs):
         pass
 
     return pl.pallas_call(
         kernel,
-        out_shape=jax.ShapeDtypeStruct(value.shape, value.dtype),
+        out_shape=place(value.shape, value.dtype),
         in_specs=[pl.BlockSpec(memory_space=pl.ANY)] * (1 + len(others)),
         out_specs=pl.BlockSpec(memory_space=pl.ANY),
         input_output_aliases={0: 0},
-    )(value, *others)
-
-
-def copy_after(value, other):
-    def kernel(value_ref, other_ref, out_ref):
-        out_ref[...] = value_ref[...]
-
-    return call(kernel, [VM, HBM], [(value.shape, value.dtype)])(value, other)[0]
+        compiler_params=pltpu.CompilerParams(vmem_limit_bytes=2**20),
+        cost_estimate=pl.CostEstimate(flops=0, bytes_accessed=0, transcendentals=0),
+    )(pltpu.with_memory_space_constraint(value, place), *others)
 
 
 FEED_LANES = FF_PART * 3 + D
@@ -158,7 +154,7 @@
             sent[2 * y + z, ROWS:, :] = low
 
 
-def unpack_kernel(place, near, far, cot, feed, head, whole, rows, arrived):
+def unpack_kernel(place, near, far, cot, feed, heads, whole, rows, arrived):
     loads = [
         pltpu.make_async_copy(source.at[:, ROWS:, :], rows.at[i], arrived.at[i])
         for i, source in enumerate((near, far))
@@ -193,7 +189,9 @@
         cols = jnp.concatenate(
             [jnp.where(second, b[40:44, 128:256], b[40:44, 0:128]) for b in blocks], 0
         )
-        head[0, here, :] = cols.astype(bf16)
+        cols = cols.astype(bf16)
+        for w in range(DP):
+            heads[w, here, :] = cols
 
 
 def block_of(place, chip, other):
@@ -201,13 +199,10 @@
 
 
 def attend_kernel(
-    place, length, near, far, h0, h1, h2, h3, h4, h5, h6, h7, cos, sin,
+    place, length, near, far, head_cols, cos, sin,
     sent, q_out, k_out, v_out, o_out, lse_out, cols_out,
-    q_t, k_t, v_t, head_cols,
+    q_t, k_t, v_t,
 ):
-    for step, head in enumerate((h0, h1, h2, h3, h4, h5, h6, h7)):
-        k, by = step // 4, step % 4
-        head_cols[(place[5] ^ k) * 4 + lax.rem(place[4] + 4 - by, 4)] = head[0]
     cols = head_cols[...].reshape(D, 128).astype(f32).T
     cols_out[...] = cols
     gain = cols[96:97, :]
@@ -514,23 +509,32 @@
         grad[...] = jnp.sum(column, 0)[0:4]
 
 
-VM = pl.BlockSpec(memory_space=pltpu.VMEM)
-SM = pl.BlockSpec(memory_space=pltpu.SMEM)
-HBM = pl.BlockSpec(memory_space=pl.ANY)
-
-
-def call(kernel, specs, outs, scratch=()):
-    return pl.pallas_call(
+def call(kernel, ins, outs, scratch=(), vmem=8):
+    places = {"V": pltpu.VMEM, "H": pltpu.VMEM, "A": pl.ANY, "P": pl.ANY, "S": pltpu.SMEM}
+    inner = pl.pallas_call(
         kernel,
-        out_shape=tuple(jax.ShapeDtypeStruct(shape, kind) for shape, kind in outs),
-        in_specs=specs,
-        out_specs=tuple(VM for _ in outs),
+        out_shape=tuple(
+            (pltpu.VMEM if where == "V" else pltpu.HBM)(shape, kind) for shape, kind, where in outs
+        ),
+        in_specs=[pl.BlockSpec(memory_space=places[where]) for where in ins],
+        out_specs=tuple(pl.BlockSpec(memory_space=pltpu.VMEM) for _ in outs),
         scratch_shapes=[
             pltpu.SemaphoreType.DMA((s,)) if isinstance(s, int) else pltpu.VMEM(*s) for s in scratch
         ],
-        compiler_params=pltpu.CompilerParams(vmem_limit_bytes=56 * 2**20),
+        compiler_params=pltpu.CompilerParams(vmem_limit_bytes=vmem * 2**20),
         cost_estimate=pl.CostEstimate(flops=0, bytes_accessed=0, transcendentals=0),
     )
+
+    def run(*args):
+        assert len(args) == len(ins)
+        return inner(
+            *(
+                pltpu.with_memory_space_constraint(x, pltpu.HBM) if where in "HA" else x
+                for x, where in zip(args, ins)
+            )
+        )
+
+    return run
 
 
 def rope_tables():
@@ -552,15 +556,6 @@
 
 def swap(value, axis):
     return lax.ppermute(value, axis, [(0, 1), (1, 0)])
-
-
-def step_dp(value, k, by):
-    if k == by == 0:
-        return value
-    moves = [
-        (4 * z + x, 4 * (z ^ k) + (x + by) % 4) for z in range(2) for x in range(4)
-    ]
-    return lax.ppermute(value, ("z_lo", "x"), moves)
 
 
 def shift(value, by):
@@ -580,68 +575,80 @@
 
     (packed,) = call(
         pack_kernel,
-        [VM] * 13,
-        [((8, MSG_ROWS, D), bf16)],
+        "H" * 13,
+        [((8, MSG_ROWS, D), bf16, "H")],
     )(
         tokens, w_query, w_key, w_value, w_output, w_gate, w_up, w_down,
         norm1_gain, norm1_bias, norm2_gain, norm2_bias, order,
     )
     near = exchange(packed, CHIPS)
     cot_pair = jnp.concatenate([cotangent, swap(cotangent, "z")], 0)
-    near = after(near, cot_pair)
+    near = after(near, cot_pair, place=pltpu.VMEM)
     far = swap(near, "core")
     cot_far = swap(cot_pair, "core")
 
-    feed_rows, head, whole = call(
+    feed_rows, heads, whole = call(
         unpack_kernel,
-        [SM, HBM, HBM, HBM],
-        [((1, 64, FEED_LANES), bf16), ((1, 64, 128), bf16), ((1, 64, 3 * D), bf16)],
+        "SPPP",
+        [
+            ((1, 64, FEED_LANES), bf16, "H"),
+            ((DP, 64, 128), bf16, "H"),
+            ((1, 64, 3 * D), bf16, "H"),
+        ],
         [((2, 8, 48, D), bf16), 2],
     )(place, near, far, cot_far)
-    heads = [step_dp(head, k, by) for k in range(2) for by in range(4)]
+    head_cols = exchange(heads, WINDOWS).reshape(D, 128)
     feed_rows = jnp.concatenate([feed_rows, swap(feed_rows, "z_lo")], 0)
-    feed_weights = lax.all_gather(after(feed_rows, *heads[1:]), "x")
+    feed_weights = lax.all_gather(after(feed_rows, head_cols), "x")
     whole_other = swap(whole, "z_lo")
 
     sent, q_t, k_t, v_t, o_t, lse, head_cols = call(
         attend_kernel,
-        [SM, SM] + [VM] * 12,
+        "SSVVVHH",
         [
-            ((SEQ, HEAD, TEAM_ROWS), bf16),
-            ((HEAD, LEN), bf16),
-            ((HEAD, LEN), bf16),
-            ((HEAD, LEN), bf16),
-            ((HEAD, LEN), f32),
-            ((1, LEN), f32),
-            ((128, D), f32),
+            ((SEQ, HEAD, TEAM_ROWS), bf16, "H"),
+            ((HEAD, LEN), bf16, "H"),
+            ((HEAD, LEN), bf16, "H"),
+            ((HEAD, LEN), bf16, "H"),
+            ((HEAD, LEN), f32, "H"),
+            ((1, LEN), f32, "H"),
+            ((128, D), f32, "H"),
         ],
-        [((HEAD, LEN), bf16)] * 3
-        + [((DP, 64, 128), bf16)],
-    )(place, lengths, near, far, *heads, cos, sin)
+        [((HEAD, LEN), bf16)] * 3,
+        vmem=24,
+    )(place, lengths, near, far, head_cols, cos, sin)
     mixed = exchange(after(sent, whole_other), WINDOW)
     whole = jnp.concatenate([whole, whole_other], 0)
+
     d_sent, kept, swapped, grads, norm_rows = call(
         feed_kernel,
-        [SM, SM, VM, HBM, HBM, VM, VM, HBM, VM, HBM],
-        [((HEADS, HEAD, TEAM_ROWS), bf16)]
-        + [((2, ROWS, 2 * D), bf16)] * 2
-        + [((4, 2, 64, FEED_LANES), bf16), ((8, D), f32)],
+        "SSVPPHHAHA",
+        [
+            ((HEADS, HEAD, TEAM_ROWS), bf16, "H"),
+            ((2, ROWS, 2 * D), bf16, "H"),
+            ((2, ROWS, 2 * D), bf16, "H"),
+            ((4, 2, 64, FEED_LANES), bf16, "H"),
+            ((8, D), f32, "H"),
+        ],
         [((TEAM_ROWS, D), bf16)] * 4 + [((4, 2, 4, 64, 512), bf16), 32, 4],
+        vmem=24,
     )(
-        place, lengths, mixed, near, far, cot_pair, cot_far,
-        feed_weights, head_cols, whole,
+        place, lengths, mixed, near, far, cot_pair, cot_far, feed_weights, head_cols, whole,
     )
-    row_weights = lax.all_gather(after(whole, grads), "x")
     d_mixed = exchange(d_sent, WINDOW)
     feed_grads = lax.psum_scatter(
         grads.reshape(D, FEED_LANES), "x", scatter_dimension=0, tiled=True
     )
-    w0, w1 = call(add_kernel, [VM] * 2, [((ROWS, 2 * D), bf16)] * 2)(kept, swap(swapped, "core"))
+    row_weights = lax.all_gather(after(whole, pltpu.with_memory_space_constraint(norm_rows, pltpu.HBM)), "x")
+    w0, w1 = call(
+        add_kernel, "HV", [((ROWS, 2 * D), bf16, "H")] * 2
+    )(kept, swap(swapped, "core"))
     w1 = swap(w1, "z")
+
     (lin_sent,) = call(
         attend_back_kernel,
-        [SM] + [VM] * 8,
-        [((SEQ, 96, ROWS), bf16)],
+        "SVHHHHHHH",
+        [((SEQ, 96, ROWS), bf16, "H")],
         [
             ((HEAD, LEN), bf16),
             ((LEN, LEN), bf16),
@@ -650,34 +657,36 @@
             ((HEAD, LEN), f32),
             ((HEAD, LEN), f32),
         ],
+        vmem=40,
     )(lengths, d_mixed, q_t, k_t, v_t, o_t, lse, cos, sin)
     lin_sent = after(lin_sent, w1)
     back = exchange(lin_sent, WINDOW)
     head_grads = call(
         head_grad_kernel,
-        [VM] * 5 + [SM],
-        [((2, 64, 128), bf16)] * 4,
+        "VVHHHS",
+        [((2, 64, 128), bf16, "H")] * 4,
         [((D, 128), f32)],
+        vmem=16,
     )(near, far, head_cols, lin_sent, norm_rows, place)
     head_grads = [head_grads[0]] + [shift(head_grads[step], step) for step in range(1, 4)]
     (grad_sent,) = call(
         regroup_kernel,
-        [VM] * 5,
-        [((2 * SEQ, 4, GRAD_LANES), bf16)],
+        "HVVVH",
+        [((2 * SEQ, 4, GRAD_LANES), bf16, "H")],
     )(*head_grads, feed_grads)
     grad_parts = exchange(after(grad_sent, back), SLICE)
 
     grad_tokens, layer_output = call(
         input_grad_kernel,
-        [SM, SM] + [VM] * 2 + [HBM] + [VM] * 3,
-        [((1, ROWS, D), f32), ((1, ROWS, D), bf16)],
+        "SSHVAHHH",
+        [((1, ROWS, D), f32, "H"), ((1, ROWS, D), bf16, "H")],
         [((3, 2, 4, 64, 512), bf16), 24],
     )(place, lengths, tokens, back, row_weights, w0, w1, head_cols)
     weight_grads = call(
         sum_kernel,
-        [VM] * 2,
-        [((4,), f32)] * 2 + [((4, D), f32)] * 4 + [((4,), f32)] * 2
-        + [((4, FF), f32)] * 2 + [((16, D), f32)],
+        "VH",
+        [((4,), f32, "H")] * 2 + [((4, D), f32, "H")] * 4 + [((4,), f32, "H")] * 2
+        + [((4, FF), f32, "H")] * 2 + [((16, D), f32, "H")],
     )(grad_parts, order)
     return (layer_output, grad_tokens) + tuple(weight_grads)
 

time: 192 us -> 178 us (0.927)
  local copies, waits for them, and re-layouts: 11.3 us -> 4.03 us
  Pallas kernels: 55.4 us -> 51.8 us
  starting transfers between devices: 56.9 us -> 53.9 us
    ppermute x7 -> x0, starting transfers between devices: 9.09 us -> none  [step_dp(): return lax.ppermute(value, ('z_lo', 'x'), moves)]
    unnamed x54 -> x12, local copies, waits for them, and re-layouts: 10.7 us -> 2.31 us
    all_to_all x5 -> x6, starting transfers between devices: 33.3 us -> 39.8 us  [exchange(): return lax.all_to_all(value, axes, 0, 0, tiled=True)]
    pallas_call x16, Pallas kernels: 55.4 us -> 51.8 us  [the longest x10 51.8 us: run(): inner(*(pltpu.with_memory_space_constraint(x, pltpu.HBM) if where in 'HA'...]
    ppermute x7, waiting for transfers between devices: 21 us -> 23.3 us  [swap(): return lax.ppermute(value, axis, [(0, 1), (1, 0)])]
    ppermute x7 -> x0, waiting for transfers between devices: 2.09 us -> none  [step_dp(): return lax.ppermute(value, ('z_lo', 'x'), moves)]
    all_to_all x5 -> x6, waiting for transfers between devices: 23.3 us -> 21.4 us  [exchange(): return lax.all_to_all(value, axes, 0, 0, tiled=True)]
  transfers between devices with their start and end apart: 25 -> 19, of which waited for: 11 -> 11; matrix products, arithmetic and copies ran while one was open for 1% -> 3% of each run, Pallas kernels for 20% -> 20%
where the time goes in v3:
time: 178 us; the launch traced here: 177 us
  starting transfers between devices  53.9 us (30%)
  Pallas kernels  51.8 us (29%)
  waiting for transfers between devices  50.4 us (28%)
  between operations  14.5 us (8%)
  local copies, waits for them, and re-layouts  4.03 us (2%)
  other arithmetic  1.81 us (1%)
    pallas_call x10, Pallas kernels, run(): inner(*(pltpu.with_memory_space_constraint(x, pltpu.HBM) if where in 'HA'...  51.8 us
    all_to_all x6, starting transfers between devices, exchange(): return lax.all_to_all(value, axes, 0, 0, tiled=True)  39.8 us
    ppermute x7, waiting for transfers between devices, swap(): return lax.ppermute(value, axis, [(0, 1), (1, 0)])  23.3 us
    all_to_all x6, waiting for transfers between devices, exchange(): return lax.all_to_all(value, axes, 0, 0, tiled=True)  21.4 us
    ppermute x7, starting transfers between devices, swap(): return lax.ppermute(value, axis, [(0, 1), (1, 0)])  10.3 us
    ppermute x3, waiting for transfers between devices, shift(): return lax.ppermute(value, 'x', [(i, (i + by) % 4) for i in range(4)])  3.65 us
  transfers between devices with their start and end apart: 19, of which 11 were waited for; matrix products, arithmetic and copies ran while one was open for 3% of the time, Pallas kernels for 20%

profile of v3, /device:TPU:1, one launch (start us, length us, event | category | flops | bytes accessed | tf_op | source)
XLA Modules:
  0.0 176.6 jit_solution(3957211740416318655)
XLA Ops:
  7.2 2.6 %shard_map.264 = bf16[8,176,512]{2,1,0:T(8,128)(2,1)} custom-call(bf16[1,128,512]{2,1,0:T(8,128)(2,1)} %tokens.3, bf16[4,512]{1,0:T(4,128)(2,1)} %w_query.1, bf16[4,512]{1,0:T(4,128)(2,1)} %w_key.1, bf16[4,512]{1,0:T(4,128)(2,1)} %w_value.1, bf16[4,512]{1,0:T(4,128)(2,1)} %w_output.1, bf16[4,2048]{1,0:T(4,128)(2,1)} %w_gate.1, bf16[4,2048]{1,0:T(4,128)(2,1)} %w_up.1, ...), custom_call_target="tpu_custom_call" | custom-call | tf_op jit(solution)/shard_map/pallas_call | solution.py:530
  9.8 8.5 %all-to-all-start = ((bf16[8,176,512]{2,1,0:T(8,128)(2,1)}), bf16[8,176,512]{2,1,0:T(8,128)(2,1)S(1)}, u32[]{:S(2)}, u32[]{:S(2)}) async-start(bf16[8,176,512]{2,1,0:T(8,128)(2,1)} %shard_map.264), calls=%async_computation | async-start | bytes 2883584 | tf_op jit(solution)/shard_map/all_to_all | solution.py:554
  18.3 3.0 %collective-permute-start = (bf16[1,128,512]{2,1,0:T(8,128)(2,1)S(1)}, bf16[1,128,512]{2,1,0:T(8,128)(2,1)S(1)}, u32[]{:S(2)}, u32[]{:S(2)}) collective-permute-start(bf16[1,128,512]{2,1,0:T(8,128)(2,1)S(1)} %copy-done.4), channel_id=1, source_target_pairs={{0,2},{2,0},{1,3},{3,1},{4,6},{6,4},{5,7},{7,5},{8,10},{10,8},{9,1... | collective-permute-start | bytes 393224 | tf_op jit(solution)/shard_map/ppermute | solution.py:558
  21.2 18.2 %collective-permute-done = bf16[1,128,512]{2,1,0:T(8,128)(2,1)S(1)} collective-permute-done((bf16[1,128,512]{2,1,0:T(8,128)(2,1)S(1)}, bf16[1,128,512]{2,1,0:T(8,128)(2,1)S(1)}, u32[]{:S(2)}, u32[]{:S(2)}) %collective-permute-start) | collective-permute-done | bytes 131104 | tf_op jit(solution)/shard_map/ppermute | solution.py:558
  39.5 1.9 %collective-permute-start.1 = (bf16[8,176,512]{2,1,0:T(8,128)(2,1)S(1)}, bf16[8,176,512]{2,1,0:T(8,128)(2,1)S(1)}, u32[]{:S(2)}, u32[]{:S(2)}) collective-permute-start(bf16[8,176,512]{2,1,0:T(8,128)(2,1)S(1)} %shard_map.265.near), channel_id=1, source_target_pairs={{0,1},{1,0},{2,3},{3,2},{4,5},{5,4},{6,7},{7,6},{8,9},{9,8},{10,11... | collective-permute-start | bytes 4325384 | tf_op jit(solution)/shard_map/ppermute | solution.py:558
  42.1 2.6 %collective-permute-done.2.cot.cot_far = bf16[2,128,512]{2,1,0:T(8,128)(2,1)S(1)} collective-permute-done((bf16[2,128,512]{2,1,0:T(8,128)(2,1)S(1)}, bf16[2,128,512]{2,1,0:T(8,128)(2,1)S(1)}, u32[]{:S(2)}, u32[]{:S(2)}) %collective-permute-start.2) | collective-permute-done | bytes 262176 | tf_op jit(solution)/shard_map/ppermute | solution.py:558
  44.7 1.6 shard_map.266
  47.1 4.5 %all-to-all-start.1 = ((bf16[8,64,128]{2,1,0:T(8,128)(2,1)}), bf16[8,64,128]{2,1,0:T(8,128)(2,1)S(1)}, u32[]{:S(2)}, u32[]{:S(2)}) async-start(bf16[8,64,128]{2,1,0:T(8,128)(2,1)} %get-tuple-element.47), calls=%async_computation.1 | async-start | bytes 262144 | tf_op jit(solution)/shard_map/all_to_all | solution.py:554
  51.7 2.5 %collective-permute-done.4 = bf16[1,64,2048]{2,1,0:T(8,128)(2,1)S(1)} collective-permute-done((bf16[1,64,2048]{2,1,0:T(8,128)(2,1)}, bf16[1,64,2048]{2,1,0:T(8,128)(2,1)S(1)}, u32[]{:S(2)}, u32[]{:S(2)}) %collective-permute-start.4) | collective-permute-done | bytes 262176 | tf_op jit(solution)/shard_map/ppermute | solution.py:558
  54.1 1.8 %pad_maximum_fusion.refs_0_ = bf16[2,64,2048]{2,1,0:T(8,128)(2,1)} fusion(bf16[1,64,2048]{2,1,0:T(8,128)(2,1)S(1)} %collective-permute-done.4, bf16[1,64,2048]{2,1,0:T(8,128)(2,1)} %get-tuple-element.50), kind=kLoop, calls=%fused_computation | loop fusion | flops 262144 | bytes 1048576 | tf_op jit(solution)/shard_map/concatenate | solution.py:601
  58.1 10.2 %shard_map.267 = (bf16[16,32,512]{2,1,0:T(8,128)(2,1)}, bf16[32,2048]{1,0:T(8,128)(2,1)}, bf16[32,2048]{1,0:T(8,128)(2,1)}, bf16[32,2048]{1,0:T(8,128)(2,1)}, f3...) custom-call(s32[6]{0:T(128)S(1)} %stack.27.place, s32[1]{0:T(128)S(6)} %copy.44.length, ...), custom_call_target="tpu_custom_call" | custom-call | tf_op jit(solution)/shard_map/pallas_call | solution.py:530
  69.0 6.8 %all-to-all-start.2 = ((bf16[16,32,512]{2,1,0:T(8,128)(2,1)}), bf16[16,32,512]{2,1,0:T(8,128)(2,1)S(1)}, u32[]{:S(2)}, u32[]{:S(2)}) async-start(bf16[16,32,512]{2,1,0:T(8,128)(2,1)} %shard_map.268), calls=%async_computation.2 | async-start | bytes 1048576 | tf_op jit(solution)/shard_map/all_to_all | solution.py:554
  76.0 1.6 constant_dynamic-update-slice_fusion.3
  77.6 1.6 constant_dynamic-update-slice_fusion.2.other.refs_0_
  79.2 7.7 %all-to-all-done.2.mixed = bf16[16,32,512]{2,1,0:T(8,128)(2,1)S(1)} async-done(((bf16[16,32,512]{2,1,0:T(8,128)(2,1)}), bf16[16,32,512]{2,1,0:T(8,128)(2,1)S(1)}, u32[]{:S(2)}, u32[]{:S(2)}) %all-to-all-start.2) | async-done | bytes 524320 | tf_op jit(solution)/shard_map/all_to_all | solution.py:554
  87.6 9.6 %shard_map.270 = (bf16[16,32,512]{2,1,0:T(8,128)(2,1)}, bf16[2,128,1024]{2,1,0:T(8,128)(2,1)}, bf16[2,128,1024]{2,1,0:T(8,128)(2,1)}, bf16[4,2,64,2048]{3,2,1,0:T(8,128)(2,1)}, f32[8,512]{1,0:T(8,128)}) custom-call(s32[6]{0:T(128)S(1)} %stack.27.place, s32[1]{0:T(128)S(6)} %copy.44.length, bf16[16,32,512]{2,1,0:T(8,128)(2,1)S(1)} %all-to-all-done.2.mixed, ...), custom_call_target="tpu_custom_call" | custom-call | tf_op jit(solution)/shard_map/pallas_call | solution.py:530
  98.8 7.0 %all-to-all-start.3 = ((bf16[16,32,512]{2,1,0:T(8,128)(2,1)}), bf16[16,32,512]{2,1,0:T(8,128)(2,1)S(1)}, u32[]{:S(2)}, u32[]{:S(2)}) async-start(bf16[16,32,512]{2,1,0:T(8,128)(2,1)} %get-tuple-element.52), calls=%async_computation.3 | async-start | bytes 1048576 | tf_op jit(solution)/shard_map/all_to_all | solution.py:554
  105.8 2.3 %shard_map.272 = (bf16[128,1024]{1,0:T(8,128)(2,1)}, bf16[128,1024]{1,0:T(8,128)(2,1)}) custom-call(bf16[2,128,1024]{2,1,0:T(8,128)(2,1)} %get-tuple-element.58.kept, bf16[2,128,1024]{2,1,0:T(8,128)(2,1)} %collective-permute-done.5.arrived), custom_call_target="tpu_custom_call" | custom-call | tf_op jit(solution)/shard_map/pallas_call | solution.py:530
  108.1 2.9 %collective-permute-start.6 = (bf16[128,1024]{1,0:T(8,128)(2,1)}, bf16[128,1024]{1,0:T(8,128)(2,1)}, u32[]{:S(2)}, u32[]{:S(2)}) collective-permute-start(bf16[128,1024]{1,0:T(8,128)(2,1)} %get-tuple-element.60), channel_id=1, source_target_pairs={{0,2},{2,0},{1,3},{3,1},{4,6},{6,4},{5,7},{7,5},{8,10},{10,8},{9,1... | collective-permute-start | bytes 786440 | tf_op jit(solution)/shard_map/ppermute | solution.py:558
  111.0 6.0 %all-to-all-done.3.d_mixed = bf16[16,32,512]{2,1,0:T(8,128)(2,1)S(1)} async-done(((bf16[16,32,512]{2,1,0:T(8,128)(2,1)}), bf16[16,32,512]{2,1,0:T(8,128)(2,1)S(1)}, u32[]{:S(2)}, u32[]{:S(2)}) %all-to-all-start.3) | async-done | bytes 524320 | tf_op jit(solution)/shard_map/all_to_all | solution.py:554
  116.9 12.7 %shard_map.271.refs_0_ = bf16[16,96,128]{2,1,0:T(8,128)(2,1)} custom-call(s32[1]{0:T(128)S(6)} %copy.44.length, bf16[16,32,512]{2,1,0:T(8,128)(2,1)S(1)} %all-to-all-done.3.d_mixed, bf16[32,2048]{1,0:T(8,128)(2,1)} %get-tuple-element.53.q_in, bf16[32,2048]{1,0:T(8,128)(2,1)} %get-tuple-element.54.k_in, bf16[32,2048]{1,0:T(8,128)(2,1)} %get-tuple-element.55.v_in, ...), custom_call_target="tpu_custom_call" | custom-call | tf_op jit(solution)/shard_map/pallas_call | solution.py:530
  129.7 4.6 %all-to-all-start.4 = ((bf16[16,96,128]{2,1,0:T(8,128)(2,1)}), bf16[16,96,128]{2,1,0:T(8,128)(2,1)S(1)}, u32[]{:S(2)}, u32[]{:S(2)}) async-start(bf16[16,96,128]{2,1,0:T(8,128)(2,1)} %shard_map.273.d_lin), calls=%async_computation.4 | async-start | bytes 786432 | tf_op jit(solution)/shard_map/all_to_all | solution.py:554
  134.3 4.2 %shard_map.276 = (bf16[2,64,128]{2,1,0:T(8,128)(2,1)}, bf16[2,64,128]{2,1,0:T(8,128)(2,1)}, bf16[2,64,128]{2,1,0:T(8,128)(2,1)}, bf16[2,64,128]{2,1,0:T(8,128)(2,1)}) custom-call(bf16[8,176,512]{2,1,0:T(8,128)(2,1)S(1)} %shard_map.265.near, bf16[8,176,512]{2,1,0:T(8,128)(2,1)S(1)} %collective-permute-done.1.far, f32[128,512]{1,0:T(8,128)} %get-tuple-element.51.head_cols, ...), custom_call_target="tpu_custom_call" | custom-call | tf_op jit(solution)/shard_map/pallas_call | solution.py:530
  138.8 1.5 collective-permute-start.8
  140.3 1.8 %collective-permute-start.9 = (bf16[2,64,128]{2,1,0:T(8,128)(2,1)}, bf16[2,64,128]{2,1,0:T(8,128)(2,1)S(1)}, u32[]{:S(2)}, u32[]{:S(2)}) collective-permute-start(bf16[2,64,128]{2,1,0:T(8,128)(2,1)} %get-tuple-element.68), channel_id=1, source_target_pairs={{0,48},{16,0},{32,16},{48,32},{1,49},{17,1},{33,17},{49,33},{2,50}... | collective-permute-start | bytes 98312 | tf_op jit(solution)/shard_map/ppermute | solution.py:562
  142.1 2.1 %collective-permute-done.7.part1 = bf16[2,64,128]{2,1,0:T(8,128)(2,1)S(1)} collective-permute-done((bf16[2,64,128]{2,1,0:T(8,128)(2,1)}, bf16[2,64,128]{2,1,0:T(8,128)(2,1)S(1)}, u32[]{:S(2)}, u32[]{:S(2)}) %collective-permute-start.7) | collective-permute-done | bytes 32800 | tf_op jit(solution)/shard_map/ppermute | solution.py:562
  144.2 1.6 collective-permute-done.9.part3
  145.7 1.9 %shard_map.277.refs_0_ = bf16[32,4,2176]{2,1,0:T(4,128)(2,1)} custom-call(bf16[2,64,128]{2,1,0:T(8,128)(2,1)} %get-tuple-element.65.part0, bf16[2,64,128]{2,1,0:T(8,128)(2,1)S(1)} %collective-permute-done.7.part1, bf16[2,64,128]{2,1,0:T(8,128)(2,1)S(1)} %collective-permute-done.8.part2, bf16[2,64,128]{2,1,0:T(8,128)(2,1)S(1)} %collective-permute-done.9.part3, ...), custom_call_target="tpu_custom_call" | custom-call | tf_op jit(solution)/shard_map/pallas_call | solution.py:530
  147.7 8.5 %all-to-all-start.5 = ((bf16[32,4,2176]{2,1,0:T(4,128)(2,1)}), bf16[32,4,2176]{2,1,0:T(4,128)(2,1)S(1)}, u32[]{:S(2)}, u32[]{:S(2)}) async-start(bf16[32,4,2176]{2,1,0:T(4,128)(2,1)} %shard_map.278), calls=%async_computation.6 | async-start | bytes 1114112 | tf_op jit(solution)/shard_map/all_to_all | solution.py:554
  156.7 4.5 %shard_map.275 = (f32[1,128,512]{2,1,0:T(8,128)}, bf16[1,128,512]{2,1,0:T(8,128)(2,1)}) custom-call(s32[6]{0:T(128)S(1)} %stack.27.place, s32[1]{0:T(128)S(6)} %copy.44.length, bf16[1,128,512]{2,1,0:T(8,128)(2,1)} %tokens.3, bf16[16,96,128]{2,1,0:T(8,128)(2,1)S(1)} %all-to-all-done.4.d_lin.refs_1_, bf16[4,2,64,1536]{3,2,1,0:T(8,128)(2,1)} %bitcast.14, ...), custom_call_target="tpu_custom_call" | custom-call | tf_op jit(solution)/shard_map/pallas_call | solution.py:530
  161.3 6.7 %all-to-all-done.5.parts = bf16[32,4,2176]{2,1,0:T(4,128)(2,1)S(1)} async-done(((bf16[32,4,2176]{2,1,0:T(4,128)(2,1)}), bf16[32,4,2176]{2,1,0:T(4,128)(2,1)S(1)}, u32[]{:S(2)}, u32[]{:S(2)}) %all-to-all-start.5) | async-done | bytes 557088 | tf_op jit(solution)/shard_map/all_to_all | solution.py:554
  167.9 2.1 %shard_map.279 = (f32[4]{0:T(128)}, f32[4]{0:T(128)}, f32[4,512]{1,0:T(4,128)}, f32[4,512]{1,0:T(4,128)}, f32[4,512]{1,0:T(4,128)}, /*index=5*/f32[4,512]{1,0:T(...) custom-call(bf16[32,4,2176]{2,1,0:T(4,128)(2,1)S(1)} %all-to-all-done.5.parts, ...), custom_call_target="tpu_custom_call" | custom-call | tf_op jit(solution)/shard_map/pallas_call | solution.py:530
  (41 shorter events, 7.1 us)
Async XLA Ops:
  9.8 8.5 %copy-start.4 = (bf16[1,128,512]{2,1,0:T(8,128)(2,1)S(1)}, bf16[1,128,512]{2,1,0:T(8,128)(2,1)}, u32[]{:S(2)}) copy-start(bf16[1,128,512]{2,1,0:T(8,128)(2,1)} %param.30) | copy-start | bytes 393220
  9.8 29.7 %all-to-all-start = ((bf16[8,176,512]{2,1,0:T(8,128)(2,1)}), bf16[8,176,512]{2,1,0:T(8,128)(2,1)S(1)}, u32[]{:S(2)}, u32[]{:S(2)}) async-start(bf16[8,176,512]{2,1,0:T(8,128)(2,1)} %shard_map.264), calls=%async_computation | async-start | bytes 2883584 | tf_op jit(solution)/shard_map/all_to_all | solution.py:554
  18.3 21.2 %collective-permute-start = (bf16[1,128,512]{2,1,0:T(8,128)(2,1)S(1)}, bf16[1,128,512]{2,1,0:T(8,128)(2,1)S(1)}, u32[]{:S(2)}, u32[]{:S(2)}) collective-permute-start(bf16[1,128,512]{2,1,0:T(8,128)(2,1)S(1)} %copy-done.4), channel_id=1, source_target_pairs={{0,2},{2,0},{1,3},{3,1},{4,6},{6,4},{5,7},{7,5},{8,10},{10,8},{9,1... | collective-permute-start | bytes 393224 | tf_op jit(solution)/shard_map/ppermute | solution.py:558
  39.5 2.0 %copy-start = (bf16[2,128,512]{2,1,0:T(8,128)(2,1)}, bf16[2,128,512]{2,1,0:T(8,128)(2,1)S(1)}, u32[]{:S(2)}) copy-start(bf16[2,128,512]{2,1,0:T(8,128)(2,1)S(1)} %constant_dynamic-update-slice_fusion.refs_1_.cot_near) | copy-start | bytes 786436
  39.5 5.2 %collective-permute-start.1 = (bf16[8,176,512]{2,1,0:T(8,128)(2,1)S(1)}, bf16[8,176,512]{2,1,0:T(8,128)(2,1)S(1)}, u32[]{:S(2)}, u32[]{:S(2)}) collective-permute-start(bf16[8,176,512]{2,1,0:T(8,128)(2,1)S(1)} %shard_map.265.near), channel_id=1, source_target_pairs={{0,1},{1,0},{2,3},{3,2},{4,5},{5,4},{6,7},{7,6},{8,9},{9,8},{10,11... | collective-permute-start | bytes 4325384 | tf_op jit(solution)/shard_map/ppermute | solution.py:558
  41.5 3.2 %collective-permute-start.2 = (bf16[2,128,512]{2,1,0:T(8,128)(2,1)S(1)}, bf16[2,128,512]{2,1,0:T(8,128)(2,1)S(1)}, u32[]{:S(2)}, u32[]{:S(2)}) collective-permute-start(bf16[2,128,512]{2,1,0:T(8,128)(2,1)S(1)} %constant_dynamic-update-slice_fusion.refs_1_.cot_near), channel_id=1, source_target_pairs={{0,1},{1,0},{2,3},{3,2},{4,5},{5,4},{6,7},{7,6},{8,9},{9,8},{10,11... | collective-permute-start | bytes 786440 | tf_op jit(solution)/shard_map/ppermute | solution.py:558
  44.7 1.6 copy-start.1
  46.3 7.8 %collective-permute-start.4 = (bf16[1,64,2048]{2,1,0:T(8,128)(2,1)}, bf16[1,64,2048]{2,1,0:T(8,128)(2,1)S(1)}, u32[]{:S(2)}, u32[]{:S(2)}) collective-permute-start(bf16[1,64,2048]{2,1,0:T(8,128)(2,1)} %get-tuple-element.50), channel_id=1, source_target_pairs={{0,64},{64,0},{1,65},{65,1},{2,66},{66,2},{3,67},{67,3},{4,68},{68... | collective-permute-start | bytes 786440 | tf_op jit(solution)/shard_map/ppermute | solution.py:558
  47.1 9.9 %all-to-all-start.1 = ((bf16[8,64,128]{2,1,0:T(8,128)(2,1)}), bf16[8,64,128]{2,1,0:T(8,128)(2,1)S(1)}, u32[]{:S(2)}, u32[]{:S(2)}) async-start(bf16[8,64,128]{2,1,0:T(8,128)(2,1)} %get-tuple-element.47), calls=%async_computation.1 | async-start | bytes 262144 | tf_op jit(solution)/shard_map/all_to_all | solution.py:554
  51.6 5.5 %copy-start.3 = (bf16[1,64,1536]{2,1,0:T(8,128)(2,1)S(1)}, bf16[1,64,1536]{2,1,0:T(8,128)(2,1)}, u32[]{:S(2)}) copy-start(bf16[1,64,1536]{2,1,0:T(8,128)(2,1)} %get-tuple-element.49) | copy-start | bytes 589828
  51.6 36.0 %all-gather.5.cloned.1.call-start = ((), (), s32[]{:S(2)}) async-start(), calls=%async_computation.8 | async-start | bytes 2621440 | tf_op jit(solution)/shard_map/all_gather | solution.py:602
  57.1 11.2 %collective-permute-start.3 = (bf16[1,64,1536]{2,1,0:T(8,128)(2,1)S(1)}, bf16[1,64,1536]{2,1,0:T(8,128)(2,1)S(1)}, u32[]{:S(2)}, u32[]{:S(2)}) collective-permute-start(bf16[1,64,1536]{2,1,0:T(8,128)(2,1)S(1)} %copy-done.3), channel_id=1, source_target_pairs={{0,64},{64,0},{1,65},{65,1},{2,66},{66,2},{3,67},{67,3},{4,68},{68... | collective-permute-start | bytes 589832 | tf_op jit(solution)/shard_map/ppermute | solution.py:558
  68.3 0.7 copy-start.2
  69.0 17.9 %all-to-all-start.2 = ((bf16[16,32,512]{2,1,0:T(8,128)(2,1)}), bf16[16,32,512]{2,1,0:T(8,128)(2,1)S(1)}, u32[]{:S(2)}, u32[]{:S(2)}) async-start(bf16[16,32,512]{2,1,0:T(8,128)(2,1)} %shard_map.268), calls=%async_computation.2 | async-start | bytes 1048576 | tf_op jit(solution)/shard_map/all_to_all | solution.py:554
  75.8 70.0 %reduce-scatter.2.cloned.1.call-start = ((), (), s32[]{:S(2)}) async-start(), calls=%async_computation.7 | async-start | bytes 2621440 | tf_op jit(solution)/shard_map/reduce_scatter | solution.py:639
  97.3 59.4 %all-gather.7.cloned.1.call-start = ((), (), s32[]{:S(2)}) async-start(), calls=%async_computation.9 | async-start | bytes 1966080 | tf_op jit(solution)/shard_map/all_gather | solution.py:642
  98.0 7.8 %collective-permute-start.5 = (bf16[2,128,1024]{2,1,0:T(8,128)(2,1)}, bf16[2,128,1024]{2,1,0:T(8,128)(2,1)}, u32[]{:S(2)}, u32[]{:S(2)}) collective-permute-start(bf16[2,128,1024]{2,1,0:T(8,128)(2,1)} %get-tuple-element.59), channel_id=1, source_target_pairs={{0,1},{1,0},{2,3},{3,2},{4,5},{5,4},{6,7},{7,6},{8,9},{9,8},{10,11... | collective-permute-start | bytes 1572872 | tf_op jit(solution)/shard_map/ppermute | solution.py:558
  98.8 18.1 %all-to-all-start.3 = ((bf16[16,32,512]{2,1,0:T(8,128)(2,1)}), bf16[16,32,512]{2,1,0:T(8,128)(2,1)S(1)}, u32[]{:S(2)}, u32[]{:S(2)}) async-start(bf16[16,32,512]{2,1,0:T(8,128)(2,1)} %get-tuple-element.52), calls=%async_computation.3 | async-start | bytes 1048576 | tf_op jit(solution)/shard_map/all_to_all | solution.py:554
  108.1 21.6 %collective-permute-start.6 = (bf16[128,1024]{1,0:T(8,128)(2,1)}, bf16[128,1024]{1,0:T(8,128)(2,1)}, u32[]{:S(2)}, u32[]{:S(2)}) collective-permute-start(bf16[128,1024]{1,0:T(8,128)(2,1)} %get-tuple-element.60), channel_id=1, source_target_pairs={{0,2},{2,0},{1,3},{3,1},{4,6},{6,4},{5,7},{7,5},{8,10},{10,8},{9,1... | collective-permute-start | bytes 786440 | tf_op jit(solution)/shard_map/ppermute | solution.py:558
  129.7 18.0 %all-to-all-start.4 = ((bf16[16,96,128]{2,1,0:T(8,128)(2,1)}), bf16[16,96,128]{2,1,0:T(8,128)(2,1)S(1)}, u32[]{:S(2)}, u32[]{:S(2)}) async-start(bf16[16,96,128]{2,1,0:T(8,128)(2,1)} %shard_map.273.d_lin), calls=%async_computation.4 | async-start | bytes 786432 | tf_op jit(solution)/shard_map/all_to_all | solution.py:554
  138.5 5.6 %collective-permute-start.7 = (bf16[2,64,128]{2,1,0:T(8,128)(2,1)}, bf16[2,64,128]{2,1,0:T(8,128)(2,1)S(1)}, u32[]{:S(2)}, u32[]{:S(2)}) collective-permute-start(bf16[2,64,128]{2,1,0:T(8,128)(2,1)} %get-tuple-element.66), channel_id=1, source_target_pairs={{0,16},{16,32},{32,48},{48,0},{1,17},{17,33},{33,49},{49,1},{2,18}... | collective-permute-start | bytes 98312 | tf_op jit(solution)/shard_map/ppermute | solution.py:562
  138.8 5.4 %collective-permute-start.8 = (bf16[2,64,128]{2,1,0:T(8,128)(2,1)}, bf16[2,64,128]{2,1,0:T(8,128)(2,1)S(1)}, u32[]{:S(2)}, u32[]{:S(2)}) collective-permute-start(bf16[2,64,128]{2,1,0:T(8,128)(2,1)} %get-tuple-element.67), channel_id=1, source_target_pairs={{0,32},{16,48},{32,0},{48,16},{1,33},{17,49},{33,1},{49,17},{2,34}... | collective-permute-start | bytes 98312 | tf_op jit(solution)/shard_map/ppermute | solution.py:562
  140.3 5.4 %collective-permute-start.9 = (bf16[2,64,128]{2,1,0:T(8,128)(2,1)}, bf16[2,64,128]{2,1,0:T(8,128)(2,1)S(1)}, u32[]{:S(2)}, u32[]{:S(2)}) collective-permute-start(bf16[2,64,128]{2,1,0:T(8,128)(2,1)} %get-tuple-element.68), channel_id=1, source_target_pairs={{0,48},{16,0},{32,16},{48,32},{1,49},{17,1},{33,17},{49,33},{2,50}... | collective-permute-start | bytes 98312 | tf_op jit(solution)/shard_map/ppermute | solution.py:562
  147.7 20.3 %all-to-all-start.5 = ((bf16[32,4,2176]{2,1,0:T(4,128)(2,1)}), bf16[32,4,2176]{2,1,0:T(4,128)(2,1)S(1)}, u32[]{:S(2)}, u32[]{:S(2)}) async-start(bf16[32,4,2176]{2,1,0:T(4,128)(2,1)} %shard_map.278), calls=%async_computation.6 | async-start | bytes 1114112 | tf_op jit(solution)/shard_map/all_to_all | solution.py:554
Sparse Core Ops, SparseCore 0:
  57.2 30.4 all-gather.4
  97.4 29.7 reduce-scatter.1
  129.0 27.7 all-gather.6

commit v4 on v3

--- a/solution.py
+++ b/solution.py
@@ -83,6 +83,10 @@
 def with_rows(data_t, rows):
     pad = jnp.zeros((AUG - HEAD - len(rows), data_t.shape[1]), f32)
     return jnp.concatenate([data_t.astype(f32)] + rows + [pad], 0).astype(bf16)
+
+
+def in_hbm(value):
+    return pltpu.with_memory_space_constraint(value, pltpu.HBM)
 
 
 def after(value, *others, place=pltpu.HBM):
@@ -269,7 +273,7 @@
 
 
 def feed_kernel(
-    place, length, mixed, near, far, cot_near, cot_far, weights, head_cols, other,
+    place, length, mixed, near, far, cot_near, cot_far, weights, head_cols, other1, other2,
     sent, kept, swapped, grads, norm_rows,
     tokens, cot, back, ahead, parts, arrived, tokens_arrived,
 ):
@@ -360,9 +364,23 @@
     other[...] = (kept[1].astype(f32) + arrived[1].astype(f32)).astype(bf16)
 
 
+def scale_kernel(place, near, far, other, scaled):
+    for index in range(8):
+        source, first = (near, far)[index // 4], 2 * (index % 4)
+        x = source[first : first + 2, 0:ROWS, :].reshape(2 * ROWS, D).astype(f32)
+        low = norm_parts(x)[0].astype(bf16)
+        for one in range(2):
+            block = block_of(place, first + one, index // 4)
+            scaled[block] = low[one * ROWS : (one + 1) * ROWS]
+
+
 def attend_back_kernel(
-    length, d_mixed, q_in, k_in, v_in, o_in, lse_in, cos, sin, sent, d_o, probs, d_scores, dq, dk, dv
+    place, length, d_mixed, q_in, k_in, v_in, o_in, lse_in, cos, sin, scaled, head_cols, norm_rows,
+    sent, sent0, sent1, sent2, sent3,
+    d_o, probs, d_scores, dq, dk, dv, table, normal, here_now,
 ):
+    load = pltpu.make_async_copy(scaled, normal, here_now.at[0])
+    load.start()
     for y in range(LEN // TEAM_ROWS):
         total = d_mixed[TEAM * y].astype(f32)
         for t in range(1, TEAM):
@@ -401,36 +419,26 @@
         sent[b, 0:32] = dq_t[:, here]
         sent[b, 32:64] = dk_t[:, here]
         sent[b, 64:96] = dv_t[:, here]
-
-
-def head_grad_kernel(
-    near, far, head_cols, d_lin, norm_rows, place, sent0, sent1, sent2, sent3, table
-):
+    d_lin = jnp.concatenate([dq_t, dk_t, dv_t], 0)
+    load.wait()
+    product = nn(d_lin, normal[...].reshape(LEN, D))
+    total = jnp.sum(d_lin.astype(f32), 1, keepdims=True)
+    weights = head_cols[0:96, :]
     gain = head_cols[96:97, :]
     bias = head_cols[97:98, :]
-    weights_t = head_cols[0:96, :].astype(bf16)
-    total = jnp.zeros((96, D), f32)
-    d_gain = jnp.zeros((1, D), f32)
-    d_bias = jnp.zeros((1, D), f32)
-    for index in range(8):
-        source, first = (near, far)[index // 4], 2 * (index % 4)
-        x = source[first : first + 2, 0:ROWS, :].reshape(2 * ROWS, D).astype(f32)
-        scaled, _ = norm_parts(x)
-        normed = (scaled * gain + bias).astype(bf16)
-        d_part = jnp.concatenate(
-            [d_lin[block_of(place, first + one, index // 4)] for one in range(2)], 1
-        )
-        total = total + nn(d_part, normed)
-        d_normed = tn(d_part, weights_t)
-        d_gain = d_gain + jnp.sum(d_normed * scaled, 0, keepdims=True)
-        d_bias = d_bias + jnp.sum(d_normed, 0, keepdims=True)
-    pad = jnp.zeros((28, D), f32)
-    table[...] = jnp.concatenate([total, d_gain, d_bias, norm_rows[0:2, :], pad], 0).T
-    for step, sent in enumerate((sent0, sent1, sent2, sent3)):
+    rows = [
+        product * gain + total * bias,
+        jnp.sum(product * weights, 0, keepdims=True),
+        jnp.sum(total * weights, 0, keepdims=True),
+        norm_rows[0:2, :],
+        jnp.zeros((28, D), f32),
+    ]
+    table[...] = jnp.concatenate(rows, 0).T
+    for step, part in enumerate((sent0, sent1, sent2, sent3)):
         x = lax.rem(place[4] + step, 4)
         for k in range(2):
             at = pl.multiple_of((4 * k + x) * 64, 64)
-            sent[k] = table[pl.ds(at, 64), :].astype(bf16)
+            part[k] = table[pl.ds(at, 64), :].astype(bf16)
 
 
 def regroup_kernel(part0, part1, part2, part3, feed, sent):
@@ -509,27 +517,29 @@
         grad[...] = jnp.sum(column, 0)[0:4]
 
 
-def call(kernel, ins, outs, scratch=(), vmem=8):
-    places = {"V": pltpu.VMEM, "H": pltpu.VMEM, "A": pl.ANY, "P": pl.ANY, "S": pltpu.SMEM}
+def call(kernel, ins, outs, scratch=(), vmem=8, flops=0):
+    places = {"V": pltpu.VMEM, "U": pltpu.VMEM, "H": pltpu.VMEM, "A": pl.ANY, "P": pl.ANY, "S": pltpu.SMEM}
     inner = pl.pallas_call(
         kernel,
         out_shape=tuple(
             (pltpu.VMEM if where == "V" else pltpu.HBM)(shape, kind) for shape, kind, where in outs
         ),
         in_specs=[pl.BlockSpec(memory_space=places[where]) for where in ins],
-        out_specs=tuple(pl.BlockSpec(memory_space=pltpu.VMEM) for _ in outs),
+        out_specs=tuple(pl.BlockSpec(memory_space=places[where]) for _, _, where in outs),
         scratch_shapes=[
             pltpu.SemaphoreType.DMA((s,)) if isinstance(s, int) else pltpu.VMEM(*s) for s in scratch
         ],
         compiler_params=pltpu.CompilerParams(vmem_limit_bytes=vmem * 2**20),
-        cost_estimate=pl.CostEstimate(flops=0, bytes_accessed=0, transcendentals=0),
+        cost_estimate=pl.CostEstimate(flops=flops, bytes_accessed=0, transcendentals=0),
     )
 
     def run(*args):
         assert len(args) == len(ins)
         return inner(
             *(
-                pltpu.with_memory_space_constraint(x, pltpu.HBM) if where in "HA" else x
+                pltpu.with_memory_space_constraint(x, pltpu.HBM if where in "HA" else pltpu.VMEM)
+                if where in "HAV"
+                else x
                 for x, where in zip(args, ins)
             )
         )
@@ -591,7 +601,7 @@
         unpack_kernel,
         "SPPP",
         [
-            ((1, 64, FEED_LANES), bf16, "H"),
+            ((1, 64, FEED_LANES), bf16, "V"),
             ((DP, 64, 128), bf16, "H"),
             ((1, 64, 3 * D), bf16, "H"),
         ],
@@ -617,23 +627,27 @@
         [((HEAD, LEN), bf16)] * 3,
         vmem=24,
     )(place, lengths, near, far, head_cols, cos, sin)
-    mixed = exchange(after(sent, whole_other), WINDOW)
+    sent = after(sent, whole_other)
+    (scaled,) = call(
+        scale_kernel, "SUUA", [((SEQ, ROWS, D), bf16, "H")], vmem=12
+    )(place, near, far, sent)
+    mixed = exchange(sent, WINDOW)
     whole = jnp.concatenate([whole, whole_other], 0)
 
     d_sent, kept, swapped, grads, norm_rows = call(
         feed_kernel,
-        "SSVPPHHAHA",
+        "SSHPPHHAHAA",
         [
             ((HEADS, HEAD, TEAM_ROWS), bf16, "H"),
             ((2, ROWS, 2 * D), bf16, "H"),
-            ((2, ROWS, 2 * D), bf16, "H"),
+            ((2, ROWS, 2 * D), bf16, "V"),
             ((4, 2, 64, FEED_LANES), bf16, "H"),
             ((8, D), f32, "H"),
         ],
         [((TEAM_ROWS, D), bf16)] * 4 + [((4, 2, 4, 64, 512), bf16), 32, 4],
         vmem=24,
     )(
-        place, lengths, mixed, near, far, cot_pair, cot_far, feed_weights, head_cols, whole,
+        place, lengths, mixed, near, far, cot_pair, cot_far, feed_weights, head_cols, whole, scaled,
     )
     d_mixed = exchange(d_sent, WINDOW)
     feed_grads = lax.psum_scatter(
@@ -645,10 +659,10 @@
     )(kept, swap(swapped, "core"))
     w1 = swap(w1, "z")
 
-    (lin_sent,) = call(
+    lin_sent, *head_grads = call(
         attend_back_kernel,
-        "SVHHHHHHH",
-        [((SEQ, 96, ROWS), bf16, "H")],
+        "SSVHHHHHHHAHH",
+        [((SEQ, 96, ROWS), bf16, "H")] + [((2, 64, 128), bf16, "V")] * 4,
         [
             ((HEAD, LEN), bf16),
             ((LEN, LEN), bf16),
@@ -656,22 +670,18 @@
             ((HEAD, LEN), f32),
             ((HEAD, LEN), f32),
             ((HEAD, LEN), f32),
+            ((D, 128), f32),
+            ((SEQ, ROWS, D), bf16),
+            1,
         ],
         vmem=40,
-    )(lengths, d_mixed, q_t, k_t, v_t, o_t, lse, cos, sin)
+    )(place, lengths, d_mixed, q_t, k_t, v_t, o_t, lse, cos, sin, scaled, head_cols, norm_rows)
     lin_sent = after(lin_sent, w1)
     back = exchange(lin_sent, WINDOW)
-    head_grads = call(
-        head_grad_kernel,
-        "VVHHHS",
-        [((2, 64, 128), bf16, "H")] * 4,
-        [((D, 128), f32)],
-        vmem=16,
-    )(near, far, head_cols, lin_sent, norm_rows, place)
     head_grads = [head_grads[0]] + [shift(head_grads[step], step) for step in range(1, 4)]
     (grad_sent,) = call(
         regroup_kernel,
-        "HVVVH",
+        "UUUUH",
         [((2 * SEQ, 4, GRAD_LANES), bf16, "H")],
     )(*head_grads, feed_grads)
     grad_parts = exchange(after(grad_sent, back), SLICE)

time: 178 us -> 172 us (0.966)
  starting transfers between devices: 53.9 us -> 50.5 us
  local copies, waits for them, and re-layouts: 4.03 us -> 1.52 us
    all_gather x1, waiting for transfers between devices: 0.61 us -> 4.99 us  [shards(): lax.all_gather(after(whole, pltpu.with_memory_space_constraint(norm_rows,...]
    all_to_all x6, starting transfers between devices: 39.8 us -> 36.9 us  [exchange(): return lax.all_to_all(value, axes, 0, 0, tiled=True)]
    all_to_all x6, waiting for transfers between devices: 21.4 us -> 19.1 us  [exchange(): return lax.all_to_all(value, axes, 0, 0, tiled=True)]
    ppermute x3, waiting for transfers between devices: 3.65 us -> 1.65 us  [shift(): return lax.ppermute(value, 'x', [(i, (i + by) % 4) for i in range(4)])]
  transfers between devices with their start and end apart: 19 -> 19, of which waited for: 11 -> 13; matrix products, arithmetic and copies ran while one was open for 3% -> 2% of each run, Pallas kernels for 20% -> 20%
where the time goes in v4:
time: 172 us; the launch traced here: 171 us
  waiting for transfers between devices  51.4 us (30%)
  Pallas kernels  50.9 us (30%)
  starting transfers between devices  50.5 us (29%)
  between operations  14.6 us (8%)
  other arithmetic  1.8 us (1%)
    pallas_call x10, Pallas kernels, run(): inner(*(pltpu.with_memory_space_constraint(x, pltpu.HBM if where in 'HA'...  50.9 us
    all_to_all x6, starting transfers between devices, exchange(): return lax.all_to_all(value, axes, 0, 0, tiled=True)  36.9 us
    ppermute x7, waiting for transfers between devices, swap(): return lax.ppermute(value, axis, [(0, 1), (1, 0)])  23.8 us
    all_to_all x6, waiting for transfers between devices, exchange(): return lax.all_to_all(value, axes, 0, 0, tiled=True)  19.1 us
    ppermute x7, starting transfers between devices, swap(): return lax.ppermute(value, axis, [(0, 1), (1, 0)])  9.81 us
    all_gather x1, waiting for transfers between devices, shards(): lax.all_gather(after(whole, pltpu.with_memory_space_constraint(norm_rows,...  4.99 us
    ppermute x3, starting transfers between devices, shift(): return lax.ppermute(value, 'x', [(i, (i + by) % 4) for i in range(4)])  3.55 us
  transfers between devices with their start and end apart: 19, of which 13 were waited for; matrix products, arithmetic and copies ran while one was open for 2% of the time, Pallas kernels for 20%

profile of v4, /device:TPU:1, one launch (start us, length us, event | category | flops | bytes accessed | tf_op | source)
XLA Modules:
  0.0 170.8 jit_solution(16925688165153824791)
XLA Ops:
  7.2 2.6 %shard_map.264 = bf16[8,176,512]{2,1,0:T(8,128)(2,1)} custom-call(bf16[1,128,512]{2,1,0:T(8,128)(2,1)} %tokens.3, bf16[4,512]{1,0:T(4,128)(2,1)} %w_query.1, bf16[4,512]{1,0:T(4,128)(2,1)} %w_key.1, bf16[4,512]{1,0:T(4,128)(2,1)} %w_value.1, bf16[4,512]{1,0:T(4,128)(2,1)} %w_output.1, bf16[4,2048]{1,0:T(4,128)(2,1)} %w_gate.1, bf16[4,2048]{1,0:T(4,128)(2,1)} %w_up.1, ...), custom_call_target="tpu_custom_call" | custom-call | tf_op jit(solution)/shard_map/pallas_call | solution.py:538
  9.8 8.5 %all-to-all-start = ((bf16[8,176,512]{2,1,0:T(8,128)(2,1)}), bf16[8,176,512]{2,1,0:T(8,128)(2,1)S(1)}, u32[]{:S(2)}, u32[]{:S(2)}) async-start(bf16[8,176,512]{2,1,0:T(8,128)(2,1)} %shard_map.264), calls=%async_computation | async-start | bytes 2883584 | tf_op jit(solution)/shard_map/all_to_all | solution.py:564
  18.3 3.0 %collective-permute-start = (bf16[1,128,512]{2,1,0:T(8,128)(2,1)S(1)}, bf16[1,128,512]{2,1,0:T(8,128)(2,1)S(1)}, u32[]{:S(2)}, u32[]{:S(2)}) collective-permute-start(bf16[1,128,512]{2,1,0:T(8,128)(2,1)S(1)} %copy-done.4), channel_id=1, source_target_pairs={{0,2},{2,0},{1,3},{3,1},{4,6},{6,4},{5,7},{7,5},{8,10},{10,8},{9,1... | collective-permute-start | bytes 393224 | tf_op jit(solution)/shard_map/ppermute | solution.py:568
  21.2 18.2 %collective-permute-done = bf16[1,128,512]{2,1,0:T(8,128)(2,1)S(1)} collective-permute-done((bf16[1,128,512]{2,1,0:T(8,128)(2,1)S(1)}, bf16[1,128,512]{2,1,0:T(8,128)(2,1)S(1)}, u32[]{:S(2)}, u32[]{:S(2)}) %collective-permute-start) | collective-permute-done | bytes 131104 | tf_op jit(solution)/shard_map/ppermute | solution.py:568
  39.5 1.9 %collective-permute-start.1 = (bf16[8,176,512]{2,1,0:T(8,128)(2,1)S(1)}, bf16[8,176,512]{2,1,0:T(8,128)(2,1)S(1)}, u32[]{:S(2)}, u32[]{:S(2)}) collective-permute-start(bf16[8,176,512]{2,1,0:T(8,128)(2,1)S(1)} %shard_map.265.near), channel_id=1, source_target_pairs={{0,1},{1,0},{2,3},{3,2},{4,5},{5,4},{6,7},{7,6},{8,9},{9,8},{10,11... | collective-permute-start | bytes 4325384 | tf_op jit(solution)/shard_map/ppermute | solution.py:568
  41.6 3.0 %collective-permute-done.2.cot.cot_far = bf16[2,128,512]{2,1,0:T(8,128)(2,1)S(1)} collective-permute-done((bf16[2,128,512]{2,1,0:T(8,128)(2,1)S(1)}, bf16[2,128,512]{2,1,0:T(8,128)(2,1)S(1)}, u32[]{:S(2)}, u32[]{:S(2)}) %collective-permute-start.2) | collective-permute-done | bytes 262176 | tf_op jit(solution)/shard_map/ppermute | solution.py:568
  44.7 1.6 shard_map.266
  47.1 4.5 %all-to-all-start.1 = ((bf16[8,64,128]{2,1,0:T(8,128)(2,1)}), bf16[8,64,128]{2,1,0:T(8,128)(2,1)S(1)}, u32[]{:S(2)}, u32[]{:S(2)}) async-start(bf16[8,64,128]{2,1,0:T(8,128)(2,1)} %get-tuple-element.48), calls=%async_computation.1 | async-start | bytes 262144 | tf_op jit(solution)/shard_map/all_to_all | solution.py:564
  51.6 2.5 %collective-permute-done.4 = bf16[1,64,2048]{2,1,0:T(8,128)(2,1)S(1)} collective-permute-done((bf16[1,64,2048]{2,1,0:T(8,128)(2,1)}, bf16[1,64,2048]{2,1,0:T(8,128)(2,1)S(1)}, u32[]{:S(2)}, u32[]{:S(2)}) %collective-permute-start.4) | collective-permute-done | bytes 262176 | tf_op jit(solution)/shard_map/ppermute | solution.py:568
  54.1 1.8 %pad_maximum_fusion.refs_0_ = bf16[2,64,2048]{2,1,0:T(8,128)(2,1)} fusion(bf16[1,64,2048]{2,1,0:T(8,128)(2,1)S(1)} %collective-permute-done.4, bf16[1,64,2048]{2,1,0:T(8,128)(2,1)} %get-tuple-element.51), kind=kLoop, calls=%fused_computation | loop fusion | flops 262144 | bytes 1048576 | tf_op jit(solution)/shard_map/concatenate | solution.py:611
  55.9 1.1 all-to-all-done.1
  58.1 10.3 %shard_map.267 = (bf16[16,32,512]{2,1,0:T(8,128)(2,1)}, bf16[32,2048]{1,0:T(8,128)(2,1)}, bf16[32,2048]{1,0:T(8,128)(2,1)}, bf16[32,2048]{1,0:T(8,128)(2,1)}, f3...) custom-call(s32[6]{0:T(128)S(1)} %stack.27.place, s32[1]{0:T(128)S(6)} %copy.44.length, ...), custom_call_target="tpu_custom_call" | custom-call | tf_op jit(solution)/shard_map/pallas_call | solution.py:538
  68.3 6.8 %all-to-all-start.2 = ((bf16[16,32,512]{2,1,0:T(8,128)(2,1)}), bf16[16,32,512]{2,1,0:T(8,128)(2,1)}, u32[]{:S(2)}, u32[]{:S(2)}) async-start(bf16[16,32,512]{2,1,0:T(8,128)(2,1)} %shard_map.268.other), calls=%async_computation.2 | async-start | bytes 1048576 | tf_op jit(solution)/shard_map/all_to_all | solution.py:564
  76.0 3.2 %shard_map.270.other2.scaled = bf16[16,128,512]{2,1,0:T(8,128)(2,1)} custom-call(s32[6]{0:T(128)S(1)} %stack.27.place, bf16[8,176,512]{2,1,0:T(8,128)(2,1)S(1)} %shard_map.265.near, bf16[8,176,512]{2,1,0:T(8,128)(2,1)S(1)} %collective-permute-done.1.far, bf16[16,32,512]{2,1,0:T(8,128)(2,1)} %shard_map.268.other), custom_call_target="tpu_custom_call" | custom-call | tf_op jit(solution)/shard_map/pallas_call | solution.py:538
  79.9 6.4 %all-to-all-done.2.mixed = bf16[16,32,512]{2,1,0:T(8,128)(2,1)} async-done(((bf16[16,32,512]{2,1,0:T(8,128)(2,1)}), bf16[16,32,512]{2,1,0:T(8,128)(2,1)}, u32[]{:S(2)}, u32[]{:S(2)}) %all-to-all-start.2) | async-done | bytes 524320 | tf_op jit(solution)/shard_map/all_to_all | solution.py:564
  86.4 1.3 all-gather.5.cloned.1.call-done
  87.6 9.8 %shard_map.271 = (bf16[16,32,512]{2,1,0:T(8,128)(2,1)}, bf16[2,128,1024]{2,1,0:T(8,128)(2,1)}, bf16[2,128,1024]{2,1,0:T(8,128)(2,1)S(1)}, bf16[4,2,64,2048]{3,2,1,0:T(8,128)(2,1)}, f32[8,512]{1,0:T(8,128)}) custom-call(s32[6]{0:T(128)S(1)} %stack.27.place, s32[1]{0:T(128)S(6)} %copy.44.length, bf16[16,32,512]{2,1,0:T(8,128)(2,1)} %all-to-all-done.2.mixed, ...), custom_call_target="tpu_custom_call" | custom-call | tf_op jit(solution)/shard_map/pallas_call | solution.py:538
  98.9 7.0 %all-to-all-start.3 = ((bf16[16,32,512]{2,1,0:T(8,128)(2,1)}), bf16[16,32,512]{2,1,0:T(8,128)(2,1)S(1)}, u32[]{:S(2)}, u32[]{:S(2)}) async-start(bf16[16,32,512]{2,1,0:T(8,128)(2,1)} %get-tuple-element.53), calls=%async_computation.3 | async-start | bytes 1048576 | tf_op jit(solution)/shard_map/all_to_all | solution.py:564
  106.0 2.1 %shard_map.273 = (bf16[128,1024]{1,0:T(8,128)(2,1)}, bf16[128,1024]{1,0:T(8,128)(2,1)}) custom-call(bf16[2,128,1024]{2,1,0:T(8,128)(2,1)} %get-tuple-element.61.kept, bf16[2,128,1024]{2,1,0:T(8,128)(2,1)S(1)} %collective-permute-done.5.arrived), custom_call_target="tpu_custom_call" | custom-call | tf_op jit(solution)/shard_map/pallas_call | solution.py:538
  108.0 2.9 %collective-permute-start.6 = (bf16[128,1024]{1,0:T(8,128)(2,1)}, bf16[128,1024]{1,0:T(8,128)(2,1)S(1)}, u32[]{:S(2)}, u32[]{:S(2)}) collective-permute-start(bf16[128,1024]{1,0:T(8,128)(2,1)} %get-tuple-element.63), channel_id=1, source_target_pairs={{0,2},{2,0},{1,3},{3,1},{4,6},{6,4},{5,7},{7,5},{8,10},{10,8},{9,1... | collective-permute-start | bytes 786440 | tf_op jit(solution)/shard_map/ppermute | solution.py:568
  110.9 6.2 %all-to-all-done.3.d_mixed = bf16[16,32,512]{2,1,0:T(8,128)(2,1)S(1)} async-done(((bf16[16,32,512]{2,1,0:T(8,128)(2,1)}), bf16[16,32,512]{2,1,0:T(8,128)(2,1)S(1)}, u32[]{:S(2)}, u32[]{:S(2)}) %all-to-all-start.3) | async-done | bytes 524320 | tf_op jit(solution)/shard_map/all_to_all | solution.py:564
  117.1 12.9 %shard_map.272 = (bf16[16,96,128]{2,1,0:T(8,128)(2,1)}, bf16[2,64,128]{2,1,0:T(8,128)(2,1)S(1)}, bf16[2,64,128]{2,1,0:T(8,128)(2,1)S(1)}, bf16[2,64,128]{2,1,0:T(8,128)(2,1)S(1)}, bf16[2,64,128]{2,1,0:T(8,128)(2,1)S(1)}) custom-call(s32[6]{0:T(128)S(1)} %stack.27.place, s32[1]{0:T(128)S(6)} %copy.44.length, bf16[16,32,512]{2,1,0:T(8,128)(2,1)S(1)} %all-to-all-done.3.d_mixed, ...), custom_call_target="tpu_custom_call" | custom-call | tf_op jit(solution)/shard_map/pallas_call | solution.py:538
  130.0 4.7 %all-to-all-start.4 = ((bf16[16,96,128]{2,1,0:T(8,128)(2,1)}), bf16[16,96,128]{2,1,0:T(8,128)(2,1)S(1)}, u32[]{:S(2)}, u32[]{:S(2)}) async-start(bf16[16,96,128]{2,1,0:T(8,128)(2,1)} %shard_map.274), calls=%async_computation.4 | async-start | bytes 786432 | tf_op jit(solution)/shard_map/all_to_all | solution.py:564
  134.9 1.5 collective-permute-start.8
  136.4 1.8 %collective-permute-start.9 = (bf16[2,64,128]{2,1,0:T(8,128)(2,1)S(1)}, bf16[2,64,128]{2,1,0:T(8,128)(2,1)S(1)}, u32[]{:S(2)}, u32[]{:S(2)}) collective-permute-start(bf16[2,64,128]{2,1,0:T(8,128)(2,1)S(1)} %get-tuple-element.70), channel_id=1, source_target_pairs={{0,48},{16,0},{32,16},{48,32},{1,49},{17,1},{33,17},{49,33},{2,50}... | collective-permute-start | bytes 98312 | tf_op jit(solution)/shard_map/ppermute | solution.py:572
  139.8 1.9 %shard_map.277.refs_0_ = bf16[32,4,2176]{2,1,0:T(4,128)(2,1)} custom-call(bf16[2,64,128]{2,1,0:T(8,128)(2,1)S(1)} %get-tuple-element.67.part0, bf16[2,64,128]{2,1,0:T(8,128)(2,1)S(1)} %collective-permute-done.7.part1, bf16[2,64,128]{2,1,0:T(8,128)(2,1)S(1)} %collective-permute-done.8.part2, bf16[2,64,128]{2,1,0:T(8,128)(2,1)S(1)} %collective-permute-done.9.part3, ...), custom_call_target="tpu_custom_call" | custom-call | tf_op jit(solution)/shard_map/pallas_call | solution.py:538
  141.7 3.0 %all-to-all-done.4.d_lin.refs_1_ = bf16[16,96,128]{2,1,0:T(8,128)(2,1)S(1)} async-done(((bf16[16,96,128]{2,1,0:T(8,128)(2,1)}), bf16[16,96,128]{2,1,0:T(8,128)(2,1)S(1)}, u32[]{:S(2)}, u32[]{:S(2)}) %all-to-all-start.4) | async-done | bytes 393248 | tf_op jit(solution)/shard_map/all_to_all | solution.py:564
  144.8 5.5 %all-to-all-start.5 = ((bf16[32,4,2176]{2,1,0:T(4,128)(2,1)}), bf16[32,4,2176]{2,1,0:T(4,128)(2,1)S(1)}, u32[]{:S(2)}, u32[]{:S(2)}) async-start(bf16[32,4,2176]{2,1,0:T(4,128)(2,1)} %shard_map.278), calls=%async_computation.6 | async-start | bytes 1114112 | tf_op jit(solution)/shard_map/all_to_all | solution.py:564
  150.3 5.0 %all-gather.7.cloned.1.call-done = bf16[8,64,1536]{2,1,0:T(8,128)(2,1)} async-done(((bf16[2,64,1536]{2,1,0:T(8,128)(2,1)}), bf16[8,64,1536]{2,1,0:T(8,128)(2,1)}) %all-gather.7.cloned.1.call-update) | async-done | bytes 1572880 | tf_op jit(solution)/shard_map/all_gather | solution.py:656
  155.3 4.5 %shard_map.276 = (f32[1,128,512]{2,1,0:T(8,128)}, bf16[1,128,512]{2,1,0:T(8,128)(2,1)}) custom-call(s32[6]{0:T(128)S(1)} %stack.27.place, s32[1]{0:T(128)S(6)} %copy.44.length, bf16[1,128,512]{2,1,0:T(8,128)(2,1)} %tokens.3, bf16[16,96,128]{2,1,0:T(8,128)(2,1)S(1)} %all-to-all-done.4.d_lin.refs_1_, bf16[4,2,64,1536]{3,2,1,0:T(8,128)(2,1)} %bitcast.14, ...), custom_call_target="tpu_custom_call" | custom-call | tf_op jit(solution)/shard_map/pallas_call | solution.py:538
  159.9 2.3 %all-to-all-done.5.parts = bf16[32,4,2176]{2,1,0:T(4,128)(2,1)S(1)} async-done(((bf16[32,4,2176]{2,1,0:T(4,128)(2,1)}), bf16[32,4,2176]{2,1,0:T(4,128)(2,1)S(1)}, u32[]{:S(2)}, u32[]{:S(2)}) %all-to-all-start.5) | async-done | bytes 557088 | tf_op jit(solution)/shard_map/all_to_all | solution.py:564
  162.1 2.1 %shard_map.279 = (f32[4]{0:T(128)}, f32[4]{0:T(128)}, f32[4,512]{1,0:T(4,128)}, f32[4,512]{1,0:T(4,128)}, f32[4,512]{1,0:T(4,128)}, /*index=5*/f32[4,512]{1,0:T(...) custom-call(bf16[32,4,2176]{2,1,0:T(4,128)(2,1)S(1)} %all-to-all-done.5.parts, ...), custom_call_target="tpu_custom_call" | custom-call | tf_op jit(solution)/shard_map/pallas_call | solution.py:538
  (41 shorter events, 6.5 us)
Async XLA Ops:
  9.8 8.5 %copy-start.4 = (bf16[1,128,512]{2,1,0:T(8,128)(2,1)S(1)}, bf16[1,128,512]{2,1,0:T(8,128)(2,1)}, u32[]{:S(2)}) copy-start(bf16[1,128,512]{2,1,0:T(8,128)(2,1)} %param.30) | copy-start | bytes 393220
  9.8 29.7 %all-to-all-start = ((bf16[8,176,512]{2,1,0:T(8,128)(2,1)}), bf16[8,176,512]{2,1,0:T(8,128)(2,1)S(1)}, u32[]{:S(2)}, u32[]{:S(2)}) async-start(bf16[8,176,512]{2,1,0:T(8,128)(2,1)} %shard_map.264), calls=%async_computation | async-start | bytes 2883584 | tf_op jit(solution)/shard_map/all_to_all | solution.py:564
  18.3 21.2 %collective-permute-start = (bf16[1,128,512]{2,1,0:T(8,128)(2,1)S(1)}, bf16[1,128,512]{2,1,0:T(8,128)(2,1)S(1)}, u32[]{:S(2)}, u32[]{:S(2)}) collective-permute-start(bf16[1,128,512]{2,1,0:T(8,128)(2,1)S(1)} %copy-done.4), channel_id=1, source_target_pairs={{0,2},{2,0},{1,3},{3,1},{4,6},{6,4},{5,7},{7,5},{8,10},{10,8},{9,1... | collective-permute-start | bytes 393224 | tf_op jit(solution)/shard_map/ppermute | solution.py:568
  39.5 2.1 %copy-start = (bf16[2,128,512]{2,1,0:T(8,128)(2,1)}, bf16[2,128,512]{2,1,0:T(8,128)(2,1)S(1)}, u32[]{:S(2)}) copy-start(bf16[2,128,512]{2,1,0:T(8,128)(2,1)S(1)} %constant_dynamic-update-slice_fusion.refs_1_.cot_near) | copy-start | bytes 786436
  39.5 5.2 %collective-permute-start.1 = (bf16[8,176,512]{2,1,0:T(8,128)(2,1)S(1)}, bf16[8,176,512]{2,1,0:T(8,128)(2,1)S(1)}, u32[]{:S(2)}, u32[]{:S(2)}) collective-permute-start(bf16[8,176,512]{2,1,0:T(8,128)(2,1)S(1)} %shard_map.265.near), channel_id=1, source_target_pairs={{0,1},{1,0},{2,3},{3,2},{4,5},{5,4},{6,7},{7,6},{8,9},{9,8},{10,11... | collective-permute-start | bytes 4325384 | tf_op jit(solution)/shard_map/ppermute | solution.py:568
  41.4 3.2 %collective-permute-start.2 = (bf16[2,128,512]{2,1,0:T(8,128)(2,1)S(1)}, bf16[2,128,512]{2,1,0:T(8,128)(2,1)S(1)}, u32[]{:S(2)}, u32[]{:S(2)}) collective-permute-start(bf16[2,128,512]{2,1,0:T(8,128)(2,1)S(1)} %constant_dynamic-update-slice_fusion.refs_1_.cot_near), channel_id=1, source_target_pairs={{0,1},{1,0},{2,3},{3,2},{4,5},{5,4},{6,7},{7,6},{8,9},{9,8},{10,11... | collective-permute-start | bytes 786440 | tf_op jit(solution)/shard_map/ppermute | solution.py:568
  44.7 1.6 copy-start.1
  46.3 10.8 %copy-start.3 = (bf16[1,64,1536]{2,1,0:T(8,128)(2,1)S(1)}, bf16[1,64,1536]{2,1,0:T(8,128)(2,1)}, u32[]{:S(2)}) copy-start(bf16[1,64,1536]{2,1,0:T(8,128)(2,1)} %get-tuple-element.50) | copy-start | bytes 589828
  46.3 7.8 %collective-permute-start.4 = (bf16[1,64,2048]{2,1,0:T(8,128)(2,1)}, bf16[1,64,2048]{2,1,0:T(8,128)(2,1)S(1)}, u32[]{:S(2)}, u32[]{:S(2)}) collective-permute-start(bf16[1,64,2048]{2,1,0:T(8,128)(2,1)} %get-tuple-element.51), channel_id=1, source_target_pairs={{0,64},{64,0},{1,65},{65,1},{2,66},{66,2},{3,67},{67,3},{4,68},{68... | collective-permute-start | bytes 786440 | tf_op jit(solution)/shard_map/ppermute | solution.py:568
  47.1 9.9 %all-to-all-start.1 = ((bf16[8,64,128]{2,1,0:T(8,128)(2,1)}), bf16[8,64,128]{2,1,0:T(8,128)(2,1)S(1)}, u32[]{:S(2)}, u32[]{:S(2)}) async-start(bf16[8,64,128]{2,1,0:T(8,128)(2,1)} %get-tuple-element.48), calls=%async_computation.1 | async-start | bytes 262144 | tf_op jit(solution)/shard_map/all_to_all | solution.py:564
  51.6 36.0 %all-gather.5.cloned.1.call-start = ((), (), s32[]{:S(2)}) async-start(), calls=%async_computation.8 | async-start | bytes 2621440 | tf_op jit(solution)/shard_map/all_gather | solution.py:612
  57.1 11.3 %collective-permute-start.3 = (bf16[1,64,1536]{2,1,0:T(8,128)(2,1)S(1)}, bf16[1,64,1536]{2,1,0:T(8,128)(2,1)S(1)}, u32[]{:S(2)}, u32[]{:S(2)}) collective-permute-start(bf16[1,64,1536]{2,1,0:T(8,128)(2,1)S(1)} %copy-done.3), channel_id=1, source_target_pairs={{0,64},{64,0},{1,65},{65,1},{2,66},{66,2},{3,67},{67,3},{4,68},{68... | collective-permute-start | bytes 589832 | tf_op jit(solution)/shard_map/ppermute | solution.py:568
  68.3 18.0 %all-to-all-start.2 = ((bf16[16,32,512]{2,1,0:T(8,128)(2,1)}), bf16[16,32,512]{2,1,0:T(8,128)(2,1)}, u32[]{:S(2)}, u32[]{:S(2)}) async-start(bf16[16,32,512]{2,1,0:T(8,128)(2,1)} %shard_map.268.other), calls=%async_computation.2 | async-start | bytes 1048576 | tf_op jit(solution)/shard_map/all_to_all | solution.py:564
  75.1 64.7 %reduce-scatter.2.cloned.1.call-start = ((), (), s32[]{:S(2)}) async-start(), calls=%async_computation.7 | async-start | bytes 2621440 | tf_op jit(solution)/shard_map/reduce_scatter | solution.py:653
  97.5 57.9 %all-gather.7.cloned.1.call-start = ((), (), s32[]{:S(2)}) async-start(), calls=%async_computation.9 | async-start | bytes 1966080 | tf_op jit(solution)/shard_map/all_gather | solution.py:656
  98.2 7.8 %collective-permute-start.5 = (bf16[2,128,1024]{2,1,0:T(8,128)(2,1)S(1)}, bf16[2,128,1024]{2,1,0:T(8,128)(2,1)S(1)}, u32[]{:S(2)}, u32[]{:S(2)}) collective-permute-start(bf16[2,128,1024]{2,1,0:T(8,128)(2,1)S(1)} %get-tuple-element.62), channel_id=1, source_target_pairs={{0,1},{1,0},{2,3},{3,2},{4,5},{5,4},{6,7},{7,6},{8,9},{9,8},{10,11... | collective-permute-start | bytes 1572872 | tf_op jit(solution)/shard_map/ppermute | solution.py:568
  98.9 18.1 %all-to-all-start.3 = ((bf16[16,32,512]{2,1,0:T(8,128)(2,1)}), bf16[16,32,512]{2,1,0:T(8,128)(2,1)S(1)}, u32[]{:S(2)}, u32[]{:S(2)}) async-start(bf16[16,32,512]{2,1,0:T(8,128)(2,1)} %get-tuple-element.53), calls=%async_computation.3 | async-start | bytes 1048576 | tf_op jit(solution)/shard_map/all_to_all | solution.py:564
  108.0 21.9 %collective-permute-start.6 = (bf16[128,1024]{1,0:T(8,128)(2,1)}, bf16[128,1024]{1,0:T(8,128)(2,1)S(1)}, u32[]{:S(2)}, u32[]{:S(2)}) collective-permute-start(bf16[128,1024]{1,0:T(8,128)(2,1)} %get-tuple-element.63), channel_id=1, source_target_pairs={{0,2},{2,0},{1,3},{3,1},{4,6},{6,4},{5,7},{7,5},{8,10},{10,8},{9,1... | collective-permute-start | bytes 786440 | tf_op jit(solution)/shard_map/ppermute | solution.py:568
  130.0 14.8 %copy-start.2 = (bf16[128,1024]{1,0:T(8,128)(2,1)}, bf16[128,1024]{1,0:T(8,128)(2,1)S(1)}, u32[]{:S(2)}) copy-start(bf16[128,1024]{1,0:T(8,128)(2,1)S(1)} %collective-permute-done.6.refs_1_.w1) | copy-start | bytes 786436
  130.0 14.8 %all-to-all-start.4 = ((bf16[16,96,128]{2,1,0:T(8,128)(2,1)}), bf16[16,96,128]{2,1,0:T(8,128)(2,1)S(1)}, u32[]{:S(2)}, u32[]{:S(2)}) async-start(bf16[16,96,128]{2,1,0:T(8,128)(2,1)} %shard_map.274), calls=%async_computation.4 | async-start | bytes 786432 | tf_op jit(solution)/shard_map/all_to_all | solution.py:564
  134.6 4.0 %collective-permute-start.7 = (bf16[2,64,128]{2,1,0:T(8,128)(2,1)S(1)}, bf16[2,64,128]{2,1,0:T(8,128)(2,1)S(1)}, u32[]{:S(2)}, u32[]{:S(2)}) collective-permute-start(bf16[2,64,128]{2,1,0:T(8,128)(2,1)S(1)} %get-tuple-element.68), channel_id=1, source_target_pairs={{0,16},{16,32},{32,48},{48,0},{1,17},{17,33},{33,49},{49,1},{2,18}... | collective-permute-start | bytes 98312 | tf_op jit(solution)/shard_map/ppermute | solution.py:572
  134.9 4.6 %collective-permute-start.8 = (bf16[2,64,128]{2,1,0:T(8,128)(2,1)S(1)}, bf16[2,64,128]{2,1,0:T(8,128)(2,1)S(1)}, u32[]{:S(2)}, u32[]{:S(2)}) collective-permute-start(bf16[2,64,128]{2,1,0:T(8,128)(2,1)S(1)} %get-tuple-element.69), channel_id=1, source_target_pairs={{0,32},{16,48},{32,0},{48,16},{1,33},{17,49},{33,1},{49,17},{2,34}... | collective-permute-start | bytes 98312 | tf_op jit(solution)/shard_map/ppermute | solution.py:572
  136.4 3.4 %collective-permute-start.9 = (bf16[2,64,128]{2,1,0:T(8,128)(2,1)S(1)}, bf16[2,64,128]{2,1,0:T(8,128)(2,1)S(1)}, u32[]{:S(2)}, u32[]{:S(2)}) collective-permute-start(bf16[2,64,128]{2,1,0:T(8,128)(2,1)S(1)} %get-tuple-element.70), channel_id=1, source_target_pairs={{0,48},{16,0},{32,16},{48,32},{1,49},{17,1},{33,17},{49,33},{2,50}... | collective-permute-start | bytes 98312 | tf_op jit(solution)/shard_map/ppermute | solution.py:572
  144.8 17.4 %all-to-all-start.5 = ((bf16[32,4,2176]{2,1,0:T(4,128)(2,1)}), bf16[32,4,2176]{2,1,0:T(4,128)(2,1)S(1)}, u32[]{:S(2)}, u32[]{:S(2)}) async-start(bf16[32,4,2176]{2,1,0:T(4,128)(2,1)} %shard_map.278), calls=%async_computation.6 | async-start | bytes 1114112 | tf_op jit(solution)/shard_map/all_to_all | solution.py:564
Sparse Core Ops, SparseCore 0:
  57.2 30.3 all-gather.4
  97.6 29.7 reduce-scatter.1
  129.1 26.1 all-gather.6

commit v5 on v4

--- a/solution.py
+++ b/solution.py
@@ -22,6 +22,7 @@
 DEVICES = 128
 SEQ = 16
 DP = 8
+KEY_CHUNK = 256
 AUG = 48
 
 EPS = 1e-05
@@ -109,10 +110,24 @@
 MSG_ROWS = ROWS + 48
 
 
+def column_order():
+    n = lax.broadcasted_iota(jnp.int32, (512, 1), 0)
+    to = ((n >> 2) & 3) * 128 + (n >> 7) * 32 + ((n >> 4) & 7) * 4 + (n & 3)
+    lane = lax.broadcasted_iota(jnp.int32, (512, 512), 1)
+    return jnp.where(lane == to, 1.0, 0.0).astype(bf16)
+
+
 def pack_kernel(
     tokens, w_query, w_key, w_value, w_output, w_gate, w_up, w_down, gain1, bias1, gain2, bias2,
-    order, sent,
+    sent,
+    rows, left,
 ):
+    leaving = [
+        pltpu.make_async_copy(tokens.at[0], sent.at[chip, 0:ROWS, :], left.at[chip])
+        for chip in range(8)
+    ]
+    for copy in leaving:
+        copy.start()
     narrow = [w[...].astype(f32) for w in (w_query, w_key, w_value)]
     gate = w_gate[...].astype(f32)
     up = w_up[...].astype(f32)
@@ -121,7 +136,7 @@
     for u in range(4):
         here = slice(512 * u, 512 * (u + 1))
         pieces.append(jnp.concatenate([gate[:, here], up[:, here]], 0))
-    wide = nn(jnp.concatenate(pieces, 0).astype(bf16), order[...])
+    wide = nn(jnp.concatenate(pieces, 0).astype(bf16), column_order())
     lane = lax.broadcasted_iota(jnp.int32, (4, 128), 1)
     row = lax.broadcasted_iota(jnp.int32, (4, 128), 0)
     norms = jnp.zeros((4, 128), f32)
@@ -154,8 +169,11 @@
                 )
             heads = jnp.concatenate(heads + [nothing[:, :256]], 1)
             low = jnp.concatenate([mine, heads, nothing], 0).astype(bf16)
-            sent[2 * y + z, 0:ROWS, :] = tokens[0]
-            sent[2 * y + z, ROWS:, :] = low
+            rows[2 * y + z] = low
+    copy = pltpu.make_async_copy(rows, sent.at[:, ROWS:, :], left.at[8])
+    copy.start()
+    leaving.append(copy)
+    finish(leaving)
 
 
 def unpack_kernel(place, near, far, cot, feed, heads, whole, rows, arrived):
@@ -198,6 +216,12 @@
             heads[w, here, :] = cols
 
 
+def join_kernel(own, other, feed, out):
+    for i, rows in enumerate((own, other)):
+        feed[i] = rows[0, :, 0 : 3 * D]
+        out[i] = rows[0, :, 3 * D : 4 * D]
+
+
 def block_of(place, chip, other):
     return 2 * chip + (place[0] ^ other)
 
@@ -205,10 +229,18 @@
 def attend_kernel(
     place, length, near, far, head_cols, cos, sin,
     sent, q_out, k_out, v_out, o_out, lse_out, cols_out,
-    q_t, k_t, v_t,
+    q_t, k_t, v_t, own_cols, left,
 ):
+    leaving = []
+
+    def send(source, target):
+        copy = pltpu.make_async_copy(source, target, left.at[len(leaving)])
+        copy.start()
+        leaving.append(copy)
+
     cols = head_cols[...].reshape(D, 128).astype(f32).T
-    cols_out[...] = cols
+    own_cols[...] = cols
+    send(own_cols, cols_out)
     gain = cols[96:97, :]
     bias = cols[97:98, :]
     weights_t = cols[0:96, :].astype(bf16)
@@ -232,27 +264,33 @@
             ).astype(bf16)
             k_t[:, here] = jnp.concatenate([k1 * c - k2 * s, k2 * c + k1 * s], 0).astype(bf16)
             v_t[:, here] = part[64:96].astype(bf16)
-    q_out[...] = q_t[...]
-    k_out[...] = k_t[...]
-    v_out[...] = v_t[...]
+    send(q_t, q_out)
+    send(k_t, k_out)
+    send(v_t, v_out)
     keys = key_columns(k_t[...].astype(f32), length[0])
     one_row = jnp.ones((1, LEN), f32)
     values_t = with_rows(v_t[...], [one_row])
-    tile = TEAM_ROWS
-    for i in range(LEN // tile):
-        here = slice(i * tile, (i + 1) * tile)
-        queries_t = with_rows(q_t[:, here], [jnp.ones((1, tile), f32)])
-        scores = nn(keys, queries_t)
-        top = jnp.max(scores, axis=0, keepdims=True)
-        weights = jnp.exp2(scores - top).astype(bf16)
-        mixed = nn(values_t, weights)
-        total = mixed[HEAD : HEAD + 1]
-        out = mixed[:HEAD] / total
-        o_out[:, here] = out
-        lse_out[:, here] = top + jnp.log2(total)
-        low = out.astype(bf16)
+    queries_t = with_rows(q_t[...], [one_row])
+    top = mixed = None
+    for i in range(LEN // KEY_CHUNK):
+        here = slice(i * KEY_CHUNK, (i + 1) * KEY_CHUNK)
+        scores = nn(keys[here, :], queries_t)
+        new_top = jnp.max(scores, axis=0, keepdims=True)
+        if i:
+            new_top = jnp.maximum(top, new_top)
+        weights = jnp.exp2(scores - new_top).astype(bf16)
+        added = nn(values_t[:, here], weights)
+        mixed = mixed * jnp.exp2(top - new_top) + added if i else added
+        top = new_top
+    total = mixed[HEAD : HEAD + 1]
+    out = mixed[:HEAD] / total
+    o_out[...] = out
+    lse_out[...] = top + jnp.log2(total)
+    low = out.astype(bf16)
+    for i in range(LEN // TEAM_ROWS):
         for t in range(TEAM):
-            sent[TEAM * i + t] = low
+            sent[TEAM * i + t] = low[:, i * TEAM_ROWS : (i + 1) * TEAM_ROWS]
+    finish(leaving)
 
 
 def load_part(place, weights, parts, arrived, i):
@@ -274,42 +312,59 @@
 
 def feed_kernel(
     place, length, mixed, near, far, cot_near, cot_far, weights, head_cols, other1, other2,
+    out0, out1, out2, out3,
     sent, kept, swapped, grads, norm_rows,
-    tokens, cot, back, ahead, parts, arrived, tokens_arrived,
+    mixed_rows, tokens, cot, norms, back, ahead, parts, own_sent, own_kept, own_grads,
+    arrived, tokens_arrived, left,
 ):
     core, team, z = place[0], place[1], place[2]
-    token_loads = []
+    first = [
+        pltpu.make_async_copy(mixed, mixed_rows, tokens_arrived.at[8]),
+        pltpu.make_async_copy(head_cols.at[96:104, :], norms, tokens_arrived.at[9]),
+    ]
+    later = []
     for one in range(2):
-        for other, source in enumerate((near, far)):
+        for other in range(2):
             here = pl.ds(pl.multiple_of((2 * (z ^ one) + (core ^ other)) * ROWS, ROWS), ROWS)
-            token_loads.append(
+            first.append(
                 pltpu.make_async_copy(
-                    source.at[2 * team + (z ^ one), 0:ROWS, :],
+                    (near, far)[other].at[2 * team + (z ^ one), 0:ROWS, :],
                     tokens.at[here, :],
                     tokens_arrived.at[2 * one + other],
                 )
             )
-    for load in token_loads:
-        load.start()
-    member = 2 * z + core
-    for one in range(2):
-        here = pl.ds(pl.multiple_of((2 * (z ^ one) + core) * ROWS, ROWS), ROWS)
-        there = pl.ds(pl.multiple_of((2 * (z ^ one) + 1 - core) * ROWS, ROWS), ROWS)
-        cot[here, :] = cot_near[one]
-        cot[there, :] = cot_far[one]
-    gain = head_cols[98:99, :]
-    bias = head_cols[99:100, :]
-    loads = [load_part(place, weights, parts, arrived, i) for i in (3, 0, 1, 2)]
-    for load in loads:
+            later.append(
+                pltpu.make_async_copy(
+                    (cot_near, cot_far)[other].at[one],
+                    cot.at[here, :],
+                    tokens_arrived.at[4 + 2 * one + other],
+                )
+            )
+    loads = [
+        [
+            pltpu.make_async_copy(
+                rows.at[place[5] ^ k],
+                parts.at[3, k, lax.rem(place[4] + 4 - step, 4)],
+                arrived.at[24 + 4 * k + step],
+            )
+            for k in range(2)
+            for step, rows in enumerate((out0, out1, out2, out3))
+        ]
+    ]
+    loads += [load_part(place, weights, parts, arrived, i) for i in range(3)]
+    for load in [loads[0], first, *loads[1:], later]:
         for copy in load:
             copy.start()
-    mixed_t = mixed[...].reshape(D, TEAM_ROWS)
-    finish(token_loads)
-    finish(loads[0])
-    w_out = parts[3].reshape(D, D)
+    member = 2 * z + core
     row = lax.broadcasted_iota(jnp.int32, (TEAM_ROWS, 1), 0)
     live = (team * TEAM_ROWS + row) < length[0]
     own = (row // ROWS) == member
+    finish(first)
+    finish(loads[0])
+    gain = norms[2:3, :]
+    bias = norms[3:4, :]
+    mixed_t = mixed_rows[...].reshape(D, TEAM_ROWS)
+    w_out = parts[3].reshape(D, D)
     middle = tokens[...].astype(f32) + tn(mixed_t, w_out)
     scaled, inv = norm_parts(middle)
     normed = (scaled * gain + bias).astype(bf16)
@@ -320,43 +375,54 @@
     w_up = parts[1].reshape(D, FF_PART)
     up = nn(normed, w_up)
     finish(loads[3])
+    finish(later)
     w_down = parts[2].reshape(FF_PART, D)
+    d_out = jnp.where(live, cot[...].astype(f32), 0.0)
+    d_out_low = d_out.astype(bf16)
+    d_hidden = nt(d_out_low, w_down)
     sig = jax.nn.sigmoid(gate)
     act = gate * sig
     hidden = (act * up).astype(bf16)
     out_part = nn(hidden, w_down) + jnp.where(own, middle, 0.0)
-    d_out = jnp.where(live, cot[...].astype(f32), 0.0)
-    d_out_low = d_out.astype(bf16)
-    d_hidden = nt(d_out_low, w_down)
     d_up = (d_hidden * act).astype(bf16)
     d_gate = (d_hidden * up * sig * (1.0 + gate * (1.0 - sig))).astype(bf16)
     d_normed = nt(d_gate, w_gate) + nt(d_up, w_up)
-    d_middle = jnp.where(own, d_out, 0.0) + norm_back(d_normed, scaled, inv, gain)
-    d_middle_low = d_middle.astype(bf16)
-    sent[...] = nt(w_out, d_middle_low).astype(bf16).reshape(HEADS, HEAD, TEAM_ROWS)
-    back[...] = d_middle_low
-    ahead[...] = out_part.astype(bf16)
-    for one in range(2):
-        for target, other in ((kept, core), (swapped, 1 - core)):
-            here = pl.ds(pl.multiple_of((2 * (z ^ one) + other) * ROWS, ROWS), ROWS)
-            target[one, :, 0:D] = back[here, :]
-            target[one, :, D : 2 * D] = ahead[here, :]
-    for i, grad in enumerate(
-        (
-            tn(normed, d_gate),
-            tn(normed, d_up),
-            tn(hidden, d_out_low),
-            nn(mixed_t, d_middle_low),
-        )
-    ):
+
+    leaving = []
+
+    def send(source, target):
+        copy = pltpu.make_async_copy(source, target, left.at[len(leaving)])
+        copy.start()
+        leaving.append(copy)
+
+    def send_grad(i, grad):
         low = grad.astype(bf16)
         for k in range(2):
             for x in range(4):
                 at = 64 * (4 * k + x)
-                grads[x, k, :, D * i : D * (i + 1)] = low[at : at + 64]
+                own_grads[i, x, k] = low[at : at + 64]
+        send(own_grads.at[i], grads.at[:, :, :, D * i : D * (i + 1)])
+
+    send_grad(2, tn(hidden, d_out_low))
+    send_grad(0, tn(normed, d_gate))
+    send_grad(1, tn(normed, d_up))
+    d_middle = jnp.where(own, d_out, 0.0) + norm_back(d_normed, scaled, inv, gain)
+    d_middle_low = d_middle.astype(bf16)
+    own_sent[...] = nt(w_out, d_middle_low).astype(bf16).reshape(HEADS, HEAD, TEAM_ROWS)
+    send(own_sent, sent)
+    back[...] = d_middle_low
+    ahead[...] = out_part.astype(bf16)
+    for one in range(2):
+        for target, other in ((own_kept, core), (swapped, 1 - core)):
+            here = pl.ds(pl.multiple_of((2 * (z ^ one) + other) * ROWS, ROWS), ROWS)
+            target[one, :, 0:D] = back[here, :]
+            target[one, :, D : 2 * D] = ahead[here, :]
+    send(own_kept, kept)
+    send_grad(3, nn(mixed_t, d_middle_low))
     norm_rows[0:1, :] = jnp.sum(d_normed * scaled, 0, keepdims=True)
     norm_rows[1:2, :] = jnp.sum(d_normed, 0, keepdims=True)
     norm_rows[2:8, :] = jnp.zeros((6, D), f32)
+    finish(leaving)
 
 
 def add_kernel(kept, arrived, own, other):
@@ -377,10 +443,22 @@
 def attend_back_kernel(
     place, length, d_mixed, q_in, k_in, v_in, o_in, lse_in, cos, sin, scaled, head_cols, norm_rows,
     sent, sent0, sent1, sent2, sent3,
-    d_o, probs, d_scores, dq, dk, dv, table, normal, here_now,
+    d_o, probs, d_scores, dq, dk, dv, table, normal, cos_now, sin_now, cols, norms, own_sent, here_now, left,
 ):
-    load = pltpu.make_async_copy(scaled, normal, here_now.at[0])
-    load.start()
+    loads = [
+        pltpu.make_async_copy(source, target, here_now.at[i])
+        for i, (source, target) in enumerate(
+            (
+                (cos, cos_now),
+                (sin, sin_now),
+                (scaled, normal),
+                (head_cols.at[0:104, :], cols),
+                (norm_rows, norms),
+            )
+        )
+    ]
+    for load in loads:
+        load.start()
     for y in range(LEN // TEAM_ROWS):
         total = d_mixed[TEAM * y].astype(f32)
         for t in range(1, TEAM):
@@ -407,8 +485,9 @@
         dq[:, here] = nn(keys_t, ds) * SCALE
     dk[...] = nt(q_in[...], d_scores[...]) * LN2
     dv[...] = nt(d_o_t, probs[...])
-    c = cos[...]
-    s = sin[...]
+    finish(loads)
+    c = cos_now[...]
+    s = sin_now[...]
     q1, q2 = dq[0:HALF], dq[HALF:HEAD]
     k1, k2 = dk[0:HALF], dk[HALF:HEAD]
     dq_t = jnp.concatenate([q1 * c + q2 * s, q2 * c - q1 * s], 0).astype(bf16)
@@ -416,21 +495,22 @@
     dv_t = dv[...].astype(bf16)
     for b in range(SEQ):
         here = slice(b * ROWS, (b + 1) * ROWS)
-        sent[b, 0:32] = dq_t[:, here]
-        sent[b, 32:64] = dk_t[:, here]
-        sent[b, 64:96] = dv_t[:, here]
+        own_sent[b, 0:32] = dq_t[:, here]
+        own_sent[b, 32:64] = dk_t[:, here]
+        own_sent[b, 64:96] = dv_t[:, here]
+    leaving = pltpu.make_async_copy(own_sent, sent, left.at[0])
+    leaving.start()
     d_lin = jnp.concatenate([dq_t, dk_t, dv_t], 0)
-    load.wait()
     product = nn(d_lin, normal[...].reshape(LEN, D))
     total = jnp.sum(d_lin.astype(f32), 1, keepdims=True)
-    weights = head_cols[0:96, :]
-    gain = head_cols[96:97, :]
-    bias = head_cols[97:98, :]
+    weights = cols[0:96, :]
+    gain = cols[96:97, :]
+    bias = cols[97:98, :]
     rows = [
         product * gain + total * bias,
         jnp.sum(product * weights, 0, keepdims=True),
         jnp.sum(total * weights, 0, keepdims=True),
-        norm_rows[0:2, :],
+        norms[0:2, :],
         jnp.zeros((28, D), f32),
     ]
     table[...] = jnp.concatenate(rows, 0).T
@@ -439,6 +519,7 @@
         for k in range(2):
             at = pl.multiple_of((4 * k + x) * 64, 64)
             part[k] = table[pl.ds(at, 64), :].astype(bf16)
+    leaving.wait()
 
 
 def regroup_kernel(part0, part1, part2, part3, feed, sent):
@@ -475,7 +556,7 @@
 
 
 def sum_kernel(
-    parts, order, gain1, bias1, grad_query, grad_key, grad_value, grad_output, gain2, bias2,
+    parts, gain1, bias1, grad_query, grad_key, grad_value, grad_output, gain2, bias2,
     grad_gate, grad_up, grad_down,
 ):
     members = []
@@ -493,7 +574,8 @@
     wide = jnp.concatenate(pieces, 0)
     high = wide.astype(bf16)
     low = (wide - high.astype(f32)).astype(bf16)
-    wide = nt(high, order[...]) + nt(low, order[...])
+    order = column_order()
+    wide = nt(high, order) + nt(low, order)
     for u in range(4):
         here = slice(512 * u, 512 * (u + 1))
         grad_gate[:, here] = wide[8 * u : 8 * u + 4]
@@ -553,13 +635,6 @@
     return np.cos(angles).astype(np.float32), np.sin(angles).astype(np.float32)
 
 
-def column_order():
-    order = np.arange(512).reshape(4, 8, TEAM, 4).transpose(2, 0, 1, 3).reshape(-1)
-    table = np.zeros((512, 512), np.float32)
-    table[order, np.arange(512)] = 1.0
-    return table
-
-
 def exchange(value, axes):
     return lax.all_to_all(value, axes, 0, 0, tiled=True)
 
@@ -581,15 +656,15 @@
     core = lax.axis_index("core")
     place = jnp.stack([core, y, z, 4 * y + 2 * z + core, lax.axis_index("x"), lax.axis_index("z_lo")]).astype(jnp.int32)
     cos, sin = (jnp.asarray(table) for table in rope_tables())
-    order = jnp.asarray(column_order(), bf16)
 
     (packed,) = call(
         pack_kernel,
-        "H" * 13,
-        [((8, MSG_ROWS, D), bf16, "H")],
+        "H" * 12,
+        [((8, MSG_ROWS, D), bf16, "A")],
+        [((8, MSG_ROWS - ROWS, D), bf16), 9],
     )(
         tokens, w_query, w_key, w_value, w_output, w_gate, w_up, w_down,
-        norm1_gain, norm1_bias, norm2_gain, norm2_bias, order,
+        norm1_gain, norm1_bias, norm2_gain, norm2_bias,
     )
     near = exchange(packed, CHIPS)
     cot_pair = jnp.concatenate([cotangent, swap(cotangent, "z")], 0)
@@ -608,26 +683,37 @@
         [((2, 8, 48, D), bf16), 2],
     )(place, near, far, cot_far)
     head_cols = exchange(heads, WINDOWS).reshape(D, 128)
-    feed_rows = jnp.concatenate([feed_rows, swap(feed_rows, "z_lo")], 0)
-    feed_weights = lax.all_gather(after(feed_rows, head_cols), "x")
+    feed_other = after(swap(feed_rows, "z_lo"), in_hbm(whole), place=pltpu.VMEM)
+    feed_rows, out_rows = call(
+        join_kernel, "UU", [((2, 64, 3 * D), bf16, "V"), ((2, 64, D), bf16, "V")]
+    )(feed_rows, feed_other)
+    feed_weights = lax.all_gather(feed_rows, "x")
+    out_rows = [out_rows] + [shift(out_rows, step) for step in range(1, 4)]
     whole_other = swap(whole, "z_lo")
 
     sent, q_t, k_t, v_t, o_t, lse, head_cols = call(
         attend_kernel,
-        "SSVVVHH",
+        "SSVVUHH",
         [
             ((SEQ, HEAD, TEAM_ROWS), bf16, "H"),
-            ((HEAD, LEN), bf16, "H"),
-            ((HEAD, LEN), bf16, "H"),
-            ((HEAD, LEN), bf16, "H"),
+            ((HEAD, LEN), bf16, "A"),
+            ((HEAD, LEN), bf16, "A"),
+            ((HEAD, LEN), bf16, "A"),
             ((HEAD, LEN), f32, "H"),
             ((1, LEN), f32, "H"),
-            ((128, D), f32, "H"),
+            ((128, D), f32, "A"),
         ],
-        [((HEAD, LEN), bf16)] * 3,
+        [
+            ((HEAD, LEN), bf16),
+            ((HEAD, LEN), bf16),
+            ((HEAD, LEN), bf16),
+            ((128, D), f32),
+            4,
+        ],
         vmem=24,
+        flops=19 * 10**9,
     )(place, lengths, near, far, head_cols, cos, sin)
-    sent = after(sent, whole_other)
+    sent = after(sent, whole_other, *out_rows[1:])
     (scaled,) = call(
         scale_kernel, "SUUA", [((SEQ, ROWS, D), bf16, "H")], vmem=12
     )(place, near, far, sent)
@@ -636,18 +722,31 @@
 
     d_sent, kept, swapped, grads, norm_rows = call(
         feed_kernel,
-        "SSHPPHHAHAA",
+        "SSAPPAAAAAA" + "A" * 4,
         [
-            ((HEADS, HEAD, TEAM_ROWS), bf16, "H"),
-            ((2, ROWS, 2 * D), bf16, "H"),
+            ((HEADS, HEAD, TEAM_ROWS), bf16, "A"),
+            ((2, ROWS, 2 * D), bf16, "A"),
             ((2, ROWS, 2 * D), bf16, "V"),
-            ((4, 2, 64, FEED_LANES), bf16, "H"),
+            ((4, 2, 64, FEED_LANES), bf16, "A"),
             ((8, D), f32, "H"),
         ],
-        [((TEAM_ROWS, D), bf16)] * 4 + [((4, 2, 4, 64, 512), bf16), 32, 4],
-        vmem=24,
+        [
+            ((HEADS, HEAD, TEAM_ROWS), bf16),
+            ((TEAM_ROWS, D), bf16),
+            ((TEAM_ROWS, D), bf16),
+            ((8, D), f32),
+            ((TEAM_ROWS, D), bf16),
+            ((TEAM_ROWS, D), bf16),
+            ((4, 2, 4, 64, 512), bf16),
+            ((HEADS, HEAD, TEAM_ROWS), bf16),
+            ((2, ROWS, 2 * D), bf16),
+            ((4, 4, 2, 64, 512), bf16),
+            32, 10, 6,
+        ],
+        vmem=28,
     )(
         place, lengths, mixed, near, far, cot_pair, cot_far, feed_weights, head_cols, whole, scaled,
+        *out_rows,
     )
     d_mixed = exchange(d_sent, WINDOW)
     feed_grads = lax.psum_scatter(
@@ -661,8 +760,8 @@
 
     lin_sent, *head_grads = call(
         attend_back_kernel,
-        "SSVHHHHHHHAHH",
-        [((SEQ, 96, ROWS), bf16, "H")] + [((2, 64, 128), bf16, "V")] * 4,
+        "SSVHHHHHAAAAA",
+        [((SEQ, 96, ROWS), bf16, "A")] + [((2, 64, 128), bf16, "V")] * 4,
         [
             ((HEAD, LEN), bf16),
             ((LEN, LEN), bf16),
@@ -672,9 +771,14 @@
             ((HEAD, LEN), f32),
             ((D, 128), f32),
             ((SEQ, ROWS, D), bf16),
-            1,
+            ((HALF, LEN), f32),
+            ((HALF, LEN), f32),
+            ((104, D), f32),
+            ((8, D), f32),
+            ((SEQ, 96, ROWS), bf16),
+            5, 1,
         ],
-        vmem=40,
+        vmem=42,
     )(place, lengths, d_mixed, q_t, k_t, v_t, o_t, lse, cos, sin, scaled, head_cols, norm_rows)
     lin_sent = after(lin_sent, w1)
     back = exchange(lin_sent, WINDOW)
@@ -694,10 +798,10 @@
     )(place, lengths, tokens, back, row_weights, w0, w1, head_cols)
     weight_grads = call(
         sum_kernel,
-        "VH",
+        "V",
         [((4,), f32, "H")] * 2 + [((4, D), f32, "H")] * 4 + [((4,), f32, "H")] * 2
         + [((4, FF), f32, "H")] * 2 + [((16, D), f32, "H")],
-    )(grad_parts, order)
+    )(grad_parts)
     return (layer_output, grad_tokens) + tuple(weight_grads)
 
 

time: 172 us -> 169 us (0.983)
  starting transfers between devices: 50.5 us -> 55.3 us
  waiting for transfers between devices: 51.4 us -> 47.4 us
  Pallas kernels: 50.9 us -> 48.1 us
  other arithmetic: 1.8 us -> 0 us
    ppermute x3 -> x6, starting transfers between devices: 3.55 us -> 7.88 us  [shift(): return lax.ppermute(value, 'x', [(i, (i + by) % 4) for i in range(4)])]
    pallas_call x10 -> x11, Pallas kernels: 50.9 us -> 48.1 us  [run(): inner(*(pltpu.with_memory_space_constraint(x, pltpu.HBM if where in 'HA'...]
    all_gather x1, waiting for transfers between devices: 4.99 us -> 3.02 us  [shards(): lax.all_gather(after(whole, pltpu.with_memory_space_constraint(norm_rows,...]
    concatenate x1 -> x0, other arithmetic: 1.8 us -> none  [shards(): feed_rows = jnp.concatenate([feed_rows, swap(feed_rows, 'z_lo')], 0)]
  transfers between devices with their start and end apart: 19 -> 22, of which waited for: 13 -> 11; matrix products, arithmetic and copies ran while one was open for 2% -> 1% of each run, Pallas kernels for 20% -> 21%
where the time goes in v5:
time: 169 us; the launch traced here: 168 us
  starting transfers between devices  55.3 us (33%)
  Pallas kernels  48.1 us (28%)
  waiting for transfers between devices  47.4 us (28%)
  between operations  14.6 us (9%)
  local copies, waits for them, and re-layouts  2.48 us (1%)
    pallas_call x11, Pallas kernels, run(): inner(*(pltpu.with_memory_space_constraint(x, pltpu.HBM if where in 'HA'...  48.1 us
    all_to_all x6, starting transfers between devices, exchange(): return lax.all_to_all(value, axes, 0, 0, tiled=True)  35.8 us
    ppermute x7, waiting for transfers between devices, swap(): return lax.ppermute(value, axis, [(0, 1), (1, 0)])  23.3 us
    all_to_all x6, waiting for transfers between devices, exchange(): return lax.all_to_all(value, axes, 0, 0, tiled=True)  18.2 us
    ppermute x7, starting transfers between devices, swap(): return lax.ppermute(value, axis, [(0, 1), (1, 0)])  11.4 us
    ppermute x6, starting transfers between devices, shift(): return lax.ppermute(value, 'x', [(i, (i + by) % 4) for i in range(4)])  7.88 us
  transfers between devices with their start and end apart: 22, of which 11 were waited for; matrix products, arithmetic and copies ran while one was open for 1% of the time, Pallas kernels for 21%

profile of v5, /device:TPU:1, one launch (start us, length us, event | category | flops | bytes accessed | tf_op | source)
XLA Modules:
  0.0 168.0 jit_solution(17148700180442849212)
XLA Ops:
  7.2 2.2 %shard_map.255 = bf16[8,176,512]{2,1,0:T(8,128)(2,1)} custom-call(bf16[1,128,512]{2,1,0:T(8,128)(2,1)} %tokens.3, bf16[4,512]{1,0:T(4,128)(2,1)} %w_query.1, bf16[4,512]{1,0:T(4,128)(2,1)} %w_key.1, bf16[4,512]{1,0:T(4,128)(2,1)} %w_value.1, bf16[4,512]{1,0:T(4,128)(2,1)} %w_output.1, bf16[4,2048]{1,0:T(4,128)(2,1)} %w_gate.1, bf16[4,2048]{1,0:T(4,128)(2,1)} %w_up.1, ...), custom_call_target="tpu_custom_call" | custom-call | tf_op jit(solution)/shard_map/pallas_call | solution.py:620
  9.4 8.5 %all-to-all-start = ((bf16[8,176,512]{2,1,0:T(8,128)(2,1)}), bf16[8,176,512]{2,1,0:T(8,128)(2,1)S(1)}, u32[]{:S(2)}, u32[]{:S(2)}) async-start(bf16[8,176,512]{2,1,0:T(8,128)(2,1)} %shard_map.255), calls=%async_computation | async-start | bytes 2883584 | tf_op jit(solution)/shard_map/all_to_all | solution.py:639
  17.9 3.0 %collective-permute-start = (bf16[1,128,512]{2,1,0:T(8,128)(2,1)S(1)}, bf16[1,128,512]{2,1,0:T(8,128)(2,1)S(1)}, u32[]{:S(2)}, u32[]{:S(2)}) collective-permute-start(bf16[1,128,512]{2,1,0:T(8,128)(2,1)S(1)} %copy-done.6), channel_id=1, source_target_pairs={{0,2},{2,0},{1,3},{3,1},{4,6},{6,4},{5,7},{7,5},{8,10},{10,8},{9,1... | collective-permute-start | bytes 393224 | tf_op jit(solution)/shard_map/ppermute | solution.py:643
  20.9 18.2 %collective-permute-done = bf16[1,128,512]{2,1,0:T(8,128)(2,1)S(1)} collective-permute-done((bf16[1,128,512]{2,1,0:T(8,128)(2,1)S(1)}, bf16[1,128,512]{2,1,0:T(8,128)(2,1)S(1)}, u32[]{:S(2)}, u32[]{:S(2)}) %collective-permute-start) | collective-permute-done | bytes 131104 | tf_op jit(solution)/shard_map/ppermute | solution.py:643
  39.2 1.9 %collective-permute-start.1 = (bf16[8,176,512]{2,1,0:T(8,128)(2,1)S(1)}, bf16[8,176,512]{2,1,0:T(8,128)(2,1)S(1)}, u32[]{:S(2)}, u32[]{:S(2)}) collective-permute-start(bf16[8,176,512]{2,1,0:T(8,128)(2,1)S(1)} %shard_map.256.near), channel_id=1, source_target_pairs={{0,1},{1,0},{2,3},{3,2},{4,5},{5,4},{6,7},{7,6},{8,9},{9,8},{10,11... | collective-permute-start | bytes 4325384 | tf_op jit(solution)/shard_map/ppermute | solution.py:643
  41.8 2.5 %collective-permute-done.2.cot.cot_far = bf16[2,128,512]{2,1,0:T(8,128)(2,1)S(1)} collective-permute-done((bf16[2,128,512]{2,1,0:T(8,128)(2,1)S(1)}, bf16[2,128,512]{2,1,0:T(8,128)(2,1)S(1)}, u32[]{:S(2)}, u32[]{:S(2)}) %collective-permute-start.2) | collective-permute-done | bytes 262176 | tf_op jit(solution)/shard_map/ppermute | solution.py:643
  44.3 1.6 shard_map.257
  46.8 4.5 %all-to-all-start.1 = ((bf16[8,64,128]{2,1,0:T(8,128)(2,1)}), bf16[8,64,128]{2,1,0:T(8,128)(2,1)}, u32[]{:S(2)}, u32[]{:S(2)}) async-start(bf16[8,64,128]{2,1,0:T(8,128)(2,1)} %get-tuple-element.50), calls=%async_computation.1 | async-start | bytes 262144 | tf_op jit(solution)/shard_map/all_to_all | solution.py:639
  51.3 2.5 %collective-permute-done.4.refs_0_ = bf16[1,64,2048]{2,1,0:T(8,128)(2,1)S(1)} collective-permute-done((bf16[1,64,2048]{2,1,0:T(8,128)(2,1)}, bf16[1,64,2048]{2,1,0:T(8,128)(2,1)S(1)}, u32[]{:S(2)}, u32[]{:S(2)}) %collective-permute-start.4) | collective-permute-done | bytes 262176 | tf_op jit(solution)/shard_map/ppermute | solution.py:643
  53.8 1.8 %shard_map.260 = (bf16[2,64,1536]{2,1,0:T(8,128)(2,1)}, bf16[2,64,512]{2,1,0:T(8,128)(2,1)}) custom-call(bf16[1,64,2048]{2,1,0:T(8,128)(2,1)} %get-tuple-element.53.own, bf16[1,64,2048]{2,1,0:T(8,128)(2,1)S(1)} %shard_map.259.other), custom_call_target="tpu_custom_call" | custom-call | tf_op jit(solution)/shard_map/pallas_call | solution.py:620
  57.1 2.8 %collective-permute-start.7 = (bf16[2,64,512]{2,1,0:T(8,128)(2,1)}, bf16[2,64,512]{2,1,0:T(8,128)(2,1)S(1)}, u32[]{:S(2)}, u32[]{:S(2)}) collective-permute-start(bf16[2,64,512]{2,1,0:T(8,128)(2,1)} %get-tuple-element.54.out0), channel_id=1, source_target_pairs={{0,48},{16,0},{32,16},{48,32},{1,49},{17,1},{33,17},{49,33},{2,50}... | collective-permute-start | bytes 393224 | tf_op jit(solution)/shard_map/ppermute | solution.py:647
  61.1 8.4 %shard_map.258 = (bf16[16,32,512]{2,1,0:T(8,128)(2,1)}, bf16[32,2048]{1,0:T(8,128)(2,1)}, bf16[32,2048]{1,0:T(8,128)(2,1)}, bf16[32,2048]{1,0:T(8,128)(2,1)}, f3...) custom-call(s32[6]{0:T(128)S(1)} %stack.27.place, s32[1]{0:T(128)S(6)} %copy.43.length, ...), custom_call_target="tpu_custom_call" | custom-call | flops 19000000512 | tf_op jit(solution)/shard_map/pallas_call | solution.py:620
  69.6 8.0 %all-to-all-start.2 = ((bf16[16,32,512]{2,1,0:T(8,128)(2,1)}), bf16[16,32,512]{2,1,0:T(8,128)(2,1)}, u32[]{:S(2)}, u32[]{:S(2)}) async-start(bf16[16,32,512]{2,1,0:T(8,128)(2,1)} %shard_map.261.other), calls=%async_computation.2 | async-start | bytes 1048576 | tf_op jit(solution)/shard_map/all_to_all | solution.py:639
  77.8 1.6 constant_dynamic-update-slice_fusion.3
  80.2 3.2 %shard_map.262.other2.scaled = bf16[16,128,512]{2,1,0:T(8,128)(2,1)} custom-call(s32[6]{0:T(128)S(1)} %stack.27.place, bf16[8,176,512]{2,1,0:T(8,128)(2,1)S(1)} %shard_map.256.near, bf16[8,176,512]{2,1,0:T(8,128)(2,1)S(1)} %collective-permute-done.1.far, bf16[16,32,512]{2,1,0:T(8,128)(2,1)} %shard_map.261.other), custom_call_target="tpu_custom_call" | custom-call | tf_op jit(solution)/shard_map/pallas_call | solution.py:620
  83.4 5.5 %all-to-all-done.2.mixed = bf16[16,32,512]{2,1,0:T(8,128)(2,1)} async-done(((bf16[16,32,512]{2,1,0:T(8,128)(2,1)}), bf16[16,32,512]{2,1,0:T(8,128)(2,1)}, u32[]{:S(2)}, u32[]{:S(2)}) %all-to-all-start.2) | async-done | bytes 524320 | tf_op jit(solution)/shard_map/all_to_all | solution.py:639
  88.8 8.3 %shard_map.263 = (bf16[16,32,512]{2,1,0:T(8,128)(2,1)}, bf16[2,128,1024]{2,1,0:T(8,128)(2,1)}, bf16[2,128,1024]{2,1,0:T(8,128)(2,1)S(1)}, bf16[4,2,64,2048]{3,2,1,0:T(8,128)(2,1)}, f32[8,512]{1,0:T(8,128)}) custom-call(s32[6]{0:T(128)S(1)} %stack.27.place, s32[1]{0:T(128)S(6)} %copy.43.length, bf16[16,32,512]{2,1,0:T(8,128)(2,1)} %all-to-all-done.2.mixed, ...), custom_call_target="tpu_custom_call" | custom-call | tf_op jit(solution)/shard_map/pallas_call | solution.py:620
  97.9 1.4 collective-permute-start.8
  99.3 3.5 %all-to-all-start.3 = ((bf16[16,32,512]{2,1,0:T(8,128)(2,1)}), bf16[16,32,512]{2,1,0:T(8,128)(2,1)S(1)}, u32[]{:S(2)}, u32[]{:S(2)}) async-start(bf16[16,32,512]{2,1,0:T(8,128)(2,1)} %get-tuple-element.57), calls=%async_computation.3 | async-start | bytes 1048576 | tf_op jit(solution)/shard_map/all_to_all | solution.py:639
  102.8 2.0 %shard_map.265 = (bf16[128,1024]{1,0:T(8,128)(2,1)}, bf16[128,1024]{1,0:T(8,128)(2,1)}) custom-call(bf16[2,128,1024]{2,1,0:T(8,128)(2,1)} %get-tuple-element.65.kept, bf16[2,128,1024]{2,1,0:T(8,128)(2,1)S(1)} %collective-permute-done.8.arrived), custom_call_target="tpu_custom_call" | custom-call | tf_op jit(solution)/shard_map/pallas_call | solution.py:620
  104.8 2.8 %collective-permute-start.9 = (bf16[128,1024]{1,0:T(8,128)(2,1)}, bf16[128,1024]{1,0:T(8,128)(2,1)S(1)}, u32[]{:S(2)}, u32[]{:S(2)}) collective-permute-start(bf16[128,1024]{1,0:T(8,128)(2,1)} %get-tuple-element.67), channel_id=1, source_target_pairs={{0,2},{2,0},{1,3},{3,1},{4,6},{6,4},{5,7},{7,5},{8,10},{10,8},{9,1... | collective-permute-start | bytes 786440 | tf_op jit(solution)/shard_map/ppermute | solution.py:643
  107.6 6.3 %all-to-all-done.3.d_mixed = bf16[16,32,512]{2,1,0:T(8,128)(2,1)S(1)} async-done(((bf16[16,32,512]{2,1,0:T(8,128)(2,1)}), bf16[16,32,512]{2,1,0:T(8,128)(2,1)S(1)}, u32[]{:S(2)}, u32[]{:S(2)}) %all-to-all-start.3) | async-done | bytes 524320 | tf_op jit(solution)/shard_map/all_to_all | solution.py:639
  113.9 12.9 %shard_map.264 = (bf16[16,96,128]{2,1,0:T(8,128)(2,1)}, bf16[2,64,128]{2,1,0:T(8,128)(2,1)S(1)}, bf16[2,64,128]{2,1,0:T(8,128)(2,1)S(1)}, bf16[2,64,128]{2,1,0:T(8,128)(2,1)S(1)}, bf16[2,64,128]{2,1,0:T(8,128)(2,1)S(1)}) custom-call(s32[6]{0:T(128)S(1)} %stack.27.place, s32[1]{0:T(128)S(6)} %copy.43.length, bf16[16,32,512]{2,1,0:T(8,128)(2,1)S(1)} %all-to-all-done.3.d_mixed, ...), custom_call_target="tpu_custom_call" | custom-call | tf_op jit(solution)/shard_map/pallas_call | solution.py:620
  126.9 4.7 %all-to-all-start.4 = ((bf16[16,96,128]{2,1,0:T(8,128)(2,1)}), bf16[16,96,128]{2,1,0:T(8,128)(2,1)S(1)}, u32[]{:S(2)}, u32[]{:S(2)}) async-start(bf16[16,96,128]{2,1,0:T(8,128)(2,1)} %shard_map.266), calls=%async_computation.4 | async-start | bytes 786432 | tf_op jit(solution)/shard_map/all_to_all | solution.py:639
  132.9 1.4 collective-permute-start.11
  135.5 1.6 collective-permute-done.11.part2
  137.6 1.9 %shard_map.269.refs_0_ = bf16[32,4,2176]{2,1,0:T(4,128)(2,1)} custom-call(bf16[2,64,128]{2,1,0:T(8,128)(2,1)S(1)} %get-tuple-element.71.part0, bf16[2,64,128]{2,1,0:T(8,128)(2,1)S(1)} %collective-permute-done.10.part1, bf16[2,64,128]{2,1,0:T(8,128)(2,1)S(1)} %collective-permute-done.11.part2, bf16[2,64,128]{2,1,0:T(8,128)(2,1)S(1)} %collective-permute-done.12.part3, ...), custom_call_target="tpu_custom_call" | custom-call | tf_op jit(solution)/shard_map/pallas_call | solution.py:620
  139.5 2.2 %all-to-all-done.4.d_lin.refs_1_ = bf16[16,96,128]{2,1,0:T(8,128)(2,1)S(1)} async-done(((bf16[16,96,128]{2,1,0:T(8,128)(2,1)}), bf16[16,96,128]{2,1,0:T(8,128)(2,1)S(1)}, u32[]{:S(2)}, u32[]{:S(2)}) %all-to-all-start.4) | async-done | bytes 393248 | tf_op jit(solution)/shard_map/all_to_all | solution.py:639
  141.7 6.7 %all-to-all-start.5 = ((bf16[32,4,2176]{2,1,0:T(4,128)(2,1)}), bf16[32,4,2176]{2,1,0:T(4,128)(2,1)S(1)}, u32[]{:S(2)}, u32[]{:S(2)}) async-start(bf16[32,4,2176]{2,1,0:T(4,128)(2,1)} %shard_map.270), calls=%async_computation.6 | async-start | bytes 1114112 | tf_op jit(solution)/shard_map/all_to_all | solution.py:639
  148.4 3.0 %all-gather.7.cloned.1.call-done = bf16[8,64,1536]{2,1,0:T(8,128)(2,1)} async-done(((bf16[2,64,1536]{2,1,0:T(8,128)(2,1)}), bf16[8,64,1536]{2,1,0:T(8,128)(2,1)}) %all-gather.7.cloned.1.call-update) | async-done | bytes 1572880 | tf_op jit(solution)/shard_map/all_gather | solution.py:755
  151.5 4.5 %shard_map.268 = (f32[1,128,512]{2,1,0:T(8,128)}, bf16[1,128,512]{2,1,0:T(8,128)(2,1)}) custom-call(s32[6]{0:T(128)S(1)} %stack.27.place, s32[1]{0:T(128)S(6)} %copy.43.length, bf16[1,128,512]{2,1,0:T(8,128)(2,1)} %tokens.3, bf16[16,96,128]{2,1,0:T(8,128)(2,1)S(1)} %all-to-all-done.4.d_lin.refs_1_, bf16[4,2,64,1536]{3,2,1,0:T(8,128)(2,1)} %bitcast.12, ...), custom_call_target="tpu_custom_call" | custom-call | tf_op jit(solution)/shard_map/pallas_call | solution.py:620
  156.0 4.3 %all-to-all-done.5.parts = bf16[32,4,2176]{2,1,0:T(4,128)(2,1)S(1)} async-done(((bf16[32,4,2176]{2,1,0:T(4,128)(2,1)}), bf16[32,4,2176]{2,1,0:T(4,128)(2,1)S(1)}, u32[]{:S(2)}, u32[]{:S(2)}) %all-to-all-start.5) | async-done | bytes 557088 | tf_op jit(solution)/shard_map/all_to_all | solution.py:639
  (51 shorter events, 9.7 us)
Async XLA Ops:
  9.4 8.5 %copy-start.6 = (bf16[1,128,512]{2,1,0:T(8,128)(2,1)S(1)}, bf16[1,128,512]{2,1,0:T(8,128)(2,1)}, u32[]{:S(2)}) copy-start(bf16[1,128,512]{2,1,0:T(8,128)(2,1)} %param.29) | copy-start | bytes 393220
  9.4 29.7 %all-to-all-start = ((bf16[8,176,512]{2,1,0:T(8,128)(2,1)}), bf16[8,176,512]{2,1,0:T(8,128)(2,1)S(1)}, u32[]{:S(2)}, u32[]{:S(2)}) async-start(bf16[8,176,512]{2,1,0:T(8,128)(2,1)} %shard_map.255), calls=%async_computation | async-start | bytes 2883584 | tf_op jit(solution)/shard_map/all_to_all | solution.py:639
  17.9 21.2 %collective-permute-start = (bf16[1,128,512]{2,1,0:T(8,128)(2,1)S(1)}, bf16[1,128,512]{2,1,0:T(8,128)(2,1)S(1)}, u32[]{:S(2)}, u32[]{:S(2)}) collective-permute-start(bf16[1,128,512]{2,1,0:T(8,128)(2,1)S(1)} %copy-done.6), channel_id=1, source_target_pairs={{0,2},{2,0},{1,3},{3,1},{4,6},{6,4},{5,7},{7,5},{8,10},{10,8},{9,1... | collective-permute-start | bytes 393224 | tf_op jit(solution)/shard_map/ppermute | solution.py:643
  39.1 2.0 %copy-start = (bf16[2,128,512]{2,1,0:T(8,128)(2,1)}, bf16[2,128,512]{2,1,0:T(8,128)(2,1)S(1)}, u32[]{:S(2)}) copy-start(bf16[2,128,512]{2,1,0:T(8,128)(2,1)S(1)} %constant_dynamic-update-slice_fusion.refs_1_.cot_near) | copy-start | bytes 786436
  39.2 5.2 %collective-permute-start.1 = (bf16[8,176,512]{2,1,0:T(8,128)(2,1)S(1)}, bf16[8,176,512]{2,1,0:T(8,128)(2,1)S(1)}, u32[]{:S(2)}, u32[]{:S(2)}) collective-permute-start(bf16[8,176,512]{2,1,0:T(8,128)(2,1)S(1)} %shard_map.256.near), channel_id=1, source_target_pairs={{0,1},{1,0},{2,3},{3,2},{4,5},{5,4},{6,7},{7,6},{8,9},{9,8},{10,11... | collective-permute-start | bytes 4325384 | tf_op jit(solution)/shard_map/ppermute | solution.py:643
  41.1 3.2 %collective-permute-start.2 = (bf16[2,128,512]{2,1,0:T(8,128)(2,1)S(1)}, bf16[2,128,512]{2,1,0:T(8,128)(2,1)S(1)}, u32[]{:S(2)}, u32[]{:S(2)}) collective-permute-start(bf16[2,128,512]{2,1,0:T(8,128)(2,1)S(1)} %constant_dynamic-update-slice_fusion.refs_1_.cot_near), channel_id=1, source_target_pairs={{0,1},{1,0},{2,3},{3,2},{4,5},{5,4},{6,7},{7,6},{8,9},{9,8},{10,11... | collective-permute-start | bytes 786440 | tf_op jit(solution)/shard_map/ppermute | solution.py:643
  44.3 1.6 copy-start.1
  46.0 7.8 %collective-permute-start.4 = (bf16[1,64,2048]{2,1,0:T(8,128)(2,1)}, bf16[1,64,2048]{2,1,0:T(8,128)(2,1)S(1)}, u32[]{:S(2)}, u32[]{:S(2)}) collective-permute-start(bf16[1,64,2048]{2,1,0:T(8,128)(2,1)} %get-tuple-element.53.own), channel_id=1, source_target_pairs={{0,64},{64,0},{1,65},{65,1},{2,66},{66,2},{3,67},{67,3},{4,68},{68... | collective-permute-start | bytes 786440 | tf_op jit(solution)/shard_map/ppermute | solution.py:643
  46.8 14.4 %all-to-all-start.1 = ((bf16[8,64,128]{2,1,0:T(8,128)(2,1)}), bf16[8,64,128]{2,1,0:T(8,128)(2,1)}, u32[]{:S(2)}, u32[]{:S(2)}) async-start(bf16[8,64,128]{2,1,0:T(8,128)(2,1)} %get-tuple-element.50), calls=%async_computation.1 | async-start | bytes 262144 | tf_op jit(solution)/shard_map/all_to_all | solution.py:639
  51.2 37.6 %all-gather.5.cloned.1.call-start = ((), (), s32[]{:S(2)}) async-start(), calls=%async_computation.8 | async-start | bytes 1966080 | tf_op jit(solution)/shard_map/all_gather | solution.py:690
  56.3 13.3 %collective-permute-start.3 = (bf16[1,64,1536]{2,1,0:T(8,128)(2,1)}, bf16[1,64,1536]{2,1,0:T(8,128)(2,1)S(1)}, u32[]{:S(2)}, u32[]{:S(2)}) collective-permute-start(bf16[1,64,1536]{2,1,0:T(8,128)(2,1)} %get-tuple-element.52.refs_1_), channel_id=1, source_target_pairs={{0,64},{64,0},{1,65},{65,1},{2,66},{66,2},{3,67},{67,3},{4,68},{68... | collective-permute-start | bytes 589832 | tf_op jit(solution)/shard_map/ppermute | solution.py:643
  57.1 12.5 %collective-permute-start.7 = (bf16[2,64,512]{2,1,0:T(8,128)(2,1)}, bf16[2,64,512]{2,1,0:T(8,128)(2,1)S(1)}, u32[]{:S(2)}, u32[]{:S(2)}) collective-permute-start(bf16[2,64,512]{2,1,0:T(8,128)(2,1)} %get-tuple-element.54.out0), channel_id=1, source_target_pairs={{0,48},{16,0},{32,16},{48,32},{1,49},{17,1},{33,17},{49,33},{2,50}... | collective-permute-start | bytes 393224 | tf_op jit(solution)/shard_map/ppermute | solution.py:647
  59.8 9.7 %collective-permute-start.6 = (bf16[2,64,512]{2,1,0:T(8,128)(2,1)}, bf16[2,64,512]{2,1,0:T(8,128)(2,1)S(1)}, u32[]{:S(2)}, u32[]{:S(2)}) collective-permute-start(bf16[2,64,512]{2,1,0:T(8,128)(2,1)} %get-tuple-element.54.out0), channel_id=1, source_target_pairs={{0,32},{16,48},{32,0},{48,16},{1,33},{17,49},{33,1},{49,17},{2,34}... | collective-permute-start | bytes 393224 | tf_op jit(solution)/shard_map/ppermute | solution.py:647
  60.3 9.3 %collective-permute-start.5 = (bf16[2,64,512]{2,1,0:T(8,128)(2,1)}, bf16[2,64,512]{2,1,0:T(8,128)(2,1)S(1)}, u32[]{:S(2)}, u32[]{:S(2)}) collective-permute-start(bf16[2,64,512]{2,1,0:T(8,128)(2,1)} %get-tuple-element.54.out0), channel_id=1, source_target_pairs={{0,16},{16,32},{32,48},{48,0},{1,17},{17,33},{33,49},{49,1},{2,18}... | collective-permute-start | bytes 393224 | tf_op jit(solution)/shard_map/ppermute | solution.py:647
  69.6 10.6 %copy-start.3 = (bf16[2,64,512]{2,1,0:T(8,128)(2,1)}, bf16[2,64,512]{2,1,0:T(8,128)(2,1)S(1)}, u32[]{:S(2)}) copy-start(bf16[2,64,512]{2,1,0:T(8,128)(2,1)S(1)} %collective-permute-done.7.refs_4_.out3) | copy-start | bytes 393220
  69.6 10.6 %copy-start.4 = (bf16[2,64,512]{2,1,0:T(8,128)(2,1)}, bf16[2,64,512]{2,1,0:T(8,128)(2,1)S(1)}, u32[]{:S(2)}) copy-start(bf16[2,64,512]{2,1,0:T(8,128)(2,1)S(1)} %collective-permute-done.6.refs_3_.out2) | copy-start | bytes 393220
  69.6 10.6 %copy-start.5 = (bf16[2,64,512]{2,1,0:T(8,128)(2,1)}, bf16[2,64,512]{2,1,0:T(8,128)(2,1)S(1)}, u32[]{:S(2)}) copy-start(bf16[2,64,512]{2,1,0:T(8,128)(2,1)S(1)} %collective-permute-done.5.refs_2_.out1) | copy-start | bytes 393220
  69.6 19.2 %all-to-all-start.2 = ((bf16[16,32,512]{2,1,0:T(8,128)(2,1)}), bf16[16,32,512]{2,1,0:T(8,128)(2,1)}, u32[]{:S(2)}, u32[]{:S(2)}) async-start(bf16[16,32,512]{2,1,0:T(8,128)(2,1)} %shard_map.261.other), calls=%async_computation.2 | async-start | bytes 1048576 | tf_op jit(solution)/shard_map/all_to_all | solution.py:639
  77.6 60.0 %reduce-scatter.2.cloned.1.call-start = ((), (), s32[]{:S(2)}) async-start(), calls=%async_computation.7 | async-start | bytes 2621440 | tf_op jit(solution)/shard_map/reduce_scatter | solution.py:752
  97.2 54.3 %all-gather.7.cloned.1.call-start = ((), (), s32[]{:S(2)}) async-start(), calls=%async_computation.9 | async-start | bytes 1966080 | tf_op jit(solution)/shard_map/all_gather | solution.py:755
  97.9 4.9 %collective-permute-start.8 = (bf16[2,128,1024]{2,1,0:T(8,128)(2,1)S(1)}, bf16[2,128,1024]{2,1,0:T(8,128)(2,1)S(1)}, u32[]{:S(2)}, u32[]{:S(2)}) collective-permute-start(bf16[2,128,1024]{2,1,0:T(8,128)(2,1)S(1)} %get-tuple-element.66), channel_id=1, source_target_pairs={{0,1},{1,0},{2,3},{3,2},{4,5},{5,4},{6,7},{7,6},{8,9},{9,8},{10,11... | collective-permute-start | bytes 1572872 | tf_op jit(solution)/shard_map/ppermute | solution.py:643
  99.3 14.6 %all-to-all-start.3 = ((bf16[16,32,512]{2,1,0:T(8,128)(2,1)}), bf16[16,32,512]{2,1,0:T(8,128)(2,1)S(1)}, u32[]{:S(2)}, u32[]{:S(2)}) async-start(bf16[16,32,512]{2,1,0:T(8,128)(2,1)} %get-tuple-element.57), calls=%async_computation.3 | async-start | bytes 1048576 | tf_op jit(solution)/shard_map/all_to_all | solution.py:639
  104.8 22.0 %collective-permute-start.9 = (bf16[128,1024]{1,0:T(8,128)(2,1)}, bf16[128,1024]{1,0:T(8,128)(2,1)S(1)}, u32[]{:S(2)}, u32[]{:S(2)}) collective-permute-start(bf16[128,1024]{1,0:T(8,128)(2,1)} %get-tuple-element.67), channel_id=1, source_target_pairs={{0,2},{2,0},{1,3},{3,1},{4,6},{6,4},{5,7},{7,5},{8,10},{10,8},{9,1... | collective-permute-start | bytes 786440 | tf_op jit(solution)/shard_map/ppermute | solution.py:643
  126.8 14.9 %copy-start.2 = (bf16[128,1024]{1,0:T(8,128)(2,1)}, bf16[128,1024]{1,0:T(8,128)(2,1)S(1)}, u32[]{:S(2)}) copy-start(bf16[128,1024]{1,0:T(8,128)(2,1)S(1)} %collective-permute-done.9.refs_1_.w1) | copy-start | bytes 786436
  126.9 14.9 %all-to-all-start.4 = ((bf16[16,96,128]{2,1,0:T(8,128)(2,1)}), bf16[16,96,128]{2,1,0:T(8,128)(2,1)S(1)}, u32[]{:S(2)}, u32[]{:S(2)}) async-start(bf16[16,96,128]{2,1,0:T(8,128)(2,1)} %shard_map.266), calls=%async_computation.4 | async-start | bytes 786432 | tf_op jit(solution)/shard_map/all_to_all | solution.py:639
  131.6 4.0 %collective-permute-start.10 = (bf16[2,64,128]{2,1,0:T(8,128)(2,1)S(1)}, bf16[2,64,128]{2,1,0:T(8,128)(2,1)S(1)}, u32[]{:S(2)}, u32[]{:S(2)}) collective-permute-start(bf16[2,64,128]{2,1,0:T(8,128)(2,1)S(1)} %get-tuple-element.72), channel_id=1, source_target_pairs={{0,16},{16,32},{32,48},{48,0},{1,17},{17,33},{33,49},{49,1},{2,18}... | collective-permute-start | bytes 98312 | tf_op jit(solution)/shard_map/ppermute | solution.py:647
  132.9 4.3 %collective-permute-start.11 = (bf16[2,64,128]{2,1,0:T(8,128)(2,1)S(1)}, bf16[2,64,128]{2,1,0:T(8,128)(2,1)S(1)}, u32[]{:S(2)}, u32[]{:S(2)}) collective-permute-start(bf16[2,64,128]{2,1,0:T(8,128)(2,1)S(1)} %get-tuple-element.73), channel_id=1, source_target_pairs={{0,32},{16,48},{32,0},{48,16},{1,33},{17,49},{33,1},{49,17},{2,34}... | collective-permute-start | bytes 98312 | tf_op jit(solution)/shard_map/ppermute | solution.py:647
  134.3 3.3 %collective-permute-start.12 = (bf16[2,64,128]{2,1,0:T(8,128)(2,1)S(1)}, bf16[2,64,128]{2,1,0:T(8,128)(2,1)S(1)}, u32[]{:S(2)}, u32[]{:S(2)}) collective-permute-start(bf16[2,64,128]{2,1,0:T(8,128)(2,1)S(1)} %get-tuple-element.74), channel_id=1, source_target_pairs={{0,48},{16,0},{32,16},{48,32},{1,49},{17,1},{33,17},{49,33},{2,50}... | collective-permute-start | bytes 98312 | tf_op jit(solution)/shard_map/ppermute | solution.py:647
  141.7 18.6 %all-to-all-start.5 = ((bf16[32,4,2176]{2,1,0:T(4,128)(2,1)}), bf16[32,4,2176]{2,1,0:T(4,128)(2,1)S(1)}, u32[]{:S(2)}, u32[]{:S(2)}) async-start(bf16[32,4,2176]{2,1,0:T(4,128)(2,1)} %shard_map.270), calls=%async_computation.6 | async-start | bytes 1114112 | tf_op jit(solution)/shard_map/all_to_all | solution.py:639
Sparse Core Ops, SparseCore 0:
  55.7 27.1 all-gather.4
  97.3 26.0 reduce-scatter.1
  125.2 26.2 all-gather.6

commit v6 on v5

--- a/solution.py
+++ b/solution.py
@@ -522,13 +522,23 @@
     leaving.wait()
 
 
-def regroup_kernel(part0, part1, part2, part3, feed, sent):
+def regroup_kernel(feed, sent):
+    total = feed[...].astype(f32)
+    for d in range(SEQ * 2):
+        sent[d, :, :FEED_LANES] = total[4 * d : 4 * d + 4].astype(bf16)
+        sent[d, :, FEED_LANES:] = jnp.zeros((4, 128), bf16)
+
+
+def append_kernel(part0, part1, part2, part3, given, sent, rows, left):
     heads = part0[...].astype(f32)
     for part in (part1, part2, part3):
         heads = heads + part[...].astype(f32)
-    total = jnp.concatenate([feed[...].astype(f32), heads.reshape(128, 128)], 1)
+    heads = heads.reshape(128, 128)
     for d in range(SEQ * 2):
-        sent[d] = total[4 * d : 4 * d + 4].astype(bf16)
+        rows[d] = heads[4 * d : 4 * d + 4].astype(bf16)
+    copy = pltpu.make_async_copy(rows, sent.at[:, :, FEED_LANES:], left.at[0])
+    copy.start()
+    copy.wait()
 
 
 def input_grad_kernel(
@@ -599,7 +609,7 @@
         grad[...] = jnp.sum(column, 0)[0:4]
 
 
-def call(kernel, ins, outs, scratch=(), vmem=8, flops=0):
+def call(kernel, ins, outs, scratch=(), vmem=8, flops=0, aliases={}):
     places = {"V": pltpu.VMEM, "U": pltpu.VMEM, "H": pltpu.VMEM, "A": pl.ANY, "P": pl.ANY, "S": pltpu.SMEM}
     inner = pl.pallas_call(
         kernel,
@@ -611,6 +621,7 @@
         scratch_shapes=[
             pltpu.SemaphoreType.DMA((s,)) if isinstance(s, int) else pltpu.VMEM(*s) for s in scratch
         ],
+        input_output_aliases=aliases,
         compiler_params=pltpu.CompilerParams(vmem_limit_bytes=vmem * 2**20),
         cost_estimate=pl.CostEstimate(flops=flops, bytes_accessed=0, transcendentals=0),
     )
@@ -749,10 +760,10 @@
         *out_rows,
     )
     d_mixed = exchange(d_sent, WINDOW)
+    row_weights = lax.all_gather(after(whole, in_hbm(norm_rows)), "x")
     feed_grads = lax.psum_scatter(
         grads.reshape(D, FEED_LANES), "x", scatter_dimension=0, tiled=True
     )
-    row_weights = lax.all_gather(after(whole, pltpu.with_memory_space_constraint(norm_rows, pltpu.HBM)), "x")
     w0, w1 = call(
         add_kernel, "HV", [((ROWS, 2 * D), bf16, "H")] * 2
     )(kept, swap(swapped, "core"))
@@ -783,11 +794,14 @@
     lin_sent = after(lin_sent, w1)
     back = exchange(lin_sent, WINDOW)
     head_grads = [head_grads[0]] + [shift(head_grads[step], step) for step in range(1, 4)]
+    (grad_sent,) = call(regroup_kernel, "H", [((2 * SEQ, 4, GRAD_LANES), bf16, "H")])(feed_grads)
     (grad_sent,) = call(
-        regroup_kernel,
-        "UUUUH",
-        [((2 * SEQ, 4, GRAD_LANES), bf16, "H")],
-    )(*head_grads, feed_grads)
+        append_kernel,
+        "UUUUA",
+        [((2 * SEQ, 4, GRAD_LANES), bf16, "A")],
+        [((2 * SEQ, 4, 128), bf16), 1],
+        aliases={4: 0},
+    )(*head_grads, grad_sent)
     grad_parts = exchange(after(grad_sent, back), SLICE)
 
     grad_tokens, layer_output = call(

time: 169 us -> 168 us (level)
    ppermute x6, waiting for transfers between devices: 2.23 us -> 0.27 us  [shift(): return lax.ppermute(value, 'x', [(i, (i + by) % 4) for i in range(4)])]
    pallas_call x11 -> x12, Pallas kernels: 48.1 us -> 48.8 us  [run(): inner(*(pltpu.with_memory_space_constraint(x, pltpu.HBM if where in 'HA'...]
  transfers between devices with their start and end apart: 22 -> 22, of which waited for: 11 -> 9; matrix products, arithmetic and copies ran while one was open for 1% -> 1% of each run, Pallas kernels for 21% -> 21%
where the time goes in v6:
time: 168 us; the launch traced here: 167 us
  starting transfers between devices  54.1 us (32%)
  Pallas kernels  48.8 us (29%)
  waiting for transfers between devices  46.7 us (28%)
  between operations  14.7 us (9%)
  local copies, waits for them, and re-layouts  2.48 us (1%)
    pallas_call x12, Pallas kernels, run(): inner(*(pltpu.with_memory_space_constraint(x, pltpu.HBM if where in 'HA'...  48.8 us
    all_to_all x6, starting transfers between devices, exchange(): return lax.all_to_all(value, axes, 0, 0, tiled=True)  34.6 us
    ppermute x7, waiting for transfers between devices, swap(): return lax.ppermute(value, axis, [(0, 1), (1, 0)])  23.3 us
    all_to_all x6, waiting for transfers between devices, exchange(): return lax.all_to_all(value, axes, 0, 0, tiled=True)  18.2 us
    ppermute x7, starting transfers between devices, swap(): return lax.ppermute(value, axis, [(0, 1), (1, 0)])  11.4 us
    ppermute x6, starting transfers between devices, shift(): return lax.ppermute(value, 'x', [(i, (i + by) % 4) for i in range(4)])  7.88 us
    all_gather x1, waiting for transfers between devices, shards(): row_weights = lax.all_gather(after(whole, in_hbm(norm_rows)), 'x')  4.24 us
  transfers between devices with their start and end apart: 22, of which 9 were waited for; matrix products, arithmetic and copies ran while one was open for 1% of the time, Pallas kernels for 21%

profile of v6, /device:TPU:1, one launch (start us, length us, event | category | flops | bytes accessed | tf_op | source)
XLA Modules:
  0.0 166.8 jit_solution(8713562517463105054)
XLA Ops:
  7.2 2.2 %shard_map.255 = bf16[8,176,512]{2,1,0:T(8,128)(2,1)} custom-call(bf16[1,128,512]{2,1,0:T(8,128)(2,1)} %tokens.3, bf16[4,512]{1,0:T(4,128)(2,1)} %w_query.1, bf16[4,512]{1,0:T(4,128)(2,1)} %w_key.1, bf16[4,512]{1,0:T(4,128)(2,1)} %w_value.1, bf16[4,512]{1,0:T(4,128)(2,1)} %w_output.1, bf16[4,2048]{1,0:T(4,128)(2,1)} %w_gate.1, bf16[4,2048]{1,0:T(4,128)(2,1)} %w_up.1, ...), custom_call_target="tpu_custom_call" | custom-call | tf_op jit(solution)/shard_map/pallas_call | solution.py:631
  9.4 8.5 %all-to-all-start = ((bf16[8,176,512]{2,1,0:T(8,128)(2,1)}), bf16[8,176,512]{2,1,0:T(8,128)(2,1)S(1)}, u32[]{:S(2)}, u32[]{:S(2)}) async-start(bf16[8,176,512]{2,1,0:T(8,128)(2,1)} %shard_map.255), calls=%async_computation | async-start | bytes 2883584 | tf_op jit(solution)/shard_map/all_to_all | solution.py:650
  17.9 3.0 %collective-permute-start = (bf16[1,128,512]{2,1,0:T(8,128)(2,1)S(1)}, bf16[1,128,512]{2,1,0:T(8,128)(2,1)S(1)}, u32[]{:S(2)}, u32[]{:S(2)}) collective-permute-start(bf16[1,128,512]{2,1,0:T(8,128)(2,1)S(1)} %copy-done.6), channel_id=1, source_target_pairs={{0,2},{2,0},{1,3},{3,1},{4,6},{6,4},{5,7},{7,5},{8,10},{10,8},{9,1... | collective-permute-start | bytes 393224 | tf_op jit(solution)/shard_map/ppermute | solution.py:654
  20.9 18.2 %collective-permute-done = bf16[1,128,512]{2,1,0:T(8,128)(2,1)S(1)} collective-permute-done((bf16[1,128,512]{2,1,0:T(8,128)(2,1)S(1)}, bf16[1,128,512]{2,1,0:T(8,128)(2,1)S(1)}, u32[]{:S(2)}, u32[]{:S(2)}) %collective-permute-start) | collective-permute-done | bytes 131104 | tf_op jit(solution)/shard_map/ppermute | solution.py:654
  39.2 1.9 %collective-permute-start.1 = (bf16[8,176,512]{2,1,0:T(8,128)(2,1)S(1)}, bf16[8,176,512]{2,1,0:T(8,128)(2,1)S(1)}, u32[]{:S(2)}, u32[]{:S(2)}) collective-permute-start(bf16[8,176,512]{2,1,0:T(8,128)(2,1)S(1)} %shard_map.256.near), channel_id=1, source_target_pairs={{0,1},{1,0},{2,3},{3,2},{4,5},{5,4},{6,7},{7,6},{8,9},{9,8},{10,11... | collective-permute-start | bytes 4325384 | tf_op jit(solution)/shard_map/ppermute | solution.py:654
  41.8 2.5 %collective-permute-done.2.cot.cot_far = bf16[2,128,512]{2,1,0:T(8,128)(2,1)S(1)} collective-permute-done((bf16[2,128,512]{2,1,0:T(8,128)(2,1)S(1)}, bf16[2,128,512]{2,1,0:T(8,128)(2,1)S(1)}, u32[]{:S(2)}, u32[]{:S(2)}) %collective-permute-start.2) | collective-permute-done | bytes 262176 | tf_op jit(solution)/shard_map/ppermute | solution.py:654
  44.3 1.6 shard_map.257
  46.8 4.5 %all-to-all-start.1 = ((bf16[8,64,128]{2,1,0:T(8,128)(2,1)}), bf16[8,64,128]{2,1,0:T(8,128)(2,1)}, u32[]{:S(2)}, u32[]{:S(2)}) async-start(bf16[8,64,128]{2,1,0:T(8,128)(2,1)} %get-tuple-element.50), calls=%async_computation.1 | async-start | bytes 262144 | tf_op jit(solution)/shard_map/all_to_all | solution.py:650
  51.3 2.5 %collective-permute-done.4.refs_0_ = bf16[1,64,2048]{2,1,0:T(8,128)(2,1)S(1)} collective-permute-done((bf16[1,64,2048]{2,1,0:T(8,128)(2,1)}, bf16[1,64,2048]{2,1,0:T(8,128)(2,1)S(1)}, u32[]{:S(2)}, u32[]{:S(2)}) %collective-permute-start.4) | collective-permute-done | bytes 262176 | tf_op jit(solution)/shard_map/ppermute | solution.py:654
  53.8 1.8 %shard_map.260 = (bf16[2,64,1536]{2,1,0:T(8,128)(2,1)}, bf16[2,64,512]{2,1,0:T(8,128)(2,1)}) custom-call(bf16[1,64,2048]{2,1,0:T(8,128)(2,1)} %get-tuple-element.53.own, bf16[1,64,2048]{2,1,0:T(8,128)(2,1)S(1)} %shard_map.259.other), custom_call_target="tpu_custom_call" | custom-call | tf_op jit(solution)/shard_map/pallas_call | solution.py:631
  57.1 2.8 %collective-permute-start.7 = (bf16[2,64,512]{2,1,0:T(8,128)(2,1)}, bf16[2,64,512]{2,1,0:T(8,128)(2,1)S(1)}, u32[]{:S(2)}, u32[]{:S(2)}) collective-permute-start(bf16[2,64,512]{2,1,0:T(8,128)(2,1)} %get-tuple-element.54.out0), channel_id=1, source_target_pairs={{0,48},{16,0},{32,16},{48,32},{1,49},{17,1},{33,17},{49,33},{2,50}... | collective-permute-start | bytes 393224 | tf_op jit(solution)/shard_map/ppermute | solution.py:658
  61.1 8.4 %shard_map.258 = (bf16[16,32,512]{2,1,0:T(8,128)(2,1)}, bf16[32,2048]{1,0:T(8,128)(2,1)}, bf16[32,2048]{1,0:T(8,128)(2,1)}, bf16[32,2048]{1,0:T(8,128)(2,1)}, f3...) custom-call(s32[6]{0:T(128)S(1)} %stack.27.place, s32[1]{0:T(128)S(6)} %copy.45.length, ...), custom_call_target="tpu_custom_call" | custom-call | flops 19000000512 | tf_op jit(solution)/shard_map/pallas_call | solution.py:631
  69.6 8.0 %all-to-all-start.2 = ((bf16[16,32,512]{2,1,0:T(8,128)(2,1)}), bf16[16,32,512]{2,1,0:T(8,128)(2,1)}, u32[]{:S(2)}, u32[]{:S(2)}) async-start(bf16[16,32,512]{2,1,0:T(8,128)(2,1)} %shard_map.261.other), calls=%async_computation.2 | async-start | bytes 1048576 | tf_op jit(solution)/shard_map/all_to_all | solution.py:650
  77.8 1.6 constant_dynamic-update-slice_fusion.3
  80.2 3.2 %shard_map.262.other2.scaled = bf16[16,128,512]{2,1,0:T(8,128)(2,1)} custom-call(s32[6]{0:T(128)S(1)} %stack.27.place, bf16[8,176,512]{2,1,0:T(8,128)(2,1)S(1)} %shard_map.256.near, bf16[8,176,512]{2,1,0:T(8,128)(2,1)S(1)} %collective-permute-done.1.far, bf16[16,32,512]{2,1,0:T(8,128)(2,1)} %shard_map.261.other), custom_call_target="tpu_custom_call" | custom-call | tf_op jit(solution)/shard_map/pallas_call | solution.py:631
  83.4 5.5 %all-to-all-done.2.mixed = bf16[16,32,512]{2,1,0:T(8,128)(2,1)} async-done(((bf16[16,32,512]{2,1,0:T(8,128)(2,1)}), bf16[16,32,512]{2,1,0:T(8,128)(2,1)}, u32[]{:S(2)}, u32[]{:S(2)}) %all-to-all-start.2) | async-done | bytes 524320 | tf_op jit(solution)/shard_map/all_to_all | solution.py:650
  88.8 8.3 %shard_map.263 = (bf16[16,32,512]{2,1,0:T(8,128)(2,1)}, bf16[2,128,1024]{2,1,0:T(8,128)(2,1)}, bf16[2,128,1024]{2,1,0:T(8,128)(2,1)S(1)}, bf16[4,2,64,2048]{3,2,1,0:T(8,128)(2,1)}, f32[8,512]{1,0:T(8,128)}) custom-call(s32[6]{0:T(128)S(1)} %stack.27.place, s32[1]{0:T(128)S(6)} %copy.45.length, bf16[16,32,512]{2,1,0:T(8,128)(2,1)} %all-to-all-done.2.mixed, ...), custom_call_target="tpu_custom_call" | custom-call | tf_op jit(solution)/shard_map/pallas_call | solution.py:631
  97.9 1.4 collective-permute-start.8
  99.3 3.5 %all-to-all-start.3 = ((bf16[16,32,512]{2,1,0:T(8,128)(2,1)}), bf16[16,32,512]{2,1,0:T(8,128)(2,1)S(1)}, u32[]{:S(2)}, u32[]{:S(2)}) async-start(bf16[16,32,512]{2,1,0:T(8,128)(2,1)} %get-tuple-element.57), calls=%async_computation.3 | async-start | bytes 1048576 | tf_op jit(solution)/shard_map/all_to_all | solution.py:650
  102.8 2.0 %shard_map.265 = (bf16[128,1024]{1,0:T(8,128)(2,1)}, bf16[128,1024]{1,0:T(8,128)(2,1)}) custom-call(bf16[2,128,1024]{2,1,0:T(8,128)(2,1)} %get-tuple-element.65.kept, bf16[2,128,1024]{2,1,0:T(8,128)(2,1)S(1)} %collective-permute-done.8.arrived), custom_call_target="tpu_custom_call" | custom-call | tf_op jit(solution)/shard_map/pallas_call | solution.py:631
  104.8 2.8 %collective-permute-start.9 = (bf16[128,1024]{1,0:T(8,128)(2,1)}, bf16[128,1024]{1,0:T(8,128)(2,1)S(1)}, u32[]{:S(2)}, u32[]{:S(2)}) collective-permute-start(bf16[128,1024]{1,0:T(8,128)(2,1)} %get-tuple-element.67), channel_id=1, source_target_pairs={{0,2},{2,0},{1,3},{3,1},{4,6},{6,4},{5,7},{7,5},{8,10},{10,8},{9,1... | collective-permute-start | bytes 786440 | tf_op jit(solution)/shard_map/ppermute | solution.py:654
  107.6 6.3 %all-to-all-done.3.d_mixed = bf16[16,32,512]{2,1,0:T(8,128)(2,1)S(1)} async-done(((bf16[16,32,512]{2,1,0:T(8,128)(2,1)}), bf16[16,32,512]{2,1,0:T(8,128)(2,1)S(1)}, u32[]{:S(2)}, u32[]{:S(2)}) %all-to-all-start.3) | async-done | bytes 524320 | tf_op jit(solution)/shard_map/all_to_all | solution.py:650
  113.9 12.9 %shard_map.264 = (bf16[16,96,128]{2,1,0:T(8,128)(2,1)}, bf16[2,64,128]{2,1,0:T(8,128)(2,1)S(1)}, bf16[2,64,128]{2,1,0:T(8,128)(2,1)S(1)}, bf16[2,64,128]{2,1,0:T(8,128)(2,1)S(1)}, bf16[2,64,128]{2,1,0:T(8,128)(2,1)S(1)}) custom-call(s32[6]{0:T(128)S(1)} %stack.27.place, s32[1]{0:T(128)S(6)} %copy.45.length, bf16[16,32,512]{2,1,0:T(8,128)(2,1)S(1)} %all-to-all-done.3.d_mixed, ...), custom_call_target="tpu_custom_call" | custom-call | tf_op jit(solution)/shard_map/pallas_call | solution.py:631
  126.9 4.7 %all-to-all-start.4 = ((bf16[16,96,128]{2,1,0:T(8,128)(2,1)}), bf16[16,96,128]{2,1,0:T(8,128)(2,1)S(1)}, u32[]{:S(2)}, u32[]{:S(2)}) async-start(bf16[16,96,128]{2,1,0:T(8,128)(2,1)} %shard_map.266), calls=%async_computation.4 | async-start | bytes 786432 | tf_op jit(solution)/shard_map/all_to_all | solution.py:650
  131.6 1.3 collective-permute-start.10
  132.9 1.4 collective-permute-start.11
  135.4 2.0 %shard_map.269.given = bf16[32,4,2176]{2,1,0:T(4,128)(2,1)} custom-call(bf16[128,2048]{1,0:T(8,128)(2,1)} %reduce-scatter.2.cloned.1.call-done.feed), custom_call_target="tpu_custom_call" | custom-call | tf_op jit(solution)/shard_map/pallas_call | solution.py:631
  138.3 3.4 %all-to-all-done.4.d_lin.refs_1_ = bf16[16,96,128]{2,1,0:T(8,128)(2,1)S(1)} async-done(((bf16[16,96,128]{2,1,0:T(8,128)(2,1)}), bf16[16,96,128]{2,1,0:T(8,128)(2,1)S(1)}, u32[]{:S(2)}, u32[]{:S(2)}) %all-to-all-start.4) | async-done | bytes 393248 | tf_op jit(solution)/shard_map/all_to_all | solution.py:650
  141.7 5.5 %all-to-all-start.5 = ((bf16[32,4,2176]{2,1,0:T(4,128)(2,1)}), bf16[32,4,2176]{2,1,0:T(4,128)(2,1)S(1)}, u32[]{:S(2)}, u32[]{:S(2)}) async-start(bf16[32,4,2176]{2,1,0:T(4,128)(2,1)} %shard_map.271), calls=%async_computation.6 | async-start | bytes 1114112 | tf_op jit(solution)/shard_map/all_to_all | solution.py:650
  147.2 4.2 %all-gather.7.cloned.1.call-done = bf16[8,64,1536]{2,1,0:T(8,128)(2,1)} async-done(((bf16[2,64,1536]{2,1,0:T(8,128)(2,1)}), bf16[8,64,1536]{2,1,0:T(8,128)(2,1)}) %all-gather.7.cloned.1.call-update) | async-done | bytes 1572880 | tf_op jit(solution)/shard_map/all_gather | solution.py:763
  151.5 4.5 %shard_map.268 = (f32[1,128,512]{2,1,0:T(8,128)}, bf16[1,128,512]{2,1,0:T(8,128)(2,1)}) custom-call(s32[6]{0:T(128)S(1)} %stack.27.place, s32[1]{0:T(128)S(6)} %copy.45.length, bf16[1,128,512]{2,1,0:T(8,128)(2,1)} %tokens.3, bf16[16,96,128]{2,1,0:T(8,128)(2,1)S(1)} %all-to-all-done.4.d_lin.refs_1_, bf16[4,2,64,1536]{3,2,1,0:T(8,128)(2,1)} %bitcast.12, ...), custom_call_target="tpu_custom_call" | custom-call | tf_op jit(solution)/shard_map/pallas_call | solution.py:631
  156.0 3.0 %all-to-all-done.5.parts = bf16[32,4,2176]{2,1,0:T(4,128)(2,1)S(1)} async-done(((bf16[32,4,2176]{2,1,0:T(4,128)(2,1)}), bf16[32,4,2176]{2,1,0:T(4,128)(2,1)S(1)}, u32[]{:S(2)}, u32[]{:S(2)}) %all-to-all-start.5) | async-done | bytes 557088 | tf_op jit(solution)/shard_map/all_to_all | solution.py:650
  (52 shorter events, 8.6 us)
Async XLA Ops:
  9.4 8.5 %copy-start.6 = (bf16[1,128,512]{2,1,0:T(8,128)(2,1)S(1)}, bf16[1,128,512]{2,1,0:T(8,128)(2,1)}, u32[]{:S(2)}) copy-start(bf16[1,128,512]{2,1,0:T(8,128)(2,1)} %param.29) | copy-start | bytes 393220
  9.4 29.7 %all-to-all-start = ((bf16[8,176,512]{2,1,0:T(8,128)(2,1)}), bf16[8,176,512]{2,1,0:T(8,128)(2,1)S(1)}, u32[]{:S(2)}, u32[]{:S(2)}) async-start(bf16[8,176,512]{2,1,0:T(8,128)(2,1)} %shard_map.255), calls=%async_computation | async-start | bytes 2883584 | tf_op jit(solution)/shard_map/all_to_all | solution.py:650
  17.9 21.2 %collective-permute-start = (bf16[1,128,512]{2,1,0:T(8,128)(2,1)S(1)}, bf16[1,128,512]{2,1,0:T(8,128)(2,1)S(1)}, u32[]{:S(2)}, u32[]{:S(2)}) collective-permute-start(bf16[1,128,512]{2,1,0:T(8,128)(2,1)S(1)} %copy-done.6), channel_id=1, source_target_pairs={{0,2},{2,0},{1,3},{3,1},{4,6},{6,4},{5,7},{7,5},{8,10},{10,8},{9,1... | collective-permute-start | bytes 393224 | tf_op jit(solution)/shard_map/ppermute | solution.py:654
  39.1 2.0 %copy-start = (bf16[2,128,512]{2,1,0:T(8,128)(2,1)}, bf16[2,128,512]{2,1,0:T(8,128)(2,1)S(1)}, u32[]{:S(2)}) copy-start(bf16[2,128,512]{2,1,0:T(8,128)(2,1)S(1)} %constant_dynamic-update-slice_fusion.refs_1_.cot_near) | copy-start | bytes 786436
  39.2 5.2 %collective-permute-start.1 = (bf16[8,176,512]{2,1,0:T(8,128)(2,1)S(1)}, bf16[8,176,512]{2,1,0:T(8,128)(2,1)S(1)}, u32[]{:S(2)}, u32[]{:S(2)}) collective-permute-start(bf16[8,176,512]{2,1,0:T(8,128)(2,1)S(1)} %shard_map.256.near), channel_id=1, source_target_pairs={{0,1},{1,0},{2,3},{3,2},{4,5},{5,4},{6,7},{7,6},{8,9},{9,8},{10,11... | collective-permute-start | bytes 4325384 | tf_op jit(solution)/shard_map/ppermute | solution.py:654
  41.1 3.2 %collective-permute-start.2 = (bf16[2,128,512]{2,1,0:T(8,128)(2,1)S(1)}, bf16[2,128,512]{2,1,0:T(8,128)(2,1)S(1)}, u32[]{:S(2)}, u32[]{:S(2)}) collective-permute-start(bf16[2,128,512]{2,1,0:T(8,128)(2,1)S(1)} %constant_dynamic-update-slice_fusion.refs_1_.cot_near), channel_id=1, source_target_pairs={{0,1},{1,0},{2,3},{3,2},{4,5},{5,4},{6,7},{7,6},{8,9},{9,8},{10,11... | collective-permute-start | bytes 786440 | tf_op jit(solution)/shard_map/ppermute | solution.py:654
  44.3 1.6 copy-start.1
  46.0 7.8 %collective-permute-start.4 = (bf16[1,64,2048]{2,1,0:T(8,128)(2,1)}, bf16[1,64,2048]{2,1,0:T(8,128)(2,1)S(1)}, u32[]{:S(2)}, u32[]{:S(2)}) collective-permute-start(bf16[1,64,2048]{2,1,0:T(8,128)(2,1)} %get-tuple-element.53.own), channel_id=1, source_target_pairs={{0,64},{64,0},{1,65},{65,1},{2,66},{66,2},{3,67},{67,3},{4,68},{68... | collective-permute-start | bytes 786440 | tf_op jit(solution)/shard_map/ppermute | solution.py:654
  46.8 14.4 %all-to-all-start.1 = ((bf16[8,64,128]{2,1,0:T(8,128)(2,1)}), bf16[8,64,128]{2,1,0:T(8,128)(2,1)}, u32[]{:S(2)}, u32[]{:S(2)}) async-start(bf16[8,64,128]{2,1,0:T(8,128)(2,1)} %get-tuple-element.50), calls=%async_computation.1 | async-start | bytes 262144 | tf_op jit(solution)/shard_map/all_to_all | solution.py:650
  51.2 37.6 %all-gather.5.cloned.1.call-start = ((), (), s32[]{:S(2)}) async-start(), calls=%async_computation.8 | async-start | bytes 1966080 | tf_op jit(solution)/shard_map/all_gather | solution.py:701
  56.3 13.3 %collective-permute-start.3 = (bf16[1,64,1536]{2,1,0:T(8,128)(2,1)}, bf16[1,64,1536]{2,1,0:T(8,128)(2,1)S(1)}, u32[]{:S(2)}, u32[]{:S(2)}) collective-permute-start(bf16[1,64,1536]{2,1,0:T(8,128)(2,1)} %get-tuple-element.52.refs_1_), channel_id=1, source_target_pairs={{0,64},{64,0},{1,65},{65,1},{2,66},{66,2},{3,67},{67,3},{4,68},{68... | collective-permute-start | bytes 589832 | tf_op jit(solution)/shard_map/ppermute | solution.py:654
  57.1 12.5 %collective-permute-start.7 = (bf16[2,64,512]{2,1,0:T(8,128)(2,1)}, bf16[2,64,512]{2,1,0:T(8,128)(2,1)S(1)}, u32[]{:S(2)}, u32[]{:S(2)}) collective-permute-start(bf16[2,64,512]{2,1,0:T(8,128)(2,1)} %get-tuple-element.54.out0), channel_id=1, source_target_pairs={{0,48},{16,0},{32,16},{48,32},{1,49},{17,1},{33,17},{49,33},{2,50}... | collective-permute-start | bytes 393224 | tf_op jit(solution)/shard_map/ppermute | solution.py:658
  59.8 9.7 %collective-permute-start.6 = (bf16[2,64,512]{2,1,0:T(8,128)(2,1)}, bf16[2,64,512]{2,1,0:T(8,128)(2,1)S(1)}, u32[]{:S(2)}, u32[]{:S(2)}) collective-permute-start(bf16[2,64,512]{2,1,0:T(8,128)(2,1)} %get-tuple-element.54.out0), channel_id=1, source_target_pairs={{0,32},{16,48},{32,0},{48,16},{1,33},{17,49},{33,1},{49,17},{2,34}... | collective-permute-start | bytes 393224 | tf_op jit(solution)/shard_map/ppermute | solution.py:658
  60.3 9.3 %collective-permute-start.5 = (bf16[2,64,512]{2,1,0:T(8,128)(2,1)}, bf16[2,64,512]{2,1,0:T(8,128)(2,1)S(1)}, u32[]{:S(2)}, u32[]{:S(2)}) collective-permute-start(bf16[2,64,512]{2,1,0:T(8,128)(2,1)} %get-tuple-element.54.out0), channel_id=1, source_target_pairs={{0,16},{16,32},{32,48},{48,0},{1,17},{17,33},{33,49},{49,1},{2,18}... | collective-permute-start | bytes 393224 | tf_op jit(solution)/shard_map/ppermute | solution.py:658
  69.6 10.6 %copy-start.3 = (bf16[2,64,512]{2,1,0:T(8,128)(2,1)}, bf16[2,64,512]{2,1,0:T(8,128)(2,1)S(1)}, u32[]{:S(2)}) copy-start(bf16[2,64,512]{2,1,0:T(8,128)(2,1)S(1)} %collective-permute-done.7.refs_4_.out3) | copy-start | bytes 393220
  69.6 10.6 %copy-start.4 = (bf16[2,64,512]{2,1,0:T(8,128)(2,1)}, bf16[2,64,512]{2,1,0:T(8,128)(2,1)S(1)}, u32[]{:S(2)}) copy-start(bf16[2,64,512]{2,1,0:T(8,128)(2,1)S(1)} %collective-permute-done.6.refs_3_.out2) | copy-start | bytes 393220
  69.6 10.6 %copy-start.5 = (bf16[2,64,512]{2,1,0:T(8,128)(2,1)}, bf16[2,64,512]{2,1,0:T(8,128)(2,1)S(1)}, u32[]{:S(2)}) copy-start(bf16[2,64,512]{2,1,0:T(8,128)(2,1)S(1)} %collective-permute-done.5.refs_2_.out1) | copy-start | bytes 393220
  69.6 19.2 %all-to-all-start.2 = ((bf16[16,32,512]{2,1,0:T(8,128)(2,1)}), bf16[16,32,512]{2,1,0:T(8,128)(2,1)}, u32[]{:S(2)}, u32[]{:S(2)}) async-start(bf16[16,32,512]{2,1,0:T(8,128)(2,1)} %shard_map.261.other), calls=%async_computation.2 | async-start | bytes 1048576 | tf_op jit(solution)/shard_map/all_to_all | solution.py:650
  77.6 57.8 %reduce-scatter.2.cloned.1.call-start = ((), (), s32[]{:S(2)}) async-start(), calls=%async_computation.7 | async-start | bytes 2621440 | tf_op jit(solution)/shard_map/reduce_scatter | solution.py:764
  97.2 54.3 %all-gather.7.cloned.1.call-start = ((), (), s32[]{:S(2)}) async-start(), calls=%async_computation.9 | async-start | bytes 1966080 | tf_op jit(solution)/shard_map/all_gather | solution.py:763
  97.9 4.9 %collective-permute-start.8 = (bf16[2,128,1024]{2,1,0:T(8,128)(2,1)S(1)}, bf16[2,128,1024]{2,1,0:T(8,128)(2,1)S(1)}, u32[]{:S(2)}, u32[]{:S(2)}) collective-permute-start(bf16[2,128,1024]{2,1,0:T(8,128)(2,1)S(1)} %get-tuple-element.66), channel_id=1, source_target_pairs={{0,1},{1,0},{2,3},{3,2},{4,5},{5,4},{6,7},{7,6},{8,9},{9,8},{10,11... | collective-permute-start | bytes 1572872 | tf_op jit(solution)/shard_map/ppermute | solution.py:654
  99.3 14.6 %all-to-all-start.3 = ((bf16[16,32,512]{2,1,0:T(8,128)(2,1)}), bf16[16,32,512]{2,1,0:T(8,128)(2,1)S(1)}, u32[]{:S(2)}, u32[]{:S(2)}) async-start(bf16[16,32,512]{2,1,0:T(8,128)(2,1)} %get-tuple-element.57), calls=%async_computation.3 | async-start | bytes 1048576 | tf_op jit(solution)/shard_map/all_to_all | solution.py:650
  104.8 22.0 %collective-permute-start.9 = (bf16[128,1024]{1,0:T(8,128)(2,1)}, bf16[128,1024]{1,0:T(8,128)(2,1)S(1)}, u32[]{:S(2)}, u32[]{:S(2)}) collective-permute-start(bf16[128,1024]{1,0:T(8,128)(2,1)} %get-tuple-element.67), channel_id=1, source_target_pairs={{0,2},{2,0},{1,3},{3,1},{4,6},{6,4},{5,7},{7,5},{8,10},{10,8},{9,1... | collective-permute-start | bytes 786440 | tf_op jit(solution)/shard_map/ppermute | solution.py:654
  126.8 11.4 %copy-start.2 = (bf16[128,1024]{1,0:T(8,128)(2,1)}, bf16[128,1024]{1,0:T(8,128)(2,1)S(1)}, u32[]{:S(2)}) copy-start(bf16[128,1024]{1,0:T(8,128)(2,1)S(1)} %collective-permute-done.9.refs_1_.w1) | copy-start | bytes 786436
  126.9 14.9 %all-to-all-start.4 = ((bf16[16,96,128]{2,1,0:T(8,128)(2,1)}), bf16[16,96,128]{2,1,0:T(8,128)(2,1)S(1)}, u32[]{:S(2)}, u32[]{:S(2)}) async-start(bf16[16,96,128]{2,1,0:T(8,128)(2,1)} %shard_map.266), calls=%async_computation.4 | async-start | bytes 786432 | tf_op jit(solution)/shard_map/all_to_all | solution.py:650
  131.6 5.8 %collective-permute-start.10 = (bf16[2,64,128]{2,1,0:T(8,128)(2,1)S(1)}, bf16[2,64,128]{2,1,0:T(8,128)(2,1)S(1)}, u32[]{:S(2)}, u32[]{:S(2)}) collective-permute-start(bf16[2,64,128]{2,1,0:T(8,128)(2,1)S(1)} %get-tuple-element.72), channel_id=1, source_target_pairs={{0,16},{16,32},{32,48},{48,0},{1,17},{17,33},{33,49},{49,1},{2,18}... | collective-permute-start | bytes 98312 | tf_op jit(solution)/shard_map/ppermute | solution.py:658
  132.9 4.4 %collective-permute-start.11 = (bf16[2,64,128]{2,1,0:T(8,128)(2,1)S(1)}, bf16[2,64,128]{2,1,0:T(8,128)(2,1)S(1)}, u32[]{:S(2)}, u32[]{:S(2)}) collective-permute-start(bf16[2,64,128]{2,1,0:T(8,128)(2,1)S(1)} %get-tuple-element.73), channel_id=1, source_target_pairs={{0,32},{16,48},{32,0},{48,16},{1,33},{17,49},{33,1},{49,17},{2,34}... | collective-permute-start | bytes 98312 | tf_op jit(solution)/shard_map/ppermute | solution.py:658
  134.3 3.3 %collective-permute-start.12 = (bf16[2,64,128]{2,1,0:T(8,128)(2,1)S(1)}, bf16[2,64,128]{2,1,0:T(8,128)(2,1)S(1)}, u32[]{:S(2)}, u32[]{:S(2)}) collective-permute-start(bf16[2,64,128]{2,1,0:T(8,128)(2,1)S(1)} %get-tuple-element.74), channel_id=1, source_target_pairs={{0,48},{16,0},{32,16},{48,32},{1,49},{17,1},{33,17},{49,33},{2,50}... | collective-permute-start | bytes 98312 | tf_op jit(solution)/shard_map/ppermute | solution.py:658
  141.7 17.3 %all-to-all-start.5 = ((bf16[32,4,2176]{2,1,0:T(4,128)(2,1)}), bf16[32,4,2176]{2,1,0:T(4,128)(2,1)S(1)}, u32[]{:S(2)}, u32[]{:S(2)}) async-start(bf16[32,4,2176]{2,1,0:T(4,128)(2,1)} %shard_map.271), calls=%async_computation.6 | async-start | bytes 1114112 | tf_op jit(solution)/shard_map/all_to_all | solution.py:650
Sparse Core Ops, SparseCore 0:
  55.7 27.1 all-gather.4
  97.3 26.0 reduce-scatter.1
  125.2 26.2 all-gather.6

commit v7 on v6

--- a/solution.py
+++ b/solution.py
@@ -176,21 +176,17 @@
     finish(leaving)
 
 
-def unpack_kernel(place, near, far, cot, feed, heads, whole, rows, arrived):
-    loads = [
-        pltpu.make_async_copy(source.at[:, ROWS:, :], rows.at[i], arrived.at[i])
-        for i, source in enumerate((near, far))
-    ]
-    for load in loads:
-        load.start()
-    for load in loads:
-        load.wait()
+def rows_kernel(near, rows):
+    rows[...] = near[:, ROWS:, :]
+
+
+def unpack_kernel(place, near, far, feed, heads, whole):
     second = place[0] == 1
     for group in range(4):
         blocks = []
         for chip in (2 * group, 2 * group + 1):
-            own = rows[0, chip].astype(f32)
-            other = rows[1, chip].astype(f32)
+            own = near[chip].astype(f32)
+            other = far[chip].astype(f32)
             blocks += [jnp.where(second, other, own), jnp.where(second, own, other)]
         here = slice(16 * group, 16 * (group + 1))
         for i in range(3):
@@ -227,7 +223,7 @@
 
 
 def attend_kernel(
-    place, length, near, far, head_cols, cos, sin,
+    place, length, near, far, head_cols, cos, sin, other,
     sent, q_out, k_out, v_out, o_out, lse_out, cols_out,
     q_t, k_t, v_t, own_cols, left,
 ):
@@ -680,23 +676,25 @@
     near = exchange(packed, CHIPS)
     cot_pair = jnp.concatenate([cotangent, swap(cotangent, "z")], 0)
     near = after(near, cot_pair, place=pltpu.VMEM)
-    far = swap(near, "core")
-    cot_far = swap(cot_pair, "core")
+    (near_rows,) = call(rows_kernel, "U", [((8, MSG_ROWS - ROWS, D), bf16, "V")])(near)
+    far_rows = swap(near_rows, "core")
 
     feed_rows, heads, whole = call(
         unpack_kernel,
-        "SPPP",
+        "SUU",
         [
             ((1, 64, FEED_LANES), bf16, "V"),
             ((DP, 64, 128), bf16, "H"),
             ((1, 64, 3 * D), bf16, "H"),
         ],
-        [((2, 8, 48, D), bf16), 2],
-    )(place, near, far, cot_far)
+    )(place, near_rows, far_rows)
+    near = after(near, in_hbm(heads), place=pltpu.VMEM)
+    far = swap(near, "core")
+    cot_far = swap(cot_pair, "core")
     head_cols = exchange(heads, WINDOWS).reshape(D, 128)
     feed_other = after(swap(feed_rows, "z_lo"), in_hbm(whole), place=pltpu.VMEM)
     feed_rows, out_rows = call(
-        join_kernel, "UU", [((2, 64, 3 * D), bf16, "V"), ((2, 64, D), bf16, "V")]
+        join_kernel, "UU", [((2, 64, 3 * D), bf16, "H"), ((2, 64, D), bf16, "H")]
     )(feed_rows, feed_other)
     feed_weights = lax.all_gather(feed_rows, "x")
     out_rows = [out_rows] + [shift(out_rows, step) for step in range(1, 4)]
@@ -704,7 +702,7 @@
 
     sent, q_t, k_t, v_t, o_t, lse, head_cols = call(
         attend_kernel,
-        "SSVVUHH",
+        "SSVVUHHP",
         [
             ((SEQ, HEAD, TEAM_ROWS), bf16, "H"),
             ((HEAD, LEN), bf16, "A"),
@@ -723,7 +721,7 @@
         ],
         vmem=24,
         flops=19 * 10**9,
-    )(place, lengths, near, far, head_cols, cos, sin)
+    )(place, lengths, near, far, head_cols, cos, sin, cot_far)
     sent = after(sent, whole_other, *out_rows[1:])
     (scaled,) = call(
         scale_kernel, "SUUA", [((SEQ, ROWS, D), bf16, "H")], vmem=12

time: 168 us -> 166 us (0.988)
    ppermute x7 -> x8, waiting for transfers between devices: 23.3 us -> 21.8 us  [swap(): return lax.ppermute(value, axis, [(0, 1), (1, 0)])]
    pallas_call x12 -> x13, Pallas kernels: 48.8 us -> 48.6 us  [run(): inner(*(pltpu.with_memory_space_constraint(x, pltpu.HBM if where in 'HA'...]
    ppermute x7 -> x8, starting transfers between devices: 11.4 us -> 11.5 us  [swap(): return lax.ppermute(value, axis, [(0, 1), (1, 0)])]
  transfers between devices with their start and end apart: 22 -> 23, of which waited for: 9 -> 10; matrix products, arithmetic and copies ran while one was open for 1% -> 1% of each run, Pallas kernels for 21% -> 21%
where the time goes in v7:
time: 166 us; the launch traced here: 165 us
  starting transfers between devices  54 us (33%)
  Pallas kernels  48.7 us (29%)
  waiting for transfers between devices  45.2 us (27%)
  between operations  14.6 us (9%)
  local copies, waits for them, and re-layouts  2.48 us (1%)
    pallas_call x13, Pallas kernels, run(): inner(*(pltpu.with_memory_space_constraint(x, pltpu.HBM if where in 'HA'...  48.6 us
    all_to_all x6, starting transfers between devices, exchange(): return lax.all_to_all(value, axes, 0, 0, tiled=True)  34.3 us
    ppermute x8, waiting for transfers between devices, swap(): return lax.ppermute(value, axis, [(0, 1), (1, 0)])  21.8 us
    all_to_all x6, waiting for transfers between devices, exchange(): return lax.all_to_all(value, axes, 0, 0, tiled=True)  18.3 us
    ppermute x8, starting transfers between devices, swap(): return lax.ppermute(value, axis, [(0, 1), (1, 0)])  11.5 us
    ppermute x6, starting transfers between devices, shift(): return lax.ppermute(value, 'x', [(i, (i + by) % 4) for i in range(4)])  7.97 us
    all_gather x1, waiting for transfers between devices, shards(): row_weights = lax.all_gather(after(whole, in_hbm(norm_rows)), 'x')  4.26 us
  transfers between devices with their start and end apart: 23, of which 10 were waited for; matrix products, arithmetic and copies ran while one was open for 1% of the time, Pallas kernels for 21%

profile of v7, /device:TPU:1, one launch (start us, length us, event | category | flops | bytes accessed | tf_op | source)
XLA Modules:
  0.0 165.0 jit_solution(15953007284238605563)
XLA Ops:
  7.2 2.2 %shard_map.255 = bf16[8,176,512]{2,1,0:T(8,128)(2,1)} custom-call(bf16[1,128,512]{2,1,0:T(8,128)(2,1)} %tokens.3, bf16[4,512]{1,0:T(4,128)(2,1)} %w_query.1, bf16[4,512]{1,0:T(4,128)(2,1)} %w_key.1, bf16[4,512]{1,0:T(4,128)(2,1)} %w_value.1, bf16[4,512]{1,0:T(4,128)(2,1)} %w_output.1, bf16[4,2048]{1,0:T(4,128)(2,1)} %w_gate.1, bf16[4,2048]{1,0:T(4,128)(2,1)} %w_up.1, ...), custom_call_target="tpu_custom_call" | custom-call | tf_op jit(solution)/shard_map/pallas_call | solution.py:627
  9.4 8.5 %all-to-all-start = ((bf16[8,176,512]{2,1,0:T(8,128)(2,1)}), bf16[8,176,512]{2,1,0:T(8,128)(2,1)S(1)}, u32[]{:S(2)}, u32[]{:S(2)}) async-start(bf16[8,176,512]{2,1,0:T(8,128)(2,1)} %shard_map.255), calls=%async_computation | async-start | bytes 2883584 | tf_op jit(solution)/shard_map/all_to_all | solution.py:646
  17.9 3.0 %collective-permute-start = (bf16[1,128,512]{2,1,0:T(8,128)(2,1)S(1)}, bf16[1,128,512]{2,1,0:T(8,128)(2,1)S(1)}, u32[]{:S(2)}, u32[]{:S(2)}) collective-permute-start(bf16[1,128,512]{2,1,0:T(8,128)(2,1)S(1)} %copy-done.4), channel_id=1, source_target_pairs={{0,2},{2,0},{1,3},{3,1},{4,6},{6,4},{5,7},{7,5},{8,10},{10,8},{9,1... | collective-permute-start | bytes 393224 | tf_op jit(solution)/shard_map/ppermute | solution.py:650
  20.9 18.2 %collective-permute-done = bf16[1,128,512]{2,1,0:T(8,128)(2,1)S(1)} collective-permute-done((bf16[1,128,512]{2,1,0:T(8,128)(2,1)S(1)}, bf16[1,128,512]{2,1,0:T(8,128)(2,1)S(1)}, u32[]{:S(2)}, u32[]{:S(2)}) %collective-permute-start) | collective-permute-done | bytes 131104 | tf_op jit(solution)/shard_map/ppermute | solution.py:650
  39.2 1.9 %collective-permute-start.1 = (bf16[8,48,512]{2,1,0:T(8,128)(2,1)S(1)}, bf16[8,48,512]{2,1,0:T(8,128)(2,1)S(1)}, u32[]{:S(2)}, u32[]{:S(2)}) collective-permute-start(bf16[8,48,512]{2,1,0:T(8,128)(2,1)S(1)} %shard_map.257.near), channel_id=1, source_target_pairs={{0,1},{1,0},{2,3},{3,2},{4,5},{5,4},{6,7},{7,6},{8,9},{9,8},{10,11... | collective-permute-start | bytes 1179656 | tf_op jit(solution)/shard_map/ppermute | solution.py:650
  41.2 1.3 collective-permute-done.1.far
  42.4 1.5 shard_map.258
  45.5 4.5 %all-to-all-start.1 = ((bf16[8,64,128]{2,1,0:T(8,128)(2,1)}), bf16[8,64,128]{2,1,0:T(8,128)(2,1)}, u32[]{:S(2)}, u32[]{:S(2)}) async-start(bf16[8,64,128]{2,1,0:T(8,128)(2,1)} %get-tuple-element.50.refs_1_), calls=%async_computation.1 | async-start | bytes 262144 | tf_op jit(solution)/shard_map/all_to_all | solution.py:646
  50.0 2.3 %collective-permute-done.5.refs_0_ = bf16[1,64,2048]{2,1,0:T(8,128)(2,1)S(1)} collective-permute-done((bf16[1,64,2048]{2,1,0:T(8,128)(2,1)}, bf16[1,64,2048]{2,1,0:T(8,128)(2,1)S(1)}, u32[]{:S(2)}, u32[]{:S(2)}) %collective-permute-start.5) | collective-permute-done | bytes 262176 | tf_op jit(solution)/shard_map/ppermute | solution.py:650
  52.3 1.8 %shard_map.262 = (bf16[2,64,1536]{2,1,0:T(8,128)(2,1)}, bf16[2,64,512]{2,1,0:T(8,128)(2,1)}) custom-call(bf16[1,64,2048]{2,1,0:T(8,128)(2,1)} %get-tuple-element.53.own, bf16[1,64,2048]{2,1,0:T(8,128)(2,1)S(1)} %shard_map.261.other), custom_call_target="tpu_custom_call" | custom-call | tf_op jit(solution)/shard_map/pallas_call | solution.py:627
  55.6 2.8 %collective-permute-start.8 = (bf16[2,64,512]{2,1,0:T(8,128)(2,1)}, bf16[2,64,512]{2,1,0:T(8,128)(2,1)S(1)}, u32[]{:S(2)}, u32[]{:S(2)}) collective-permute-start(bf16[2,64,512]{2,1,0:T(8,128)(2,1)} %get-tuple-element.54.out0), channel_id=1, source_target_pairs={{0,48},{16,0},{32,16},{48,32},{1,49},{17,1},{33,17},{49,33},{2,50}... | collective-permute-start | bytes 393224 | tf_op jit(solution)/shard_map/ppermute | solution.py:654
  59.8 8.4 %shard_map.260 = (bf16[16,32,512]{2,1,0:T(8,128)(2,1)}, bf16[32,2048]{1,0:T(8,128)(2,1)}, bf16[32,2048]{1,0:T(8,128)(2,1)}, bf16[32,2048]{1,0:T(8,128)(2,1)}, f3...) custom-call(s32[6]{0:T(128)S(1)} %stack.27.place, s32[1]{0:T(128)S(6)} %copy.47.length, ...), custom_call_target="tpu_custom_call" | custom-call | flops 19000000512 | tf_op jit(solution)/shard_map/pallas_call | solution.py:627
  68.2 7.6 %all-to-all-start.2 = ((bf16[16,32,512]{2,1,0:T(8,128)(2,1)}), bf16[16,32,512]{2,1,0:T(8,128)(2,1)}, u32[]{:S(2)}, u32[]{:S(2)}) async-start(bf16[16,32,512]{2,1,0:T(8,128)(2,1)} %shard_map.263.other), calls=%async_computation.2 | async-start | bytes 1048576 | tf_op jit(solution)/shard_map/all_to_all | solution.py:646
  76.1 1.6 constant_dynamic-update-slice_fusion.3
  78.4 3.2 %shard_map.264.other2.scaled = bf16[16,128,512]{2,1,0:T(8,128)(2,1)} custom-call(s32[6]{0:T(128)S(1)} %stack.27.place, bf16[8,176,512]{2,1,0:T(8,128)(2,1)S(1)} %shard_map.259.near, bf16[8,176,512]{2,1,0:T(8,128)(2,1)S(1)} %collective-permute-done.2.far, bf16[16,32,512]{2,1,0:T(8,128)(2,1)} %shard_map.263.other), custom_call_target="tpu_custom_call" | custom-call | tf_op jit(solution)/shard_map/pallas_call | solution.py:627
  81.6 5.5 %all-to-all-done.2.mixed = bf16[16,32,512]{2,1,0:T(8,128)(2,1)} async-done(((bf16[16,32,512]{2,1,0:T(8,128)(2,1)}), bf16[16,32,512]{2,1,0:T(8,128)(2,1)}, u32[]{:S(2)}, u32[]{:S(2)}) %all-to-all-start.2) | async-done | bytes 524320 | tf_op jit(solution)/shard_map/all_to_all | solution.py:646
  87.1 8.3 %shard_map.265 = (bf16[16,32,512]{2,1,0:T(8,128)(2,1)}, bf16[2,128,1024]{2,1,0:T(8,128)(2,1)}, bf16[2,128,1024]{2,1,0:T(8,128)(2,1)S(1)}, bf16[4,2,64,2048]{3,2,1,0:T(8,128)(2,1)}, f32[8,512]{1,0:T(8,128)}) custom-call(s32[6]{0:T(128)S(1)} %stack.27.place, s32[1]{0:T(128)S(6)} %copy.47.length, bf16[16,32,512]{2,1,0:T(8,128)(2,1)} %all-to-all-done.2.mixed, ...), custom_call_target="tpu_custom_call" | custom-call | tf_op jit(solution)/shard_map/pallas_call | solution.py:627
  96.2 1.4 collective-permute-start.9
  97.6 3.5 %all-to-all-start.3 = ((bf16[16,32,512]{2,1,0:T(8,128)(2,1)}), bf16[16,32,512]{2,1,0:T(8,128)(2,1)S(1)}, u32[]{:S(2)}, u32[]{:S(2)}) async-start(bf16[16,32,512]{2,1,0:T(8,128)(2,1)} %get-tuple-element.57), calls=%async_computation.3 | async-start | bytes 1048576 | tf_op jit(solution)/shard_map/all_to_all | solution.py:646
  101.1 2.0 %shard_map.267 = (bf16[128,1024]{1,0:T(8,128)(2,1)}, bf16[128,1024]{1,0:T(8,128)(2,1)}) custom-call(bf16[2,128,1024]{2,1,0:T(8,128)(2,1)} %get-tuple-element.65.kept, bf16[2,128,1024]{2,1,0:T(8,128)(2,1)S(1)} %collective-permute-done.9.arrived), custom_call_target="tpu_custom_call" | custom-call | tf_op jit(solution)/shard_map/pallas_call | solution.py:627
  103.0 2.8 %collective-permute-start.10 = (bf16[128,1024]{1,0:T(8,128)(2,1)}, bf16[128,1024]{1,0:T(8,128)(2,1)S(1)}, u32[]{:S(2)}, u32[]{:S(2)}) collective-permute-start(bf16[128,1024]{1,0:T(8,128)(2,1)} %get-tuple-element.67), channel_id=1, source_target_pairs={{0,2},{2,0},{1,3},{3,1},{4,6},{6,4},{5,7},{7,5},{8,10},{10,8},{9,1... | collective-permute-start | bytes 786440 | tf_op jit(solution)/shard_map/ppermute | solution.py:650
  105.9 6.3 %all-to-all-done.3.d_mixed = bf16[16,32,512]{2,1,0:T(8,128)(2,1)S(1)} async-done(((bf16[16,32,512]{2,1,0:T(8,128)(2,1)}), bf16[16,32,512]{2,1,0:T(8,128)(2,1)S(1)}, u32[]{:S(2)}, u32[]{:S(2)}) %all-to-all-start.3) | async-done | bytes 524320 | tf_op jit(solution)/shard_map/all_to_all | solution.py:646
  112.2 12.9 %shard_map.266 = (bf16[16,96,128]{2,1,0:T(8,128)(2,1)}, bf16[2,64,128]{2,1,0:T(8,128)(2,1)S(1)}, bf16[2,64,128]{2,1,0:T(8,128)(2,1)S(1)}, bf16[2,64,128]{2,1,0:T(8,128)(2,1)S(1)}, bf16[2,64,128]{2,1,0:T(8,128)(2,1)S(1)}) custom-call(s32[6]{0:T(128)S(1)} %stack.27.place, s32[1]{0:T(128)S(6)} %copy.47.length, bf16[16,32,512]{2,1,0:T(8,128)(2,1)S(1)} %all-to-all-done.3.d_mixed, ...), custom_call_target="tpu_custom_call" | custom-call | tf_op jit(solution)/shard_map/pallas_call | solution.py:627
  125.1 4.7 %all-to-all-start.4 = ((bf16[16,96,128]{2,1,0:T(8,128)(2,1)}), bf16[16,96,128]{2,1,0:T(8,128)(2,1)S(1)}, u32[]{:S(2)}, u32[]{:S(2)}) async-start(bf16[16,96,128]{2,1,0:T(8,128)(2,1)} %shard_map.268), calls=%async_computation.4 | async-start | bytes 786432 | tf_op jit(solution)/shard_map/all_to_all | solution.py:646
  129.8 1.4 collective-permute-start.11
  131.2 1.4 collective-permute-start.12
  133.7 2.0 %shard_map.271.given = bf16[32,4,2176]{2,1,0:T(4,128)(2,1)} custom-call(bf16[128,2048]{1,0:T(8,128)(2,1)} %reduce-scatter.2.cloned.1.call-done.feed), custom_call_target="tpu_custom_call" | custom-call | tf_op jit(solution)/shard_map/pallas_call | solution.py:627
  136.5 3.4 %all-to-all-done.4.d_lin.refs_1_ = bf16[16,96,128]{2,1,0:T(8,128)(2,1)S(1)} async-done(((bf16[16,96,128]{2,1,0:T(8,128)(2,1)}), bf16[16,96,128]{2,1,0:T(8,128)(2,1)S(1)}, u32[]{:S(2)}, u32[]{:S(2)}) %all-to-all-start.4) | async-done | bytes 393248 | tf_op jit(solution)/shard_map/all_to_all | solution.py:646
  140.0 5.5 %all-to-all-start.5 = ((bf16[32,4,2176]{2,1,0:T(4,128)(2,1)}), bf16[32,4,2176]{2,1,0:T(4,128)(2,1)S(1)}, u32[]{:S(2)}, u32[]{:S(2)}) async-start(bf16[32,4,2176]{2,1,0:T(4,128)(2,1)} %shard_map.273), calls=%async_computation.6 | async-start | bytes 1114112 | tf_op jit(solution)/shard_map/all_to_all | solution.py:646
  145.5 4.3 %all-gather.7.cloned.1.call-done = bf16[8,64,1536]{2,1,0:T(8,128)(2,1)} async-done(((bf16[2,64,1536]{2,1,0:T(8,128)(2,1)}), bf16[8,64,1536]{2,1,0:T(8,128)(2,1)}) %all-gather.7.cloned.1.call-update) | async-done | bytes 1572880 | tf_op jit(solution)/shard_map/all_gather | solution.py:761
  149.7 4.5 %shard_map.270 = (f32[1,128,512]{2,1,0:T(8,128)}, bf16[1,128,512]{2,1,0:T(8,128)(2,1)}) custom-call(s32[6]{0:T(128)S(1)} %stack.27.place, s32[1]{0:T(128)S(6)} %copy.47.length, bf16[1,128,512]{2,1,0:T(8,128)(2,1)} %tokens.3, bf16[16,96,128]{2,1,0:T(8,128)(2,1)S(1)} %all-to-all-done.4.d_lin.refs_1_, bf16[4,2,64,1536]{3,2,1,0:T(8,128)(2,1)} %bitcast.12, ...), custom_call_target="tpu_custom_call" | custom-call | tf_op jit(solution)/shard_map/pallas_call | solution.py:627
  154.3 3.0 %all-to-all-done.5.parts = bf16[32,4,2176]{2,1,0:T(4,128)(2,1)S(1)} async-done(((bf16[32,4,2176]{2,1,0:T(4,128)(2,1)}), bf16[32,4,2176]{2,1,0:T(4,128)(2,1)S(1)}, u32[]{:S(2)}, u32[]{:S(2)}) %all-to-all-start.5) | async-done | bytes 557088 | tf_op jit(solution)/shard_map/all_to_all | solution.py:646
  (52 shorter events, 8.9 us)
Async XLA Ops:
  9.4 8.5 %copy-start.4 = (bf16[1,128,512]{2,1,0:T(8,128)(2,1)S(1)}, bf16[1,128,512]{2,1,0:T(8,128)(2,1)}, u32[]{:S(2)}) copy-start(bf16[1,128,512]{2,1,0:T(8,128)(2,1)} %param.29) | copy-start | bytes 393220
  9.4 29.7 %all-to-all-start = ((bf16[8,176,512]{2,1,0:T(8,128)(2,1)}), bf16[8,176,512]{2,1,0:T(8,128)(2,1)S(1)}, u32[]{:S(2)}, u32[]{:S(2)}) async-start(bf16[8,176,512]{2,1,0:T(8,128)(2,1)} %shard_map.255), calls=%async_computation | async-start | bytes 2883584 | tf_op jit(solution)/shard_map/all_to_all | solution.py:646
  17.9 21.2 %collective-permute-start = (bf16[1,128,512]{2,1,0:T(8,128)(2,1)S(1)}, bf16[1,128,512]{2,1,0:T(8,128)(2,1)S(1)}, u32[]{:S(2)}, u32[]{:S(2)}) collective-permute-start(bf16[1,128,512]{2,1,0:T(8,128)(2,1)S(1)} %copy-done.4), channel_id=1, source_target_pairs={{0,2},{2,0},{1,3},{3,1},{4,6},{6,4},{5,7},{7,5},{8,10},{10,8},{9,1... | collective-permute-start | bytes 393224 | tf_op jit(solution)/shard_map/ppermute | solution.py:650
  39.1 6.0 %copy-start = (bf16[2,128,512]{2,1,0:T(8,128)(2,1)}, bf16[2,128,512]{2,1,0:T(8,128)(2,1)S(1)}, u32[]{:S(2)}) copy-start(bf16[2,128,512]{2,1,0:T(8,128)(2,1)S(1)} %constant_dynamic-update-slice_fusion.refs_1_.cot_near) | copy-start | bytes 786436
  39.2 3.3 %collective-permute-start.1 = (bf16[8,48,512]{2,1,0:T(8,128)(2,1)S(1)}, bf16[8,48,512]{2,1,0:T(8,128)(2,1)S(1)}, u32[]{:S(2)}, u32[]{:S(2)}) collective-permute-start(bf16[8,48,512]{2,1,0:T(8,128)(2,1)S(1)} %shard_map.257.near), channel_id=1, source_target_pairs={{0,1},{1,0},{2,3},{3,2},{4,5},{5,4},{6,7},{7,6},{8,9},{9,8},{10,11... | collective-permute-start | bytes 1179656 | tf_op jit(solution)/shard_map/ppermute | solution.py:650
  44.0 15.8 %collective-permute-start.2 = (bf16[8,176,512]{2,1,0:T(8,128)(2,1)S(1)}, bf16[8,176,512]{2,1,0:T(8,128)(2,1)S(1)}, u32[]{:S(2)}, u32[]{:S(2)}) collective-permute-start(bf16[8,176,512]{2,1,0:T(8,128)(2,1)S(1)} %shard_map.259.near), channel_id=1, source_target_pairs={{0,1},{1,0},{2,3},{3,2},{4,5},{5,4},{6,7},{7,6},{8,9},{9,8},{10,11... | collective-permute-start | bytes 4325384 | tf_op jit(solution)/shard_map/ppermute | solution.py:650
  44.3 8.0 %collective-permute-start.5 = (bf16[1,64,2048]{2,1,0:T(8,128)(2,1)}, bf16[1,64,2048]{2,1,0:T(8,128)(2,1)S(1)}, u32[]{:S(2)}, u32[]{:S(2)}) collective-permute-start(bf16[1,64,2048]{2,1,0:T(8,128)(2,1)} %get-tuple-element.53.own), channel_id=1, source_target_pairs={{0,64},{64,0},{1,65},{65,1},{2,66},{66,2},{3,67},{67,3},{4,68},{68... | collective-permute-start | bytes 786440 | tf_op jit(solution)/shard_map/ppermute | solution.py:650
  45.1 13.8 %collective-permute-start.3 = (bf16[2,128,512]{2,1,0:T(8,128)(2,1)S(1)}, bf16[2,128,512]{2,1,0:T(8,128)(2,1)}, u32[]{:S(2)}, u32[]{:S(2)}) collective-permute-start(bf16[2,128,512]{2,1,0:T(8,128)(2,1)S(1)} %constant_dynamic-update-slice_fusion.refs_1_.cot_near), channel_id=1, source_target_pairs={{0,1},{1,0},{2,3},{3,2},{4,5},{5,4},{6,7},{7,6},{8,9},{9,8},{10,11... | collective-permute-start | bytes 786440 | tf_op jit(solution)/shard_map/ppermute | solution.py:650
  45.5 14.2 %all-to-all-start.1 = ((bf16[8,64,128]{2,1,0:T(8,128)(2,1)}), bf16[8,64,128]{2,1,0:T(8,128)(2,1)}, u32[]{:S(2)}, u32[]{:S(2)}) async-start(bf16[8,64,128]{2,1,0:T(8,128)(2,1)} %get-tuple-element.50.refs_1_), calls=%async_computation.1 | async-start | bytes 262144 | tf_op jit(solution)/shard_map/all_to_all | solution.py:646
  50.0 37.1 %all-gather.5.cloned.1.call-start = ((), (), s32[]{:S(2)}) async-start(), calls=%async_computation.8 | async-start | bytes 1966080 | tf_op jit(solution)/shard_map/all_gather | solution.py:699
  54.8 13.4 %collective-permute-start.4 = (bf16[1,64,1536]{2,1,0:T(8,128)(2,1)}, bf16[1,64,1536]{2,1,0:T(8,128)(2,1)S(1)}, u32[]{:S(2)}, u32[]{:S(2)}) collective-permute-start(bf16[1,64,1536]{2,1,0:T(8,128)(2,1)} %get-tuple-element.52.refs_1_), channel_id=1, source_target_pairs={{0,64},{64,0},{1,65},{65,1},{2,66},{66,2},{3,67},{67,3},{4,68},{68... | collective-permute-start | bytes 589832 | tf_op jit(solution)/shard_map/ppermute | solution.py:650
  55.6 12.5 %collective-permute-start.8 = (bf16[2,64,512]{2,1,0:T(8,128)(2,1)}, bf16[2,64,512]{2,1,0:T(8,128)(2,1)S(1)}, u32[]{:S(2)}, u32[]{:S(2)}) collective-permute-start(bf16[2,64,512]{2,1,0:T(8,128)(2,1)} %get-tuple-element.54.out0), channel_id=1, source_target_pairs={{0,48},{16,0},{32,16},{48,32},{1,49},{17,1},{33,17},{49,33},{2,50}... | collective-permute-start | bytes 393224 | tf_op jit(solution)/shard_map/ppermute | solution.py:654
  58.4 9.8 %collective-permute-start.7 = (bf16[2,64,512]{2,1,0:T(8,128)(2,1)}, bf16[2,64,512]{2,1,0:T(8,128)(2,1)}, u32[]{:S(2)}, u32[]{:S(2)}) collective-permute-start(bf16[2,64,512]{2,1,0:T(8,128)(2,1)} %get-tuple-element.54.out0), channel_id=1, source_target_pairs={{0,32},{16,48},{32,0},{48,16},{1,33},{17,49},{33,1},{49,17},{2,34}... | collective-permute-start | bytes 393224 | tf_op jit(solution)/shard_map/ppermute | solution.py:654
  58.9 9.3 %collective-permute-start.6 = (bf16[2,64,512]{2,1,0:T(8,128)(2,1)}, bf16[2,64,512]{2,1,0:T(8,128)(2,1)S(1)}, u32[]{:S(2)}, u32[]{:S(2)}) collective-permute-start(bf16[2,64,512]{2,1,0:T(8,128)(2,1)} %get-tuple-element.54.out0), channel_id=1, source_target_pairs={{0,16},{16,32},{32,48},{48,0},{1,17},{17,33},{33,49},{49,1},{2,18}... | collective-permute-start | bytes 393224 | tf_op jit(solution)/shard_map/ppermute | solution.py:654
  68.2 9.5 %copy-start.2 = (bf16[2,64,512]{2,1,0:T(8,128)(2,1)}, bf16[2,64,512]{2,1,0:T(8,128)(2,1)S(1)}, u32[]{:S(2)}) copy-start(bf16[2,64,512]{2,1,0:T(8,128)(2,1)S(1)} %collective-permute-done.8.refs_4_.out3) | copy-start | bytes 393220
  68.2 9.5 %copy-start.3 = (bf16[2,64,512]{2,1,0:T(8,128)(2,1)}, bf16[2,64,512]{2,1,0:T(8,128)(2,1)S(1)}, u32[]{:S(2)}) copy-start(bf16[2,64,512]{2,1,0:T(8,128)(2,1)S(1)} %collective-permute-done.6.refs_2_.out1) | copy-start | bytes 393220
  68.2 18.9 %all-to-all-start.2 = ((bf16[16,32,512]{2,1,0:T(8,128)(2,1)}), bf16[16,32,512]{2,1,0:T(8,128)(2,1)}, u32[]{:S(2)}, u32[]{:S(2)}) async-start(bf16[16,32,512]{2,1,0:T(8,128)(2,1)} %shard_map.263.other), calls=%async_computation.2 | async-start | bytes 1048576 | tf_op jit(solution)/shard_map/all_to_all | solution.py:646
  75.8 57.8 %reduce-scatter.2.cloned.1.call-start = ((), (), s32[]{:S(2)}) async-start(), calls=%async_computation.7 | async-start | bytes 2621440 | tf_op jit(solution)/shard_map/reduce_scatter | solution.py:762
  95.4 54.3 %all-gather.7.cloned.1.call-start = ((), (), s32[]{:S(2)}) async-start(), calls=%async_computation.9 | async-start | bytes 1966080 | tf_op jit(solution)/shard_map/all_gather | solution.py:761
  96.2 4.9 %collective-permute-start.9 = (bf16[2,128,1024]{2,1,0:T(8,128)(2,1)S(1)}, bf16[2,128,1024]{2,1,0:T(8,128)(2,1)S(1)}, u32[]{:S(2)}, u32[]{:S(2)}) collective-permute-start(bf16[2,128,1024]{2,1,0:T(8,128)(2,1)S(1)} %get-tuple-element.66), channel_id=1, source_target_pairs={{0,1},{1,0},{2,3},{3,2},{4,5},{5,4},{6,7},{7,6},{8,9},{9,8},{10,11... | collective-permute-start | bytes 1572872 | tf_op jit(solution)/shard_map/ppermute | solution.py:650
  97.6 14.6 %all-to-all-start.3 = ((bf16[16,32,512]{2,1,0:T(8,128)(2,1)}), bf16[16,32,512]{2,1,0:T(8,128)(2,1)S(1)}, u32[]{:S(2)}, u32[]{:S(2)}) async-start(bf16[16,32,512]{2,1,0:T(8,128)(2,1)} %get-tuple-element.57), calls=%async_computation.3 | async-start | bytes 1048576 | tf_op jit(solution)/shard_map/all_to_all | solution.py:646
  103.0 22.1 %collective-permute-start.10 = (bf16[128,1024]{1,0:T(8,128)(2,1)}, bf16[128,1024]{1,0:T(8,128)(2,1)S(1)}, u32[]{:S(2)}, u32[]{:S(2)}) collective-permute-start(bf16[128,1024]{1,0:T(8,128)(2,1)} %get-tuple-element.67), channel_id=1, source_target_pairs={{0,2},{2,0},{1,3},{3,1},{4,6},{6,4},{5,7},{7,5},{8,10},{10,8},{9,1... | collective-permute-start | bytes 786440 | tf_op jit(solution)/shard_map/ppermute | solution.py:650
  125.1 10.5 %copy-start.1 = (bf16[128,1024]{1,0:T(8,128)(2,1)}, bf16[128,1024]{1,0:T(8,128)(2,1)S(1)}, u32[]{:S(2)}) copy-start(bf16[128,1024]{1,0:T(8,128)(2,1)S(1)} %collective-permute-done.10.refs_1_.w1) | copy-start | bytes 786436
  125.1 14.8 %all-to-all-start.4 = ((bf16[16,96,128]{2,1,0:T(8,128)(2,1)}), bf16[16,96,128]{2,1,0:T(8,128)(2,1)S(1)}, u32[]{:S(2)}, u32[]{:S(2)}) async-start(bf16[16,96,128]{2,1,0:T(8,128)(2,1)} %shard_map.268), calls=%async_computation.4 | async-start | bytes 786432 | tf_op jit(solution)/shard_map/all_to_all | solution.py:646
  129.8 5.8 %collective-permute-start.11 = (bf16[2,64,128]{2,1,0:T(8,128)(2,1)S(1)}, bf16[2,64,128]{2,1,0:T(8,128)(2,1)S(1)}, u32[]{:S(2)}, u32[]{:S(2)}) collective-permute-start(bf16[2,64,128]{2,1,0:T(8,128)(2,1)S(1)} %get-tuple-element.72), channel_id=1, source_target_pairs={{0,16},{16,32},{32,48},{48,0},{1,17},{17,33},{33,49},{49,1},{2,18}... | collective-permute-start | bytes 98312 | tf_op jit(solution)/shard_map/ppermute | solution.py:654
  131.2 4.6 %collective-permute-start.12 = (bf16[2,64,128]{2,1,0:T(8,128)(2,1)S(1)}, bf16[2,64,128]{2,1,0:T(8,128)(2,1)S(1)}, u32[]{:S(2)}, u32[]{:S(2)}) collective-permute-start(bf16[2,64,128]{2,1,0:T(8,128)(2,1)S(1)} %get-tuple-element.73), channel_id=1, source_target_pairs={{0,32},{16,48},{32,0},{48,16},{1,33},{17,49},{33,1},{49,17},{2,34}... | collective-permute-start | bytes 98312 | tf_op jit(solution)/shard_map/ppermute | solution.py:654
  132.6 3.3 %collective-permute-start.13 = (bf16[2,64,128]{2,1,0:T(8,128)(2,1)S(1)}, bf16[2,64,128]{2,1,0:T(8,128)(2,1)S(1)}, u32[]{:S(2)}, u32[]{:S(2)}) collective-permute-start(bf16[2,64,128]{2,1,0:T(8,128)(2,1)S(1)} %get-tuple-element.74), channel_id=1, source_target_pairs={{0,48},{16,0},{32,16},{48,32},{1,49},{17,1},{33,17},{49,33},{2,50}... | collective-permute-start | bytes 98312 | tf_op jit(solution)/shard_map/ppermute | solution.py:654
  140.0 17.3 %all-to-all-start.5 = ((bf16[32,4,2176]{2,1,0:T(4,128)(2,1)}), bf16[32,4,2176]{2,1,0:T(4,128)(2,1)S(1)}, u32[]{:S(2)}, u32[]{:S(2)}) async-start(bf16[32,4,2176]{2,1,0:T(4,128)(2,1)} %shard_map.273), calls=%async_computation.6 | async-start | bytes 1114112 | tf_op jit(solution)/shard_map/all_to_all | solution.py:646
Sparse Core Ops, SparseCore 0:
  54.3 26.9 all-gather.4
  95.6 26.0 reduce-scatter.1
  123.4 26.2 all-gather.6

commit v8 on v7

--- a/solution.py
+++ b/solution.py
@@ -212,10 +212,9 @@
             heads[w, here, :] = cols
 
 
-def join_kernel(own, other, feed, out):
-    for i, rows in enumerate((own, other)):
-        feed[i] = rows[0, :, 0 : 3 * D]
-        out[i] = rows[0, :, 3 * D : 4 * D]
+def join_kernel(own, other, feed):
+    feed[0] = own[0]
+    feed[1] = other[0]
 
 
 def block_of(place, chip, other):
@@ -292,12 +291,12 @@
 def load_part(place, weights, parts, arrived, i):
     return [
         pltpu.make_async_copy(
-            weights.at[x, place[5] ^ k, :, 512 * i : 512 * (i + 1)],
-            parts.at[i, k, x],
-            arrived.at[8 * i + 4 * k + x],
+            rows.at[place[5] ^ k, :, 512 * i : 512 * (i + 1)],
+            parts.at[i, k, lax.rem(place[4] + 4 - step, 4)],
+            arrived.at[8 * i + 4 * k + step],
         )
         for k in range(2)
-        for x in range(4)
+        for step, rows in enumerate(weights)
     ]
 
 
@@ -307,9 +306,9 @@
 
 
 def feed_kernel(
-    place, length, mixed, near, far, cot_near, cot_far, weights, head_cols, other1, other2,
-    out0, out1, out2, out3,
-    sent, kept, swapped, grads, norm_rows,
+    place, length, mixed, near, far, cot_near, cot_far, head_cols, other1, other2,
+    rows0, rows1, rows2, rows3,
+    sent, kept, swapped, grads0, grads1, grads2, grads3, norm_rows,
     mixed_rows, tokens, cot, norms, back, ahead, parts, own_sent, own_kept, own_grads,
     arrived, tokens_arrived, left,
 ):
@@ -336,18 +335,8 @@
                     tokens_arrived.at[4 + 2 * one + other],
                 )
             )
-    loads = [
-        [
-            pltpu.make_async_copy(
-                rows.at[place[5] ^ k],
-                parts.at[3, k, lax.rem(place[4] + 4 - step, 4)],
-                arrived.at[24 + 4 * k + step],
-            )
-            for k in range(2)
-            for step, rows in enumerate((out0, out1, out2, out3))
-        ]
-    ]
-    loads += [load_part(place, weights, parts, arrived, i) for i in range(3)]
+    weights = (rows0, rows1, rows2, rows3)
+    loads = [load_part(place, weights, parts, arrived, i) for i in (3, 0, 1, 2)]
     for load in [loads[0], first, *loads[1:], later]:
         for copy in load:
             copy.start()
@@ -397,7 +386,11 @@
             for x in range(4):
                 at = 64 * (4 * k + x)
                 own_grads[i, x, k] = low[at : at + 64]
-        send(own_grads.at[i], grads.at[:, :, :, D * i : D * (i + 1)])
+        for step, grads in enumerate((grads0, grads1, grads2, grads3)):
+            send(
+                own_grads.at[i, lax.rem(place[4] + step, 4)],
+                grads.at[:, :, D * i : D * (i + 1)],
+            )
 
     send_grad(2, tn(hidden, d_out_low))
     send_grad(0, tn(normed, d_gate))
@@ -518,8 +511,11 @@
     leaving.wait()
 
 
-def regroup_kernel(feed, sent):
-    total = feed[...].astype(f32)
+def regroup_kernel(part0, part1, part2, part3, sent):
+    total = part0[...].astype(f32)
+    for part in (part1, part2, part3):
+        total = total + part[...].astype(f32)
+    total = total.reshape(2 * 64, FEED_LANES)
     for d in range(SEQ * 2):
         sent[d, :, :FEED_LANES] = total[4 * d : 4 * d + 4].astype(bf16)
         sent[d, :, FEED_LANES:] = jnp.zeros((4, 128), bf16)
@@ -538,10 +534,11 @@
 
 
 def input_grad_kernel(
-    place, length, tokens, d_lin, weights, w0, w1, head_cols,
+    place, length, tokens, d_lin, rows0, rows1, rows2, rows3, w0, w1, head_cols,
     grad_tokens, layer_output,
     parts, arrived,
 ):
+    weights = (rows0, rows1, rows2, rows3)
     loads = [load_part(place, weights, parts, arrived, i) for i in range(3)]
     for load in loads:
         for copy in load:
@@ -606,7 +603,7 @@
 
 
 def call(kernel, ins, outs, scratch=(), vmem=8, flops=0, aliases={}):
-    places = {"V": pltpu.VMEM, "U": pltpu.VMEM, "H": pltpu.VMEM, "A": pl.ANY, "P": pl.ANY, "S": pltpu.SMEM}
+    places = {"V": pltpu.VMEM, "U": pltpu.VMEM, "H": pltpu.VMEM, "A": pl.ANY, "P": pl.ANY, "W": pl.ANY, "S": pltpu.SMEM}
     inner = pl.pallas_call(
         kernel,
         out_shape=tuple(
@@ -627,7 +624,7 @@
         return inner(
             *(
                 pltpu.with_memory_space_constraint(x, pltpu.HBM if where in "HA" else pltpu.VMEM)
-                if where in "HAV"
+                if where in "HAVW"
                 else x
                 for x, where in zip(args, ins)
             )
@@ -693,11 +690,8 @@
     cot_far = swap(cot_pair, "core")
     head_cols = exchange(heads, WINDOWS).reshape(D, 128)
     feed_other = after(swap(feed_rows, "z_lo"), in_hbm(whole), place=pltpu.VMEM)
-    feed_rows, out_rows = call(
-        join_kernel, "UU", [((2, 64, 3 * D), bf16, "H"), ((2, 64, D), bf16, "H")]
-    )(feed_rows, feed_other)
-    feed_weights = lax.all_gather(feed_rows, "x")
-    out_rows = [out_rows] + [shift(out_rows, step) for step in range(1, 4)]
+    (feed_rows,) = call(join_kernel, "UU", [((2, 64, FEED_LANES), bf16, "H")])(feed_rows, feed_other)
+    feed_rows = [feed_rows] + [shift(feed_rows, step) for step in range(1, 4)]
     whole_other = swap(whole, "z_lo")
 
     sent, q_t, k_t, v_t, o_t, lse, head_cols = call(
@@ -722,21 +716,21 @@
         vmem=24,
         flops=19 * 10**9,
     )(place, lengths, near, far, head_cols, cos, sin, cot_far)
-    sent = after(sent, whole_other, *out_rows[1:])
+    sent = after(sent, whole_other)
     (scaled,) = call(
         scale_kernel, "SUUA", [((SEQ, ROWS, D), bf16, "H")], vmem=12
     )(place, near, far, sent)
     mixed = exchange(sent, WINDOW)
-    whole = jnp.concatenate([whole, whole_other], 0)
-
-    d_sent, kept, swapped, grads, norm_rows = call(
+    (whole,) = call(join_kernel, "HU", [((2, 64, 3 * D), bf16, "H")])(whole, whole_other)
+
+    d_sent, kept, swapped, *grads, norm_rows = call(
         feed_kernel,
-        "SSAPPAAAAAA" + "A" * 4,
+        "SSPPPAAAAA" + "A" * 4,
         [
             ((HEADS, HEAD, TEAM_ROWS), bf16, "A"),
             ((2, ROWS, 2 * D), bf16, "A"),
             ((2, ROWS, 2 * D), bf16, "V"),
-            ((4, 2, 64, FEED_LANES), bf16, "A"),
+            *[((2, 64, FEED_LANES), bf16, "A")] * 4,
             ((8, D), f32, "H"),
         ],
         [
@@ -750,18 +744,17 @@
             ((HEADS, HEAD, TEAM_ROWS), bf16),
             ((2, ROWS, 2 * D), bf16),
             ((4, 4, 2, 64, 512), bf16),
-            32, 10, 6,
+            32, 10, 18,
         ],
         vmem=28,
     )(
-        place, lengths, mixed, near, far, cot_pair, cot_far, feed_weights, head_cols, whole, scaled,
-        *out_rows,
+        place, lengths, mixed, near, far, cot_pair, cot_far, head_cols, whole, scaled,
+        *feed_rows,
     )
-    d_mixed = exchange(d_sent, WINDOW)
-    row_weights = lax.all_gather(after(whole, in_hbm(norm_rows)), "x")
-    feed_grads = lax.psum_scatter(
-        grads.reshape(D, FEED_LANES), "x", scatter_dimension=0, tiled=True
-    )
+    row_weights = [whole] + [shift(whole, step) for step in range(1, 4)]
+    d_mixed = exchange(after(d_sent, row_weights[1], row_weights[3]), WINDOW)
+    grads[3] = after(grads[3], row_weights[2])
+    feed_grads = [grads[0]] + [shift(grads[step], step) for step in range(1, 4)]
     w0, w1 = call(
         add_kernel, "HV", [((ROWS, 2 * D), bf16, "H")] * 2
     )(kept, swap(swapped, "core"))
@@ -792,7 +785,7 @@
     lin_sent = after(lin_sent, w1)
     back = exchange(lin_sent, WINDOW)
     head_grads = [head_grads[0]] + [shift(head_grads[step], step) for step in range(1, 4)]
-    (grad_sent,) = call(regroup_kernel, "H", [((2 * SEQ, 4, GRAD_LANES), bf16, "H")])(feed_grads)
+    (grad_sent,) = call(regroup_kernel, "HUUU", [((2 * SEQ, 4, GRAD_LANES), bf16, "H")])(*feed_grads)
     (grad_sent,) = call(
         append_kernel,
         "UUUUA",
@@ -804,10 +797,10 @@
 
     grad_tokens, layer_output = call(
         input_grad_kernel,
-        "SSHVAHHH",
+        "SSHVAPPPHHH",
         [((1, ROWS, D), f32, "H"), ((1, ROWS, D), bf16, "H")],
         [((3, 2, 4, 64, 512), bf16), 24],
-    )(place, lengths, tokens, back, row_weights, w0, w1, head_cols)
+    )(place, lengths, tokens, back, *row_weights, w0, w1, head_cols)
     weight_grads = call(
         sum_kernel,
         "V",

time: 166 us -> 152 us (0.916)
  between operations: 14.6 us -> 1.49 us
  waiting for transfers between devices: 45.2 us -> 39.5 us
  starting transfers between devices: 54 us -> 59.4 us
  local copies, waits for them, and re-layouts: 2.48 us -> 0.12 us
  Pallas kernels: 48.7 us -> 50.9 us
    all_gather x2 -> x0, waiting for transfers between devices: 4.26 us -> none  [the longest x1 4.26 us: shards(): row_weights = lax.all_gather(after(whole, in_hbm(norm_rows)), 'x')]
    ppermute x6 -> x12, starting transfers between devices: 7.97 us -> 12 us  [shift(): return lax.ppermute(value, 'x', [(i, (i + by) % 4) for i in range(4)])]
    ppermute x6 -> x12, waiting for transfers between devices: 0.25 us -> 2.52 us  [shift(): return lax.ppermute(value, 'x', [(i, (i + by) % 4) for i in range(4)])]
    pallas_call x13 -> x14, Pallas kernels: 48.6 us -> 50.9 us  [run(): inner(*(pltpu.with_memory_space_constraint(x, pltpu.HBM if where in 'HA'...]
    ppermute x8, waiting for transfers between devices: 21.8 us -> 19.6 us  [swap(): return lax.ppermute(value, axis, [(0, 1), (1, 0)])]
  transfers between devices with their start and end apart: 23 -> 26, of which waited for: 10 -> 9; matrix products, arithmetic and copies ran while one was open for 1% -> 0% of each run, Pallas kernels for 21% -> 30%
where the time goes in v8:
time: 152 us; the launch traced here: 151 us
  starting transfers between devices  59.4 us (39%)
  Pallas kernels  50.9 us (33%)
  waiting for transfers between devices  39.5 us (26%)
    pallas_call x14, Pallas kernels, run(): inner(*(pltpu.with_memory_space_constraint(x, pltpu.HBM if where in 'HA'...  50.9 us
    all_to_all x6, starting transfers between devices, exchange(): return lax.all_to_all(value, axes, 0, 0, tiled=True)  35.1 us
    ppermute x8, waiting for transfers between devices, swap(): return lax.ppermute(value, axis, [(0, 1), (1, 0)])  19.6 us
    all_to_all x6, waiting for transfers between devices, exchange(): return lax.all_to_all(value, axes, 0, 0, tiled=True)  17.4 us
    ppermute x8, starting transfers between devices, swap(): return lax.ppermute(value, axis, [(0, 1), (1, 0)])  12.3 us
    ppermute x12, starting transfers between devices, shift(): return lax.ppermute(value, 'x', [(i, (i + by) % 4) for i in range(4)])  12 us
  transfers between devices with their start and end apart: 26, of which 9 were waited for; matrix products, arithmetic and copies ran while one was open for 0% of the time, Pallas kernels for 30%

profile of v8, /device:TPU:1, one launch (start us, length us, event | category | flops | bytes accessed | tf_op | source)
XLA Modules:
  0.0 151.4 jit_solution(11294597651106654126)
XLA Ops:
  0.6 2.2 %shard_map.255 = bf16[8,176,512]{2,1,0:T(8,128)(2,1)} custom-call(bf16[1,128,512]{2,1,0:T(8,128)(2,1)} %tokens.3, bf16[4,512]{1,0:T(4,128)(2,1)} %w_query.1, bf16[4,512]{1,0:T(4,128)(2,1)} %w_key.1, bf16[4,512]{1,0:T(4,128)(2,1)} %w_value.1, bf16[4,512]{1,0:T(4,128)(2,1)} %w_output.1, bf16[4,2048]{1,0:T(4,128)(2,1)} %w_gate.1, bf16[4,2048]{1,0:T(4,128)(2,1)} %w_up.1, ...), custom_call_target="tpu_custom_call" | custom-call | tf_op jit(solution)/shard_map/pallas_call | solution.py:624
  2.9 8.5 %all-to-all-start = ((bf16[8,176,512]{2,1,0:T(8,128)(2,1)}), bf16[8,176,512]{2,1,0:T(8,128)(2,1)S(1)}, u32[]{:S(2)}, u32[]{:S(2)}) async-start(bf16[8,176,512]{2,1,0:T(8,128)(2,1)} %shard_map.255), calls=%async_computation | async-start | bytes 2883584 | tf_op jit(solution)/shard_map/all_to_all | solution.py:643
  11.4 3.0 %collective-permute-start = (bf16[1,128,512]{2,1,0:T(8,128)(2,1)S(1)}, bf16[1,128,512]{2,1,0:T(8,128)(2,1)S(1)}, u32[]{:S(2)}, u32[]{:S(2)}) collective-permute-start(bf16[1,128,512]{2,1,0:T(8,128)(2,1)S(1)} %copy-done.2), channel_id=1, source_target_pairs={{0,2},{2,0},{1,3},{3,1},{4,6},{6,4},{5,7},{7,5},{8,10},{10,8},{9,1... | collective-permute-start | bytes 393224 | tf_op jit(solution)/shard_map/ppermute | solution.py:647
  14.3 18.2 %collective-permute-done = bf16[1,128,512]{2,1,0:T(8,128)(2,1)S(1)} collective-permute-done((bf16[1,128,512]{2,1,0:T(8,128)(2,1)S(1)}, bf16[1,128,512]{2,1,0:T(8,128)(2,1)S(1)}, u32[]{:S(2)}, u32[]{:S(2)}) %collective-permute-start) | collective-permute-done | bytes 131104 | tf_op jit(solution)/shard_map/ppermute | solution.py:647
  32.6 1.9 %collective-permute-start.1 = (bf16[8,48,512]{2,1,0:T(8,128)(2,1)S(1)}, bf16[8,48,512]{2,1,0:T(8,128)(2,1)S(1)}, u32[]{:S(2)}, u32[]{:S(2)}) collective-permute-start(bf16[8,48,512]{2,1,0:T(8,128)(2,1)S(1)} %shard_map.257.near), channel_id=1, source_target_pairs={{0,1},{1,0},{2,3},{3,2},{4,5},{5,4},{6,7},{7,6},{8,9},{9,8},{10,11... | collective-permute-start | bytes 1179656 | tf_op jit(solution)/shard_map/ppermute | solution.py:647
  35.9 1.5 %shard_map.258 = (bf16[1,64,2048]{2,1,0:T(8,128)(2,1)}, bf16[8,64,128]{2,1,0:T(8,128)(2,1)}, bf16[1,64,1536]{2,1,0:T(8,128)(2,1)}) custom-call(s32[6]{0:T(128)S(1)} %stack.27.place, bf16[8,48,512]{2,1,0:T(8,128)(2,1)S(1)} %shard_map.257.near, bf16[8,48,512]{2,1,0:T(8,128)(2,1)S(1)} %collective-permute-done.1.far), custom_call_target="tpu_custom_call" | custom-call | tf_op jit(solution)/shard_map/pallas_call | solution.py:624
  39.0 4.5 %all-to-all-start.1 = ((bf16[8,64,128]{2,1,0:T(8,128)(2,1)}), bf16[8,64,128]{2,1,0:T(8,128)(2,1)S(1)}, u32[]{:S(2)}, u32[]{:S(2)}) async-start(bf16[8,64,128]{2,1,0:T(8,128)(2,1)} %get-tuple-element.51.refs_1_), calls=%async_computation.1 | async-start | bytes 262144 | tf_op jit(solution)/shard_map/all_to_all | solution.py:643
  44.1 1.5 %collective-permute-start.4 = (bf16[1,64,1536]{2,1,0:T(8,128)(2,1)}, bf16[1,64,1536]{2,1,0:T(8,128)(2,1)}, u32[]{:S(2)}, u32[]{:S(2)}) collective-permute-start(bf16[1,64,1536]{2,1,0:T(8,128)(2,1)} %get-tuple-element.53.own.refs_1_), channel_id=1, source_target_pairs={{0,64},{64,0},{1,65},{65,1},{2,66},{66,2},{3,67},{67,3},{4,68},{68... | collective-permute-start | bytes 589832 | tf_op jit(solution)/shard_map/ppermute | solution.py:647
  45.8 1.8 %shard_map.265.rows0 = bf16[2,64,2048]{2,1,0:T(8,128)(2,1)} custom-call(bf16[1,64,2048]{2,1,0:T(8,128)(2,1)} %get-tuple-element.55.own, bf16[1,64,2048]{2,1,0:T(8,128)(2,1)S(1)} %shard_map.264.other), custom_call_target="tpu_custom_call" | custom-call | tf_op jit(solution)/shard_map/pallas_call | solution.py:624
  48.8 2.5 %collective-permute-start.7 = (bf16[2,64,2048]{2,1,0:T(8,128)(2,1)}, bf16[2,64,2048]{2,1,0:T(8,128)(2,1)}, u32[]{:S(2)}, u32[]{:S(2)}) collective-permute-start(bf16[2,64,2048]{2,1,0:T(8,128)(2,1)} %shard_map.265.rows0), channel_id=1, source_target_pairs={{0,32},{16,48},{32,0},{48,16},{1,33},{17,49},{33,1},{49,17},{2,34}... | collective-permute-start | bytes 1572872 | tf_op jit(solution)/shard_map/ppermute | solution.py:651
  52.4 8.3 %shard_map.260 = (bf16[16,32,512]{2,1,0:T(8,128)(2,1)}, bf16[32,2048]{1,0:T(8,128)(2,1)}, bf16[32,2048]{1,0:T(8,128)(2,1)}, bf16[32,2048]{1,0:T(8,128)(2,1)}, f3...) custom-call(s32[6]{0:T(128)S(1)} %stack.27.place, s32[1]{0:T(128)S(6)} %copy.48.length, ...), custom_call_target="tpu_custom_call" | custom-call | flops 19000000512 | tf_op jit(solution)/shard_map/pallas_call | solution.py:624
  60.8 6.6 %all-to-all-start.2 = ((bf16[16,32,512]{2,1,0:T(8,128)(2,1)}), bf16[16,32,512]{2,1,0:T(8,128)(2,1)S(1)}, u32[]{:S(2)}, u32[]{:S(2)}) async-start(bf16[16,32,512]{2,1,0:T(8,128)(2,1)} %shard_map.261.other), calls=%async_computation.2 | async-start | bytes 1048576 | tf_op jit(solution)/shard_map/all_to_all | solution.py:643
  67.4 1.8 %shard_map.262.other1.rows0 = bf16[2,64,1536]{2,1,0:T(8,128)(2,1)} custom-call(bf16[1,64,1536]{2,1,0:T(8,128)(2,1)} %get-tuple-element.53.own.refs_1_, bf16[1,64,1536]{2,1,0:T(8,128)(2,1)} %collective-permute-done.4.refs_1_.other), custom_call_target="tpu_custom_call" | custom-call | tf_op jit(solution)/shard_map/pallas_call | solution.py:624
  69.2 1.5 collective-permute-start.9
  70.7 3.2 %shard_map.263.other2.scaled = bf16[16,128,512]{2,1,0:T(8,128)(2,1)} custom-call(s32[6]{0:T(128)S(1)} %stack.27.place, bf16[8,176,512]{2,1,0:T(8,128)(2,1)S(1)} %shard_map.259.near, bf16[8,176,512]{2,1,0:T(8,128)(2,1)S(1)} %collective-permute-done.2.far, bf16[16,32,512]{2,1,0:T(8,128)(2,1)} %shard_map.261.other), custom_call_target="tpu_custom_call" | custom-call | tf_op jit(solution)/shard_map/pallas_call | solution.py:624
  73.9 4.6 %all-to-all-done.2.mixed = bf16[16,32,512]{2,1,0:T(8,128)(2,1)S(1)} async-done(((bf16[16,32,512]{2,1,0:T(8,128)(2,1)}), bf16[16,32,512]{2,1,0:T(8,128)(2,1)S(1)}, u32[]{:S(2)}, u32[]{:S(2)}) %all-to-all-start.2) | async-done | bytes 524320 | tf_op jit(solution)/shard_map/all_to_all | solution.py:643
  78.5 8.6 %shard_map.266 = (bf16[16,32,512]{2,1,0:T(8,128)(2,1)}, bf16[2,128,1024]{2,1,0:T(8,128)(2,1)}, bf16[2,128,1024]{2,1,0:T(8,128)(2,1)}, bf16[2,64,2048]{2,1,0:T(8,...) custom-call(s32[6]{0:T(128)S(1)} %stack.27.place, ...), custom_call_target="tpu_custom_call" | custom-call | tf_op jit(solution)/shard_map/pallas_call | solution.py:624
  87.1 1.4 collective-permute-start.11
  88.6 5.1 %all-to-all-start.3 = ((bf16[16,32,512]{2,1,0:T(8,128)(2,1)}), bf16[16,32,512]{2,1,0:T(8,128)(2,1)S(1)}, u32[]{:S(2)}, u32[]{:S(2)}) async-start(bf16[16,32,512]{2,1,0:T(8,128)(2,1)} %shard_map.267), calls=%async_computation.3 | async-start | bytes 1048576 | tf_op jit(solution)/shard_map/all_to_all | solution.py:643
  93.7 1.9 %shard_map.269 = (bf16[128,1024]{1,0:T(8,128)(2,1)}, bf16[128,1024]{1,0:T(8,128)(2,1)}) custom-call(bf16[2,128,1024]{2,1,0:T(8,128)(2,1)} %get-tuple-element.64.kept, bf16[2,128,1024]{2,1,0:T(8,128)(2,1)S(1)} %collective-permute-done.11.arrived), custom_call_target="tpu_custom_call" | custom-call | tf_op jit(solution)/shard_map/pallas_call | solution.py:624
  95.6 2.9 %collective-permute-start.12 = (bf16[128,1024]{1,0:T(8,128)(2,1)}, bf16[128,1024]{1,0:T(8,128)(2,1)S(1)}, u32[]{:S(2)}, u32[]{:S(2)}) collective-permute-start(bf16[128,1024]{1,0:T(8,128)(2,1)} %get-tuple-element.66), channel_id=1, source_target_pairs={{0,2},{2,0},{1,3},{3,1},{4,6},{6,4},{5,7},{7,5},{8,10},{10,8},{9,1... | collective-permute-start | bytes 786440 | tf_op jit(solution)/shard_map/ppermute | solution.py:647
  98.5 2.4 %collective-permute-done.13.rows2.refs_1_ = bf16[2,64,1536]{2,1,0:T(8,128)(2,1)S(1)} collective-permute-done((bf16[2,64,1536]{2,1,0:T(8,128)(2,1)}, bf16[2,64,1536]{2,1,0:T(8,128)(2,1)S(1)}, u32[]{:S(2)}, u32[]{:S(2)}) %collective-permute-start.13) | collective-permute-done | bytes 393248 | tf_op jit(solution)/shard_map/ppermute | solution.py:651
  100.9 1.5 collective-permute-start.17
  102.9 1.9 %all-to-all-done.3.d_mixed = bf16[16,32,512]{2,1,0:T(8,128)(2,1)S(1)} async-done(((bf16[16,32,512]{2,1,0:T(8,128)(2,1)}), bf16[16,32,512]{2,1,0:T(8,128)(2,1)S(1)}, u32[]{:S(2)}, u32[]{:S(2)}) %all-to-all-start.3) | async-done | bytes 524320 | tf_op jit(solution)/shard_map/all_to_all | solution.py:643
  104.8 12.9 %shard_map.268 = (bf16[16,96,128]{2,1,0:T(8,128)(2,1)}, bf16[2,64,128]{2,1,0:T(8,128)(2,1)S(1)}, bf16[2,64,128]{2,1,0:T(8,128)(2,1)S(1)}, bf16[2,64,128]{2,1,0:T(8,128)(2,1)S(1)}, bf16[2,64,128]{2,1,0:T(8,128)(2,1)S(1)}) custom-call(s32[6]{0:T(128)S(1)} %stack.27.place, s32[1]{0:T(128)S(6)} %copy.48.length, bf16[16,32,512]{2,1,0:T(8,128)(2,1)S(1)} %all-to-all-done.3.d_mixed, ...), custom_call_target="tpu_custom_call" | custom-call | tf_op jit(solution)/shard_map/pallas_call | solution.py:624
  117.8 4.7 %all-to-all-start.4 = ((bf16[16,96,128]{2,1,0:T(8,128)(2,1)}), bf16[16,96,128]{2,1,0:T(8,128)(2,1)S(1)}, u32[]{:S(2)}, u32[]{:S(2)}) async-start(bf16[16,96,128]{2,1,0:T(8,128)(2,1)} %shard_map.270), calls=%async_computation.4 | async-start | bytes 786432 | tf_op jit(solution)/shard_map/all_to_all | solution.py:643
  122.4 2.4 %collective-permute-start.15 = (bf16[2,64,128]{2,1,0:T(8,128)(2,1)S(1)}, bf16[2,64,128]{2,1,0:T(8,128)(2,1)S(1)}, u32[]{:S(2)}, u32[]{:S(2)}) collective-permute-start(bf16[2,64,128]{2,1,0:T(8,128)(2,1)S(1)} %get-tuple-element.72), channel_id=1, source_target_pairs={{0,32},{16,48},{32,0},{48,16},{1,33},{17,49},{33,1},{49,17},{2,34}... | collective-permute-start | bytes 98312 | tf_op jit(solution)/shard_map/ppermute | solution.py:651
  126.2 2.1 %shard_map.273.given = bf16[32,4,2176]{2,1,0:T(4,128)(2,1)} custom-call(bf16[2,64,2048]{2,1,0:T(8,128)(2,1)} %get-tuple-element.74.part0, bf16[2,64,2048]{2,1,0:T(8,128)(2,1)S(1)} %collective-permute-done.17.part1, bf16[2,64,2048]{2,1,0:T(8,128)(2,1)S(1)} %collective-permute-done.18.part2, bf16[2,64,2048]{2,1,0:T(8,128)(2,1)S(1)} %collective-permute-done.19.part3), custom_call_target="tpu_custom_call" | custom-call | tf_op jit(solution)/shard_map/pallas_call | solution.py:624
  129.1 3.5 %all-to-all-done.4.d_lin.refs_1_ = bf16[16,96,128]{2,1,0:T(8,128)(2,1)S(1)} async-done(((bf16[16,96,128]{2,1,0:T(8,128)(2,1)}), bf16[16,96,128]{2,1,0:T(8,128)(2,1)S(1)}, u32[]{:S(2)}, u32[]{:S(2)}) %all-to-all-start.4) | async-done | bytes 393248 | tf_op jit(solution)/shard_map/all_to_all | solution.py:643
  132.6 5.8 %all-to-all-start.5 = ((bf16[32,4,2176]{2,1,0:T(4,128)(2,1)}), bf16[32,4,2176]{2,1,0:T(4,128)(2,1)S(1)}, u32[]{:S(2)}, u32[]{:S(2)}) async-start(bf16[32,4,2176]{2,1,0:T(4,128)(2,1)} %shard_map.275), calls=%async_computation.5 | async-start | bytes 1114112 | tf_op jit(solution)/shard_map/all_to_all | solution.py:643
  138.4 4.5 %shard_map.271 = (f32[1,128,512]{2,1,0:T(8,128)}, bf16[1,128,512]{2,1,0:T(8,128)(2,1)}) custom-call(s32[6]{0:T(128)S(1)} %stack.27.place, s32[1]{0:T(128)S(6)} %copy.48.length, bf16[1,128,512]{2,1,0:T(8,128)(2,1)} %tokens.3, bf16[16,96,128]{2,1,0:T(8,128)(2,1)S(1)} %all-to-all-done.4.d_lin.refs_1_, bf16[2,64,1536]{2,1,0:T(8,128)(2,1)} %shard_map.262.other1.rows0, ...), custom_call_target="tpu_custom_call" | custom-call | tf_op jit(solution)/shard_map/pallas_call | solution.py:624
  142.9 7.3 %all-to-all-done.5.parts = bf16[32,4,2176]{2,1,0:T(4,128)(2,1)S(1)} async-done(((bf16[32,4,2176]{2,1,0:T(4,128)(2,1)}), bf16[32,4,2176]{2,1,0:T(4,128)(2,1)S(1)}, u32[]{:S(2)}, u32[]{:S(2)}) %all-to-all-start.5) | async-done | bytes 557088 | tf_op jit(solution)/shard_map/all_to_all | solution.py:643
  (51 shorter events, 9.2 us)
Async XLA Ops:
  2.9 8.5 %copy-start.2 = (bf16[1,128,512]{2,1,0:T(8,128)(2,1)S(1)}, bf16[1,128,512]{2,1,0:T(8,128)(2,1)}, u32[]{:S(2)}) copy-start(bf16[1,128,512]{2,1,0:T(8,128)(2,1)} %param.29) | copy-start | bytes 393220
  2.9 29.7 %all-to-all-start = ((bf16[8,176,512]{2,1,0:T(8,128)(2,1)}), bf16[8,176,512]{2,1,0:T(8,128)(2,1)S(1)}, u32[]{:S(2)}, u32[]{:S(2)}) async-start(bf16[8,176,512]{2,1,0:T(8,128)(2,1)} %shard_map.255), calls=%async_computation | async-start | bytes 2883584 | tf_op jit(solution)/shard_map/all_to_all | solution.py:643
  11.4 21.2 %collective-permute-start = (bf16[1,128,512]{2,1,0:T(8,128)(2,1)S(1)}, bf16[1,128,512]{2,1,0:T(8,128)(2,1)S(1)}, u32[]{:S(2)}, u32[]{:S(2)}) collective-permute-start(bf16[1,128,512]{2,1,0:T(8,128)(2,1)S(1)} %copy-done.2), channel_id=1, source_target_pairs={{0,2},{2,0},{1,3},{3,1},{4,6},{6,4},{5,7},{7,5},{8,10},{10,8},{9,1... | collective-permute-start | bytes 393224 | tf_op jit(solution)/shard_map/ppermute | solution.py:647
  32.6 6.0 %copy-start = (bf16[2,128,512]{2,1,0:T(8,128)(2,1)}, bf16[2,128,512]{2,1,0:T(8,128)(2,1)S(1)}, u32[]{:S(2)}) copy-start(bf16[2,128,512]{2,1,0:T(8,128)(2,1)S(1)} %constant_dynamic-update-slice_fusion.refs_1_.cot_near) | copy-start | bytes 786436
  32.6 3.3 %collective-permute-start.1 = (bf16[8,48,512]{2,1,0:T(8,128)(2,1)S(1)}, bf16[8,48,512]{2,1,0:T(8,128)(2,1)S(1)}, u32[]{:S(2)}, u32[]{:S(2)}) collective-permute-start(bf16[8,48,512]{2,1,0:T(8,128)(2,1)S(1)} %shard_map.257.near), channel_id=1, source_target_pairs={{0,1},{1,0},{2,3},{3,2},{4,5},{5,4},{6,7},{7,6},{8,9},{9,8},{10,11... | collective-permute-start | bytes 1179656 | tf_op jit(solution)/shard_map/ppermute | solution.py:647
  37.5 15.0 %collective-permute-start.2 = (bf16[8,176,512]{2,1,0:T(8,128)(2,1)S(1)}, bf16[8,176,512]{2,1,0:T(8,128)(2,1)S(1)}, u32[]{:S(2)}, u32[]{:S(2)}) collective-permute-start(bf16[8,176,512]{2,1,0:T(8,128)(2,1)S(1)} %shard_map.259.near), channel_id=1, source_target_pairs={{0,1},{1,0},{2,3},{3,2},{4,5},{5,4},{6,7},{7,6},{8,9},{9,8},{10,11... | collective-permute-start | bytes 4325384 | tf_op jit(solution)/shard_map/ppermute | solution.py:647
  37.8 8.0 %collective-permute-start.5 = (bf16[1,64,2048]{2,1,0:T(8,128)(2,1)}, bf16[1,64,2048]{2,1,0:T(8,128)(2,1)S(1)}, u32[]{:S(2)}, u32[]{:S(2)}) collective-permute-start(bf16[1,64,2048]{2,1,0:T(8,128)(2,1)} %get-tuple-element.55.own), channel_id=1, source_target_pairs={{0,64},{64,0},{1,65},{65,1},{2,66},{66,2},{3,67},{67,3},{4,68},{68... | collective-permute-start | bytes 786440 | tf_op jit(solution)/shard_map/ppermute | solution.py:647
  38.6 12.7 %collective-permute-start.3 = (bf16[2,128,512]{2,1,0:T(8,128)(2,1)S(1)}, bf16[2,128,512]{2,1,0:T(8,128)(2,1)}, u32[]{:S(2)}, u32[]{:S(2)}) collective-permute-start(bf16[2,128,512]{2,1,0:T(8,128)(2,1)S(1)} %constant_dynamic-update-slice_fusion.refs_1_.cot_near), channel_id=1, source_target_pairs={{0,1},{1,0},{2,3},{3,2},{4,5},{5,4},{6,7},{7,6},{8,9},{9,8},{10,11... | collective-permute-start | bytes 786440 | tf_op jit(solution)/shard_map/ppermute | solution.py:647
  39.0 13.4 %all-to-all-start.1 = ((bf16[8,64,128]{2,1,0:T(8,128)(2,1)}), bf16[8,64,128]{2,1,0:T(8,128)(2,1)S(1)}, u32[]{:S(2)}, u32[]{:S(2)}) async-start(bf16[8,64,128]{2,1,0:T(8,128)(2,1)} %get-tuple-element.51.refs_1_), calls=%async_computation.1 | async-start | bytes 262144 | tf_op jit(solution)/shard_map/all_to_all | solution.py:643
  44.1 16.6 %collective-permute-start.4 = (bf16[1,64,1536]{2,1,0:T(8,128)(2,1)}, bf16[1,64,1536]{2,1,0:T(8,128)(2,1)}, u32[]{:S(2)}, u32[]{:S(2)}) collective-permute-start(bf16[1,64,1536]{2,1,0:T(8,128)(2,1)} %get-tuple-element.53.own.refs_1_), channel_id=1, source_target_pairs={{0,64},{64,0},{1,65},{65,1},{2,66},{66,2},{3,67},{67,3},{4,68},{68... | collective-permute-start | bytes 589832 | tf_op jit(solution)/shard_map/ppermute | solution.py:647
  47.6 26.3 %collective-permute-start.6 = (bf16[2,64,2048]{2,1,0:T(8,128)(2,1)}, bf16[2,64,2048]{2,1,0:T(8,128)(2,1)}, u32[]{:S(2)}, u32[]{:S(2)}) collective-permute-start(bf16[2,64,2048]{2,1,0:T(8,128)(2,1)} %shard_map.265.rows0), channel_id=1, source_target_pairs={{0,16},{16,32},{32,48},{48,0},{1,17},{17,33},{33,49},{49,1},{2,18}... | collective-permute-start | bytes 1572872 | tf_op jit(solution)/shard_map/ppermute | solution.py:651
  48.8 25.1 %collective-permute-start.7 = (bf16[2,64,2048]{2,1,0:T(8,128)(2,1)}, bf16[2,64,2048]{2,1,0:T(8,128)(2,1)}, u32[]{:S(2)}, u32[]{:S(2)}) collective-permute-start(bf16[2,64,2048]{2,1,0:T(8,128)(2,1)} %shard_map.265.rows0), channel_id=1, source_target_pairs={{0,32},{16,48},{32,0},{48,16},{1,33},{17,49},{33,1},{49,17},{2,34}... | collective-permute-start | bytes 1572872 | tf_op jit(solution)/shard_map/ppermute | solution.py:651
  51.3 22.6 %collective-permute-start.8 = (bf16[2,64,2048]{2,1,0:T(8,128)(2,1)}, bf16[2,64,2048]{2,1,0:T(8,128)(2,1)}, u32[]{:S(2)}, u32[]{:S(2)}) collective-permute-start(bf16[2,64,2048]{2,1,0:T(8,128)(2,1)} %shard_map.265.rows0), channel_id=1, source_target_pairs={{0,48},{16,0},{32,16},{48,32},{1,49},{17,1},{33,17},{49,33},{2,50}... | collective-permute-start | bytes 1572872 | tf_op jit(solution)/shard_map/ppermute | solution.py:651
  60.8 17.7 %all-to-all-start.2 = ((bf16[16,32,512]{2,1,0:T(8,128)(2,1)}), bf16[16,32,512]{2,1,0:T(8,128)(2,1)S(1)}, u32[]{:S(2)}, u32[]{:S(2)}) async-start(bf16[16,32,512]{2,1,0:T(8,128)(2,1)} %shard_map.261.other), calls=%async_computation.2 | async-start | bytes 1048576 | tf_op jit(solution)/shard_map/all_to_all | solution.py:643
  69.2 19.4 %collective-permute-start.10 = (bf16[2,64,1536]{2,1,0:T(8,128)(2,1)}, bf16[2,64,1536]{2,1,0:T(8,128)(2,1)}, u32[]{:S(2)}, u32[]{:S(2)}) collective-permute-start(bf16[2,64,1536]{2,1,0:T(8,128)(2,1)} %shard_map.262.other1.rows0), channel_id=1, source_target_pairs={{0,48},{16,0},{32,16},{48,32},{1,49},{17,1},{33,17},{49,33},{2,50}... | collective-permute-start | bytes 1179656 | tf_op jit(solution)/shard_map/ppermute | solution.py:651
  69.2 19.4 %collective-permute-start.9 = (bf16[2,64,1536]{2,1,0:T(8,128)(2,1)}, bf16[2,64,1536]{2,1,0:T(8,128)(2,1)}, u32[]{:S(2)}, u32[]{:S(2)}) collective-permute-start(bf16[2,64,1536]{2,1,0:T(8,128)(2,1)} %shard_map.262.other1.rows0), channel_id=1, source_target_pairs={{0,16},{16,32},{32,48},{48,0},{1,17},{17,33},{33,49},{49,1},{2,18}... | collective-permute-start | bytes 1179656 | tf_op jit(solution)/shard_map/ppermute | solution.py:651
  87.1 6.5 %collective-permute-start.11 = (bf16[2,128,1024]{2,1,0:T(8,128)(2,1)}, bf16[2,128,1024]{2,1,0:T(8,128)(2,1)S(1)}, u32[]{:S(2)}, u32[]{:S(2)}) collective-permute-start(bf16[2,128,1024]{2,1,0:T(8,128)(2,1)} %get-tuple-element.65), channel_id=1, source_target_pairs={{0,1},{1,0},{2,3},{3,2},{4,5},{5,4},{6,7},{7,6},{8,9},{9,8},{10,11... | collective-permute-start | bytes 1572872 | tf_op jit(solution)/shard_map/ppermute | solution.py:647
  88.5 12.4 %collective-permute-start.13 = (bf16[2,64,1536]{2,1,0:T(8,128)(2,1)}, bf16[2,64,1536]{2,1,0:T(8,128)(2,1)S(1)}, u32[]{:S(2)}, u32[]{:S(2)}) collective-permute-start(bf16[2,64,1536]{2,1,0:T(8,128)(2,1)} %shard_map.262.other1.rows0), channel_id=1, source_target_pairs={{0,32},{16,48},{32,0},{48,16},{1,33},{17,49},{33,1},{49,17},{2,34}... | collective-permute-start | bytes 1179656 | tf_op jit(solution)/shard_map/ppermute | solution.py:651
  88.6 16.2 %all-to-all-start.3 = ((bf16[16,32,512]{2,1,0:T(8,128)(2,1)}), bf16[16,32,512]{2,1,0:T(8,128)(2,1)S(1)}, u32[]{:S(2)}, u32[]{:S(2)}) async-start(bf16[16,32,512]{2,1,0:T(8,128)(2,1)} %shard_map.267), calls=%async_computation.3 | async-start | bytes 1048576 | tf_op jit(solution)/shard_map/all_to_all | solution.py:643
  95.6 22.1 %collective-permute-start.12 = (bf16[128,1024]{1,0:T(8,128)(2,1)}, bf16[128,1024]{1,0:T(8,128)(2,1)S(1)}, u32[]{:S(2)}, u32[]{:S(2)}) collective-permute-start(bf16[128,1024]{1,0:T(8,128)(2,1)} %get-tuple-element.66), channel_id=1, source_target_pairs={{0,2},{2,0},{1,3},{3,1},{4,6},{6,4},{5,7},{7,5},{8,10},{10,8},{9,1... | collective-permute-start | bytes 786440 | tf_op jit(solution)/shard_map/ppermute | solution.py:647
  100.9 23.9 %collective-permute-start.19 = (bf16[2,64,2048]{2,1,0:T(8,128)(2,1)}, bf16[2,64,2048]{2,1,0:T(8,128)(2,1)S(1)}, u32[]{:S(2)}, u32[]{:S(2)}) collective-permute-start(bf16[2,64,2048]{2,1,0:T(8,128)(2,1)} %shard_map.272), channel_id=1, source_target_pairs={{0,48},{16,0},{32,16},{48,32},{1,49},{17,1},{33,17},{49,33},{2,50}... | collective-permute-start | bytes 1572872 | tf_op jit(solution)/shard_map/ppermute | solution.py:651
  100.9 25.3 %collective-permute-start.17 = (bf16[2,64,2048]{2,1,0:T(8,128)(2,1)}, bf16[2,64,2048]{2,1,0:T(8,128)(2,1)S(1)}, u32[]{:S(2)}, u32[]{:S(2)}) collective-permute-start(bf16[2,64,2048]{2,1,0:T(8,128)(2,1)} %get-tuple-element.75), channel_id=1, source_target_pairs={{0,16},{16,32},{32,48},{48,0},{1,17},{17,33},{33,49},{49,1},{2,18}... | collective-permute-start | bytes 1572872 | tf_op jit(solution)/shard_map/ppermute | solution.py:651
  102.4 23.8 %collective-permute-start.18 = (bf16[2,64,2048]{2,1,0:T(8,128)(2,1)}, bf16[2,64,2048]{2,1,0:T(8,128)(2,1)S(1)}, u32[]{:S(2)}, u32[]{:S(2)}) collective-permute-start(bf16[2,64,2048]{2,1,0:T(8,128)(2,1)} %get-tuple-element.76), channel_id=1, source_target_pairs={{0,32},{16,48},{32,0},{48,16},{1,33},{17,49},{33,1},{49,17},{2,34}... | collective-permute-start | bytes 1572872 | tf_op jit(solution)/shard_map/ppermute | solution.py:651
  117.7 10.6 %copy-start.1 = (bf16[128,1024]{1,0:T(8,128)(2,1)}, bf16[128,1024]{1,0:T(8,128)(2,1)S(1)}, u32[]{:S(2)}) copy-start(bf16[128,1024]{1,0:T(8,128)(2,1)S(1)} %collective-permute-done.12.refs_1_.w1) | copy-start | bytes 786436
  117.8 14.8 %all-to-all-start.4 = ((bf16[16,96,128]{2,1,0:T(8,128)(2,1)}), bf16[16,96,128]{2,1,0:T(8,128)(2,1)S(1)}, u32[]{:S(2)}, u32[]{:S(2)}) async-start(bf16[16,96,128]{2,1,0:T(8,128)(2,1)} %shard_map.270), calls=%async_computation.4 | async-start | bytes 786432 | tf_op jit(solution)/shard_map/all_to_all | solution.py:643
  122.4 6.0 %collective-permute-start.14 = (bf16[2,64,128]{2,1,0:T(8,128)(2,1)S(1)}, bf16[2,64,128]{2,1,0:T(8,128)(2,1)S(1)}, u32[]{:S(2)}, u32[]{:S(2)}) collective-permute-start(bf16[2,64,128]{2,1,0:T(8,128)(2,1)S(1)} %get-tuple-element.71), channel_id=1, source_target_pairs={{0,16},{16,32},{32,48},{48,0},{1,17},{17,33},{33,49},{49,1},{2,18}... | collective-permute-start | bytes 98312 | tf_op jit(solution)/shard_map/ppermute | solution.py:651
  122.4 6.0 %collective-permute-start.15 = (bf16[2,64,128]{2,1,0:T(8,128)(2,1)S(1)}, bf16[2,64,128]{2,1,0:T(8,128)(2,1)S(1)}, u32[]{:S(2)}, u32[]{:S(2)}) collective-permute-start(bf16[2,64,128]{2,1,0:T(8,128)(2,1)S(1)} %get-tuple-element.72), channel_id=1, source_target_pairs={{0,32},{16,48},{32,0},{48,16},{1,33},{17,49},{33,1},{49,17},{2,34}... | collective-permute-start | bytes 98312 | tf_op jit(solution)/shard_map/ppermute | solution.py:651
  124.9 3.5 %collective-permute-start.16 = (bf16[2,64,128]{2,1,0:T(8,128)(2,1)S(1)}, bf16[2,64,128]{2,1,0:T(8,128)(2,1)S(1)}, u32[]{:S(2)}, u32[]{:S(2)}) collective-permute-start(bf16[2,64,128]{2,1,0:T(8,128)(2,1)S(1)} %get-tuple-element.73), channel_id=1, source_target_pairs={{0,48},{16,0},{32,16},{48,32},{1,49},{17,1},{33,17},{49,33},{2,50}... | collective-permute-start | bytes 98312 | tf_op jit(solution)/shard_map/ppermute | solution.py:651
  132.6 17.7 %all-to-all-start.5 = ((bf16[32,4,2176]{2,1,0:T(4,128)(2,1)}), bf16[32,4,2176]{2,1,0:T(4,128)(2,1)S(1)}, u32[]{:S(2)}, u32[]{:S(2)}) async-start(bf16[32,4,2176]{2,1,0:T(4,128)(2,1)} %shard_map.275), calls=%async_computation.5 | async-start | bytes 1114112 | tf_op jit(solution)/shard_map/all_to_all | solution.py:643

commit v9 on v8

--- a/solution.py
+++ b/solution.py
@@ -518,7 +518,6 @@
     total = total.reshape(2 * 64, FEED_LANES)
     for d in range(SEQ * 2):
         sent[d, :, :FEED_LANES] = total[4 * d : 4 * d + 4].astype(bf16)
-        sent[d, :, FEED_LANES:] = jnp.zeros((4, 128), bf16)
 
 
 def append_kernel(part0, part1, part2, part3, given, sent, rows, left):

time: 152 us -> 152 us (level)
  no operation moved by 1% of the time
where the time goes in v9:
time: 152 us; the launch traced here: 151 us
  starting transfers between devices  59.4 us (39%)
  Pallas kernels  50.9 us (33%)
  waiting for transfers between devices  39.5 us (26%)
    pallas_call x14, Pallas kernels, run(): inner(*(pltpu.with_memory_space_constraint(x, pltpu.HBM if where in 'HA'...  50.9 us
    all_to_all x6, starting transfers between devices, exchange(): return lax.all_to_all(value, axes, 0, 0, tiled=True)  35.1 us
    ppermute x8, waiting for transfers between devices, swap(): return lax.ppermute(value, axis, [(0, 1), (1, 0)])  19.6 us
    all_to_all x6, waiting for transfers between devices, exchange(): return lax.all_to_all(value, axes, 0, 0, tiled=True)  17.4 us
    ppermute x8, starting transfers between devices, swap(): return lax.ppermute(value, axis, [(0, 1), (1, 0)])  12.3 us
    ppermute x12, starting transfers between devices, shift(): return lax.ppermute(value, 'x', [(i, (i + by) % 4) for i in range(4)])  12 us
  transfers between devices with their start and end apart: 26, of which 9 were waited for; matrix products, arithmetic and copies ran while one was open for 0% of the time, Pallas kernels for 30%

profile of v9, /device:TPU:1, one launch (start us, length us, event | category | flops | bytes accessed | tf_op | source)
XLA Modules:
  0.0 151.4 jit_solution(16346415964304152074)
XLA Ops:
  0.6 2.2 %shard_map.255 = bf16[8,176,512]{2,1,0:T(8,128)(2,1)} custom-call(bf16[1,128,512]{2,1,0:T(8,128)(2,1)} %tokens.3, bf16[4,512]{1,0:T(4,128)(2,1)} %w_query.1, bf16[4,512]{1,0:T(4,128)(2,1)} %w_key.1, bf16[4,512]{1,0:T(4,128)(2,1)} %w_value.1, bf16[4,512]{1,0:T(4,128)(2,1)} %w_output.1, bf16[4,2048]{1,0:T(4,128)(2,1)} %w_gate.1, bf16[4,2048]{1,0:T(4,128)(2,1)} %w_up.1, ...), custom_call_target="tpu_custom_call" | custom-call | tf_op jit(solution)/shard_map/pallas_call | solution.py:623
  2.9 8.5 %all-to-all-start = ((bf16[8,176,512]{2,1,0:T(8,128)(2,1)}), bf16[8,176,512]{2,1,0:T(8,128)(2,1)S(1)}, u32[]{:S(2)}, u32[]{:S(2)}) async-start(bf16[8,176,512]{2,1,0:T(8,128)(2,1)} %shard_map.255), calls=%async_computation | async-start | bytes 2883584 | tf_op jit(solution)/shard_map/all_to_all | solution.py:642
  11.4 3.0 %collective-permute-start = (bf16[1,128,512]{2,1,0:T(8,128)(2,1)S(1)}, bf16[1,128,512]{2,1,0:T(8,128)(2,1)S(1)}, u32[]{:S(2)}, u32[]{:S(2)}) collective-permute-start(bf16[1,128,512]{2,1,0:T(8,128)(2,1)S(1)} %copy-done.2), channel_id=1, source_target_pairs={{0,2},{2,0},{1,3},{3,1},{4,6},{6,4},{5,7},{7,5},{8,10},{10,8},{9,1... | collective-permute-start | bytes 393224 | tf_op jit(solution)/shard_map/ppermute | solution.py:646
  14.3 18.2 %collective-permute-done = bf16[1,128,512]{2,1,0:T(8,128)(2,1)S(1)} collective-permute-done((bf16[1,128,512]{2,1,0:T(8,128)(2,1)S(1)}, bf16[1,128,512]{2,1,0:T(8,128)(2,1)S(1)}, u32[]{:S(2)}, u32[]{:S(2)}) %collective-permute-start) | collective-permute-done | bytes 131104 | tf_op jit(solution)/shard_map/ppermute | solution.py:646
  32.6 1.9 %collective-permute-start.1 = (bf16[8,48,512]{2,1,0:T(8,128)(2,1)S(1)}, bf16[8,48,512]{2,1,0:T(8,128)(2,1)S(1)}, u32[]{:S(2)}, u32[]{:S(2)}) collective-permute-start(bf16[8,48,512]{2,1,0:T(8,128)(2,1)S(1)} %shard_map.257.near), channel_id=1, source_target_pairs={{0,1},{1,0},{2,3},{3,2},{4,5},{5,4},{6,7},{7,6},{8,9},{9,8},{10,11... | collective-permute-start | bytes 1179656 | tf_op jit(solution)/shard_map/ppermute | solution.py:646
  35.9 1.5 %shard_map.258 = (bf16[1,64,2048]{2,1,0:T(8,128)(2,1)}, bf16[8,64,128]{2,1,0:T(8,128)(2,1)}, bf16[1,64,1536]{2,1,0:T(8,128)(2,1)}) custom-call(s32[6]{0:T(128)S(1)} %stack.27.place, bf16[8,48,512]{2,1,0:T(8,128)(2,1)S(1)} %shard_map.257.near, bf16[8,48,512]{2,1,0:T(8,128)(2,1)S(1)} %collective-permute-done.1.far), custom_call_target="tpu_custom_call" | custom-call | tf_op jit(solution)/shard_map/pallas_call | solution.py:623
  39.0 4.5 %all-to-all-start.1 = ((bf16[8,64,128]{2,1,0:T(8,128)(2,1)}), bf16[8,64,128]{2,1,0:T(8,128)(2,1)S(1)}, u32[]{:S(2)}, u32[]{:S(2)}) async-start(bf16[8,64,128]{2,1,0:T(8,128)(2,1)} %get-tuple-element.51.refs_1_), calls=%async_computation.1 | async-start | bytes 262144 | tf_op jit(solution)/shard_map/all_to_all | solution.py:642
  44.1 1.5 %collective-permute-start.4 = (bf16[1,64,1536]{2,1,0:T(8,128)(2,1)}, bf16[1,64,1536]{2,1,0:T(8,128)(2,1)}, u32[]{:S(2)}, u32[]{:S(2)}) collective-permute-start(bf16[1,64,1536]{2,1,0:T(8,128)(2,1)} %get-tuple-element.53.own.refs_1_), channel_id=1, source_target_pairs={{0,64},{64,0},{1,65},{65,1},{2,66},{66,2},{3,67},{67,3},{4,68},{68... | collective-permute-start | bytes 589832 | tf_op jit(solution)/shard_map/ppermute | solution.py:646
  45.8 1.8 %shard_map.265.rows0 = bf16[2,64,2048]{2,1,0:T(8,128)(2,1)} custom-call(bf16[1,64,2048]{2,1,0:T(8,128)(2,1)} %get-tuple-element.55.own, bf16[1,64,2048]{2,1,0:T(8,128)(2,1)S(1)} %shard_map.264.other), custom_call_target="tpu_custom_call" | custom-call | tf_op jit(solution)/shard_map/pallas_call | solution.py:623
  48.8 2.5 %collective-permute-start.7 = (bf16[2,64,2048]{2,1,0:T(8,128)(2,1)}, bf16[2,64,2048]{2,1,0:T(8,128)(2,1)}, u32[]{:S(2)}, u32[]{:S(2)}) collective-permute-start(bf16[2,64,2048]{2,1,0:T(8,128)(2,1)} %shard_map.265.rows0), channel_id=1, source_target_pairs={{0,32},{16,48},{32,0},{48,16},{1,33},{17,49},{33,1},{49,17},{2,34}... | collective-permute-start | bytes 1572872 | tf_op jit(solution)/shard_map/ppermute | solution.py:650
  52.4 8.3 %shard_map.260 = (bf16[16,32,512]{2,1,0:T(8,128)(2,1)}, bf16[32,2048]{1,0:T(8,128)(2,1)}, bf16[32,2048]{1,0:T(8,128)(2,1)}, bf16[32,2048]{1,0:T(8,128)(2,1)}, f3...) custom-call(s32[6]{0:T(128)S(1)} %stack.27.place, s32[1]{0:T(128)S(6)} %copy.48.length, ...), custom_call_target="tpu_custom_call" | custom-call | flops 19000000512 | tf_op jit(solution)/shard_map/pallas_call | solution.py:623
  60.8 6.6 %all-to-all-start.2 = ((bf16[16,32,512]{2,1,0:T(8,128)(2,1)}), bf16[16,32,512]{2,1,0:T(8,128)(2,1)S(1)}, u32[]{:S(2)}, u32[]{:S(2)}) async-start(bf16[16,32,512]{2,1,0:T(8,128)(2,1)} %shard_map.261.other), calls=%async_computation.2 | async-start | bytes 1048576 | tf_op jit(solution)/shard_map/all_to_all | solution.py:642
  67.4 1.8 %shard_map.262.other1.rows0 = bf16[2,64,1536]{2,1,0:T(8,128)(2,1)} custom-call(bf16[1,64,1536]{2,1,0:T(8,128)(2,1)} %get-tuple-element.53.own.refs_1_, bf16[1,64,1536]{2,1,0:T(8,128)(2,1)} %collective-permute-done.4.refs_1_.other), custom_call_target="tpu_custom_call" | custom-call | tf_op jit(solution)/shard_map/pallas_call | solution.py:623
  69.2 1.5 collective-permute-start.9
  70.7 3.2 %shard_map.263.other2.scaled = bf16[16,128,512]{2,1,0:T(8,128)(2,1)} custom-call(s32[6]{0:T(128)S(1)} %stack.27.place, bf16[8,176,512]{2,1,0:T(8,128)(2,1)S(1)} %shard_map.259.near, bf16[8,176,512]{2,1,0:T(8,128)(2,1)S(1)} %collective-permute-done.2.far, bf16[16,32,512]{2,1,0:T(8,128)(2,1)} %shard_map.261.other), custom_call_target="tpu_custom_call" | custom-call | tf_op jit(solution)/shard_map/pallas_call | solution.py:623
  73.9 4.6 %all-to-all-done.2.mixed = bf16[16,32,512]{2,1,0:T(8,128)(2,1)S(1)} async-done(((bf16[16,32,512]{2,1,0:T(8,128)(2,1)}), bf16[16,32,512]{2,1,0:T(8,128)(2,1)S(1)}, u32[]{:S(2)}, u32[]{:S(2)}) %all-to-all-start.2) | async-done | bytes 524320 | tf_op jit(solution)/shard_map/all_to_all | solution.py:642
  78.5 8.6 %shard_map.266 = (bf16[16,32,512]{2,1,0:T(8,128)(2,1)}, bf16[2,128,1024]{2,1,0:T(8,128)(2,1)}, bf16[2,128,1024]{2,1,0:T(8,128)(2,1)}, bf16[2,64,2048]{2,1,0:T(8,...) custom-call(s32[6]{0:T(128)S(1)} %stack.27.place, ...), custom_call_target="tpu_custom_call" | custom-call | tf_op jit(solution)/shard_map/pallas_call | solution.py:623
  87.1 1.4 collective-permute-start.11
  88.6 5.1 %all-to-all-start.3 = ((bf16[16,32,512]{2,1,0:T(8,128)(2,1)}), bf16[16,32,512]{2,1,0:T(8,128)(2,1)S(1)}, u32[]{:S(2)}, u32[]{:S(2)}) async-start(bf16[16,32,512]{2,1,0:T(8,128)(2,1)} %shard_map.267), calls=%async_computation.3 | async-start | bytes 1048576 | tf_op jit(solution)/shard_map/all_to_all | solution.py:642
  93.7 1.9 %shard_map.269 = (bf16[128,1024]{1,0:T(8,128)(2,1)}, bf16[128,1024]{1,0:T(8,128)(2,1)}) custom-call(bf16[2,128,1024]{2,1,0:T(8,128)(2,1)} %get-tuple-element.64.kept, bf16[2,128,1024]{2,1,0:T(8,128)(2,1)S(1)} %collective-permute-done.11.arrived), custom_call_target="tpu_custom_call" | custom-call | tf_op jit(solution)/shard_map/pallas_call | solution.py:623
  95.6 2.9 %collective-permute-start.12 = (bf16[128,1024]{1,0:T(8,128)(2,1)}, bf16[128,1024]{1,0:T(8,128)(2,1)S(1)}, u32[]{:S(2)}, u32[]{:S(2)}) collective-permute-start(bf16[128,1024]{1,0:T(8,128)(2,1)} %get-tuple-element.66), channel_id=1, source_target_pairs={{0,2},{2,0},{1,3},{3,1},{4,6},{6,4},{5,7},{7,5},{8,10},{10,8},{9,1... | collective-permute-start | bytes 786440 | tf_op jit(solution)/shard_map/ppermute | solution.py:646
  98.5 2.4 %collective-permute-done.13.rows2.refs_1_ = bf16[2,64,1536]{2,1,0:T(8,128)(2,1)S(1)} collective-permute-done((bf16[2,64,1536]{2,1,0:T(8,128)(2,1)}, bf16[2,64,1536]{2,1,0:T(8,128)(2,1)S(1)}, u32[]{:S(2)}, u32[]{:S(2)}) %collective-permute-start.13) | collective-permute-done | bytes 393248 | tf_op jit(solution)/shard_map/ppermute | solution.py:650
  100.9 1.5 collective-permute-start.17
  102.9 1.9 %all-to-all-done.3.d_mixed = bf16[16,32,512]{2,1,0:T(8,128)(2,1)S(1)} async-done(((bf16[16,32,512]{2,1,0:T(8,128)(2,1)}), bf16[16,32,512]{2,1,0:T(8,128)(2,1)S(1)}, u32[]{:S(2)}, u32[]{:S(2)}) %all-to-all-start.3) | async-done | bytes 524320 | tf_op jit(solution)/shard_map/all_to_all | solution.py:642
  104.8 12.9 %shard_map.268 = (bf16[16,96,128]{2,1,0:T(8,128)(2,1)}, bf16[2,64,128]{2,1,0:T(8,128)(2,1)S(1)}, bf16[2,64,128]{2,1,0:T(8,128)(2,1)S(1)}, bf16[2,64,128]{2,1,0:T(8,128)(2,1)S(1)}, bf16[2,64,128]{2,1,0:T(8,128)(2,1)S(1)}) custom-call(s32[6]{0:T(128)S(1)} %stack.27.place, s32[1]{0:T(128)S(6)} %copy.48.length, bf16[16,32,512]{2,1,0:T(8,128)(2,1)S(1)} %all-to-all-done.3.d_mixed, ...), custom_call_target="tpu_custom_call" | custom-call | tf_op jit(solution)/shard_map/pallas_call | solution.py:623
  117.8 4.7 %all-to-all-start.4 = ((bf16[16,96,128]{2,1,0:T(8,128)(2,1)}), bf16[16,96,128]{2,1,0:T(8,128)(2,1)S(1)}, u32[]{:S(2)}, u32[]{:S(2)}) async-start(bf16[16,96,128]{2,1,0:T(8,128)(2,1)} %shard_map.270), calls=%async_computation.4 | async-start | bytes 786432 | tf_op jit(solution)/shard_map/all_to_all | solution.py:642
  122.4 2.4 %collective-permute-start.15 = (bf16[2,64,128]{2,1,0:T(8,128)(2,1)S(1)}, bf16[2,64,128]{2,1,0:T(8,128)(2,1)S(1)}, u32[]{:S(2)}, u32[]{:S(2)}) collective-permute-start(bf16[2,64,128]{2,1,0:T(8,128)(2,1)S(1)} %get-tuple-element.72), channel_id=1, source_target_pairs={{0,32},{16,48},{32,0},{48,16},{1,33},{17,49},{33,1},{49,17},{2,34}... | collective-permute-start | bytes 98312 | tf_op jit(solution)/shard_map/ppermute | solution.py:650
  126.2 2.1 %shard_map.273.given = bf16[32,4,2176]{2,1,0:T(4,128)(2,1)} custom-call(bf16[2,64,2048]{2,1,0:T(8,128)(2,1)} %get-tuple-element.74.part0, bf16[2,64,2048]{2,1,0:T(8,128)(2,1)S(1)} %collective-permute-done.17.part1, bf16[2,64,2048]{2,1,0:T(8,128)(2,1)S(1)} %collective-permute-done.18.part2, bf16[2,64,2048]{2,1,0:T(8,128)(2,1)S(1)} %collective-permute-done.19.part3), custom_call_target="tpu_custom_call" | custom-call | tf_op jit(solution)/shard_map/pallas_call | solution.py:623
  129.1 3.5 %all-to-all-done.4.d_lin.refs_1_ = bf16[16,96,128]{2,1,0:T(8,128)(2,1)S(1)} async-done(((bf16[16,96,128]{2,1,0:T(8,128)(2,1)}), bf16[16,96,128]{2,1,0:T(8,128)(2,1)S(1)}, u32[]{:S(2)}, u32[]{:S(2)}) %all-to-all-start.4) | async-done | bytes 393248 | tf_op jit(solution)/shard_map/all_to_all | solution.py:642
  132.6 5.8 %all-to-all-start.5 = ((bf16[32,4,2176]{2,1,0:T(4,128)(2,1)}), bf16[32,4,2176]{2,1,0:T(4,128)(2,1)S(1)}, u32[]{:S(2)}, u32[]{:S(2)}) async-start(bf16[32,4,2176]{2,1,0:T(4,128)(2,1)} %shard_map.275), calls=%async_computation.5 | async-start | bytes 1114112 | tf_op jit(solution)/shard_map/all_to_all | solution.py:642
  138.4 4.5 %shard_map.271 = (f32[1,128,512]{2,1,0:T(8,128)}, bf16[1,128,512]{2,1,0:T(8,128)(2,1)}) custom-call(s32[6]{0:T(128)S(1)} %stack.27.place, s32[1]{0:T(128)S(6)} %copy.48.length, bf16[1,128,512]{2,1,0:T(8,128)(2,1)} %tokens.3, bf16[16,96,128]{2,1,0:T(8,128)(2,1)S(1)} %all-to-all-done.4.d_lin.refs_1_, bf16[2,64,1536]{2,1,0:T(8,128)(2,1)} %shard_map.262.other1.rows0, ...), custom_call_target="tpu_custom_call" | custom-call | tf_op jit(solution)/shard_map/pallas_call | solution.py:623
  142.9 7.3 %all-to-all-done.5.parts = bf16[32,4,2176]{2,1,0:T(4,128)(2,1)S(1)} async-done(((bf16[32,4,2176]{2,1,0:T(4,128)(2,1)}), bf16[32,4,2176]{2,1,0:T(4,128)(2,1)S(1)}, u32[]{:S(2)}, u32[]{:S(2)}) %all-to-all-start.5) | async-done | bytes 557088 | tf_op jit(solution)/shard_map/all_to_all | solution.py:642
  (51 shorter events, 9.2 us)
Async XLA Ops:
  2.9 8.5 %copy-start.2 = (bf16[1,128,512]{2,1,0:T(8,128)(2,1)S(1)}, bf16[1,128,512]{2,1,0:T(8,128)(2,1)}, u32[]{:S(2)}) copy-start(bf16[1,128,512]{2,1,0:T(8,128)(2,1)} %param.29) | copy-start | bytes 393220
  2.9 29.7 %all-to-all-start = ((bf16[8,176,512]{2,1,0:T(8,128)(2,1)}), bf16[8,176,512]{2,1,0:T(8,128)(2,1)S(1)}, u32[]{:S(2)}, u32[]{:S(2)}) async-start(bf16[8,176,512]{2,1,0:T(8,128)(2,1)} %shard_map.255), calls=%async_computation | async-start | bytes 2883584 | tf_op jit(solution)/shard_map/all_to_all | solution.py:642
  11.4 21.2 %collective-permute-start = (bf16[1,128,512]{2,1,0:T(8,128)(2,1)S(1)}, bf16[1,128,512]{2,1,0:T(8,128)(2,1)S(1)}, u32[]{:S(2)}, u32[]{:S(2)}) collective-permute-start(bf16[1,128,512]{2,1,0:T(8,128)(2,1)S(1)} %copy-done.2), channel_id=1, source_target_pairs={{0,2},{2,0},{1,3},{3,1},{4,6},{6,4},{5,7},{7,5},{8,10},{10,8},{9,1... | collective-permute-start | bytes 393224 | tf_op jit(solution)/shard_map/ppermute | solution.py:646
  32.6 6.0 %copy-start = (bf16[2,128,512]{2,1,0:T(8,128)(2,1)}, bf16[2,128,512]{2,1,0:T(8,128)(2,1)S(1)}, u32[]{:S(2)}) copy-start(bf16[2,128,512]{2,1,0:T(8,128)(2,1)S(1)} %constant_dynamic-update-slice_fusion.refs_1_.cot_near) | copy-start | bytes 786436
  32.6 3.3 %collective-permute-start.1 = (bf16[8,48,512]{2,1,0:T(8,128)(2,1)S(1)}, bf16[8,48,512]{2,1,0:T(8,128)(2,1)S(1)}, u32[]{:S(2)}, u32[]{:S(2)}) collective-permute-start(bf16[8,48,512]{2,1,0:T(8,128)(2,1)S(1)} %shard_map.257.near), channel_id=1, source_target_pairs={{0,1},{1,0},{2,3},{3,2},{4,5},{5,4},{6,7},{7,6},{8,9},{9,8},{10,11... | collective-permute-start | bytes 1179656 | tf_op jit(solution)/shard_map/ppermute | solution.py:646
  37.5 15.0 %collective-permute-start.2 = (bf16[8,176,512]{2,1,0:T(8,128)(2,1)S(1)}, bf16[8,176,512]{2,1,0:T(8,128)(2,1)S(1)}, u32[]{:S(2)}, u32[]{:S(2)}) collective-permute-start(bf16[8,176,512]{2,1,0:T(8,128)(2,1)S(1)} %shard_map.259.near), channel_id=1, source_target_pairs={{0,1},{1,0},{2,3},{3,2},{4,5},{5,4},{6,7},{7,6},{8,9},{9,8},{10,11... | collective-permute-start | bytes 4325384 | tf_op jit(solution)/shard_map/ppermute | solution.py:646
  37.8 8.0 %collective-permute-start.5 = (bf16[1,64,2048]{2,1,0:T(8,128)(2,1)}, bf16[1,64,2048]{2,1,0:T(8,128)(2,1)S(1)}, u32[]{:S(2)}, u32[]{:S(2)}) collective-permute-start(bf16[1,64,2048]{2,1,0:T(8,128)(2,1)} %get-tuple-element.55.own), channel_id=1, source_target_pairs={{0,64},{64,0},{1,65},{65,1},{2,66},{66,2},{3,67},{67,3},{4,68},{68... | collective-permute-start | bytes 786440 | tf_op jit(solution)/shard_map/ppermute | solution.py:646
  38.6 12.7 %collective-permute-start.3 = (bf16[2,128,512]{2,1,0:T(8,128)(2,1)S(1)}, bf16[2,128,512]{2,1,0:T(8,128)(2,1)}, u32[]{:S(2)}, u32[]{:S(2)}) collective-permute-start(bf16[2,128,512]{2,1,0:T(8,128)(2,1)S(1)} %constant_dynamic-update-slice_fusion.refs_1_.cot_near), channel_id=1, source_target_pairs={{0,1},{1,0},{2,3},{3,2},{4,5},{5,4},{6,7},{7,6},{8,9},{9,8},{10,11... | collective-permute-start | bytes 786440 | tf_op jit(solution)/shard_map/ppermute | solution.py:646
  39.0 13.4 %all-to-all-start.1 = ((bf16[8,64,128]{2,1,0:T(8,128)(2,1)}), bf16[8,64,128]{2,1,0:T(8,128)(2,1)S(1)}, u32[]{:S(2)}, u32[]{:S(2)}) async-start(bf16[8,64,128]{2,1,0:T(8,128)(2,1)} %get-tuple-element.51.refs_1_), calls=%async_computation.1 | async-start | bytes 262144 | tf_op jit(solution)/shard_map/all_to_all | solution.py:642
  44.1 16.6 %collective-permute-start.4 = (bf16[1,64,1536]{2,1,0:T(8,128)(2,1)}, bf16[1,64,1536]{2,1,0:T(8,128)(2,1)}, u32[]{:S(2)}, u32[]{:S(2)}) collective-permute-start(bf16[1,64,1536]{2,1,0:T(8,128)(2,1)} %get-tuple-element.53.own.refs_1_), channel_id=1, source_target_pairs={{0,64},{64,0},{1,65},{65,1},{2,66},{66,2},{3,67},{67,3},{4,68},{68... | collective-permute-start | bytes 589832 | tf_op jit(solution)/shard_map/ppermute | solution.py:646
  47.6 26.3 %collective-permute-start.6 = (bf16[2,64,2048]{2,1,0:T(8,128)(2,1)}, bf16[2,64,2048]{2,1,0:T(8,128)(2,1)}, u32[]{:S(2)}, u32[]{:S(2)}) collective-permute-start(bf16[2,64,2048]{2,1,0:T(8,128)(2,1)} %shard_map.265.rows0), channel_id=1, source_target_pairs={{0,16},{16,32},{32,48},{48,0},{1,17},{17,33},{33,49},{49,1},{2,18}... | collective-permute-start | bytes 1572872 | tf_op jit(solution)/shard_map/ppermute | solution.py:650
  48.8 25.1 %collective-permute-start.7 = (bf16[2,64,2048]{2,1,0:T(8,128)(2,1)}, bf16[2,64,2048]{2,1,0:T(8,128)(2,1)}, u32[]{:S(2)}, u32[]{:S(2)}) collective-permute-start(bf16[2,64,2048]{2,1,0:T(8,128)(2,1)} %shard_map.265.rows0), channel_id=1, source_target_pairs={{0,32},{16,48},{32,0},{48,16},{1,33},{17,49},{33,1},{49,17},{2,34}... | collective-permute-start | bytes 1572872 | tf_op jit(solution)/shard_map/ppermute | solution.py:650
  51.3 22.6 %collective-permute-start.8 = (bf16[2,64,2048]{2,1,0:T(8,128)(2,1)}, bf16[2,64,2048]{2,1,0:T(8,128)(2,1)}, u32[]{:S(2)}, u32[]{:S(2)}) collective-permute-start(bf16[2,64,2048]{2,1,0:T(8,128)(2,1)} %shard_map.265.rows0), channel_id=1, source_target_pairs={{0,48},{16,0},{32,16},{48,32},{1,49},{17,1},{33,17},{49,33},{2,50}... | collective-permute-start | bytes 1572872 | tf_op jit(solution)/shard_map/ppermute | solution.py:650
  60.8 17.7 %all-to-all-start.2 = ((bf16[16,32,512]{2,1,0:T(8,128)(2,1)}), bf16[16,32,512]{2,1,0:T(8,128)(2,1)S(1)}, u32[]{:S(2)}, u32[]{:S(2)}) async-start(bf16[16,32,512]{2,1,0:T(8,128)(2,1)} %shard_map.261.other), calls=%async_computation.2 | async-start | bytes 1048576 | tf_op jit(solution)/shard_map/all_to_all | solution.py:642
  69.2 19.4 %collective-permute-start.10 = (bf16[2,64,1536]{2,1,0:T(8,128)(2,1)}, bf16[2,64,1536]{2,1,0:T(8,128)(2,1)}, u32[]{:S(2)}, u32[]{:S(2)}) collective-permute-start(bf16[2,64,1536]{2,1,0:T(8,128)(2,1)} %shard_map.262.other1.rows0), channel_id=1, source_target_pairs={{0,48},{16,0},{32,16},{48,32},{1,49},{17,1},{33,17},{49,33},{2,50}... | collective-permute-start | bytes 1179656 | tf_op jit(solution)/shard_map/ppermute | solution.py:650
  69.2 19.4 %collective-permute-start.9 = (bf16[2,64,1536]{2,1,0:T(8,128)(2,1)}, bf16[2,64,1536]{2,1,0:T(8,128)(2,1)}, u32[]{:S(2)}, u32[]{:S(2)}) collective-permute-start(bf16[2,64,1536]{2,1,0:T(8,128)(2,1)} %shard_map.262.other1.rows0), channel_id=1, source_target_pairs={{0,16},{16,32},{32,48},{48,0},{1,17},{17,33},{33,49},{49,1},{2,18}... | collective-permute-start | bytes 1179656 | tf_op jit(solution)/shard_map/ppermute | solution.py:650
  87.1 6.5 %collective-permute-start.11 = (bf16[2,128,1024]{2,1,0:T(8,128)(2,1)}, bf16[2,128,1024]{2,1,0:T(8,128)(2,1)S(1)}, u32[]{:S(2)}, u32[]{:S(2)}) collective-permute-start(bf16[2,128,1024]{2,1,0:T(8,128)(2,1)} %get-tuple-element.65), channel_id=1, source_target_pairs={{0,1},{1,0},{2,3},{3,2},{4,5},{5,4},{6,7},{7,6},{8,9},{9,8},{10,11... | collective-permute-start | bytes 1572872 | tf_op jit(solution)/shard_map/ppermute | solution.py:646
  88.5 12.4 %collective-permute-start.13 = (bf16[2,64,1536]{2,1,0:T(8,128)(2,1)}, bf16[2,64,1536]{2,1,0:T(8,128)(2,1)S(1)}, u32[]{:S(2)}, u32[]{:S(2)}) collective-permute-start(bf16[2,64,1536]{2,1,0:T(8,128)(2,1)} %shard_map.262.other1.rows0), channel_id=1, source_target_pairs={{0,32},{16,48},{32,0},{48,16},{1,33},{17,49},{33,1},{49,17},{2,34}... | collective-permute-start | bytes 1179656 | tf_op jit(solution)/shard_map/ppermute | solution.py:650
  88.6 16.2 %all-to-all-start.3 = ((bf16[16,32,512]{2,1,0:T(8,128)(2,1)}), bf16[16,32,512]{2,1,0:T(8,128)(2,1)S(1)}, u32[]{:S(2)}, u32[]{:S(2)}) async-start(bf16[16,32,512]{2,1,0:T(8,128)(2,1)} %shard_map.267), calls=%async_computation.3 | async-start | bytes 1048576 | tf_op jit(solution)/shard_map/all_to_all | solution.py:642
  95.6 22.1 %collective-permute-start.12 = (bf16[128,1024]{1,0:T(8,128)(2,1)}, bf16[128,1024]{1,0:T(8,128)(2,1)S(1)}, u32[]{:S(2)}, u32[]{:S(2)}) collective-permute-start(bf16[128,1024]{1,0:T(8,128)(2,1)} %get-tuple-element.66), channel_id=1, source_target_pairs={{0,2},{2,0},{1,3},{3,1},{4,6},{6,4},{5,7},{7,5},{8,10},{10,8},{9,1... | collective-permute-start | bytes 786440 | tf_op jit(solution)/shard_map/ppermute | solution.py:646
  100.9 23.9 %collective-permute-start.19 = (bf16[2,64,2048]{2,1,0:T(8,128)(2,1)}, bf16[2,64,2048]{2,1,0:T(8,128)(2,1)S(1)}, u32[]{:S(2)}, u32[]{:S(2)}) collective-permute-start(bf16[2,64,2048]{2,1,0:T(8,128)(2,1)} %shard_map.272), channel_id=1, source_target_pairs={{0,48},{16,0},{32,16},{48,32},{1,49},{17,1},{33,17},{49,33},{2,50}... | collective-permute-start | bytes 1572872 | tf_op jit(solution)/shard_map/ppermute | solution.py:650
  100.9 25.3 %collective-permute-start.17 = (bf16[2,64,2048]{2,1,0:T(8,128)(2,1)}, bf16[2,64,2048]{2,1,0:T(8,128)(2,1)S(1)}, u32[]{:S(2)}, u32[]{:S(2)}) collective-permute-start(bf16[2,64,2048]{2,1,0:T(8,128)(2,1)} %get-tuple-element.75), channel_id=1, source_target_pairs={{0,16},{16,32},{32,48},{48,0},{1,17},{17,33},{33,49},{49,1},{2,18}... | collective-permute-start | bytes 1572872 | tf_op jit(solution)/shard_map/ppermute | solution.py:650
  102.4 23.8 %collective-permute-start.18 = (bf16[2,64,2048]{2,1,0:T(8,128)(2,1)}, bf16[2,64,2048]{2,1,0:T(8,128)(2,1)S(1)}, u32[]{:S(2)}, u32[]{:S(2)}) collective-permute-start(bf16[2,64,2048]{2,1,0:T(8,128)(2,1)} %get-tuple-element.76), channel_id=1, source_target_pairs={{0,32},{16,48},{32,0},{48,16},{1,33},{17,49},{33,1},{49,17},{2,34}... | collective-permute-start | bytes 1572872 | tf_op jit(solution)/shard_map/ppermute | solution.py:650
  117.7 10.6 %copy-start.1 = (bf16[128,1024]{1,0:T(8,128)(2,1)}, bf16[128,1024]{1,0:T(8,128)(2,1)S(1)}, u32[]{:S(2)}) copy-start(bf16[128,1024]{1,0:T(8,128)(2,1)S(1)} %collective-permute-done.12.refs_1_.w1) | copy-start | bytes 786436
  117.8 14.8 %all-to-all-start.4 = ((bf16[16,96,128]{2,1,0:T(8,128)(2,1)}), bf16[16,96,128]{2,1,0:T(8,128)(2,1)S(1)}, u32[]{:S(2)}, u32[]{:S(2)}) async-start(bf16[16,96,128]{2,1,0:T(8,128)(2,1)} %shard_map.270), calls=%async_computation.4 | async-start | bytes 786432 | tf_op jit(solution)/shard_map/all_to_all | solution.py:642
  122.4 6.0 %collective-permute-start.14 = (bf16[2,64,128]{2,1,0:T(8,128)(2,1)S(1)}, bf16[2,64,128]{2,1,0:T(8,128)(2,1)S(1)}, u32[]{:S(2)}, u32[]{:S(2)}) collective-permute-start(bf16[2,64,128]{2,1,0:T(8,128)(2,1)S(1)} %get-tuple-element.71), channel_id=1, source_target_pairs={{0,16},{16,32},{32,48},{48,0},{1,17},{17,33},{33,49},{49,1},{2,18}... | collective-permute-start | bytes 98312 | tf_op jit(solution)/shard_map/ppermute | solution.py:650
  122.4 6.0 %collective-permute-start.15 = (bf16[2,64,128]{2,1,0:T(8,128)(2,1)S(1)}, bf16[2,64,128]{2,1,0:T(8,128)(2,1)S(1)}, u32[]{:S(2)}, u32[]{:S(2)}) collective-permute-start(bf16[2,64,128]{2,1,0:T(8,128)(2,1)S(1)} %get-tuple-element.72), channel_id=1, source_target_pairs={{0,32},{16,48},{32,0},{48,16},{1,33},{17,49},{33,1},{49,17},{2,34}... | collective-permute-start | bytes 98312 | tf_op jit(solution)/shard_map/ppermute | solution.py:650
  124.9 3.5 %collective-permute-start.16 = (bf16[2,64,128]{2,1,0:T(8,128)(2,1)S(1)}, bf16[2,64,128]{2,1,0:T(8,128)(2,1)S(1)}, u32[]{:S(2)}, u32[]{:S(2)}) collective-permute-start(bf16[2,64,128]{2,1,0:T(8,128)(2,1)S(1)} %get-tuple-element.73), channel_id=1, source_target_pairs={{0,48},{16,0},{32,16},{48,32},{1,49},{17,1},{33,17},{49,33},{2,50}... | collective-permute-start | bytes 98312 | tf_op jit(solution)/shard_map/ppermute | solution.py:650
  132.6 17.7 %all-to-all-start.5 = ((bf16[32,4,2176]{2,1,0:T(4,128)(2,1)}), bf16[32,4,2176]{2,1,0:T(4,128)(2,1)S(1)}, u32[]{:S(2)}, u32[]{:S(2)}) async-start(bf16[32,4,2176]{2,1,0:T(4,128)(2,1)} %shard_map.275), calls=%async_computation.5 | async-start | bytes 1114112 | tf_op jit(solution)/shard_map/all_to_all | solution.py:642
